TPU v7x, 32 devices: a whole 2x2x4 slice. The times are simulated.
32 devices in a mesh: ctx: 4 (over z), exp: 2 (over y), doc: 4 (over x, core).
Axes of the slice: x: 2, y: 2, z: 4, core: 2. Of those that a mesh axis runs over, the one named last changes fastest.
Arguments:
- projected: bfloat16 [2, 512, 4096], P(None, ('doc', 'ctx'), 'exp'), parts along dimension 1, may hold values from -6 to 6
- carried_tail: bfloat16 [12, 4096], P('doc', 'exp'), parts along dimension 0, may hold values from -6 to 6
- carried_state: float32 [64, 4096], P('doc', 'exp'), parts along dimension 0, may hold values from -6 to 6
- filter_taps: float32 [4, 4096], P(None, 'exp'), may hold values from -3 to 3
- filter_bias: float32 [4096], P('exp'), may hold values from -0.5 to 0.5
- select_weight: bfloat16 [160, 4096], P(None, 'exp'), may hold values from -0.09375 to 0.09375
- step_weight: bfloat16 [128, 4096], P(None, 'exp'), may hold values from -0.25 to 0.25
- step_bias: float32 [4096], P('exp'), may hold values from -7 to -2
- log_rate: float32 [16, 4096], P(None, 'exp'), may hold values from -1 to 1.5
- skip_gain: float32 [4096], P('exp'), may hold values from 0.5 to 1.5
- output_weight: bfloat16 [4096, 2048], P('exp', 'ctx'), may hold values from -0.09375 to 0.09375
- residual: bfloat16 [512, 2048], P(('doc', 'ctx', 'exp')), parts along dimension 0, may hold values from -6 to 6
- norm_gain: float32 [2048], replicated, may hold values from 0.5 to 1.5
- router: bfloat16 [2048, 4], replicated, may hold values from -0.125 to 0.125
- gate_weight: bfloat16 [57344, 2048], P(('ctx', 'exp')), may hold values from -0.125 to 0.125
- up_weight: bfloat16 [57344, 2048], P(('ctx', 'exp')), may hold values from -0.125 to 0.125
- down_weight: bfloat16 [57344, 2048], P(('ctx', 'exp')), may hold values from -0.046875 to 0.046875
- routes: int32 [512, 2], P(('doc', 'ctx', 'exp')), parts along dimension 0, may hold values from 0 to 3, all different within a row; in each aligned block of 16 rows (0 to 15, 16 to 31, ...) at most 10 rows name the same one
Outputs:
- layer_output: bfloat16 [512, 2048], P(('doc', 'ctx', 'exp')), parts along dimension 0
There are 4 independent parts, one for each index of `doc`. A program takes and returns all parts, laid end to end along the dimension named above; an argument that names none is the same for every part. Nothing has to cross between parts.
Inputs may be any that keep to these rules, and one draw needn't show every extreme that they name: `routes`: the two ids of a row differ; within the 16 rows of one device no id is named more than 10 times.
All inputs are finite; a program needn't handle non-finite values.
Results may differ from a plain program's by a relative error of at most 0.0085.
Values may be sent and summed in bfloat16 or wider, within the bound.
No kernel may reach another device: no remote copies, remote signals or barrier semaphores. Data moves between devices by JAX's collectives and lax.ppermute only.
A program may use at most 192 MiB of HBM per device.

v0:
```python
import math

import jax
import jax.numpy as jnp
from jax import lax
from jax.sharding import PartitionSpec as P

EXPERTS = 4
CAP = 10


def shifted(value, axis, steps):
    count = lax.axis_size(axis)
    first, last = (max(0, -steps), min(count, count - steps))
    return lax.ppermute(value, axis, [(source, source + steps) for source in range(first, last)])


def contract_cols(left, right):
    return lax.dot_general(
        left, right, (((1,), (1,)), ((), ())), preferred_element_type=jnp.float32
    )


def slot_matrix(chosen, expert_count, capacity):
    expert_ids = jnp.arange(expert_count, dtype=jnp.int32)
    named = jnp.any(chosen[:, :, None] == expert_ids[None, None, :], axis=1)
    running = jnp.cumsum(named.astype(jnp.int32), axis=0) - 1
    position = jnp.where(named, running, -1)
    slot_ids = jnp.arange(capacity, dtype=jnp.int32)
    return (jnp.transpose(position)[:, None, :] == slot_ids[None, :, None]).astype(jnp.float32)


def run_experts(piece, gate_weight, up_weight, down_weight):
    piece_shape = piece.shape
    slot_rows = piece.reshape(-1, piece_shape[-1])
    gate_act = contract_cols(slot_rows, gate_weight)
    up_act = contract_cols(slot_rows, up_weight)
    hidden = (jax.nn.silu(gate_act) * up_act).astype(jnp.bfloat16)
    partial_out = jnp.dot(hidden, down_weight, preferred_element_type=jnp.float32).astype(
        jnp.bfloat16
    )
    return partial_out.reshape(piece_shape)


def body(
    projected,
    carried_tail,
    carried_state,
    filter_taps,
    filter_bias,
    select_weight,
    step_weight,
    step_bias,
    log_rate,
    skip_gain,
    output_weight,
    residual,
    norm_gain,
    router,
    gate_weight,
    up_weight,
    down_weight,
    routes,
):
    x_input = projected[0]
    z_input = projected[1]
    block_tokens = x_input.shape[0]
    tap_count = filter_taps.shape[0]
    tail_rows = shifted(x_input[block_tokens - (tap_count - 1) :], "ctx", 1)
    at_start = lax.axis_index("ctx") == 0
    tail_rows = jnp.where(at_start, carried_tail, tail_rows)
    padded = jnp.concatenate([tail_rows, x_input], axis=0).astype(jnp.float32)
    filtered = filter_bias[None, :] + jnp.zeros(x_input.shape, jnp.float32)
    for offset in range(tap_count):
        filtered = filtered + filter_taps[offset][None, :] * padded[offset : offset + block_tokens]
    activated = jax.nn.silu(filtered).astype(jnp.bfloat16)
    projections = lax.psum(contract_cols(activated, select_weight), "exp")
    rank_size = step_weight.shape[0]
    state_size = log_rate.shape[0]
    channel_count = log_rate.shape[1]
    delta_low = projections[:, :rank_size].astype(jnp.bfloat16)
    step_size = jax.nn.softplus(
        jnp.dot(delta_low, step_weight, preferred_element_type=jnp.float32) + step_bias[None, :]
    )
    input_coef = projections[:, rank_size : rank_size + state_size]
    output_coef = projections[:, rank_size + state_size :]
    decay_rate = -jnp.exp(log_rate)
    active_values = activated.astype(jnp.float32)
    block_len = math.gcd(block_tokens, 16)
    block_count = block_tokens // block_len
    stacked = (
        step_size.reshape(block_count, block_len, channel_count),
        (step_size * active_values).reshape(block_count, block_len, channel_count),
        input_coef.reshape(block_count, block_len, state_size),
        output_coef.reshape(block_count, block_len, state_size),
    )

    def local_block(carry, block):
        cum_now, local_now = carry
        steps, scaled, in_rows, out_rows = block
        outputs = []
        for token in range(block_len):
            factor = jnp.exp(steps[token][None, :] * decay_rate)
            cum_now = factor * cum_now
            local_now = factor * local_now + scaled[token][None, :] * in_rows[token][:, None]
            outputs.append(jnp.sum(out_rows[token][:, None] * local_now, axis=0))
        return ((cum_now, local_now), jnp.stack(outputs))

    start_carry = (
        jnp.ones((state_size, channel_count), jnp.float32),
        jnp.zeros((state_size, channel_count), jnp.float32),
    )
    totals, local_out = lax.scan(local_block, start_carry, stacked)

    def relay_step(turn_index, entering):
        leaving = totals[0] * entering + totals[1]
        incoming = shifted(leaving, "ctx", 1)
        return jnp.where(at_start, carried_state, incoming)

    state_in = lax.fori_loop(0, lax.axis_size("ctx") - 1, relay_step, carried_state)

    def carry_block(entering, block):
        steps, scaled, in_rows, out_rows = block
        outputs = []
        for token in range(block_len):
            entering = jnp.exp(steps[token][None, :] * decay_rate) * entering
            outputs.append(jnp.sum(out_rows[token][:, None] * entering, axis=0))
        return (entering, jnp.stack(outputs))

    leftover, carried_out = lax.scan(carry_block, state_in, stacked)
    scan_out = (local_out + carried_out).reshape(block_tokens, channel_count)
    gated = (
        (scan_out + skip_gain[None, :] * active_values) * jax.nn.silu(z_input.astype(jnp.float32))
    ).astype(jnp.bfloat16)
    mixer_terms = jnp.dot(
        gated,
        lax.all_gather(output_weight, "ctx", axis=1, tiled=True),
        preferred_element_type=jnp.float32,
    )
    mixer_out = lax.psum_scatter(mixer_terms, "exp", scatter_dimension=0, tiled=True)
    mixed = (residual.astype(jnp.float32) + mixer_out).astype(jnp.bfloat16)
    mixed_values = mixed.astype(jnp.float32)
    mean_square = jnp.mean(mixed_values * mixed_values, axis=-1, keepdims=True) + 1e-06
    normed = (mixed_values * lax.rsqrt(mean_square) * norm_gain[None, :]).astype(jnp.bfloat16)
    logits = jnp.dot(normed, router, preferred_element_type=jnp.float32)
    expert_ids = jnp.arange(EXPERTS, dtype=jnp.int32)
    first_hot = (routes[:, 0:1] == expert_ids[None, :]).astype(jnp.float32)
    second_hot = (routes[:, 1:2] == expert_ids[None, :]).astype(jnp.float32)
    first_logit = jnp.sum(logits * first_hot, axis=1)
    second_logit = jnp.sum(logits * second_hot, axis=1)
    first_gate = 1.0 / (1.0 + jnp.exp(second_logit - first_logit))
    second_gate = 1.0 / (1.0 + jnp.exp(first_logit - second_logit))
    weights = first_gate[:, None] * first_hot + second_gate[:, None] * second_hot
    own_slots = slot_matrix(routes, EXPERTS, CAP)
    group_size = lax.axis_size("ctx") // EXPERTS
    model_width = normed.shape[1]
    slots = jnp.einsum(
        "ekt,td->ekd", own_slots.astype(jnp.bfloat16), normed, preferred_element_type=jnp.float32
    ).astype(jnp.bfloat16)
    outgoing = jnp.repeat(slots, group_size, axis=0)
    arrived = lax.all_to_all(outgoing, "ctx", split_axis=0, concat_axis=0, tiled=True)
    computed = run_experts(
        lax.all_gather(arrived[:, None], "exp", axis=1, tiled=True),
        gate_weight,
        up_weight,
        down_weight,
    )
    returned = lax.all_to_all(
        lax.all_to_all(computed, "ctx", split_axis=0, concat_axis=0, tiled=True),
        "exp",
        split_axis=1,
        concat_axis=1,
        tiled=True,
    )
    per_sender = jnp.sum(returned.astype(jnp.float32), axis=1)
    expert_sum = jnp.sum(per_sender.reshape(EXPERTS, group_size, CAP, model_width), axis=1)
    weighted_slots = own_slots * jnp.transpose(weights)[:, None, :]
    moe = jnp.einsum("ekt,ekd->td", weighted_slots, expert_sum, precision=lax.Precision.HIGHEST)
    return (mixed_values + moe).astype(jnp.bfloat16)


def solution(mesh):
    placed = (
        P(None, ("doc", "ctx"), "exp"),
        P("doc", "exp"),
        P("doc", "exp"),
        P(None, "exp"),
        P("exp"),
        P(None, "exp"),
        P(None, "exp"),
        P("exp"),
        P(None, "exp"),
        P("exp"),
        P("exp", "ctx"),
        P(("doc", "ctx", "exp"), None),
        P(),
        P(),
        P(("ctx", "exp"), None),
        P(("ctx", "exp"), None),
        P(("ctx", "exp"), None),
        P(("doc", "ctx", "exp"), None),
    )
    return jax.shard_map(
        body, mesh=mesh, in_specs=placed, out_specs=P(("doc", "ctx", "exp"), None), check_vma=False
    )
```

profile of v0, /device:TPU:0, one launch (start us, length us, event | category | flops | bytes accessed | tf_op | source)
XLA Modules:
  0.0 278.0 jit_solution(11041927078336322088)
XLA Ops:
  6.5 0.8 slice_bitcast_fusion.1
  7.4 4.9 %collective-permute-start.1 = (bf16[3,2048]{1,0:T(4,128)(2,1)S(1)}, bf16[3,2048]{1,0:T(4,128)(2,1)S(1)}, u32[]{:S(2)}, u32[]{:S(2)}) collective-permute-start(bf16[3,2048]{1,0:T(4,128)(2,1)S(1)} %slice_bitcast_fusion.1), channel_id=1, source_target_pairs={{0,8},{8,16},{16,24},{1,9},{9,17},{17,25},{2,10},{10,18},{18,26},{... | collective-permute-start | bytes 36872 | tf_op jit(solution)/shard_map/ppermute | solution.py:15
  12.4 0.9 slice_bitcast_fusion
  13.3 0.9 exponential_negate_fusion
  14.2 0.9 fusion.95
  15.2 0.9 copy.67
  16.1 0.7 broadcast_select_fusion.1
  16.9 0.9 multiply_convert_fusion
  17.8 0.3 fusion.96
  18.1 8.5 %psum.7 = f32[32,160]{1,0:T(8,128)S(1)} all-reduce(f32[32,160]{1,0:T(8,128)S(1)} %fusion.96), channel_id=1, replica_groups=mesh['ctx'=4,'exp'=2,'doc'=4] {'exp'}, use_global_device_ids=true, to_apply=%region_0.1 | all-reduce | flops 5120 | bytes 40960 | tf_op jit(solution)/shard_map/psum | solution.py:77
  26.7 1.4 convert_multiply_fusion.2
  28.1 5.2 %while.39 = (s32[]{:T(128)}, f32[16,2048]{1,0:T(8,128)S(1)}, f32[16,2048]{1,0:T(8,128)S(1)}, f32[2,16,2048]{2,1,0:T(8,128)S(1)}, f32[2,16,2048]{2,1,0:T(8,128)S(...) while((s32[]{:T(128)}, f32[16,2048]{1,0:T(8,128)S(1)}, ...), condition=%wide.region_18.19_spmd.clone, body=%wide.region_1.18_spmd.clone.sunk | while | flops 5832722 | bytes 4005161 | solution.py:113
  28.1 0.4 constant_dynamic-slice_fusion.99
  28.8 0.6 multiply_reduce_fusion.43
  29.4 0.3 multiply_reduce_fusion.47
  29.7 0.2 multiply_reduce_fusion.46
  29.9 0.2 multiply_reduce_fusion.45
  30.1 0.2 stack.122
  30.4 0.3 fusion.114
  30.7 0.4 constant_dynamic-slice_fusion.99
  31.4 0.6 multiply_reduce_fusion.43
  32.0 0.3 multiply_reduce_fusion.47
  32.3 0.2 multiply_reduce_fusion.46
  32.5 0.2 multiply_reduce_fusion.45
  32.7 0.2 stack.122
  32.9 0.3 fusion.114
  33.3 36.6 %while.37 = (s32[]{:T(128)}, f32[16,2048]{1,0:T(8,128)S(1)}, pred[]{:T(512)}, f32[16,2048]{1,0:T(8,128)S(1)}, f32[16,2048]{1,0:T(8,128)S(1)}, /*index=5*/f32[16,2048]{1,0:T(8,128)S(1)}, s32[]{:T(128)}) while((s32[]{:T(128)}, f32[16,2048]{1,0:T(8,128)S(1)}, pred[]{:T(512)}, f32[16,2048]{1,0:T(8,128)S(1)}, f32[16,2048]{1,0:T(8,128)S(1)}, ...), condition=%wide.region_20.21_spmd, body=%wide.region_19.20_spmd.sunk | while | flops 98306 | bytes 1441910 | solution.py:120
  33.3 2.8 %collective-permute-start = (f32[16,2048]{1,0:T(8,128)S(1)}, f32[16,2048]{1,0:T(8,128)S(1)}, u32[]{:S(2)}, u32[]{:S(2)}) collective-permute-start(f32[16,2048]{1,0:T(8,128)S(1)} %multiply_add_fusion.21), channel_id=1, source_target_pairs={{0,8},{8,16},{16,24},{1,9},{9,17},{17,25},{2,10},{10,18},{18,26},{... | collective-permute-start | bytes 393224 | tf_op jit(solution)/shard_map/while/body/eval_jaxpr/ppermute | solution.py:15
  36.1 5.4 %collective-permute-done = f32[16,2048]{1,0:T(8,128)S(1)} collective-permute-done((f32[16,2048]{1,0:T(8,128)S(1)}, f32[16,2048]{1,0:T(8,128)S(1)}, u32[]{:S(2)}, u32[]{:S(2)}) %collective-permute-start) | collective-permute-done | bytes 131104 | tf_op jit(solution)/shard_map/while/body/eval_jaxpr/ppermute | solution.py:15
  41.6 7.8 %collective-permute-start = (f32[16,2048]{1,0:T(8,128)S(1)}, f32[16,2048]{1,0:T(8,128)S(1)}, u32[]{:S(2)}, u32[]{:S(2)}) collective-permute-start(f32[16,2048]{1,0:T(8,128)S(1)} %multiply_add_fusion.21), channel_id=1, source_target_pairs={{0,8},{8,16},{16,24},{1,9},{9,17},{17,25},{2,10},{10,18},{18,26},{... | collective-permute-start | bytes 393224 | tf_op jit(solution)/shard_map/while/body/eval_jaxpr/ppermute | solution.py:15
  49.4 5.8 %collective-permute-done = f32[16,2048]{1,0:T(8,128)S(1)} collective-permute-done((f32[16,2048]{1,0:T(8,128)S(1)}, f32[16,2048]{1,0:T(8,128)S(1)}, u32[]{:S(2)}, u32[]{:S(2)}) %collective-permute-start) | collective-permute-done | bytes 131104 | tf_op jit(solution)/shard_map/while/body/eval_jaxpr/ppermute | solution.py:15
  55.3 8.5 %collective-permute-start = (f32[16,2048]{1,0:T(8,128)S(1)}, f32[16,2048]{1,0:T(8,128)S(1)}, u32[]{:S(2)}, u32[]{:S(2)}) collective-permute-start(f32[16,2048]{1,0:T(8,128)S(1)} %multiply_add_fusion.21), channel_id=1, source_target_pairs={{0,8},{8,16},{16,24},{1,9},{9,17},{17,25},{2,10},{10,18},{18,26},{... | collective-permute-start | bytes 393224 | tf_op jit(solution)/shard_map/while/body/eval_jaxpr/ppermute | solution.py:15
  63.8 6.0 %collective-permute-done = f32[16,2048]{1,0:T(8,128)S(1)} collective-permute-done((f32[16,2048]{1,0:T(8,128)S(1)}, f32[16,2048]{1,0:T(8,128)S(1)}, u32[]{:S(2)}, u32[]{:S(2)}) %collective-permute-start) | collective-permute-done | bytes 131104 | tf_op jit(solution)/shard_map/while/body/eval_jaxpr/ppermute | solution.py:15
  69.9 3.0 %while.38 = (s32[]{:T(128)}, f32[16,2048]{1,0:T(8,128)S(1)}, f32[2,16,2048]{2,1,0:T(8,128)S(1)}, f32[2,16,2048]{2,1,0:T(8,128)S(1)}, f32[16,2048]{1,0:T(8,128)S(...) while((s32[]{:T(128)}, f32[16,2048]{1,0:T(8,128)S(1)}, ...), condition=%wide.region_38.39_spmd, body=%wide.region_21.38_spmd.sunk | while | flops 2916369 | bytes 2862597 | solution.py:130
  70.2 0.3 multiply_reduce_fusion.40
  70.5 0.3 multiply_reduce_fusion.42
  70.8 0.3 multiply_reduce_fusion.41
  71.1 0.2 stack.121
  71.7 0.3 multiply_reduce_fusion.40
  72.0 0.3 multiply_reduce_fusion.42
  72.3 0.3 multiply_reduce_fusion.41
  72.6 0.2 stack.121
  73.0 0.3 fusion.71
  73.3 93.3 %all-gather.3.cloned.1.call-done = bf16[2048,2048]{1,0:T(8,128)(2,1)} async-done(((bf16[2048,512]{1,0:T(8,128)(2,1)}), bf16[2048,2048]{1,0:T(8,128)(2,1)}) %all-gather.3.cloned.1.call-update) | async-done | bytes 8388624 | tf_op jit(solution)/shard_map/all_gather | solution.py:137
  166.6 5.6 %fusion.97 = f32[32,2048]{1,0:T(8,128)} fusion(bf16[32,2048]{1,0:T(8,128)(2,1)S(1)} %fusion.71, bf16[2048,2048]{1,0:T(8,128)(2,1)} %all-gather.3.cloned.1.call-done), kind=kOutput, calls=%fused_computation.317 | convolution fusion | flops 268435456 | bytes 8781824 | tf_op jit(solution)/shard_map/dot_general | solution.py:135
  172.6 13.7 %reduce-scatter.2.cloned.1.call-done = f32[16,2048]{1,0:T(8,128)} async-done(((f32[32,2048]{1,0:T(8,128)}), f32[16,2048]{1,0:T(8,128)}) %reduce-scatter.2.cloned.1.call-update) | async-done | bytes 131088 | tf_op jit(solution)/shard_map/reduce_scatter | solution.py:140
  186.3 1.0 fusion.79
  187.4 0.6 copy-done.3
  188.0 0.3 convolution_convert_fusion.1
  188.3 13.3 %all_to_all.15 = bf16[4,10,2048]{2,1,0:T(8,128)(2,1)S(1)} all-to-all(bf16[4,10,2048]{2,1,0:T(8,128)(2,1)S(1)} %convolution_convert_fusion.1), channel_id=1, replica_groups=mesh['ctx'=4,'exp'=2,'doc'=4] {'ctx'}, dimensions={0} | all-to-all | bytes 327680 | tf_op jit(solution)/shard_map/all_to_all | solution.py:161
  201.7 6.2 %all-gather = bf16[4,20,2048]{2,0,1:T(4,128)(2,1)S(1)} all-gather(bf16[4,10,2048]{2,0,1:T(4,128)(2,1)S(1)} %copy.44), channel_id=2, replica_groups=mesh['ctx'=4,'exp'=2,'doc'=4] {'exp'}, dimensions={1}, use_global_device_ids=true | all-gather | bytes 491520 | tf_op jit(solution)/shard_map/all_gather | solution.py:163
  207.9 0.2 copy.45
  208.2 14.3 %fusion.98 = f32[80,7168]{1,0:T(8,128)S(1)} fusion(bf16[80,2048]{1,0:T(8,128)(2,1)S(1)} %reshape.367, bf16[7168,2048]{1,0:T(8,128)(2,1)} %param.38), kind=kOutput, calls=%fused_computation.318 | convolution fusion | flops 2348810240 | bytes 31981568 | tf_op jit(solution)/shard_map/dot_general | solution.py:19
  222.5 23.1 %convolution_convert_fusion = bf16[80,2048]{1,0:T(8,128)(2,1)} fusion(bf16[7168,2048]{1,0:T(8,128)(2,1)} %param.40, bf16[80,2048]{1,0:T(8,128)(2,1)S(1)} %reshape.367, bf16[7168,2048]{1,0:T(8,128)(2,1)} %param.39, f32[80,7168]{1,0:T(8,128)S(1)} %fusion.98), kind=kOutput, calls=%fused_computation.247 | convolution fusion | flops 4701224960 | bytes 61669376 | tf_op jit(solution)/shard_map/dot_general | solution.py:39
  245.6 1.1 reshape.368
  246.7 1.0 copy.46
  247.7 3.5 %all-to-all-start.1 = ((bf16[4,2,10,2048]{3,1,2,0:T(2,128)(2,1)}), bf16[4,2,10,2048]{3,1,2,0:T(2,128)(2,1)S(1)}, u32[]{:S(2)}, u32[]{:S(2)}) async-start(bf16[4,2,10,2048]{3,1,2,0:T(2,128)(2,1)} %copy.46), calls=%async_computation.2 | async-start | bytes 655360 | tf_op jit(solution)/shard_map/all_to_all | solution.py:169
  251.2 0.2 select_reduce_fusion.1
  251.5 8.1 %all-to-all-done.1 = bf16[4,2,10,2048]{3,1,2,0:T(2,128)(2,1)S(1)} async-done(((bf16[4,2,10,2048]{3,1,2,0:T(2,128)(2,1)}), bf16[4,2,10,2048]{3,1,2,0:T(2,128)(2,1)S(1)}, u32[]{:S(2)}, u32[]{:S(2)}) %all-to-all-start.1) | async-done | bytes 327712 | tf_op jit(solution)/shard_map/all_to_all | solution.py:169
  259.5 1.0 copy.47
  260.5 3.5 %all-to-all-start.2 = ((bf16[4,2,10,2048]{3,0,2,1:T(4,128)(2,1)}), bf16[4,2,10,2048]{3,0,2,1:T(4,128)(2,1)S(1)}, u32[]{:S(2)}, u32[]{:S(2)}) async-start(bf16[4,2,10,2048]{3,0,2,1:T(4,128)(2,1)} %copy.47), calls=%async_computation.3 | async-start | bytes 655360 | tf_op jit(solution)/shard_map/all_to_all | solution.py:168
  264.0 5.5 %all-to-all-done.2 = bf16[4,2,10,2048]{3,0,2,1:T(4,128)(2,1)S(1)} async-done(((bf16[4,2,10,2048]{3,0,2,1:T(4,128)(2,1)}), bf16[4,2,10,2048]{3,0,2,1:T(4,128)(2,1)S(1)}, u32[]{:S(2)}, u32[]{:S(2)}) %all-to-all-start.2) | async-done | bytes 327712 | tf_op jit(solution)/shard_map/all_to_all | solution.py:168
  269.5 0.2 convert_reduce_fusion
  269.7 1.5 fusion.66
  (68 shorter events, 2.2 us)
Async XLA Ops:
  6.5 11.3 %copy-start = (bf16[160,2048]{1,0:T(8,128)(2,1)S(1)}, bf16[160,2048]{1,0:T(8,128)(2,1)}, u32[]{:S(2)}) copy-start(bf16[160,2048]{1,0:T(8,128)(2,1)} %param.29) | copy-start | bytes 1966084
  6.5 160.1 %all-gather.3.cloned.1.call-start = ((), (), s32[]{:S(2)}) async-start(), calls=%async_computation.4 | async-start | bytes 10485760 | tf_op jit(solution)/shard_map/all_gather | solution.py:137
  7.4 8.8 %collective-permute-start.1 = (bf16[3,2048]{1,0:T(4,128)(2,1)S(1)}, bf16[3,2048]{1,0:T(4,128)(2,1)S(1)}, u32[]{:S(2)}, u32[]{:S(2)}) collective-permute-start(bf16[3,2048]{1,0:T(4,128)(2,1)S(1)} %slice_bitcast_fusion.1), channel_id=1, source_target_pairs={{0,8},{8,16},{16,24},{1,9},{9,17},{17,25},{2,10},{10,18},{18,26},{... | collective-permute-start | bytes 36872 | tf_op jit(solution)/shard_map/ppermute | solution.py:15
  12.3 174.0 %reduce-scatter.2.cloned.1.call-start = ((), (), s32[]{:S(2)}) async-start(), calls=%async_computation.5 | async-start | bytes 393216 | tf_op jit(solution)/shard_map/reduce_scatter | solution.py:140
  28.1 5.2 %copy-start.2 = (f32[16,2048]{1,0:T(8,128)S(1)}, f32[16,2048]{1,0:T(8,128)}, u32[]{:S(2)}) copy-start(f32[16,2048]{1,0:T(8,128)} %param.26) | copy-start | bytes 393220
  33.3 8.3 %collective-permute-start = (f32[16,2048]{1,0:T(8,128)S(1)}, f32[16,2048]{1,0:T(8,128)S(1)}, u32[]{:S(2)}, u32[]{:S(2)}) collective-permute-start(f32[16,2048]{1,0:T(8,128)S(1)} %multiply_add_fusion.21), channel_id=1, source_target_pairs={{0,8},{8,16},{16,24},{1,9},{9,17},{17,25},{2,10},{10,18},{18,26},{... | collective-permute-start | bytes 393224 | tf_op jit(solution)/shard_map/while/body/eval_jaxpr/ppermute | solution.py:15
  41.6 13.6 %collective-permute-start = (f32[16,2048]{1,0:T(8,128)S(1)}, f32[16,2048]{1,0:T(8,128)S(1)}, u32[]{:S(2)}, u32[]{:S(2)}) collective-permute-start(f32[16,2048]{1,0:T(8,128)S(1)} %multiply_add_fusion.21), channel_id=1, source_target_pairs={{0,8},{8,16},{16,24},{1,9},{9,17},{17,25},{2,10},{10,18},{18,26},{... | collective-permute-start | bytes 393224 | tf_op jit(solution)/shard_map/while/body/eval_jaxpr/ppermute | solution.py:15
  55.3 14.5 %collective-permute-start = (f32[16,2048]{1,0:T(8,128)S(1)}, f32[16,2048]{1,0:T(8,128)S(1)}, u32[]{:S(2)}, u32[]{:S(2)}) collective-permute-start(f32[16,2048]{1,0:T(8,128)S(1)} %multiply_add_fusion.21), channel_id=1, source_target_pairs={{0,8},{8,16},{16,24},{1,9},{9,17},{17,25},{2,10},{10,18},{18,26},{... | collective-permute-start | bytes 393224 | tf_op jit(solution)/shard_map/while/body/eval_jaxpr/ppermute | solution.py:15
  69.9 3.0 %copy-start.5 = (bf16[2,32,2048]{2,1,0:T(8,128)(2,1)S(1)}, bf16[2,32,2048]{2,1,0:T(8,128)(2,1)}, u32[]{:S(2)}) copy-start(bf16[2,32,2048]{2,1,0:T(8,128)(2,1)} %param.24) | copy-start | bytes 786436
  69.9 3.0 %copy-start.7 = (f32[2048]{0:T(1024)S(1)}, f32[2048]{0:T(1024)}, u32[]{:S(2)}) copy-start(f32[2048]{0:T(1024)} %param.28) | copy-start | bytes 24580
  69.9 3.0 %copy-start.8 = (f32[2048]{0:T(1024)S(1)}, f32[2048]{0:T(1024)}, u32[]{:S(2)}) copy-start(f32[2048]{0:T(1024)} %param.33) | copy-start | bytes 24580
  73.0 99.3 %copy-start.10 = (s32[16,2]{0,1:T(2,128)S(1)}, s32[16,2]{0,1:T(2,128)}, u32[]{:S(2)}) copy-start(s32[16,2]{0,1:T(2,128)} %param.41) | copy-start | bytes 388
  73.0 113.4 %copy-start.6 = (bf16[16,2048]{1,0:T(8,128)(2,1)S(1)}, bf16[16,2048]{1,0:T(8,128)(2,1)}, u32[]{:S(2)}) copy-start(bf16[16,2048]{1,0:T(8,128)(2,1)} %param.35) | copy-start | bytes 196612
  73.0 115.0 %copy-start.9 = (f32[2048]{0:T(1024)S(1)}, f32[2048]{0:T(1024)}, u32[]{:S(2)}) copy-start(f32[2048]{0:T(1024)} %param.36) | copy-start | bytes 24580
  187.4 0.6 copy-start.3
  222.5 28.7 %copy-start.4 = (bf16[16,2048]{1,0:T(8,128)(2,1)S(1)}, bf16[16,2048]{1,0:T(8,128)(2,1)}, u32[]{:S(2)}) copy-start(bf16[16,2048]{1,0:T(8,128)(2,1)} %copy-done.3) | copy-start | bytes 196612
  222.5 28.7 %copy-start.11 = (bf16[2048,4]{0,1:T(4,128)(2,1)S(1)}, bf16[2048,4]{0,1:T(4,128)(2,1)}, u32[]{:S(2)}) copy-start(bf16[2048,4]{0,1:T(4,128)(2,1)} %param.37) | copy-start | bytes 49156
  222.5 48.6 %copy-start.1 = (bf16[160,2048]{1,0:T(8,128)(2,1)S(1)}, bf16[160,2048]{1,0:T(8,128)(2,1)}, u32[]{:S(2)}) copy-start(bf16[160,2048]{1,0:T(8,128)(2,1)} %param.29) | copy-start | bytes 1966084
  247.7 11.8 %all-to-all-start.1 = ((bf16[4,2,10,2048]{3,1,2,0:T(2,128)(2,1)}), bf16[4,2,10,2048]{3,1,2,0:T(2,128)(2,1)S(1)}, u32[]{:S(2)}, u32[]{:S(2)}) async-start(bf16[4,2,10,2048]{3,1,2,0:T(2,128)(2,1)} %copy.46), calls=%async_computation.2 | async-start | bytes 655360 | tf_op jit(solution)/shard_map/all_to_all | solution.py:169
  260.5 9.0 %all-to-all-start.2 = ((bf16[4,2,10,2048]{3,0,2,1:T(4,128)(2,1)}), bf16[4,2,10,2048]{3,0,2,1:T(4,128)(2,1)S(1)}, u32[]{:S(2)}, u32[]{:S(2)}) async-start(bf16[4,2,10,2048]{3,0,2,1:T(4,128)(2,1)} %copy.47), calls=%async_computation.3 | async-start | bytes 655360 | tf_op jit(solution)/shard_map/all_to_all | solution.py:168
Sparse Core Ops, SparseCore 0:
  12.5 154.0 all-gather.2
  172.4 13.9 reduce-scatter.1
where the time goes:
time: 279 us; the launch traced here: 278 us
  waiting for transfers between devices  138 us (49%)
  matrix products  46.7 us (17%)
  starting transfers between devices  31 us (11%)
  blocking collectives  27.9 us (10%)
  between operations  13.8 us (5%)
  local copies, waits for them, and re-layouts  10.7 us (4%)
  other arithmetic  9.63 us (3%)
    all_gather x1, waiting for transfers between devices, body(): lax.all_gather(output_weight, 'ctx', axis=1, tiled=True)  93.3 us
    ppermute x4, starting transfers between devices, shifted(): lax.ppermute(value, axis, [(source, source + steps) for source in range(f...  24 us
    dot_general x1, matrix products, run_experts(): jnp.dot(hidden, down_weight, preferred_element_type=jnp.float32)  23.1 us
    ppermute x4, waiting for transfers between devices, shifted(): lax.ppermute(value, axis, [(source, source + steps) for source in range(f...  17.3 us
    dot_general x2, matrix products, contract_cols(): lax.dot_general(left, right, (((1,), (1,)), ((), ())), preferred_element_...  14.6 us
    reduce_scatter x1, waiting for transfers between devices, body(): lax.psum_scatter(mixer_terms, 'exp', scatter_dimension=0, tiled=True)  13.7 us
    all_to_all x1, blocking collectives, body(): lax.all_to_all(outgoing, 'ctx', split_axis=0, concat_axis=0, tiled=True)  13.3 us
    psum x1, blocking collectives, body(): projections = lax.psum(contract_cols(activated, select_weight), 'exp')  8.48 us
  transfers between devices with their start and end apart: 8, of which 7 were waited for; matrix products, arithmetic and copies ran while one was open for 6% of the time, Pallas kernels for 0%

commit v1 on v0

v1 whole, which is shorter than its diff:
```python
import functools
import math

import jax
import jax.numpy as jnp
from jax import lax
from jax.experimental import pallas as pl
from jax.experimental.pallas import tpu as pltpu
from jax.sharding import PartitionSpec as P

EXPERTS = 4
LANES = 128
FEW = 4
LOG2E = 1.4426950408889634
VMEM = pltpu.VMEM
SMEM = pltpu.SMEM
F32 = jnp.float32
BF16 = jnp.bfloat16


def contract_last(left, right):
    return lax.dot_general(left, right, (((1,), (1,)), ((), ())), preferred_element_type=F32)


def rotate(value, axis, steps):
    count = lax.axis_size(axis)
    return lax.ppermute(value, axis, [(i, (i + steps) % count) for i in range(count)])


def ring_places(axis):
    count = lax.axis_size(axis)
    if count > FEW:
        return jnp.zeros((1,), jnp.int32)
    me = lax.axis_index(axis)
    return jnp.stack([lax.rem(me + count - s, count) for s in range(count)]).astype(jnp.int32)


def spread(make, axis, join):
    count = lax.axis_size(axis)
    me = lax.axis_index(axis)
    if count <= FEW:
        return [make(me)] + [rotate(make(lax.rem(me + s, count)), axis, s) for s in range(1, count)]
    stacked = jnp.stack([make(jnp.int32(k)) for k in range(count)])
    moved = lax.all_to_all(stacked, axis, split_axis=0, concat_axis=0, tiled=True)
    return [jnp.concatenate([moved[k] for k in range(count)], axis=join)]


def pair_sum(value, axis):
    if lax.axis_size(axis) == 2:
        return [value, rotate(value, axis, 1)]
    total = lax.psum(value.astype(F32), axis).astype(value.dtype)
    return [total, jnp.zeros_like(total)]


def activate_kernel(count, places, tail, taps, bias, select, *refs):
    pieces, (active, proj, padded) = refs[:count], refs[count:]
    rows = pieces[0].shape[0]
    tap_count = taps.shape[0]
    padded[0:8, :] = tail[...]
    for index in range(count):
        start = pl.multiple_of(8 + places[index] * rows, 8)
        padded[pl.ds(start, rows), :] = pieces[index][...].astype(F32)
    tokens = active.shape[0]
    step = 32

    def block(number, carry):
        base = pl.multiple_of(number * step, step)
        window = padded[pl.ds(base, step + 8), :]
        total = jnp.broadcast_to(bias[...], (step, bias.shape[1]))
        for k in range(tap_count):
            offset = 8 - (tap_count - 1) + k
            total = total + taps[k : k + 1, :] * window[offset : offset + step, :]
        value = total / (1.0 + jnp.exp(-total))
        active[pl.ds(base, step), :] = value.astype(BF16)
        return carry

    lax.fori_loop(0, tokens // step, block, 0)
    for number in range(tokens // LANES):
        cut = slice(number * LANES, (number + 1) * LANES)
        proj[:, cut] = contract_last(select[...], active[cut, :])


def activate(places, pieces, tail, taps, bias, select):
    count = len(pieces)
    tokens = count * pieces[0].shape[0]
    channels = pieces[0].shape[1]
    return pl.pallas_call(
        functools.partial(activate_kernel, count),
        out_shape=(
            jax.ShapeDtypeStruct((tokens, channels), BF16),
            jax.ShapeDtypeStruct((select.shape[0], tokens), F32),
        ),
        in_specs=[pl.BlockSpec(memory_space=SMEM)] + [pl.BlockSpec(memory_space=VMEM)] * (4 + count),
        out_specs=(pl.BlockSpec(memory_space=VMEM),) * 2,
        scratch_shapes=[VMEM((tokens + 8, channels), F32)],
        compiler_params=pltpu.CompilerParams(vmem_limit_bytes=24 << 20),
        cost_estimate=pl.CostEstimate(
            flops=2 * tokens * channels * select.shape[0],
            bytes_accessed=4 * tokens * channels,
            transcendentals=tokens * channels,
        ),
        name="activate",
    )(places, tail, taps, bias, select, *pieces)


def scan_kernel(
    count, columns, places, parity, own, other, active, step_weight, step_bias, log_rate, skip_gain,
    state_in, out_weight, *refs,
):
    pieces = refs[:count]
    base_out, send_out, routes_out = refs[count : count + 3]
    sums, steps, scaled, decay, state, gated, coef, sem = refs[count + 3 :]
    tokens, channels = active.shape
    rank = step_weight.shape[0]
    state_size = log_rate.shape[0]
    folds = channels // LANES
    group = min(folds, 8)
    sums[...] = own[...] + other[...]
    copy = pltpu.make_async_copy(sums.at[pl.ds(rank, 2 * state_size), :], coef, sem)
    copy.start()

    for s8 in range(state_size // 8):
        for j in range(folds):
            lanes = slice(j * LANES, (j + 1) * LANES)
            there = slice((s8 * folds + j) * 8, (s8 * folds + j) * 8 + 8)
            decay[there, :] = jnp.exp(log_rate[s8 * 8 : s8 * 8 + 8, lanes]) * (-LOG2E)
            state[there, :] = state_in[s8 * 8 : s8 * 8 + 8, lanes]

    def fold_rows(row, first):
        return pl.ds((row // 8) * (folds * 8) + row % 8 + first * 8, group, stride=8)

    for number in range(tokens // LANES):
        cut = slice(number * LANES, (number + 1) * LANES)
        low = jnp.transpose(sums[0:rank, cut]).astype(BF16)
        width = min(channels, 256)
        for w in range(channels // width):
            lanes = slice(w * width, (w + 1) * width)
            raw = jnp.dot(low, step_weight[:, lanes], preferred_element_type=F32) + step_bias[:, lanes]
            size = jnp.maximum(raw, 0.0) + jnp.log1p(jnp.exp(-jnp.abs(raw)))
            times = size * active[cut, lanes].astype(F32)
            for i in range(LANES // 8):
                for j in range(width // LANES):
                    block = (number * LANES // 8 + i) * folds + w * (width // LANES) + j
                    there = slice(block * 8, block * 8 + 8)
                    part = (slice(i * 8, i * 8 + 8), slice(j * LANES, (j + 1) * LANES))
                    steps[there, :] = size[part]
                    scaled[there, :] = times[part]
    copy.wait()

    for first in range(0, folds, group):
        rates = [decay[fold_rows(s, first), :] for s in range(state_size)]
        start = tuple(state[fold_rows(s, first), :] for s in range(state_size))

        def eight(number, held):
            base = number * (folds * 8) + first * 8
            held = list(held)
            for r in range(8):
                token = number * 8 + r
                rows = pl.ds(base + r, group, stride=8)
                size, times = steps[rows, :], scaled[rows, :]
                total = None
                for s in range(state_size):
                    held[s] = jnp.exp2(size * rates[s]) * held[s] + times * coef[s, token]
                    term = held[s] * coef[state_size + s, token]
                    total = term if total is None else total + term
                steps[rows, :] = total
            return tuple(held)

        lax.fori_loop(0, tokens // 8, eight, start)

    rows = pieces[0].shape[0]
    tile = 16
    for index in range(count):
        begin = pl.multiple_of(places[index] * rows, tile)
        routes_out[pl.ds(begin, rows), :] = pieces[index][:, channels + columns :]

        def gate(number, carry):
            local = pl.multiple_of(number * tile, tile)
            here = pl.multiple_of(begin + local, tile)
            for j in range(folds):
                lanes = slice(j * LANES, (j + 1) * LANES)
                found = []
                for half in range(2):
                    block = pl.multiple_of((here // 8 + half) * (folds * 8) + j * 8, 8)
                    found.append(steps[pl.ds(block, 8), :])
                value = jnp.concatenate(found, axis=0)
                act = active[pl.ds(here, tile), lanes].astype(F32)
                z = pieces[index][pl.ds(local, tile), lanes].astype(F32)
                value = (value + skip_gain[:, lanes] * act) * (z / (1.0 + jnp.exp(-z)))
                gated[pl.ds(here, tile), lanes] = value.astype(BF16)
            return carry

        lax.fori_loop(0, rows // tile, gate, 0)

    step = LANES
    for number in range(tokens // step):
        cut = slice(number * step, (number + 1) * step)
        part = jnp.dot(gated[cut, :], out_weight[...], preferred_element_type=F32)
        sent = part.astype(BF16)
        send_out[cut, :] = sent
        base_out[cut, :] = sent.astype(F32)
    for index in range(count):
        begin = pl.multiple_of(places[index] * rows, tile)
        here = pl.ds(begin, rows)
        base_out[here, :] += pieces[index][:, channels : channels + columns].astype(F32)


def scan(places, parity, own, other, active, step_weight, step_bias, log_rate, skip_gain, state_in, out_weight, pieces):
    tokens, channels = active.shape
    columns = out_weight.shape[1]
    count = len(pieces)
    state_size = log_rate.shape[0]
    folded = (state_size * channels // LANES, LANES)
    return pl.pallas_call(
        functools.partial(scan_kernel, count, columns),
        out_shape=(
            jax.ShapeDtypeStruct((tokens, columns), F32),
            jax.ShapeDtypeStruct((tokens, columns), BF16),
            jax.ShapeDtypeStruct((tokens, LANES), BF16),
        ),
        in_specs=[pl.BlockSpec(memory_space=SMEM)] * 2 + [pl.BlockSpec(memory_space=VMEM)] * (9 + count),
        out_specs=(pl.BlockSpec(memory_space=VMEM),) * 3,
        scratch_shapes=[
            VMEM(own.shape, F32),
            VMEM((tokens * channels // LANES, LANES), F32),
            VMEM((tokens * channels // LANES, LANES), F32),
            VMEM(folded, F32),
            VMEM(folded, F32),
            VMEM((tokens, channels), BF16),
            SMEM((2 * state_size, tokens), F32),
            pltpu.SemaphoreType.DMA,
        ],
        compiler_params=pltpu.CompilerParams(vmem_limit_bytes=32 << 20),
        cost_estimate=pl.CostEstimate(
            flops=8 * tokens * channels * state_size,
            bytes_accessed=8 * tokens * channels,
            transcendentals=tokens * channels * state_size,
        ),
        name="scan",
    )(
        places, parity, own, other, active, step_weight, step_bias, log_rate, skip_gain, state_in,
        out_weight, *pieces,
    )


def expert_kernel(count, sends, places, targets, expert, gain, router, routes, gate, up, down, *refs):
    pieces = refs[:count]
    outs = refs[count : count + sends]
    own_rows = refs[count + sends]
    normed, total, weight = refs[count + sends + 1 : count + sends + 4]
    mixed = pieces[0] if count == 1 else refs[-1]
    number = pl.program_id(0)
    tokens, width = normed.shape
    chunk = LANES

    @pl.when(number == 0)
    def _():
        columns = pieces[0].shape[1]
        for index in range(count if count > 1 else 0):
            start = pl.multiple_of(places[index] * columns, LANES)
            mixed[:, pl.ds(start, columns)] = pieces[index][...]
        total[...] = jnp.zeros_like(total)
        for c in range(tokens // chunk):
            cut = slice(c * chunk, (c + 1) * chunk)
            value = mixed[cut, :].astype(F32)
            square = jnp.mean(value * value, axis=-1, keepdims=True) + 1e-06
            scaled = (value * lax.rsqrt(square) * gain[...]).astype(BF16)
            normed[cut, :] = scaled
            logits = contract_last(scaled, router[...])
            first = routes[cut, 0:1].astype(F32)
            second = routes[cut, 1:2].astype(F32)
            ids = lax.broadcasted_iota(jnp.int32, logits.shape, 1).astype(F32)
            first_logit = jnp.sum(jnp.where(ids == first, logits, 0.0), axis=1, keepdims=True)
            second_logit = jnp.sum(jnp.where(ids == second, logits, 0.0), axis=1, keepdims=True)
            mine = expert[0].astype(F32)
            first_gate = jnp.where(first == mine, 1.0 / (1.0 + jnp.exp(second_logit - first_logit)), 0.0)
            second_gate = jnp.where(second == mine, 1.0 / (1.0 + jnp.exp(first_logit - second_logit)), 0.0)
            weight[cut, :] = jnp.broadcast_to(first_gate + second_gate, (chunk, LANES))

    for c in range(tokens // chunk):
        cut = slice(c * chunk, (c + 1) * chunk)
        gate_act = contract_last(normed[cut, :], gate[...])
        up_act = contract_last(normed[cut, :], up[...])
        hidden = (gate_act / (1.0 + jnp.exp(-gate_act)) * up_act).astype(BF16)
        total[cut, :] += jnp.dot(hidden, down[...], preferred_element_type=F32)

    @pl.when(number == pl.num_programs(0) - 1)
    def _():
        rows = outs[0].shape[0]
        for index in range(sends):
            here = pl.ds(pl.multiple_of(targets[index] * rows, 16), rows)
            outs[index][...] = (total[here, :] * weight[here, 0:1]).astype(BF16)
        rows = own_rows.shape[0]
        here = pl.ds(pl.multiple_of(targets[sends] * rows, 16), rows)
        own_rows[...] = mixed[here, :]


def experts(places, targets, expert, gain, router, routes, gate, up, down, pieces, sends, rows, own):
    count = len(pieces)
    tokens = pieces[0].shape[0]
    hidden, width = gate.shape
    block = math.gcd(hidden, 512)
    whole = pl.BlockSpec(memory_space=VMEM)
    weights = pl.BlockSpec((block, width), lambda i: (i, 0))
    return pl.pallas_call(
        functools.partial(expert_kernel, count, sends),
        grid=(hidden // block,),
        out_shape=tuple([jax.ShapeDtypeStruct((rows, width), BF16)] * sends + [jax.ShapeDtypeStruct((own, width), BF16)]),
        in_specs=[pl.BlockSpec(memory_space=SMEM)] * 3 + [whole] * 3 + [weights] * 3 + [whole] * count,
        out_specs=tuple([whole] * (sends + 1)),
        scratch_shapes=[
            VMEM((tokens, width), BF16),
            VMEM((tokens, width), F32),
            VMEM((tokens, LANES), F32),
        ]
        + ([VMEM((tokens, width), BF16)] if count > 1 else []),
        compiler_params=pltpu.CompilerParams(vmem_limit_bytes=56 << 20),
        cost_estimate=pl.CostEstimate(
            flops=6 * tokens * hidden * width,
            bytes_accessed=6 * hidden * width,
            transcendentals=tokens * hidden,
        ),
        name="experts",
    )(places, targets, expert, gain, router, routes, gate, up, down, *pieces)


def body(
    projected,
    carried_tail,
    carried_state,
    filter_taps,
    filter_bias,
    select_weight,
    step_weight,
    step_bias,
    log_rate,
    skip_gain,
    output_weight,
    residual,
    norm_gain,
    router,
    gate_weight,
    up_weight,
    down_weight,
    routes,
):
    ctx, exp = lax.axis_size("ctx"), lax.axis_size("exp")
    ctx_at, exp_at = lax.axis_index("ctx"), lax.axis_index("exp")
    places = ring_places("ctx")
    x_input, z_input = projected[0], projected[1]
    own, width = residual.shape
    columns = output_weight.shape[1]

    x_pieces = spread(lambda k: x_input, "ctx", 0)
    extra = jnp.concatenate([residual, jnp.pad(routes.astype(BF16), ((0, 0), (0, LANES - 2)))], axis=1)
    if exp == 2:
        partner = rotate(extra, "exp", 1)
        extra = jnp.where(
            exp_at == 0,
            jnp.concatenate([extra, partner], axis=0),
            jnp.concatenate([partner, extra], axis=0),
        )
    else:
        extra = lax.all_gather(extra, "exp", axis=0, tiled=True)

    def bundle(k):
        piece = lax.dynamic_slice_in_dim(extra, k * columns, columns, axis=1)
        return jnp.concatenate([z_input, piece, extra[:, width:]], axis=1)

    z_pieces = spread(bundle, "ctx", 0)

    tail = jnp.pad(carried_tail.astype(F32), ((8 - carried_tail.shape[0], 0), (0, 0)))
    active, proj = activate(places, x_pieces, tail, filter_taps, filter_bias[None, :], select_weight)
    own_proj, other_proj = pair_sum(proj, "exp")
    base, sent, all_routes = scan(
        places,
        exp_at.astype(jnp.int32)[None],
        own_proj,
        other_proj,
        active,
        step_weight,
        step_bias[None, :],
        log_rate,
        skip_gain[None, :],
        carried_state,
        output_weight,
        z_pieces,
    )
    if exp == 2:
        mixed = (base + rotate(sent, "exp", 1).astype(F32)).astype(BF16)
    else:
        mixed = (base - sent.astype(F32) + lax.psum(sent.astype(F32), "exp")).astype(BF16)
    mixed_pieces = spread(lambda k: mixed, "ctx", 1)

    parts = ctx * exp
    me = ctx_at * exp + exp_at
    direct = parts <= 8
    sends = parts if direct else 1
    targets = [lax.rem(me + s, parts) for s in range(parts)] if direct else [jnp.int32(0)]
    targets = jnp.stack(targets + [me]).astype(jnp.int32)
    expert = (ctx_at // (ctx // EXPERTS)).astype(jnp.int32)[None]
    tokens = mixed_pieces[0].shape[0]
    results = experts(
        places,
        targets,
        expert,
        norm_gain[None, :],
        jnp.pad(router.T, ((0, 16 - EXPERTS), (0, 0))),
        all_routes,
        gate_weight,
        up_weight,
        down_weight,
        mixed_pieces,
        sends,
        own if direct else tokens,
        own,
    )
    outs, mine = results[:-1], results[-1]
    total = mine.astype(F32)
    axes = ("ctx", "exp")
    if direct:
        arrived = [outs[0]]
        for s in range(1, parts):
            arrived.append(lax.ppermute(outs[s], axes, [(i, (i + s) % parts) for i in range(parts)]))
        for piece in arrived:
            total = total + piece.astype(F32)
    else:
        moved = lax.all_to_all(outs[0], axes, split_axis=0, concat_axis=0, tiled=True)
        total = total + jnp.sum(moved.reshape(parts, own, width).astype(F32), axis=0)
    return total.astype(BF16)


def solution(mesh):
    placed = (
        P(None, ("doc", "ctx"), "exp"),
        P("doc", "exp"),
        P("doc", "exp"),
        P(None, "exp"),
        P("exp"),
        P(None, "exp"),
        P(None, "exp"),
        P("exp"),
        P(None, "exp"),
        P("exp"),
        P("exp", "ctx"),
        P(("doc", "ctx", "exp"), None),
        P(),
        P(),
        P(("ctx", "exp"), None),
        P(("ctx", "exp"), None),
        P(("ctx", "exp"), None),
        P(("doc", "ctx", "exp"), None),
    )
    return jax.shard_map(
        body, mesh=mesh, in_specs=placed, out_specs=P(("doc", "ctx", "exp"), None), check_vma=False
    )
```

time: 279 us -> 123 us (0.44)
  waiting for transfers between devices: 138 us -> 24.1 us
  Pallas kernels: 0 us -> 50.9 us
  matrix products: 46.7 us -> 0 us
  blocking collectives: 27.9 us -> 0 us
  between operations: 13.8 us -> 0.18 us
  other arithmetic: 9.63 us -> 4.95 us
    all_gather x1 -> x0, waiting for transfers between devices: 93.3 us -> none  [body(): lax.all_gather(output_weight, 'ctx', axis=1, tiled=True)]
    pallas_call x0 -> x3, Pallas kernels: none -> 50.9 us  [the longest x1 38.6 us: experts(): pl.pallas_call(functools.partial(expert_kernel, count, sends), grid=(hidd...]
    dot_general x8 -> x0, matrix products: 46.7 us -> none  [the longest x1 23.1 us: run_experts(): jnp.dot(hidden, down_weight, preferred_element_type=jnp.float32)]
    reduce_scatter x1 -> x0, waiting for transfers between devices: 13.7 us -> none  [body(): lax.psum_scatter(mixer_terms, 'exp', scatter_dimension=0, tiled=True)]
    all_to_all x2 -> x0, waiting for transfers between devices: 13.6 us -> none  [the longest x1 8.06 us: body(): lax.all_to_all(computed, 'ctx', split_axis=0, concat_axis=0, tiled=True)]
    all_to_all x1 -> x0, blocking collectives: 13.3 us -> none  [body(): lax.all_to_all(outgoing, 'ctx', split_axis=0, concat_axis=0, tiled=True)]
    psum x1 -> x0, blocking collectives: 8.48 us -> none  [body(): projections = lax.psum(contract_cols(activated, select_weight), 'exp')]
    unnamed x25 -> x30, local copies, waits for them, and re-layouts: 1.59 us -> 9.06 us
  transfers between devices with their start and end apart: 8 -> 19, of which waited for: 7 -> 11; matrix products, arithmetic and copies ran while one was open for 6% -> 4% of each run, Pallas kernels for 0% -> 2%
where the time goes in v1:
time: 123 us; the launch traced here: 122 us
  Pallas kernels  50.9 us (41%)
  starting transfers between devices  30.1 us (24%)
  waiting for transfers between devices  24.1 us (20%)
  local copies, waits for them, and re-layouts  12.1 us (10%)
  other arithmetic  4.95 us (4%)
    pallas_call x1, Pallas kernels, experts(): pl.pallas_call(functools.partial(expert_kernel, count, sends), grid=(hidd...  38.6 us
    ppermute x12, waiting for transfers between devices, rotate(): lax.ppermute(value, axis, [(i, (i + steps) % count) for i in range(count)])  20.5 us
    ppermute x12, starting transfers between devices, rotate(): lax.ppermute(value, axis, [(i, (i + steps) % count) for i in range(count)])  19 us
    ppermute x7, starting transfers between devices, body(): lax.ppermute(outs[s], axes, [(i, (i + s) % parts) for i in range(parts)])  11.1 us
    pallas_call x1, Pallas kernels, scan(): pl.pallas_call(functools.partial(scan_kernel, count, columns), out_shape=...  10.2 us
    unnamed x30, local copies, waits for them, and re-layouts  9.06 us
    ppermute x7, waiting for transfers between devices, body(): lax.ppermute(outs[s], axes, [(i, (i + s) % parts) for i in range(parts)])  3.65 us
  transfers between devices with their start and end apart: 19, of which 11 were waited for; matrix products, arithmetic and copies ran while one was open for 4% of the time, Pallas kernels for 2%

profile of v1, /device:TPU:0, one launch (start us, length us, event | category | flops | bytes accessed | tf_op | source)
XLA Modules:
  0.0 122.4 jit_solution(10620657422493103501)
XLA Ops:
  0.0 1.0 slice_bitcast_fusion
  1.0 5.1 %collective-permute-start.2 = (bf16[32,2048]{1,0:T(8,128)(2,1)S(1)}, bf16[32,2048]{1,0:T(8,128)(2,1)S(1)}, u32[]{:S(2)}, u32[]{:S(2)}) collective-permute-start(bf16[32,2048]{1,0:T(8,128)(2,1)S(1)} %get-tuple-element.34.refs_0_), channel_id=1, source_target_pairs={{0,24},{8,0},{16,8},{24,16},{1,25},{9,1},{17,9},{25,17},{2,26},{10... | collective-permute-start | bytes 393224 | tf_op jit(solution)/shard_map/ppermute | solution.py:27
  6.1 0.0 collective-permute-start.1
  6.1 1.0 collective-permute-start
  7.1 0.7 convert_element_type.46
  7.8 0.1 copy.20
  7.9 0.8 pad_maximum_fusion.8
  8.7 1.5 %collective-permute-start.4 = (bf16[16,2176]{1,0:T(8,128)(2,1)S(1)}, bf16[16,2176]{1,0:T(8,128)(2,1)S(1)}, u32[]{:S(2)}, u32[]{:S(2)}) collective-permute-start(bf16[16,2176]{1,0:T(8,128)(2,1)S(1)} %pad_maximum_fusion.8), channel_id=1, source_target_pairs={{0,4},{4,0},{1,5},{5,1},{2,6},{6,2},{3,7},{7,3},{8,12},{12,8},{9,1... | collective-permute-start | bytes 208904 | tf_op jit(solution)/shard_map/ppermute | solution.py:27
  10.3 0.7 pad_convert_fusion.tail
  11.0 2.0 %collective-permute-done.4 = bf16[16,2176]{1,0:T(8,128)(2,1)S(1)} collective-permute-done((bf16[16,2176]{1,0:T(8,128)(2,1)S(1)}, bf16[16,2176]{1,0:T(8,128)(2,1)S(1)}, u32[]{:S(2)}, u32[]{:S(2)}) %collective-permute-start.4) | collective-permute-done | bytes 69664 | tf_op jit(solution)/shard_map/ppermute | solution.py:27
  13.1 0.9 maximum_select_fusion
  14.0 0.1 pad_maximum_fusion
  14.1 2.9 %collective-permute-start.7 = (bf16[32,2688]{1,0:T(8,128)(2,1)S(1)}, bf16[32,2688]{1,0:T(8,128)(2,1)S(1)}, u32[]{:S(2)}, u32[]{:S(2)}) collective-permute-start(bf16[32,2688]{1,0:T(8,128)(2,1)S(1)} %get-tuple-element.35), channel_id=1, source_target_pairs={{0,24},{8,0},{16,8},{24,16},{1,25},{9,1},{17,9},{25,17},{2,26},{10... | collective-permute-start | bytes 516104 | tf_op jit(solution)/shard_map/ppermute | solution.py:27
  17.0 0.0 collective-permute-start.5
  17.0 0.0 collective-permute-done.2.refs_3_
  17.0 1.1 collective-permute-start.6
  18.1 0.1 pad_add_fusion.places
  18.2 0.0 collective-permute-done.1.refs_2_
  18.2 0.0 collective-permute-done.refs_1_
  18.2 0.0 copy-start
  18.2 1.1 copy-done
  19.3 0.8 copy-done.2
  20.0 0.7 copy-done.3
  20.7 2.1 %activate.1 = (bf16[128,2048]{1,0:T(8,128)(2,1)S(1)}, f32[160,128]{1,0:T(8,128)S(1)}) custom-call(s32[4]{0:T(128)S(1)} %pad_add_fusion.places, f32[8,2048]{1,0:T(8,128)S(1)} %pad_convert_fusion.tail, f32[4,2048]{1,0:T(4,128)S(1)} %copy-done.2, f32[1,2048]{1,0:T(1,128)S(1)} %bitcast.24, bf16[160,2048]{1,0:T(8,128)(2,1)S(1)} %copy-done, ...), custom_call_target="tpu_custom_call" | custom-call | flops 83886080 | bytes 1048576 | tf_op jit(solution)/shard_map/activate/pallas_call | solution.py:87
  22.9 1.6 %collective-permute-start.3 = (f32[160,128]{1,0:T(8,128)S(1)}, f32[160,128]{1,0:T(8,128)S(1)}, u32[]{:S(2)}, u32[]{:S(2)}) collective-permute-start(f32[160,128]{1,0:T(8,128)S(1)} %get-tuple-element.19.own), channel_id=1, source_target_pairs={{0,4},{4,0},{1,5},{5,1},{2,6},{6,2},{3,7},{7,3},{8,12},{12,8},{9,1... | collective-permute-start | bytes 245768 | tf_op jit(solution)/shard_map/ppermute | solution.py:27
  24.4 2.9 %collective-permute-done.3.other = f32[160,128]{1,0:T(8,128)S(1)} collective-permute-done((f32[160,128]{1,0:T(8,128)S(1)}, f32[160,128]{1,0:T(8,128)S(1)}, u32[]{:S(2)}, u32[]{:S(2)}) %collective-permute-start.3) | collective-permute-done | bytes 81952 | tf_op jit(solution)/shard_map/ppermute | solution.py:27
  27.4 0.0 collective-permute-done.7.refs_3_
  27.4 0.0 collective-permute-done.5.refs_1_
  27.4 4.7 %collective-permute-done.6.refs_2_ = bf16[32,2688]{1,0:T(8,128)(2,1)S(1)} collective-permute-done((bf16[32,2688]{1,0:T(8,128)(2,1)S(1)}, bf16[32,2688]{1,0:T(8,128)(2,1)S(1)}, u32[]{:S(2)}, u32[]{:S(2)}) %collective-permute-start.6) | collective-permute-done | bytes 172064 | tf_op jit(solution)/shard_map/ppermute | solution.py:27
  32.0 1.6 %copy-done.5 = bf16[2048,512]{1,0:T(8,128)(2,1)S(1)} copy-done((bf16[2048,512]{1,0:T(8,128)(2,1)S(1)}, bf16[2048,512]{1,0:T(8,128)(2,1)}, u32[]{:S(2)}) %copy-start.5) | copy-done | bytes 2097176
  33.6 1.0 copy-done.6
  34.7 0.9 copy-done.7
  35.6 0.9 copy-done.8
  36.5 0.7 copy-done.9
  37.2 0.7 copy-done.10
  37.9 10.2 %scan.1 = (f32[128,512]{1,0:T(8,128)S(1)}, bf16[128,512]{1,0:T(8,128)(2,1)S(1)}, bf16[128,128]{1,0:T(8,128)(2,1)S(1)}) custom-call(s32[4]{0:T(128)S(1)} %pad_add_fusion.places, s32[1]{0:T(128)} %bitcast.16.parity, f32[160,128]{1,0:T(8,128)S(1)} %get-tuple-element.19.own, f32[160,128]{1,0:T(8,128)S(1)} %collective-permute-done.3.other, ...), custom_call_target="tpu_custom_call" | custom-call | flops 33554432 | bytes 2097152 | tf_op jit(solution)/shard_map/scan/pallas_call | solution.py:214
  48.1 1.6 %collective-permute-start.8 = (bf16[128,512]{1,0:T(8,128)(2,1)S(1)}, bf16[128,512]{1,0:T(8,128)(2,1)S(1)}, u32[]{:S(2)}, u32[]{:S(2)}) collective-permute-start(bf16[128,512]{1,0:T(8,128)(2,1)S(1)} %get-tuple-element.23), channel_id=1, source_target_pairs={{0,4},{4,0},{1,5},{5,1},{2,6},{6,2},{3,7},{7,3},{8,12},{12,8},{9,1... | collective-permute-start | bytes 393224 | tf_op jit(solution)/shard_map/ppermute | solution.py:27
  49.7 3.4 %collective-permute-done.8 = bf16[128,512]{1,0:T(8,128)(2,1)S(1)} collective-permute-done((bf16[128,512]{1,0:T(8,128)(2,1)S(1)}, bf16[128,512]{1,0:T(8,128)(2,1)S(1)}, u32[]{:S(2)}, u32[]{:S(2)}) %collective-permute-start.8) | collective-permute-done | bytes 131104 | tf_op jit(solution)/shard_map/ppermute | solution.py:27
  53.2 3.6 %collective-permute-start.11 = (bf16[128,512]{1,0:T(8,128)(2,1)S(1)}, bf16[128,512]{1,0:T(8,128)(2,1)S(1)}, u32[]{:S(2)}, u32[]{:S(2)}) collective-permute-start(bf16[128,512]{1,0:T(8,128)(2,1)S(1)} %add_convert_fusion.refs_0_), channel_id=1, source_target_pairs={{0,24},{8,0},{16,8},{24,16},{1,25},{9,1},{17,9},{25,17},{2,26},{10... | collective-permute-start | bytes 393224 | tf_op jit(solution)/shard_map/ppermute | solution.py:27
  56.8 0.0 collective-permute-start.10
  56.8 0.6 collective-permute-start.9
  57.4 1.4 %pad.14.router = bf16[16,2048]{1,0:T(8,128)(2,1)} pad(bf16[4,2048]{1,0:T(4,128)(2,1)} %bitcast.27, bf16[]{:T(256)} %constant.78.clone.1), padding=0_12x0_0 | pad | bytes 81922 | tf_op jit(solution)/shard_map/jit(_pad)/pad | solution.py:408
  58.8 0.6 stack.59.targets
  59.4 1.2 %collective-permute-done.11.refs_3_ = bf16[128,512]{1,0:T(8,128)(2,1)S(1)} collective-permute-done((bf16[128,512]{1,0:T(8,128)(2,1)S(1)}, bf16[128,512]{1,0:T(8,128)(2,1)S(1)}, u32[]{:S(2)}, u32[]{:S(2)}) %collective-permute-start.11) | collective-permute-done | bytes 131104 | tf_op jit(solution)/shard_map/ppermute | solution.py:27
  60.7 6.1 %collective-permute-done.10.refs_2_ = bf16[128,512]{1,0:T(8,128)(2,1)S(1)} collective-permute-done((bf16[128,512]{1,0:T(8,128)(2,1)S(1)}, bf16[128,512]{1,0:T(8,128)(2,1)S(1)}, u32[]{:S(2)}, u32[]{:S(2)}) %collective-permute-start.10) | collective-permute-done | bytes 131104 | tf_op jit(solution)/shard_map/ppermute | solution.py:27
  66.8 0.0 collective-permute-done.9.refs_1_
  66.8 0.6 copy-done.13
  67.5 0.0 copy-done.14
  67.5 38.6 %experts.1 = (bf16[16,2048]{1,0:T(8,128)(2,1)}, bf16[16,2048]{1,0:T(8,128)(2,1)}, bf16[16,2048]{1,0:T(8,128)(2,1)}, bf16[16,2048]{1,0:T(8,128)(2,1)}, bf16[16,20...) custom-call(s32[4]{0:T(128)} %copy-done.4, ...), custom_call_target="tpu_custom_call" | custom-call | flops 11274289152 | bytes 88080384 | tf_op jit(solution)/shard_map/experts/pallas_call | solution.py:305
  106.1 1.5 %collective-permute-start.12 = (bf16[16,2048]{1,0:T(8,128)(2,1)}, bf16[16,2048]{1,0:T(8,128)(2,1)S(1)}, u32[]{:S(2)}, u32[]{:S(2)}) collective-permute-start(bf16[16,2048]{1,0:T(8,128)(2,1)} %get-tuple-element.26), channel_id=1, source_target_pairs={{0,4},{4,8},{8,12},{12,16},{16,20},{20,24},{24,28},{28,0},{1,5},{5... | collective-permute-start | bytes 196616 | tf_op jit(solution)/shard_map/ppermute | solution.py:424
  107.7 0.0 collective-permute-start.13
  107.7 2.0 %collective-permute-start.14 = (bf16[16,2048]{1,0:T(8,128)(2,1)}, bf16[16,2048]{1,0:T(8,128)(2,1)S(1)}, u32[]{:S(2)}, u32[]{:S(2)}) collective-permute-start(bf16[16,2048]{1,0:T(8,128)(2,1)} %get-tuple-element.28), channel_id=1, source_target_pairs={{0,12},{4,16},{8,20},{12,24},{16,28},{20,0},{24,4},{28,8},{1,13},{... | collective-permute-start | bytes 196616 | tf_op jit(solution)/shard_map/ppermute | solution.py:424
  109.7 1.9 %collective-permute-start.15 = (bf16[16,2048]{1,0:T(8,128)(2,1)}, bf16[16,2048]{1,0:T(8,128)(2,1)S(1)}, u32[]{:S(2)}, u32[]{:S(2)}) collective-permute-start(bf16[16,2048]{1,0:T(8,128)(2,1)} %get-tuple-element.29), channel_id=1, source_target_pairs={{0,16},{4,20},{8,24},{12,28},{16,0},{20,4},{24,8},{28,12},{1,17},{... | collective-permute-start | bytes 196616 | tf_op jit(solution)/shard_map/ppermute | solution.py:424
  111.6 1.9 %collective-permute-start.16 = (bf16[16,2048]{1,0:T(8,128)(2,1)}, bf16[16,2048]{1,0:T(8,128)(2,1)S(1)}, u32[]{:S(2)}, u32[]{:S(2)}) collective-permute-start(bf16[16,2048]{1,0:T(8,128)(2,1)} %get-tuple-element.30), channel_id=1, source_target_pairs={{0,20},{4,24},{8,28},{12,0},{16,4},{20,8},{24,12},{28,16},{1,21},{... | collective-permute-start | bytes 196616 | tf_op jit(solution)/shard_map/ppermute | solution.py:424
  113.4 0.6 collective-permute-done.12
  114.0 2.4 %collective-permute-start.17 = (bf16[16,2048]{1,0:T(8,128)(2,1)}, bf16[16,2048]{1,0:T(8,128)(2,1)S(1)}, u32[]{:S(2)}, u32[]{:S(2)}) collective-permute-start(bf16[16,2048]{1,0:T(8,128)(2,1)} %get-tuple-element.31), channel_id=1, source_target_pairs={{0,24},{4,28},{8,0},{12,4},{16,8},{20,12},{24,16},{28,20},{1,25},{... | collective-permute-start | bytes 196616 | tf_op jit(solution)/shard_map/ppermute | solution.py:424
  116.4 0.0 collective-permute-done.13
  116.4 1.4 %collective-permute-start.18 = (bf16[16,2048]{1,0:T(8,128)(2,1)}, bf16[16,2048]{1,0:T(8,128)(2,1)S(1)}, u32[]{:S(2)}, u32[]{:S(2)}) collective-permute-start(bf16[16,2048]{1,0:T(8,128)(2,1)} %get-tuple-element.32), channel_id=1, source_target_pairs={{0,28},{4,0},{8,4},{12,8},{16,12},{20,16},{24,20},{28,24},{1,29},{... | collective-permute-start | bytes 196616 | tf_op jit(solution)/shard_map/ppermute | solution.py:424
  117.8 0.7 collective-permute-done.14
  118.4 0.3 collective-permute-done.15
  118.7 0.0 collective-permute-done.16
  118.7 0.4 collective-permute-done.17
  119.1 1.8 %collective-permute-done.18 = bf16[16,2048]{1,0:T(8,128)(2,1)S(1)} collective-permute-done((bf16[16,2048]{1,0:T(8,128)(2,1)}, bf16[16,2048]{1,0:T(8,128)(2,1)S(1)}, u32[]{:S(2)}, u32[]{:S(2)}) %collective-permute-start.18) | collective-permute-done | bytes 65568 | tf_op jit(solution)/shard_map/ppermute | solution.py:424
  120.8 1.6 %add_convert_fusion.1 = bf16[16,2048]{1,0:T(8,128)(2,1)} fusion(bf16[16,2048]{1,0:T(8,128)(2,1)S(1)} %collective-permute-done.18, bf16[16,2048]{1,0:T(8,128)(2,1)S(1)} %collective-permute-done.17, bf16[16,2048]{1,0:T(8,128)(2,1)S(1)} %collective-permute-done.16, bf16[16,2048]{1,0:T(8,128)(2,1)S(1)} %collective-permute-done.15, ...), kind=kLoop, calls=%fused_computation.10 | loop fusion | flops 589824 | bytes 655360 | tf_op jit(solution)/shard_map/convert_element_type | solution.py:430
  (22 shorter events, 0.1 us)
Async XLA Ops:
  1.0 16.0 %collective-permute-start.2 = (bf16[32,2048]{1,0:T(8,128)(2,1)S(1)}, bf16[32,2048]{1,0:T(8,128)(2,1)S(1)}, u32[]{:S(2)}, u32[]{:S(2)}) collective-permute-start(bf16[32,2048]{1,0:T(8,128)(2,1)S(1)} %get-tuple-element.34.refs_0_), channel_id=1, source_target_pairs={{0,24},{8,0},{16,8},{24,16},{1,25},{9,1},{17,9},{25,17},{2,26},{10... | collective-permute-start | bytes 393224 | tf_op jit(solution)/shard_map/ppermute | solution.py:27
  6.1 12.1 %collective-permute-start.1 = (bf16[32,2048]{1,0:T(8,128)(2,1)S(1)}, bf16[32,2048]{1,0:T(8,128)(2,1)S(1)}, u32[]{:S(2)}, u32[]{:S(2)}) collective-permute-start(bf16[32,2048]{1,0:T(8,128)(2,1)S(1)} %get-tuple-element.34.refs_0_), channel_id=1, source_target_pairs={{0,16},{8,24},{16,0},{24,8},{1,17},{9,25},{17,1},{25,9},{2,18},{10... | collective-permute-start | bytes 393224 | tf_op jit(solution)/shard_map/ppermute | solution.py:27
  6.1 12.1 %collective-permute-start = (bf16[32,2048]{1,0:T(8,128)(2,1)S(1)}, bf16[32,2048]{1,0:T(8,128)(2,1)S(1)}, u32[]{:S(2)}, u32[]{:S(2)}) collective-permute-start(bf16[32,2048]{1,0:T(8,128)(2,1)S(1)} %get-tuple-element.34.refs_0_), channel_id=1, source_target_pairs={{0,8},{8,16},{16,24},{24,0},{1,9},{9,17},{17,25},{25,1},{2,10},{10... | collective-permute-start | bytes 393224 | tf_op jit(solution)/shard_map/ppermute | solution.py:27
  8.7 4.3 %collective-permute-start.4 = (bf16[16,2176]{1,0:T(8,128)(2,1)S(1)}, bf16[16,2176]{1,0:T(8,128)(2,1)S(1)}, u32[]{:S(2)}, u32[]{:S(2)}) collective-permute-start(bf16[16,2176]{1,0:T(8,128)(2,1)S(1)} %pad_maximum_fusion.8), channel_id=1, source_target_pairs={{0,4},{4,0},{1,5},{5,1},{2,6},{6,2},{3,7},{7,3},{8,12},{12,8},{9,1... | collective-permute-start | bytes 208904 | tf_op jit(solution)/shard_map/ppermute | solution.py:27
  14.1 13.3 %collective-permute-start.7 = (bf16[32,2688]{1,0:T(8,128)(2,1)S(1)}, bf16[32,2688]{1,0:T(8,128)(2,1)S(1)}, u32[]{:S(2)}, u32[]{:S(2)}) collective-permute-start(bf16[32,2688]{1,0:T(8,128)(2,1)S(1)} %get-tuple-element.35), channel_id=1, source_target_pairs={{0,24},{8,0},{16,8},{24,16},{1,25},{9,1},{17,9},{25,17},{2,26},{10... | collective-permute-start | bytes 516104 | tf_op jit(solution)/shard_map/ppermute | solution.py:27
  17.0 10.4 %collective-permute-start.5 = (bf16[32,2688]{1,0:T(8,128)(2,1)S(1)}, bf16[32,2688]{1,0:T(8,128)(2,1)S(1)}, u32[]{:S(2)}, u32[]{:S(2)}) collective-permute-start(bf16[32,2688]{1,0:T(8,128)(2,1)S(1)} %get-tuple-element.36), channel_id=1, source_target_pairs={{0,8},{8,16},{16,24},{24,0},{1,9},{9,17},{17,25},{25,1},{2,10},{10... | collective-permute-start | bytes 516104 | tf_op jit(solution)/shard_map/ppermute | solution.py:27
  17.0 15.1 %collective-permute-start.6 = (bf16[32,2688]{1,0:T(8,128)(2,1)S(1)}, bf16[32,2688]{1,0:T(8,128)(2,1)S(1)}, u32[]{:S(2)}, u32[]{:S(2)}) collective-permute-start(bf16[32,2688]{1,0:T(8,128)(2,1)S(1)} %get-tuple-element.37), channel_id=1, source_target_pairs={{0,16},{8,24},{16,0},{24,8},{1,17},{9,25},{17,1},{25,9},{2,18},{10... | collective-permute-start | bytes 516104 | tf_op jit(solution)/shard_map/ppermute | solution.py:27
  18.2 48.6 %copy-start.4 = (s32[4]{0:T(128)}, s32[4]{0:T(128)S(1)}, u32[]{:S(2)}) copy-start(s32[4]{0:T(128)S(1)} %pad_add_fusion.places) | copy-start | bytes 52
  18.2 1.1 copy-start
  19.3 0.8 copy-start.2
  20.0 0.7 copy-start.3
  22.9 4.5 %collective-permute-start.3 = (f32[160,128]{1,0:T(8,128)S(1)}, f32[160,128]{1,0:T(8,128)S(1)}, u32[]{:S(2)}, u32[]{:S(2)}) collective-permute-start(f32[160,128]{1,0:T(8,128)S(1)} %get-tuple-element.19.own), channel_id=1, source_target_pairs={{0,4},{4,0},{1,5},{5,1},{2,6},{6,2},{3,7},{7,3},{8,12},{12,8},{9,1... | collective-permute-start | bytes 245768 | tf_op jit(solution)/shard_map/ppermute | solution.py:27
  32.0 1.6 %copy-start.5 = (bf16[2048,512]{1,0:T(8,128)(2,1)S(1)}, bf16[2048,512]{1,0:T(8,128)(2,1)}, u32[]{:S(2)}) copy-start(bf16[2048,512]{1,0:T(8,128)(2,1)} %out_weight.1) | copy-start | bytes 6291460
  33.6 1.0 copy-start.6
  34.7 0.9 copy-start.7
  35.6 0.9 copy-start.8
  36.5 0.7 copy-start.9
  37.2 0.7 copy-start.10
  48.1 5.1 %copy-start.1 = (bf16[128,128]{1,0:T(8,128)(2,1)}, bf16[128,128]{1,0:T(8,128)(2,1)S(1)}, u32[]{:S(2)}) copy-start(bf16[128,128]{1,0:T(8,128)(2,1)S(1)} %get-tuple-element.21.routes) | copy-start | bytes 98308
  48.1 5.0 %collective-permute-start.8 = (bf16[128,512]{1,0:T(8,128)(2,1)S(1)}, bf16[128,512]{1,0:T(8,128)(2,1)S(1)}, u32[]{:S(2)}, u32[]{:S(2)}) collective-permute-start(bf16[128,512]{1,0:T(8,128)(2,1)S(1)} %get-tuple-element.23), channel_id=1, source_target_pairs={{0,4},{4,0},{1,5},{5,1},{2,6},{6,2},{3,7},{7,3},{8,12},{12,8},{9,1... | collective-permute-start | bytes 393224 | tf_op jit(solution)/shard_map/ppermute | solution.py:27
  53.2 13.6 %copy-start.11 = (bf16[128,512]{1,0:T(8,128)(2,1)}, bf16[128,512]{1,0:T(8,128)(2,1)S(1)}, u32[]{:S(2)}) copy-start(bf16[128,512]{1,0:T(8,128)(2,1)S(1)} %add_convert_fusion.refs_0_) | copy-start | bytes 393220
  53.2 7.4 %collective-permute-start.11 = (bf16[128,512]{1,0:T(8,128)(2,1)S(1)}, bf16[128,512]{1,0:T(8,128)(2,1)S(1)}, u32[]{:S(2)}, u32[]{:S(2)}) collective-permute-start(bf16[128,512]{1,0:T(8,128)(2,1)S(1)} %add_convert_fusion.refs_0_), channel_id=1, source_target_pairs={{0,24},{8,0},{16,8},{24,16},{1,25},{9,1},{17,9},{25,17},{2,26},{10... | collective-permute-start | bytes 393224 | tf_op jit(solution)/shard_map/ppermute | solution.py:27
  56.8 10.0 %collective-permute-start.10 = (bf16[128,512]{1,0:T(8,128)(2,1)S(1)}, bf16[128,512]{1,0:T(8,128)(2,1)S(1)}, u32[]{:S(2)}, u32[]{:S(2)}) collective-permute-start(bf16[128,512]{1,0:T(8,128)(2,1)S(1)} %add_convert_fusion.refs_0_), channel_id=1, source_target_pairs={{0,16},{8,24},{16,0},{24,8},{1,17},{9,25},{17,1},{25,9},{2,18},{10... | collective-permute-start | bytes 393224 | tf_op jit(solution)/shard_map/ppermute | solution.py:27
  56.8 10.0 %collective-permute-start.9 = (bf16[128,512]{1,0:T(8,128)(2,1)S(1)}, bf16[128,512]{1,0:T(8,128)(2,1)S(1)}, u32[]{:S(2)}, u32[]{:S(2)}) collective-permute-start(bf16[128,512]{1,0:T(8,128)(2,1)S(1)} %add_convert_fusion.refs_0_), channel_id=1, source_target_pairs={{0,8},{8,16},{16,24},{24,0},{1,9},{9,17},{17,25},{25,1},{2,10},{10... | collective-permute-start | bytes 393224 | tf_op jit(solution)/shard_map/ppermute | solution.py:27
  60.7 6.2 %copy-start.12 = (bf16[128,512]{1,0:T(8,128)(2,1)}, bf16[128,512]{1,0:T(8,128)(2,1)S(1)}, u32[]{:S(2)}) copy-start(bf16[128,512]{1,0:T(8,128)(2,1)S(1)} %collective-permute-done.11.refs_3_) | copy-start | bytes 393220
  66.8 0.7 copy-start.13
  66.8 0.7 copy-start.14
  106.1 7.9 %collective-permute-start.12 = (bf16[16,2048]{1,0:T(8,128)(2,1)}, bf16[16,2048]{1,0:T(8,128)(2,1)S(1)}, u32[]{:S(2)}, u32[]{:S(2)}) collective-permute-start(bf16[16,2048]{1,0:T(8,128)(2,1)} %get-tuple-element.26), channel_id=1, source_target_pairs={{0,4},{4,8},{8,12},{12,16},{16,20},{20,24},{24,28},{28,0},{1,5},{5... | collective-permute-start | bytes 196616 | tf_op jit(solution)/shard_map/ppermute | solution.py:424
  107.7 8.7 %collective-permute-start.13 = (bf16[16,2048]{1,0:T(8,128)(2,1)}, bf16[16,2048]{1,0:T(8,128)(2,1)S(1)}, u32[]{:S(2)}, u32[]{:S(2)}) collective-permute-start(bf16[16,2048]{1,0:T(8,128)(2,1)} %get-tuple-element.27), channel_id=1, source_target_pairs={{0,8},{4,12},{8,16},{12,20},{16,24},{20,28},{24,0},{28,4},{1,9},{5... | collective-permute-start | bytes 196616 | tf_op jit(solution)/shard_map/ppermute | solution.py:424
  107.7 10.7 %collective-permute-start.14 = (bf16[16,2048]{1,0:T(8,128)(2,1)}, bf16[16,2048]{1,0:T(8,128)(2,1)S(1)}, u32[]{:S(2)}, u32[]{:S(2)}) collective-permute-start(bf16[16,2048]{1,0:T(8,128)(2,1)} %get-tuple-element.28), channel_id=1, source_target_pairs={{0,12},{4,16},{8,20},{12,24},{16,28},{20,0},{24,4},{28,8},{1,13},{... | collective-permute-start | bytes 196616 | tf_op jit(solution)/shard_map/ppermute | solution.py:424
  109.7 9.0 %collective-permute-start.15 = (bf16[16,2048]{1,0:T(8,128)(2,1)}, bf16[16,2048]{1,0:T(8,128)(2,1)S(1)}, u32[]{:S(2)}, u32[]{:S(2)}) collective-permute-start(bf16[16,2048]{1,0:T(8,128)(2,1)} %get-tuple-element.29), channel_id=1, source_target_pairs={{0,16},{4,20},{8,24},{12,28},{16,0},{20,4},{24,8},{28,12},{1,17},{... | collective-permute-start | bytes 196616 | tf_op jit(solution)/shard_map/ppermute | solution.py:424
  111.6 7.1 %collective-permute-start.16 = (bf16[16,2048]{1,0:T(8,128)(2,1)}, bf16[16,2048]{1,0:T(8,128)(2,1)S(1)}, u32[]{:S(2)}, u32[]{:S(2)}) collective-permute-start(bf16[16,2048]{1,0:T(8,128)(2,1)} %get-tuple-element.30), channel_id=1, source_target_pairs={{0,20},{4,24},{8,28},{12,0},{16,4},{20,8},{24,12},{28,16},{1,21},{... | collective-permute-start | bytes 196616 | tf_op jit(solution)/shard_map/ppermute | solution.py:424
  114.0 5.1 %collective-permute-start.17 = (bf16[16,2048]{1,0:T(8,128)(2,1)}, bf16[16,2048]{1,0:T(8,128)(2,1)S(1)}, u32[]{:S(2)}, u32[]{:S(2)}) collective-permute-start(bf16[16,2048]{1,0:T(8,128)(2,1)} %get-tuple-element.31), channel_id=1, source_target_pairs={{0,24},{4,28},{8,0},{12,4},{16,8},{20,12},{24,16},{28,20},{1,25},{... | collective-permute-start | bytes 196616 | tf_op jit(solution)/shard_map/ppermute | solution.py:424
  116.4 4.5 %collective-permute-start.18 = (bf16[16,2048]{1,0:T(8,128)(2,1)}, bf16[16,2048]{1,0:T(8,128)(2,1)S(1)}, u32[]{:S(2)}, u32[]{:S(2)}) collective-permute-start(bf16[16,2048]{1,0:T(8,128)(2,1)} %get-tuple-element.32), channel_id=1, source_target_pairs={{0,28},{4,0},{8,4},{12,8},{16,12},{20,16},{24,20},{28,24},{1,29},{... | collective-permute-start | bytes 196616 | tf_op jit(solution)/shard_map/ppermute | solution.py:424

commit v2 on v1

v2 whole, which is shorter than its diff:
```python
import functools
import math

import jax
import jax.numpy as jnp
from jax import lax
from jax.experimental import pallas as pl
from jax.experimental.pallas import tpu as pltpu
from jax.sharding import PartitionSpec as P

EXPERTS = 4
LANES = 128
FEW = 4
LOG2E = 1.4426950408889634
VMEM = pltpu.VMEM
SMEM = pltpu.SMEM
F32 = jnp.float32
BF16 = jnp.bfloat16


def contract_last(left, right):
    return lax.dot_general(left, right, (((1,), (1,)), ((), ())), preferred_element_type=F32)


def rotate(value, axis, steps):
    count = lax.axis_size(axis)
    return lax.ppermute(value, axis, [(i, (i + steps) % count) for i in range(count)])


def ring_places(axis):
    count = lax.axis_size(axis)
    if count > FEW:
        return jnp.zeros((1,), jnp.int32)
    me = lax.axis_index(axis)
    return jnp.stack([lax.rem(me + count - s, count) for s in range(count)]).astype(jnp.int32)


def spread(make, axis, join, after=None):
    count = lax.axis_size(axis)
    me = lax.axis_index(axis)
    if count <= FEW:
        sent = [make(lax.rem(me + s, count)) for s in range(1, count)]
        if after is not None:
            sent, _ = lax.optimization_barrier((sent, after))
        return [make(me)] + [rotate(sent[s - 1], axis, s) for s in range(1, count)]
    stacked = jnp.stack([make(jnp.int32(k)) for k in range(count)])
    moved = lax.all_to_all(stacked, axis, split_axis=0, concat_axis=0, tiled=True)
    return [jnp.concatenate([moved[k] for k in range(count)], axis=join)]


def swap(value):
    count = lax.axis_size("doc")
    return lax.ppermute(value, "doc", [(i, i + 1 - 2 * (i % 2)) for i in range(count)])


def far(value):
    return pltpu.with_memory_space_constraint(value, pltpu.HBM)


def pair_sum(value, axis):
    if lax.axis_size(axis) == 2:
        return [value, rotate(value, axis, 1)]
    total = lax.psum(value.astype(F32), axis).astype(value.dtype)
    return [total, jnp.zeros_like(total)]


FAR = pl.BlockSpec(memory_space=pltpu.HBM)
WHOLE = pl.BlockSpec(memory_space=VMEM)
SCALARS = pl.BlockSpec(memory_space=SMEM)


def activate_kernel(count, taps, places, params, select, *refs):
    pieces, (active, proj, padded, held, sem) = refs[:count], refs[count:]
    copy = pltpu.make_async_copy(select, held, sem)
    copy.start()
    rows = pieces[0].shape[0]
    padded[0:8, :] = params[8:16, :]
    for index in range(count):
        start = pl.multiple_of(8 + places[index] * rows, 8)
        padded[pl.ds(start, rows), :] = pieces[index][...].astype(F32)
    tokens = active.shape[0]
    step = 32

    def block(number, carry):
        base = pl.multiple_of(number * step, step)
        window = padded[pl.ds(base, step + 8), :]
        total = jnp.broadcast_to(params[taps : taps + 1, :], (step, params.shape[1]))
        for k in range(taps):
            offset = 8 - (taps - 1) + k
            total = total + params[k : k + 1, :] * window[offset : offset + step, :]
        value = total / (1.0 + jnp.exp(-total))
        active[pl.ds(base, step), :] = value.astype(BF16)
        return carry

    lax.fori_loop(0, tokens // step, block, 0)
    copy.wait()
    for number in range(tokens // LANES):
        cut = slice(number * LANES, (number + 1) * LANES)
        proj[:, cut] = contract_last(held[...], active[cut, :])


def activate(places, pieces, params, taps, select):
    count = len(pieces)
    tokens = count * pieces[0].shape[0]
    channels = pieces[0].shape[1]
    return pl.pallas_call(
        functools.partial(activate_kernel, count, taps),
        out_shape=(
            jax.ShapeDtypeStruct((tokens, channels), BF16),
            jax.ShapeDtypeStruct((select.shape[0], tokens), F32),
        ),
        in_specs=[SCALARS, WHOLE, FAR] + [WHOLE] * count,
        out_specs=(WHOLE,) * 2,
        scratch_shapes=[
            VMEM((tokens + 8, channels), F32),
            VMEM(select.shape, BF16),
            pltpu.SemaphoreType.DMA,
        ],
        compiler_params=pltpu.CompilerParams(vmem_limit_bytes=12 << 20),
        cost_estimate=pl.CostEstimate(
            flops=2 * tokens * channels * select.shape[0],
            bytes_accessed=4 * tokens * channels,
            transcendentals=tokens * channels,
        ),
        name="activate",
    )(places, params, far(select), *pieces)


def scan_kernel(
    taps, own, other, active, params, rates_in, step_weight_hbm, state_hbm, value_out,
    sums, steps, scaled, rates, state, coef, step_weight, state_in, sems,
):
    tokens, channels = active.shape
    rank = step_weight.shape[0]
    state_size = rates_in.shape[0]
    folds = channels // LANES
    group = min(folds, 16)
    load_weight = pltpu.make_async_copy(step_weight_hbm, step_weight, sems.at[0])
    load_state = pltpu.make_async_copy(state_hbm, state_in, sems.at[1])
    load_weight.start()
    load_state.start()
    sums[...] = own[...] + other[...]
    copy = pltpu.make_async_copy(sums.at[pl.ds(rank, 2 * state_size), :], coef, sems.at[2])
    copy.start()

    def scatter(target, source):
        for s8 in range(state_size // 8):
            for j in range(folds):
                lanes = slice(j * LANES, (j + 1) * LANES)
                there = slice((s8 * folds + j) * 8, (s8 * folds + j) * 8 + 8)
                target[there, :] = source[s8 * 8 : s8 * 8 + 8, lanes]

    def fold_rows(row, first):
        return pl.ds((row // 8) * (folds * 8) + row % 8 + first * 8, group, stride=8)

    scatter(state, rates_in)
    for s in range(state_size):
        for first in range(0, folds, group):
            rates[s * folds + first : s * folds + first + group, :] = state[fold_rows(s, first), :]
    load_state.wait()
    scatter(state, state_in)
    load_weight.wait()

    for number in range(tokens // LANES):
        cut = slice(number * LANES, (number + 1) * LANES)
        low = jnp.transpose(sums[0:rank, cut]).astype(BF16)
        width = min(channels, 256)
        for w in range(channels // width):
            lanes = slice(w * width, (w + 1) * width)
            raw = jnp.dot(low, step_weight[:, lanes], preferred_element_type=F32)
            raw = raw + params[taps + 1 : taps + 2, lanes]
            size = jnp.maximum(raw, 0.0) + jnp.log(1.0 + jnp.exp(-jnp.abs(raw)))
            times = size * active[cut, lanes].astype(F32)
            for i in range(LANES // 8):
                for j in range(width // LANES):
                    block = (number * LANES // 8 + i) * folds + w * (width // LANES) + j
                    there = slice(block * 8, block * 8 + 8)
                    part = (slice(i * 8, i * 8 + 8), slice(j * LANES, (j + 1) * LANES))
                    steps[there, :] = size[part]
                    scaled[there, :] = times[part]
    copy.wait()

    for first in range(0, folds, group):
        start = tuple(state[fold_rows(s, first), :] for s in range(state_size))

        def eight(number, held):
            base = number * (folds * 8) + first * 8
            held = list(held)
            for r in range(8):
                token = number * 8 + r
                rows = pl.ds(base + r, group, stride=8)
                size, times = steps[rows, :], scaled[rows, :]
                total = None
                for s in range(state_size):
                    rate = rates[s * folds + first : s * folds + first + group, :]
                    held[s] = jnp.exp2(size * rate) * held[s] + times * coef[s, token]
                    term = held[s] * coef[state_size + s, token]
                    total = term if total is None else total + term
                steps[rows, :] = total
            return tuple(held)

        lax.fori_loop(0, tokens // 8, eight, start)

    def unfold(number, carry):
        here = pl.ds(pl.multiple_of(number * 16, 16), 16)
        for j in range(folds):
            lanes = slice(j * LANES, (j + 1) * LANES)
            found = []
            for half in range(2):
                block = pl.multiple_of((number * 2 + half) * (folds * 8) + j * 8, 8)
                found.append(steps[pl.ds(block, 8), :])
            gain = params[taps + 2 : taps + 3, lanes]
            value_out[here, lanes] = jnp.concatenate(found, axis=0) + gain * active[here, lanes].astype(F32)
        return carry

    lax.fori_loop(0, tokens // 16, unfold, 0)


def scan(own, other, active, params, taps, rates, step_weight, state_in):
    tokens, channels = active.shape
    state_size = rates.shape[0]
    folded = (state_size * channels // LANES, LANES)
    return pl.pallas_call(
        functools.partial(scan_kernel, taps),
        out_shape=jax.ShapeDtypeStruct((tokens, channels), F32),
        in_specs=[WHOLE] * 5 + [FAR] * 2,
        out_specs=WHOLE,
        scratch_shapes=[
            VMEM(own.shape, F32),
            VMEM((tokens * channels // LANES, LANES), F32),
            VMEM((tokens * channels // LANES, LANES), F32),
            VMEM(folded, F32),
            VMEM(folded, F32),
            SMEM((2 * state_size, tokens), F32),
            VMEM(step_weight.shape, BF16),
            VMEM(state_in.shape, F32),
            pltpu.SemaphoreType.DMA((3,)),
        ],
        compiler_params=pltpu.CompilerParams(vmem_limit_bytes=16 << 20),
        cost_estimate=pl.CostEstimate(
            flops=8 * tokens * channels * state_size,
            bytes_accessed=8 * tokens * channels,
            transcendentals=tokens * channels * state_size,
        ),
        name="scan",
    )(own, other, active, params, rates, far(step_weight), far(state_in))


def project_kernel(count, columns, places, value_in, weight_hbm, *refs):
    pieces = refs[:count]
    base_out, send_out, routes_out, gated, out_weight, sem = refs[count:]
    copy = pltpu.make_async_copy(weight_hbm, out_weight, sem)
    copy.start()
    tokens, channels = value_in.shape
    rows = pieces[0].shape[0]
    tile = 16
    for index in range(count):
        begin = pl.multiple_of(places[index] * rows, tile)
        routes_out[pl.ds(begin, rows), :] = pieces[index][:, channels + columns :]

        def gate(number, carry):
            local = pl.ds(pl.multiple_of(number * tile, tile), tile)
            here = pl.ds(pl.multiple_of(begin + number * tile, tile), tile)
            z = pieces[index][local, :channels].astype(F32)
            gated[here, :] = (value_in[here, :] * (z / (1.0 + jnp.exp(-z)))).astype(BF16)
            return carry

        lax.fori_loop(0, rows // tile, gate, 0)
    copy.wait()
    for number in range(tokens // LANES):
        cut = slice(number * LANES, (number + 1) * LANES)
        sent = jnp.dot(gated[cut, :], out_weight[...], preferred_element_type=F32).astype(BF16)
        send_out[cut, :] = sent
        base_out[cut, :] = sent.astype(F32)
    for index in range(count):
        here = pl.ds(pl.multiple_of(places[index] * rows, tile), rows)
        base_out[here, :] += pieces[index][:, channels : channels + columns].astype(F32)


def project(places, value, out_weight, pieces):
    tokens, channels = value.shape
    columns = out_weight.shape[1]
    count = len(pieces)
    return pl.pallas_call(
        functools.partial(project_kernel, count, columns),
        out_shape=(
            jax.ShapeDtypeStruct((tokens, columns), F32),
            jax.ShapeDtypeStruct((tokens, columns), BF16),
            jax.ShapeDtypeStruct((tokens, LANES), BF16),
        ),
        in_specs=[SCALARS, WHOLE, FAR] + [WHOLE] * count,
        out_specs=(WHOLE,) * 3,
        scratch_shapes=[
            VMEM((tokens, channels), BF16),
            VMEM(out_weight.shape, BF16),
            pltpu.SemaphoreType.DMA,
        ],
        compiler_params=pltpu.CompilerParams(vmem_limit_bytes=16 << 20),
        cost_estimate=pl.CostEstimate(
            flops=2 * tokens * channels * columns,
            bytes_accessed=8 * tokens * channels,
            transcendentals=tokens * channels,
        ),
        name="project",
    )(places, value, far(out_weight), *pieces)


def norm_kernel(count, places, spots, gain, router, routes, *refs):
    pieces = refs[:count]
    normed, weight, own_rows = refs[count : count + 3]
    mixed = pieces[0] if count == 1 else refs[-1]
    tokens = normed.shape[0]
    columns = pieces[0].shape[1]
    for index in range(count if count > 1 else 0):
        start = pl.multiple_of(places[index] * columns, LANES)
        mixed[:, pl.ds(start, columns)] = pieces[index][...]
    mine = spots[0].astype(F32)
    step = 32

    def block(number, carry):
        cut = pl.ds(pl.multiple_of(number * step, step), step)
        value = mixed[cut, :].astype(F32)
        square = jnp.mean(value * value, axis=-1, keepdims=True) + 1e-06
        scaled = (value * lax.rsqrt(square) * gain[0:1, :]).astype(BF16)
        normed[cut, :] = scaled
        return carry

    lax.fori_loop(0, tokens // step, block, 0)
    for c in range(tokens // LANES):
        cut = slice(c * LANES, (c + 1) * LANES)
        logits = contract_last(normed[cut, :], router[...])
        first = routes[cut, 0:1].astype(F32)
        second = routes[cut, 1:2].astype(F32)
        ids = lax.broadcasted_iota(jnp.int32, logits.shape, 1).astype(F32)
        first_logit = jnp.sum(jnp.where(ids == first, logits, 0.0), axis=1, keepdims=True)
        second_logit = jnp.sum(jnp.where(ids == second, logits, 0.0), axis=1, keepdims=True)
        first_gate = jnp.where(first == mine, 1.0 / (1.0 + jnp.exp(second_logit - first_logit)), 0.0)
        second_gate = jnp.where(second == mine, 1.0 / (1.0 + jnp.exp(first_logit - second_logit)), 0.0)
        weight[cut, :] = jnp.broadcast_to(first_gate + second_gate, (LANES, LANES))
    rows = own_rows.shape[0]
    own_rows[...] = mixed[pl.ds(pl.multiple_of(spots[1] * rows, 16), rows), :]


def norm(places, spots, gain, router, routes, pieces, own):
    count = len(pieces)
    tokens = pieces[0].shape[0]
    width = count * pieces[0].shape[1]
    return pl.pallas_call(
        functools.partial(norm_kernel, count),
        out_shape=(
            jax.ShapeDtypeStruct((tokens, width), BF16),
            jax.ShapeDtypeStruct((tokens, LANES), F32),
            jax.ShapeDtypeStruct((own, width), BF16),
        ),
        in_specs=[SCALARS] * 2 + [WHOLE] * (3 + count),
        out_specs=(WHOLE,) * 3,
        scratch_shapes=[VMEM((tokens, width), BF16)] if count > 1 else [],
        compiler_params=pltpu.CompilerParams(vmem_limit_bytes=8 << 20),
        name="norm",
    )(places, spots, gain, router, routes, *pieces)


def expert_kernel(groups, half, *refs):
    tokens = refs[:groups]
    gate, up, down = refs[groups : groups + 3]
    outs = refs[groups + 3 : 2 * groups + 3]
    totals = (outs[0],) + refs[2 * groups + 3 :]
    number = pl.program_id(0)

    @pl.when(number == 0)
    def _():
        for total in totals:
            total[...] = jnp.zeros_like(total)

    rows = totals[0].shape[0]
    if groups == 2 and rows == LANES:
        work = [(totals, slice(0, rows))]
    else:
        work = [((t,), slice(c, c + LANES)) for t in totals for c in range(0, rows, LANES)]
    for index, (into, cut) in enumerate(work):
        if len(into) == 2:
            value = jnp.concatenate([tokens[0][...], tokens[1][...]], axis=0)
        else:
            value = tokens[totals.index(into[0])][cut, :]
        gate_act = contract_last(value, gate[...])
        up_act = contract_last(value, up[...])
        hidden = (gate_act / (1.0 + jnp.exp(-gate_act)) * up_act).astype(BF16)
        product = jnp.dot(hidden, down[...], preferred_element_type=F32)
        for place, total in enumerate(into):
            total[cut, :] += product[place * LANES : (place + 1) * LANES, :]

    if groups == 2:

        @pl.when(number == pl.num_programs(0) - 1)
        def _():
            outs[1][...] = totals[1][...].astype(BF16)


def experts(half, tokens, gate, up, down):
    groups = len(tokens)
    rows, width = tokens[0].shape
    hidden = gate.shape[0] // groups
    block = hidden if hidden <= 512 else math.gcd(hidden, 512)
    steps = hidden // block
    weights = pl.BlockSpec((block, width), lambda i, half: (half[0] * steps + i, 0))
    shapes = [jax.ShapeDtypeStruct((rows, width), F32), jax.ShapeDtypeStruct((rows, width), BF16)]
    return pl.pallas_call(
        functools.partial(expert_kernel, groups),
        out_shape=tuple(shapes[:groups]),
        grid_spec=pltpu.PrefetchScalarGridSpec(
            num_scalar_prefetch=1,
            grid=(steps,),
            in_specs=[WHOLE] * groups + [weights] * 3,
            out_specs=(WHOLE,) * groups,
            scratch_shapes=[VMEM((rows, width), F32)] * (groups - 1),
        ),
        compiler_params=pltpu.CompilerParams(vmem_limit_bytes=40 << 20),
        cost_estimate=pl.CostEstimate(
            flops=6 * groups * rows * hidden * width,
            bytes_accessed=6 * hidden * width,
            transcendentals=rows * hidden,
        ),
        name="experts",
    )(half, *tokens, gate, up, down)


def combine_kernel(targets, own, other, weight, *outs):
    rows = outs[0].shape[0]
    for index, out in enumerate(outs):
        here = pl.ds(pl.multiple_of(targets[index] * rows, 16), rows)
        out[...] = ((own[here, :] + other[here, :].astype(F32)) * weight[here, 0:1]).astype(BF16)


def combine(targets, own, other, weight, rows):
    width = own.shape[1]
    sends = own.shape[0] // rows
    return pl.pallas_call(
        combine_kernel,
        out_shape=tuple([jax.ShapeDtypeStruct((rows, width), BF16)] * sends),
        in_specs=[SCALARS] + [WHOLE] * 3,
        out_specs=(WHOLE,) * sends,
        compiler_params=pltpu.CompilerParams(vmem_limit_bytes=8 << 20),
        name="combine",
    )(targets, own, other, weight)


def body(
    projected,
    carried_tail,
    carried_state,
    filter_taps,
    filter_bias,
    select_weight,
    step_weight,
    step_bias,
    log_rate,
    skip_gain,
    output_weight,
    residual,
    norm_gain,
    router,
    gate_weight,
    up_weight,
    down_weight,
    routes,
):
    ctx, exp = lax.axis_size("ctx"), lax.axis_size("exp")
    ctx_at, exp_at = lax.axis_index("ctx"), lax.axis_index("exp")
    places = ring_places("ctx")
    x_input, z_input = projected[0], projected[1]
    own, width = residual.shape
    columns = output_weight.shape[1]
    taps = filter_taps.shape[0]

    x_pieces = spread(lambda k: x_input, "ctx", 0)
    extra = jnp.concatenate([residual, jnp.pad(routes.astype(BF16), ((0, 0), (0, LANES - 2)))], axis=1)
    if exp == 2:
        partner = rotate(extra, "exp", 1)
        extra = jnp.where(
            exp_at == 0,
            jnp.concatenate([extra, partner], axis=0),
            jnp.concatenate([partner, extra], axis=0),
        )
    else:
        extra = lax.all_gather(extra, "exp", axis=0, tiled=True)
    tail_pad = jnp.zeros((8 - carried_tail.shape[0], carried_tail.shape[1]), F32)
    params = jnp.concatenate(
        [filter_taps, filter_bias[None], step_bias[None], skip_gain[None], jnp.zeros_like(tail_pad)[: 5 - taps],
         tail_pad, carried_tail.astype(F32)]
    )
    rates = jnp.exp(log_rate) * (-LOG2E)
    ready = [jnp.concatenate([z_input, extra[:, width:]], axis=1), extra[:, :width]]
    router_rows = jnp.pad(router.T, ((0, 16 - EXPERTS), (0, 0)))
    gain = jnp.pad(norm_gain[None, :], ((0, 7), (0, 0)))
    params, rates, router_rows, gain = lax.optimization_barrier((params, rates, router_rows, gain))

    active, proj = activate(places, x_pieces, params, taps, select_weight)
    own_proj, other_proj = pair_sum(proj, "exp")

    def bundle(k):
        piece = lax.dynamic_slice_in_dim(ready[1], k * columns, columns, axis=1)
        channels = z_input.shape[1]
        return jnp.concatenate([ready[0][:, :channels], piece, ready[0][:, channels:]], axis=1)

    z_pieces = spread(bundle, "ctx", 0, x_pieces[min(1, len(x_pieces) - 1)])
    value = scan(own_proj, other_proj, active, params, taps, rates, step_weight, carried_state)
    base, sent, all_routes = project(places, value, output_weight, z_pieces)
    if exp == 2:
        mixed = (base + rotate(sent, "exp", 1).astype(F32)).astype(BF16)
    else:
        mixed = (base - sent.astype(F32) + lax.psum(sent.astype(F32), "exp")).astype(BF16)
    mixed_pieces = spread(lambda k: mixed, "ctx", 1)

    parts = ctx * exp
    me = ctx_at * exp + exp_at
    spots = jnp.stack([ctx_at // (ctx // EXPERTS), me]).astype(jnp.int32)
    normed, weight, mine = norm(places, spots, gain, router_rows, all_routes, mixed_pieces, own)
    total = mine.astype(F32)
    axes = ("ctx", "exp")
    if parts <= 8 and normed.shape[0] == LANES and lax.axis_size("doc") % 2 == 0:
        half = lax.rem(lax.axis_index("doc"), 2).astype(jnp.int32)[None]
        kept, given = experts(half, [normed, swap(normed)], gate_weight, up_weight, down_weight)
        targets = jnp.stack([lax.rem(me + s, parts) for s in range(parts)]).astype(jnp.int32)
        outs = combine(targets, kept, swap(given), weight, own)
        arrived = [outs[0]]
        for s in range(1, parts):
            arrived.append(lax.ppermute(outs[s], axes, [(i, (i + s) % parts) for i in range(parts)]))
        for piece in arrived:
            total = total + piece.astype(F32)
    else:
        (kept,) = experts(jnp.zeros((1,), jnp.int32), [normed], gate_weight, up_weight, down_weight)
        partial = (kept * weight[:, :1]).astype(BF16)
        moved = lax.all_to_all(partial, axes, split_axis=0, concat_axis=0, tiled=True)
        total = total + jnp.sum(moved.reshape(parts, own, width).astype(F32), axis=0)
    return total.astype(BF16)


def solution(mesh):
    placed = (
        P(None, ("doc", "ctx"), "exp"),
        P("doc", "exp"),
        P("doc", "exp"),
        P(None, "exp"),
        P("exp"),
        P(None, "exp"),
        P(None, "exp"),
        P("exp"),
        P(None, "exp"),
        P("exp"),
        P("exp", "ctx"),
        P(("doc", "ctx", "exp"), None),
        P(),
        P(),
        P(("ctx", "exp"), None),
        P(("ctx", "exp"), None),
        P(("ctx", "exp"), None),
        P(("doc", "ctx", "exp"), None),
    )
    return jax.shard_map(
        body, mesh=mesh, in_specs=placed, out_specs=P(("doc", "ctx", "exp"), None), check_vma=False
    )
```

time: 123 us -> 96.2 us (0.78)
  Pallas kernels: 50.9 us -> 33 us
  local copies, waits for them, and re-layouts: 12.1 us -> 4.25 us
  waiting for transfers between devices: 24.1 us -> 22.3 us
  starting transfers between devices: 30.1 us -> 31.5 us
    pallas_call x3 -> x6, Pallas kernels: 50.9 us -> 33 us  [the longest x1 19.3 us: experts(): pl.pallas_call(functools.partial(expert_kernel, groups), out_shape=tuple(...]
    unnamed x30 -> x0, local copies, waits for them, and re-layouts: 9.06 us -> none
    ppermute x12, waiting for transfers between devices: 20.5 us -> 15.3 us  [rotate(): lax.ppermute(value, axis, [(i, (i + steps) % count) for i in range(count)])]
    ppermute x0 -> x2, waiting for transfers between devices: none -> 3.57 us  [swap(): lax.ppermute(value, 'doc', [(i, i + 1 - 2 * (i % 2)) for i in range(count)])]
    concatenate x0 -> x1, local copies, waits for them, and re-layouts: none -> 1.59 us  [body(): jnp.concatenate([filter_taps, filter_bias[None], step_bias[None], skip_ga...]
    ppermute x12, starting transfers between devices: 19 us -> 20.3 us  [rotate(): lax.ppermute(value, axis, [(i, (i + steps) % count) for i in range(count)])]
  transfers between devices with their start and end apart: 19 -> 21, of which waited for: 11 -> 11; matrix products, arithmetic and copies ran while one was open for 4% -> 7% of each run, Pallas kernels for 2% -> 9%
where the time goes in v2:
time: 96.2 us; the launch traced here: 95.6 us
  Pallas kernels  33 us (34%)
  starting transfers between devices  31.5 us (33%)
  waiting for transfers between devices  22.3 us (23%)
  other arithmetic  4.35 us (5%)
  local copies, waits for them, and re-layouts  4.25 us (4%)
    ppermute x12, starting transfers between devices, rotate(): lax.ppermute(value, axis, [(i, (i + steps) % count) for i in range(count)])  20.3 us
    pallas_call x1, Pallas kernels, experts(): pl.pallas_call(functools.partial(expert_kernel, groups), out_shape=tuple(...  19.3 us
    ppermute x12, waiting for transfers between devices, rotate(): lax.ppermute(value, axis, [(i, (i + steps) % count) for i in range(count)])  15.3 us
    ppermute x7, starting transfers between devices, body(): lax.ppermute(outs[s], axes, [(i, (i + s) % parts) for i in range(parts)])  11 us
    pallas_call x1, Pallas kernels, scan(): pl.pallas_call(functools.partial(scan_kernel, taps), out_shape=jax.ShapeD...  6.55 us
    ppermute x2, waiting for transfers between devices, swap(): lax.ppermute(value, 'doc', [(i, i + 1 - 2 * (i % 2)) for i in range(count)])  3.57 us
    ppermute x7, waiting for transfers between devices, body(): lax.ppermute(outs[s], axes, [(i, (i + s) % parts) for i in range(parts)])  3.43 us
    pallas_call x1, Pallas kernels, project(): pl.pallas_call(functools.partial(project_kernel, count, columns), out_sha...  2.62 us
  transfers between devices with their start and end apart: 21, of which 11 were waited for; matrix products, arithmetic and copies ran while one was open for 7% of the time, Pallas kernels for 9%

profile of v2, /device:TPU:0, one launch (start us, length us, event | category | flops | bytes accessed | tf_op | source)
XLA Modules:
  0.0 95.6 jit_solution(17901467915976063304)
XLA Ops:
  0.0 1.0 %slice_bitcast_fusion = (bf16[32,2048]{1,0:T(8,128)(2,1)S(1)}, bf16[32,2048]{1,0:T(8,128)(2,1)S(1)}) fusion(bf16[2,32,2048]{2,1,0:T(8,128)(2,1)} %param.18), kind=kLoop, calls=%fused_computation.11 | loop fusion | bytes 524288 | tf_op jit(solution)/shard_map/squeeze | solution.py:470
  1.0 5.1 %collective-permute-start.2 = (bf16[32,2048]{1,0:T(8,128)(2,1)S(1)}, bf16[32,2048]{1,0:T(8,128)(2,1)S(1)}, u32[]{:S(2)}, u32[]{:S(2)}) collective-permute-start(bf16[32,2048]{1,0:T(8,128)(2,1)S(1)} %get-tuple-element.56.refs_0_), channel_id=1, source_target_pairs={{0,24},{8,0},{16,8},{24,16},{1,25},{9,1},{17,9},{25,17},{2,26},{10... | collective-permute-start | bytes 393224 | tf_op jit(solution)/shard_map/ppermute | solution.py:27
  6.1 0.0 collective-permute-start.1
  6.1 1.0 %collective-permute-start = (bf16[32,2048]{1,0:T(8,128)(2,1)S(1)}, bf16[32,2048]{1,0:T(8,128)(2,1)S(1)}, u32[]{:S(2)}, u32[]{:S(2)}) collective-permute-start(bf16[32,2048]{1,0:T(8,128)(2,1)S(1)} %get-tuple-element.56.refs_0_), channel_id=1, source_target_pairs={{0,8},{8,16},{16,24},{24,0},{1,9},{9,17},{17,25},{25,1},{2,10},{10... | collective-permute-start | bytes 393224 | tf_op jit(solution)/shard_map/ppermute | solution.py:27
  7.1 0.7 convert_element_type.49
  7.8 0.1 copy.20
  7.9 0.8 pad_maximum_fusion.8
  8.7 1.5 %collective-permute-start.4 = (bf16[16,2176]{1,0:T(8,128)(2,1)S(1)}, bf16[16,2176]{1,0:T(8,128)(2,1)S(1)}, u32[]{:S(2)}, u32[]{:S(2)}) collective-permute-start(bf16[16,2176]{1,0:T(8,128)(2,1)S(1)} %pad_maximum_fusion.8), channel_id=1, source_target_pairs={{0,4},{4,0},{1,5},{5,1},{2,6},{6,2},{3,7},{7,3},{8,12},{12,8},{9,1... | collective-permute-start | bytes 208904 | tf_op jit(solution)/shard_map/ppermute | solution.py:27
  10.3 0.9 exponential_multiply_fusion.rates_in
  11.2 0.7 pad.12.router
  12.0 0.7 pad.13.gain
  12.7 1.6 %concatenate.24.params = f32[16,2048]{1,0:T(8,128)S(1)} concatenate(f32[4,2048]{1,0:T(4,128)} %param.21, f32[1,2048]{1,0:T(1,128)} %bitcast.26, f32[1,2048]{1,0:T(1,128)} %bitcast.27, f32[1,2048]{1,0:T(1,128)} %bitcast.28, f32[1,2048]{1,0:T(1,128)S(1)} %slice.15, f32[5,2048]{1,0:T(8,128)S(1)} %broadcast_in_dim.21, bf16[3,2048]{1,0:T(4,128)(2,1)} %param.19), dimensions={0} | concatenate | bytes 249856 | tf_op jit(solution)/shard_map/concatenate | solution.py:487
  14.3 0.0 collective-permute-done.4
  14.3 0.9 maximum_select_fusion
  15.3 0.1 pad_maximum_fusion
  15.4 0.1 collective-permute-done.refs_1_
  15.5 2.5 %collective-permute-start.5 = (bf16[32,2688]{1,0:T(8,128)(2,1)S(1)}, bf16[32,2688]{1,0:T(8,128)(2,1)S(1)}, u32[]{:S(2)}, u32[]{:S(2)}) collective-permute-start(bf16[32,2688]{1,0:T(8,128)(2,1)S(1)} %get-tuple-element.36), channel_id=1, source_target_pairs={{0,8},{8,16},{16,24},{24,0},{1,9},{9,17},{17,25},{25,1},{2,10},{10... | collective-permute-start | bytes 516104 | tf_op jit(solution)/shard_map/ppermute | solution.py:27
  18.0 1.9 %collective-permute-start.6 = (bf16[32,2688]{1,0:T(8,128)(2,1)S(1)}, bf16[32,2688]{1,0:T(8,128)(2,1)S(1)}, u32[]{:S(2)}, u32[]{:S(2)}) collective-permute-start(bf16[32,2688]{1,0:T(8,128)(2,1)S(1)} %get-tuple-element.37), channel_id=1, source_target_pairs={{0,16},{8,24},{16,0},{24,8},{1,17},{9,25},{17,1},{25,9},{2,18},{10... | collective-permute-start | bytes 516104 | tf_op jit(solution)/shard_map/ppermute | solution.py:27
  19.9 2.9 %collective-permute-start.7 = (bf16[32,2688]{1,0:T(8,128)(2,1)S(1)}, bf16[32,2688]{1,0:T(8,128)(2,1)S(1)}, u32[]{:S(2)}, u32[]{:S(2)}) collective-permute-start(bf16[32,2688]{1,0:T(8,128)(2,1)S(1)} %get-tuple-element.38), channel_id=1, source_target_pairs={{0,24},{8,0},{16,8},{24,16},{1,25},{9,1},{17,9},{25,17},{2,26},{10... | collective-permute-start | bytes 516104 | tf_op jit(solution)/shard_map/ppermute | solution.py:27
  22.9 0.1 pad_add_fusion.places
  22.9 0.0 collective-permute-done.2.refs_3_
  22.9 0.0 collective-permute-done.1.refs_2_
  22.9 2.1 %activate.1 = (bf16[128,2048]{1,0:T(8,128)(2,1)S(1)}, f32[160,128]{1,0:T(8,128)S(1)}) custom-call(s32[4]{0:T(128)S(1)} %pad_add_fusion.places, f32[16,2048]{1,0:T(8,128)S(1)} %concatenate.24.params, bf16[160,2048]{1,0:T(8,128)(2,1)} %select.38, bf16[32,2048]{1,0:T(8,128)(2,1)S(1)} %get-tuple-element.56.refs_0_, ...), custom_call_target="tpu_custom_call" | custom-call | flops 83886080 | bytes 1048576 | tf_op jit(solution)/shard_map/activate/pallas_call | solution.py:106
  25.1 1.6 %collective-permute-start.3 = (f32[160,128]{1,0:T(8,128)S(1)}, f32[160,128]{1,0:T(8,128)S(1)}, u32[]{:S(2)}, u32[]{:S(2)}) collective-permute-start(f32[160,128]{1,0:T(8,128)S(1)} %get-tuple-element.33.own), channel_id=1, source_target_pairs={{0,4},{4,0},{1,5},{5,1},{2,6},{6,2},{3,7},{7,3},{8,12},{12,8},{9,1... | collective-permute-start | bytes 245768 | tf_op jit(solution)/shard_map/ppermute | solution.py:27
  26.7 2.9 %collective-permute-done.3.other = f32[160,128]{1,0:T(8,128)S(1)} collective-permute-done((f32[160,128]{1,0:T(8,128)S(1)}, f32[160,128]{1,0:T(8,128)S(1)}, u32[]{:S(2)}, u32[]{:S(2)}) %collective-permute-start.3) | collective-permute-done | bytes 81952 | tf_op jit(solution)/shard_map/ppermute | solution.py:27
  29.6 6.5 %scan.1.value_in = f32[128,2048]{1,0:T(8,128)S(1)} custom-call(f32[160,128]{1,0:T(8,128)S(1)} %get-tuple-element.33.own, f32[160,128]{1,0:T(8,128)S(1)} %collective-permute-done.3.other, bf16[128,2048]{1,0:T(8,128)(2,1)S(1)} %get-tuple-element.34.active, f32[16,2048]{1,0:T(8,128)S(1)} %concatenate.24.params, ...), custom_call_target="tpu_custom_call" | custom-call | flops 33554432 | bytes 2097152 | tf_op jit(solution)/shard_map/scan/pallas_call | solution.py:223
  36.2 0.0 collective-permute-done.5.refs_1_
  36.2 0.0 collective-permute-done.6.refs_2_
  36.2 0.0 collective-permute-done.7.refs_3_
  36.2 2.6 %project.1 = (f32[128,512]{1,0:T(8,128)S(1)}, bf16[128,512]{1,0:T(8,128)(2,1)S(1)}, bf16[128,128]{1,0:T(8,128)(2,1)S(1)}) custom-call(s32[4]{0:T(128)S(1)} %pad_add_fusion.places, f32[128,2048]{1,0:T(8,128)S(1)} %scan.1.value_in, bf16[2048,512]{1,0:T(8,128)(2,1)} %weight_hbm.1, bf16[32,2688]{1,0:T(8,128)(2,1)S(1)} %get-tuple-element.60.refs_0_, ...), custom_call_target="tpu_custom_call" | custom-call | flops 268435456 | bytes 2097152 | tf_op jit(solution)/shard_map/project/pallas_call | solution.py:284
  38.8 1.6 %collective-permute-start.8 = (bf16[128,512]{1,0:T(8,128)(2,1)S(1)}, bf16[128,512]{1,0:T(8,128)(2,1)S(1)}, u32[]{:S(2)}, u32[]{:S(2)}) collective-permute-start(bf16[128,512]{1,0:T(8,128)(2,1)S(1)} %get-tuple-element.41), channel_id=1, source_target_pairs={{0,4},{4,0},{1,5},{5,1},{2,6},{6,2},{3,7},{7,3},{8,12},{12,8},{9,1... | collective-permute-start | bytes 393224 | tf_op jit(solution)/shard_map/ppermute | solution.py:27
  40.4 3.4 %collective-permute-done.8 = bf16[128,512]{1,0:T(8,128)(2,1)S(1)} collective-permute-done((bf16[128,512]{1,0:T(8,128)(2,1)S(1)}, bf16[128,512]{1,0:T(8,128)(2,1)S(1)}, u32[]{:S(2)}, u32[]{:S(2)}) %collective-permute-start.8) | collective-permute-done | bytes 131104 | tf_op jit(solution)/shard_map/ppermute | solution.py:27
  43.9 1.3 %collective-permute-start.11 = (bf16[128,512]{1,0:T(8,128)(2,1)S(1)}, bf16[128,512]{1,0:T(8,128)(2,1)S(1)}, u32[]{:S(2)}, u32[]{:S(2)}) collective-permute-start(bf16[128,512]{1,0:T(8,128)(2,1)S(1)} %add_convert_fusion.refs_0_), channel_id=1, source_target_pairs={{0,24},{8,0},{16,8},{24,16},{1,25},{9,1},{17,9},{25,17},{2,26},{10... | collective-permute-start | bytes 393224 | tf_op jit(solution)/shard_map/ppermute | solution.py:27
  45.2 0.0 collective-permute-start.10
  45.2 0.8 collective-permute-start.9
  46.0 0.1 pad_add_fusion.1.spots
  46.0 4.6 %collective-permute-done.11.refs_3_ = bf16[128,512]{1,0:T(8,128)(2,1)S(1)} collective-permute-done((bf16[128,512]{1,0:T(8,128)(2,1)S(1)}, bf16[128,512]{1,0:T(8,128)(2,1)S(1)}, u32[]{:S(2)}, u32[]{:S(2)}) %collective-permute-start.11) | collective-permute-done | bytes 131104 | tf_op jit(solution)/shard_map/ppermute | solution.py:27
  50.6 4.2 %collective-permute-done.10.refs_2_ = bf16[128,512]{1,0:T(8,128)(2,1)S(1)} collective-permute-done((bf16[128,512]{1,0:T(8,128)(2,1)S(1)}, bf16[128,512]{1,0:T(8,128)(2,1)S(1)}, u32[]{:S(2)}, u32[]{:S(2)}) %collective-permute-start.10) | collective-permute-done | bytes 131104 | tf_op jit(solution)/shard_map/ppermute | solution.py:27
  54.8 0.0 collective-permute-done.9.refs_1_
  54.8 1.6 %norm.1 = (bf16[128,2048]{1,0:T(8,128)(2,1)S(1)}, f32[128,128]{1,0:T(8,128)S(1)}, bf16[16,2048]{1,0:T(8,128)(2,1)S(1)}) custom-call(s32[4]{0:T(128)S(1)} %pad_add_fusion.places, s32[2]{0:T(128)S(1)} %pad_add_fusion.1.spots, f32[8,2048]{1,0:T(8,128)S(1)} %pad.13.gain, bf16[16,2048]{1,0:T(8,128)(2,1)S(1)} %pad.12.router, ...), custom_call_target="tpu_custom_call" | custom-call | tf_op jit(solution)/shard_map/norm/pallas_call | solution.py:348
  56.4 0.1 collective-permute-start.12
  56.5 1.9 %collective-permute-done.12.refs_1_ = bf16[128,2048]{1,0:T(8,128)(2,1)S(1)} collective-permute-done((bf16[128,2048]{1,0:T(8,128)(2,1)S(1)}, bf16[128,2048]{1,0:T(8,128)(2,1)S(1)}, u32[]{:S(2)}, u32[]{:S(2)}) %collective-permute-start.12) | collective-permute-done | bytes 524320 | tf_op jit(solution)/shard_map/ppermute | solution.py:53
  58.4 19.3 %experts.1 = (f32[128,2048]{1,0:T(8,128)S(1)}, bf16[128,2048]{1,0:T(8,128)(2,1)S(1)}) custom-call(s32[1]{0:T(128)} %bitcast.21.half, bf16[128,2048]{1,0:T(8,128)(2,1)S(1)} %get-tuple-element.43.refs_0_, bf16[128,2048]{1,0:T(8,128)(2,1)S(1)} %collective-permute-done.12.refs_1_, bf16[7168,2048]{1,0:T(8,128)(2,1)} %refs_2_.1, bf16[7168,2048]{1,0:T(8,128)(2,1)} %refs_3_.1, ...), custom_call_target="tpu_custom_call" | custom-call | flops 11274289152 | bytes 44040192 | tf_op jit(solution)/shard_map/experts/pallas_call | solution.py:407
  77.8 0.2 collective-permute-start.13
  78.0 0.1 stack.67.targets
  78.1 1.7 %collective-permute-done.13.other = bf16[128,2048]{1,0:T(8,128)(2,1)S(1)} collective-permute-done((bf16[128,2048]{1,0:T(8,128)(2,1)S(1)}, bf16[128,2048]{1,0:T(8,128)(2,1)S(1)}, u32[]{:S(2)}, u32[]{:S(2)}) %collective-permute-start.13) | collective-permute-done | bytes 524320 | tf_op jit(solution)/shard_map/ppermute | solution.py:53
  79.7 0.7 combine.1
  80.4 1.6 %collective-permute-start.14 = (bf16[16,2048]{1,0:T(8,128)(2,1)S(1)}, bf16[16,2048]{1,0:T(8,128)(2,1)S(1)}, u32[]{:S(2)}, u32[]{:S(2)}) collective-permute-start(bf16[16,2048]{1,0:T(8,128)(2,1)S(1)} %get-tuple-element.48), channel_id=1, source_target_pairs={{0,4},{4,8},{8,12},{12,16},{16,20},{20,24},{24,28},{28,0},{1,5},{5... | collective-permute-start | bytes 196616 | tf_op jit(solution)/shard_map/ppermute | solution.py:527
  82.0 0.0 collective-permute-start.15
  82.0 1.9 %collective-permute-start.16 = (bf16[16,2048]{1,0:T(8,128)(2,1)S(1)}, bf16[16,2048]{1,0:T(8,128)(2,1)S(1)}, u32[]{:S(2)}, u32[]{:S(2)}) collective-permute-start(bf16[16,2048]{1,0:T(8,128)(2,1)S(1)} %get-tuple-element.50), channel_id=1, source_target_pairs={{0,12},{4,16},{8,20},{12,24},{16,28},{20,0},{24,4},{28,8},{1,13},{... | collective-permute-start | bytes 196616 | tf_op jit(solution)/shard_map/ppermute | solution.py:527
  83.9 2.0 %collective-permute-start.17 = (bf16[16,2048]{1,0:T(8,128)(2,1)S(1)}, bf16[16,2048]{1,0:T(8,128)(2,1)S(1)}, u32[]{:S(2)}, u32[]{:S(2)}) collective-permute-start(bf16[16,2048]{1,0:T(8,128)(2,1)S(1)} %get-tuple-element.51), channel_id=1, source_target_pairs={{0,16},{4,20},{8,24},{12,28},{16,0},{20,4},{24,8},{28,12},{1,17},{... | collective-permute-start | bytes 196616 | tf_op jit(solution)/shard_map/ppermute | solution.py:527
  85.9 1.8 %collective-permute-start.18 = (bf16[16,2048]{1,0:T(8,128)(2,1)S(1)}, bf16[16,2048]{1,0:T(8,128)(2,1)S(1)}, u32[]{:S(2)}, u32[]{:S(2)}) collective-permute-start(bf16[16,2048]{1,0:T(8,128)(2,1)S(1)} %get-tuple-element.52), channel_id=1, source_target_pairs={{0,20},{4,24},{8,28},{12,0},{16,4},{20,8},{24,12},{28,16},{1,21},{... | collective-permute-start | bytes 196616 | tf_op jit(solution)/shard_map/ppermute | solution.py:527
  87.7 0.6 collective-permute-done.14
  88.2 2.4 %collective-permute-start.19 = (bf16[16,2048]{1,0:T(8,128)(2,1)S(1)}, bf16[16,2048]{1,0:T(8,128)(2,1)S(1)}, u32[]{:S(2)}, u32[]{:S(2)}) collective-permute-start(bf16[16,2048]{1,0:T(8,128)(2,1)S(1)} %get-tuple-element.53), channel_id=1, source_target_pairs={{0,24},{4,28},{8,0},{12,4},{16,8},{20,12},{24,16},{28,20},{1,25},{... | collective-permute-start | bytes 196616 | tf_op jit(solution)/shard_map/ppermute | solution.py:527
  90.6 0.0 collective-permute-done.15
  90.6 1.4 %collective-permute-start.20 = (bf16[16,2048]{1,0:T(8,128)(2,1)S(1)}, bf16[16,2048]{1,0:T(8,128)(2,1)S(1)}, u32[]{:S(2)}, u32[]{:S(2)}) collective-permute-start(bf16[16,2048]{1,0:T(8,128)(2,1)S(1)} %get-tuple-element.54), channel_id=1, source_target_pairs={{0,28},{4,0},{8,4},{12,8},{16,12},{20,16},{24,20},{28,24},{1,29},{... | collective-permute-start | bytes 196616 | tf_op jit(solution)/shard_map/ppermute | solution.py:527
  92.0 1.1 %collective-permute-done.16 = bf16[16,2048]{1,0:T(8,128)(2,1)S(1)} collective-permute-done((bf16[16,2048]{1,0:T(8,128)(2,1)S(1)}, bf16[16,2048]{1,0:T(8,128)(2,1)S(1)}, u32[]{:S(2)}, u32[]{:S(2)}) %collective-permute-start.16) | collective-permute-done | bytes 65568 | tf_op jit(solution)/shard_map/ppermute | solution.py:527
  93.1 0.8 collective-permute-done.17
  93.9 0.0 collective-permute-done.18
  93.9 0.0 collective-permute-done.19
  93.9 1.0 %collective-permute-done.20 = bf16[16,2048]{1,0:T(8,128)(2,1)S(1)} collective-permute-done((bf16[16,2048]{1,0:T(8,128)(2,1)S(1)}, bf16[16,2048]{1,0:T(8,128)(2,1)S(1)}, u32[]{:S(2)}, u32[]{:S(2)}) %collective-permute-start.20) | collective-permute-done | bytes 65568 | tf_op jit(solution)/shard_map/ppermute | solution.py:527
  94.9 0.7 add_convert_fusion.1
  (7 shorter events, 0.1 us)
Async XLA Ops:
  1.0 21.9 %collective-permute-start.2 = (bf16[32,2048]{1,0:T(8,128)(2,1)S(1)}, bf16[32,2048]{1,0:T(8,128)(2,1)S(1)}, u32[]{:S(2)}, u32[]{:S(2)}) collective-permute-start(bf16[32,2048]{1,0:T(8,128)(2,1)S(1)} %get-tuple-element.56.refs_0_), channel_id=1, source_target_pairs={{0,24},{8,0},{16,8},{24,16},{1,25},{9,1},{17,9},{25,17},{2,26},{10... | collective-permute-start | bytes 393224 | tf_op jit(solution)/shard_map/ppermute | solution.py:27
  6.1 16.8 %collective-permute-start.1 = (bf16[32,2048]{1,0:T(8,128)(2,1)S(1)}, bf16[32,2048]{1,0:T(8,128)(2,1)S(1)}, u32[]{:S(2)}, u32[]{:S(2)}) collective-permute-start(bf16[32,2048]{1,0:T(8,128)(2,1)S(1)} %get-tuple-element.56.refs_0_), channel_id=1, source_target_pairs={{0,16},{8,24},{16,0},{24,8},{1,17},{9,25},{17,1},{25,9},{2,18},{10... | collective-permute-start | bytes 393224 | tf_op jit(solution)/shard_map/ppermute | solution.py:27
  6.1 9.4 %collective-permute-start = (bf16[32,2048]{1,0:T(8,128)(2,1)S(1)}, bf16[32,2048]{1,0:T(8,128)(2,1)S(1)}, u32[]{:S(2)}, u32[]{:S(2)}) collective-permute-start(bf16[32,2048]{1,0:T(8,128)(2,1)S(1)} %get-tuple-element.56.refs_0_), channel_id=1, source_target_pairs={{0,8},{8,16},{16,24},{24,0},{1,9},{9,17},{17,25},{25,1},{2,10},{10... | collective-permute-start | bytes 393224 | tf_op jit(solution)/shard_map/ppermute | solution.py:27
  8.7 5.6 %collective-permute-start.4 = (bf16[16,2176]{1,0:T(8,128)(2,1)S(1)}, bf16[16,2176]{1,0:T(8,128)(2,1)S(1)}, u32[]{:S(2)}, u32[]{:S(2)}) collective-permute-start(bf16[16,2176]{1,0:T(8,128)(2,1)S(1)} %pad_maximum_fusion.8), channel_id=1, source_target_pairs={{0,4},{4,0},{1,5},{5,1},{2,6},{6,2},{3,7},{7,3},{8,12},{12,8},{9,1... | collective-permute-start | bytes 208904 | tf_op jit(solution)/shard_map/ppermute | solution.py:27
  15.5 20.7 %collective-permute-start.5 = (bf16[32,2688]{1,0:T(8,128)(2,1)S(1)}, bf16[32,2688]{1,0:T(8,128)(2,1)S(1)}, u32[]{:S(2)}, u32[]{:S(2)}) collective-permute-start(bf16[32,2688]{1,0:T(8,128)(2,1)S(1)} %get-tuple-element.36), channel_id=1, source_target_pairs={{0,8},{8,16},{16,24},{24,0},{1,9},{9,17},{17,25},{25,1},{2,10},{10... | collective-permute-start | bytes 516104 | tf_op jit(solution)/shard_map/ppermute | solution.py:27
  18.0 18.2 %collective-permute-start.6 = (bf16[32,2688]{1,0:T(8,128)(2,1)S(1)}, bf16[32,2688]{1,0:T(8,128)(2,1)S(1)}, u32[]{:S(2)}, u32[]{:S(2)}) collective-permute-start(bf16[32,2688]{1,0:T(8,128)(2,1)S(1)} %get-tuple-element.37), channel_id=1, source_target_pairs={{0,16},{8,24},{16,0},{24,8},{1,17},{9,25},{17,1},{25,9},{2,18},{10... | collective-permute-start | bytes 516104 | tf_op jit(solution)/shard_map/ppermute | solution.py:27
  19.9 16.2 %collective-permute-start.7 = (bf16[32,2688]{1,0:T(8,128)(2,1)S(1)}, bf16[32,2688]{1,0:T(8,128)(2,1)S(1)}, u32[]{:S(2)}, u32[]{:S(2)}) collective-permute-start(bf16[32,2688]{1,0:T(8,128)(2,1)S(1)} %get-tuple-element.38), channel_id=1, source_target_pairs={{0,24},{8,0},{16,8},{24,16},{1,25},{9,1},{17,9},{25,17},{2,26},{10... | collective-permute-start | bytes 516104 | tf_op jit(solution)/shard_map/ppermute | solution.py:27
  25.1 4.5 %collective-permute-start.3 = (f32[160,128]{1,0:T(8,128)S(1)}, f32[160,128]{1,0:T(8,128)S(1)}, u32[]{:S(2)}, u32[]{:S(2)}) collective-permute-start(f32[160,128]{1,0:T(8,128)S(1)} %get-tuple-element.33.own), channel_id=1, source_target_pairs={{0,4},{4,0},{1,5},{5,1},{2,6},{6,2},{3,7},{7,3},{8,12},{12,8},{9,1... | collective-permute-start | bytes 245768 | tf_op jit(solution)/shard_map/ppermute | solution.py:27
  38.8 5.0 %collective-permute-start.8 = (bf16[128,512]{1,0:T(8,128)(2,1)S(1)}, bf16[128,512]{1,0:T(8,128)(2,1)S(1)}, u32[]{:S(2)}, u32[]{:S(2)}) collective-permute-start(bf16[128,512]{1,0:T(8,128)(2,1)S(1)} %get-tuple-element.41), channel_id=1, source_target_pairs={{0,4},{4,0},{1,5},{5,1},{2,6},{6,2},{3,7},{7,3},{8,12},{12,8},{9,1... | collective-permute-start | bytes 393224 | tf_op jit(solution)/shard_map/ppermute | solution.py:27
  43.9 6.7 %collective-permute-start.11 = (bf16[128,512]{1,0:T(8,128)(2,1)S(1)}, bf16[128,512]{1,0:T(8,128)(2,1)S(1)}, u32[]{:S(2)}, u32[]{:S(2)}) collective-permute-start(bf16[128,512]{1,0:T(8,128)(2,1)S(1)} %add_convert_fusion.refs_0_), channel_id=1, source_target_pairs={{0,24},{8,0},{16,8},{24,16},{1,25},{9,1},{17,9},{25,17},{2,26},{10... | collective-permute-start | bytes 393224 | tf_op jit(solution)/shard_map/ppermute | solution.py:27
  45.2 9.7 %collective-permute-start.10 = (bf16[128,512]{1,0:T(8,128)(2,1)S(1)}, bf16[128,512]{1,0:T(8,128)(2,1)S(1)}, u32[]{:S(2)}, u32[]{:S(2)}) collective-permute-start(bf16[128,512]{1,0:T(8,128)(2,1)S(1)} %add_convert_fusion.refs_0_), channel_id=1, source_target_pairs={{0,16},{8,24},{16,0},{24,8},{1,17},{9,25},{17,1},{25,9},{2,18},{10... | collective-permute-start | bytes 393224 | tf_op jit(solution)/shard_map/ppermute | solution.py:27
  45.2 9.7 %collective-permute-start.9 = (bf16[128,512]{1,0:T(8,128)(2,1)S(1)}, bf16[128,512]{1,0:T(8,128)(2,1)S(1)}, u32[]{:S(2)}, u32[]{:S(2)}) collective-permute-start(bf16[128,512]{1,0:T(8,128)(2,1)S(1)} %add_convert_fusion.refs_0_), channel_id=1, source_target_pairs={{0,8},{8,16},{16,24},{24,0},{1,9},{9,17},{17,25},{25,1},{2,10},{10... | collective-permute-start | bytes 393224 | tf_op jit(solution)/shard_map/ppermute | solution.py:27
  56.4 2.0 %collective-permute-start.12 = (bf16[128,2048]{1,0:T(8,128)(2,1)S(1)}, bf16[128,2048]{1,0:T(8,128)(2,1)S(1)}, u32[]{:S(2)}, u32[]{:S(2)}) collective-permute-start(bf16[128,2048]{1,0:T(8,128)(2,1)S(1)} %get-tuple-element.43.refs_0_), channel_id=1, source_target_pairs={{0,1},{1,0},{2,3},{3,2},{4,5},{5,4},{6,7},{7,6},{8,9},{9,8},{10,11... | collective-permute-start | bytes 1572872 | tf_op jit(solution)/shard_map/ppermute | solution.py:53
  77.8 2.0 %collective-permute-start.13 = (bf16[128,2048]{1,0:T(8,128)(2,1)S(1)}, bf16[128,2048]{1,0:T(8,128)(2,1)S(1)}, u32[]{:S(2)}, u32[]{:S(2)}) collective-permute-start(bf16[128,2048]{1,0:T(8,128)(2,1)S(1)} %get-tuple-element.45), channel_id=1, source_target_pairs={{0,1},{1,0},{2,3},{3,2},{4,5},{5,4},{6,7},{7,6},{8,9},{9,8},{10,11... | collective-permute-start | bytes 1572872 | tf_op jit(solution)/shard_map/ppermute | solution.py:53
  80.4 7.8 %collective-permute-start.14 = (bf16[16,2048]{1,0:T(8,128)(2,1)S(1)}, bf16[16,2048]{1,0:T(8,128)(2,1)S(1)}, u32[]{:S(2)}, u32[]{:S(2)}) collective-permute-start(bf16[16,2048]{1,0:T(8,128)(2,1)S(1)} %get-tuple-element.48), channel_id=1, source_target_pairs={{0,4},{4,8},{8,12},{12,16},{16,20},{20,24},{24,28},{28,0},{1,5},{5... | collective-permute-start | bytes 196616 | tf_op jit(solution)/shard_map/ppermute | solution.py:527
  82.0 8.6 %collective-permute-start.15 = (bf16[16,2048]{1,0:T(8,128)(2,1)S(1)}, bf16[16,2048]{1,0:T(8,128)(2,1)S(1)}, u32[]{:S(2)}, u32[]{:S(2)}) collective-permute-start(bf16[16,2048]{1,0:T(8,128)(2,1)S(1)} %get-tuple-element.49), channel_id=1, source_target_pairs={{0,8},{4,12},{8,16},{12,20},{16,24},{20,28},{24,0},{28,4},{1,9},{5... | collective-permute-start | bytes 196616 | tf_op jit(solution)/shard_map/ppermute | solution.py:527
  82.0 11.1 %collective-permute-start.16 = (bf16[16,2048]{1,0:T(8,128)(2,1)S(1)}, bf16[16,2048]{1,0:T(8,128)(2,1)S(1)}, u32[]{:S(2)}, u32[]{:S(2)}) collective-permute-start(bf16[16,2048]{1,0:T(8,128)(2,1)S(1)} %get-tuple-element.50), channel_id=1, source_target_pairs={{0,12},{4,16},{8,20},{12,24},{16,28},{20,0},{24,4},{28,8},{1,13},{... | collective-permute-start | bytes 196616 | tf_op jit(solution)/shard_map/ppermute | solution.py:527
  83.9 10.0 %collective-permute-start.17 = (bf16[16,2048]{1,0:T(8,128)(2,1)S(1)}, bf16[16,2048]{1,0:T(8,128)(2,1)S(1)}, u32[]{:S(2)}, u32[]{:S(2)}) collective-permute-start(bf16[16,2048]{1,0:T(8,128)(2,1)S(1)} %get-tuple-element.51), channel_id=1, source_target_pairs={{0,16},{4,20},{8,24},{12,28},{16,0},{20,4},{24,8},{28,12},{1,17},{... | collective-permute-start | bytes 196616 | tf_op jit(solution)/shard_map/ppermute | solution.py:527
  85.9 8.0 %collective-permute-start.18 = (bf16[16,2048]{1,0:T(8,128)(2,1)S(1)}, bf16[16,2048]{1,0:T(8,128)(2,1)S(1)}, u32[]{:S(2)}, u32[]{:S(2)}) collective-permute-start(bf16[16,2048]{1,0:T(8,128)(2,1)S(1)} %get-tuple-element.52), channel_id=1, source_target_pairs={{0,20},{4,24},{8,28},{12,0},{16,4},{20,8},{24,12},{28,16},{1,21},{... | collective-permute-start | bytes 196616 | tf_op jit(solution)/shard_map/ppermute | solution.py:527
  88.2 5.6 %collective-permute-start.19 = (bf16[16,2048]{1,0:T(8,128)(2,1)S(1)}, bf16[16,2048]{1,0:T(8,128)(2,1)S(1)}, u32[]{:S(2)}, u32[]{:S(2)}) collective-permute-start(bf16[16,2048]{1,0:T(8,128)(2,1)S(1)} %get-tuple-element.53), channel_id=1, source_target_pairs={{0,24},{4,28},{8,0},{12,4},{16,8},{20,12},{24,16},{28,20},{1,25},{... | collective-permute-start | bytes 196616 | tf_op jit(solution)/shard_map/ppermute | solution.py:527
  90.6 4.3 %collective-permute-start.20 = (bf16[16,2048]{1,0:T(8,128)(2,1)S(1)}, bf16[16,2048]{1,0:T(8,128)(2,1)S(1)}, u32[]{:S(2)}, u32[]{:S(2)}) collective-permute-start(bf16[16,2048]{1,0:T(8,128)(2,1)S(1)} %get-tuple-element.54), channel_id=1, source_target_pairs={{0,28},{4,0},{8,4},{12,8},{16,12},{20,16},{24,20},{28,24},{1,29},{... | collective-permute-start | bytes 196616 | tf_op jit(solution)/shard_map/ppermute | solution.py:527

commit v3 on v2

--- a/solution.py
+++ b/solution.py
@@ -127,18 +127,20 @@
 
 
 def scan_kernel(
-    taps, own, other, active, params, rates_in, step_weight_hbm, state_hbm, value_out,
-    sums, steps, scaled, rates, state, coef, step_weight, state_in, sems,
+    taps, own, other, active, params, log_rate_hbm, step_weight_hbm, state_hbm, value_out,
+    sums, steps, scaled, rates, state, coef, step_weight, state_in, log_rate, sems,
 ):
     tokens, channels = active.shape
     rank = step_weight.shape[0]
-    state_size = rates_in.shape[0]
+    state_size = log_rate.shape[0]
     folds = channels // LANES
     group = min(folds, 16)
     load_weight = pltpu.make_async_copy(step_weight_hbm, step_weight, sems.at[0])
     load_state = pltpu.make_async_copy(state_hbm, state_in, sems.at[1])
+    load_rate = pltpu.make_async_copy(log_rate_hbm, log_rate, sems.at[3])
+    load_rate.start()
+    load_state.start()
     load_weight.start()
-    load_state.start()
     sums[...] = own[...] + other[...]
     copy = pltpu.make_async_copy(sums.at[pl.ds(rank, 2 * state_size), :], coef, sems.at[2])
     copy.start()
@@ -153,10 +155,13 @@
     def fold_rows(row, first):
         return pl.ds((row // 8) * (folds * 8) + row % 8 + first * 8, group, stride=8)
 
-    scatter(state, rates_in)
+    load_rate.wait()
+    scatter(state, log_rate)
     for s in range(state_size):
         for first in range(0, folds, group):
-            rates[s * folds + first : s * folds + first + group, :] = state[fold_rows(s, first), :]
+            rates[s * folds + first : s * folds + first + group, :] = (
+                jnp.exp(state[fold_rows(s, first), :]) * (-LOG2E)
+            )
     load_state.wait()
     scatter(state, state_in)
     load_weight.wait()
@@ -216,14 +221,14 @@
     lax.fori_loop(0, tokens // 16, unfold, 0)
 
 
-def scan(own, other, active, params, taps, rates, step_weight, state_in):
+def scan(own, other, active, params, taps, log_rate, step_weight, state_in):
     tokens, channels = active.shape
-    state_size = rates.shape[0]
+    state_size = log_rate.shape[0]
     folded = (state_size * channels // LANES, LANES)
     return pl.pallas_call(
         functools.partial(scan_kernel, taps),
         out_shape=jax.ShapeDtypeStruct((tokens, channels), F32),
-        in_specs=[WHOLE] * 5 + [FAR] * 2,
+        in_specs=[WHOLE] * 4 + [FAR] * 3,
         out_specs=WHOLE,
         scratch_shapes=[
             VMEM(own.shape, F32),
@@ -234,16 +239,17 @@
             SMEM((2 * state_size, tokens), F32),
             VMEM(step_weight.shape, BF16),
             VMEM(state_in.shape, F32),
-            pltpu.SemaphoreType.DMA((3,)),
+            VMEM(log_rate.shape, F32),
+            pltpu.SemaphoreType.DMA((4,)),
         ],
         compiler_params=pltpu.CompilerParams(vmem_limit_bytes=16 << 20),
         cost_estimate=pl.CostEstimate(
-            flops=8 * tokens * channels * state_size,
+            flops=3000 * tokens * channels * state_size,
             bytes_accessed=8 * tokens * channels,
             transcendentals=tokens * channels * state_size,
         ),
         name="scan",
-    )(own, other, active, params, rates, far(step_weight), far(state_in))
+    )(own, other, active, params, far(log_rate), far(step_weight), far(state_in))
 
 
 def project_kernel(count, columns, places, value_in, weight_hbm, *refs):
@@ -360,68 +366,133 @@
     )(places, spots, gain, router, routes, *pieces)
 
 
-def expert_kernel(groups, half, *refs):
-    tokens = refs[:groups]
-    gate, up, down = refs[groups : groups + 3]
-    outs = refs[groups + 3 : 2 * groups + 3]
-    totals = (outs[0],) + refs[2 * groups + 3 :]
+def fetch_kernel(parts, half, *refs):
+    count = len(refs) // 2 - 1
+    sources, targets, done, sems = refs[:count], refs[count : 2 * count], refs[-2], refs[-1]
+    rows = targets[0].shape[0]
+    part = rows // parts
+    copies = []
+    for index in range(count):
+        for k in range(parts):
+            start = pl.multiple_of(half[0] * rows + k * part, 16)
+            copies.append(
+                pltpu.make_async_copy(
+                    sources[index].at[pl.ds(start, part), :],
+                    targets[index].at[pl.ds(k * part, part), :],
+                    sems.at[index * parts + k],
+                )
+            )
+    for copy in copies:
+        copy.start()
+    for copy in copies:
+        copy.wait()
+    done[0] = half[0]
+
+
+def fetch(half, weights):
+    rows, width = weights[0].shape[0] // 2, weights[0].shape[1]
+    parts = 4
+    return pl.pallas_call(
+        functools.partial(fetch_kernel, parts),
+        out_shape=tuple([VMEM((rows, width), BF16)] * len(weights)) + (jax.ShapeDtypeStruct((1,), jnp.int32),),
+        in_specs=[SCALARS] + [FAR] * len(weights),
+        out_specs=tuple([WHOLE] * len(weights)) + (SCALARS,),
+        scratch_shapes=[pltpu.SemaphoreType.DMA((parts * len(weights),))],
+        compiler_params=pltpu.CompilerParams(vmem_limit_bytes=1 << 20),
+        cost_estimate=pl.CostEstimate(
+            flops=0, bytes_accessed=4 * rows * width * len(weights), transcendentals=0
+        ),
+        name="fetch",
+    )(half, *[far(w) for w in weights])
+
+
+def shared_kernel(steps, block, half, own, other, gate, up, down, kept, given, tokens, hidden):
     number = pl.program_id(0)
+    rows = own.shape[0]
 
     @pl.when(number == 0)
     def _():
-        for total in totals:
-            total[...] = jnp.zeros_like(total)
-
-    rows = totals[0].shape[0]
-    if groups == 2 and rows == LANES:
-        work = [(totals, slice(0, rows))]
-    else:
-        work = [((t,), slice(c, c + LANES)) for t in totals for c in range(0, rows, LANES)]
-    for index, (into, cut) in enumerate(work):
-        if len(into) == 2:
-            value = jnp.concatenate([tokens[0][...], tokens[1][...]], axis=0)
-        else:
-            value = tokens[totals.index(into[0])][cut, :]
-        gate_act = contract_last(value, gate[...])
-        up_act = contract_last(value, up[...])
-        hidden = (gate_act / (1.0 + jnp.exp(-gate_act)) * up_act).astype(BF16)
-        product = jnp.dot(hidden, down[...], preferred_element_type=F32)
-        for place, total in enumerate(into):
-            total[cut, :] += product[place * LANES : (place + 1) * LANES, :]
-
-    if groups == 2:
-
-        @pl.when(number == pl.num_programs(0) - 1)
-        def _():
-            outs[1][...] = totals[1][...].astype(BF16)
-
-
-def experts(half, tokens, gate, up, down):
-    groups = len(tokens)
-    rows, width = tokens[0].shape
-    hidden = gate.shape[0] // groups
-    block = hidden if hidden <= 512 else math.gcd(hidden, 512)
-    steps = hidden // block
-    weights = pl.BlockSpec((block, width), lambda i, half: (half[0] * steps + i, 0))
-    shapes = [jax.ShapeDtypeStruct((rows, width), F32), jax.ShapeDtypeStruct((rows, width), BF16)]
-    return pl.pallas_call(
-        functools.partial(expert_kernel, groups),
-        out_shape=tuple(shapes[:groups]),
+        tokens[0:rows, :] = own[...]
+        tokens[rows:, :] = other[...]
+
+    @pl.when(number < steps)
+    def _():
+        here = pl.ds(pl.multiple_of(number * block, block), block)
+        gate_act = contract_last(tokens[...], gate[here, :])
+        up_act = contract_last(tokens[...], up[here, :])
+        value = gate_act / (1.0 + jnp.exp(-gate_act)) * up_act
+        hidden[:, here] = value.astype(BF16)
+
+    @pl.when(number >= steps)
+    def _():
+        width = down.shape[1]
+        here = pl.ds(pl.multiple_of((number - steps) * width, width), width)
+        product = jnp.dot(hidden[...], down[...], preferred_element_type=F32)
+        kept[:, here] = product[0:rows, :]
+        given[:, here] = product[rows:, :].astype(BF16)
+
+
+def shared_experts(half, own, other, gate, up, down):
+    rows, width = own.shape
+    depth = gate.shape[0]
+    block = math.gcd(depth, 512)
+    steps = depth // block
+    columns = 256
+    return pl.pallas_call(
+        functools.partial(shared_kernel, steps, block),
+        out_shape=(jax.ShapeDtypeStruct((rows, width), F32), jax.ShapeDtypeStruct((rows, width), BF16)),
         grid_spec=pltpu.PrefetchScalarGridSpec(
             num_scalar_prefetch=1,
-            grid=(steps,),
-            in_specs=[WHOLE] * groups + [weights] * 3,
-            out_specs=(WHOLE,) * groups,
-            scratch_shapes=[VMEM((rows, width), F32)] * (groups - 1),
-        ),
+            grid=(steps + width // columns,),
+            in_specs=[WHOLE] * 4
+            + [pl.BlockSpec((depth, columns), lambda i, half: (half[0], jnp.maximum(i - steps, 0)))],
+            out_specs=(WHOLE,) * 2,
+            scratch_shapes=[VMEM((2 * rows, width), BF16), VMEM((2 * rows, depth), BF16)],
+        ),
+        compiler_params=pltpu.CompilerParams(vmem_limit_bytes=16 << 20),
+        cost_estimate=pl.CostEstimate(
+            flops=12 * rows * depth * width,
+            bytes_accessed=6 * depth * width,
+            transcendentals=2 * rows * depth,
+        ),
+        name="experts",
+    )(half, own, other, gate, up, far(down))
+
+
+def expert_kernel(tokens, gate, up, down, total):
+    number = pl.program_id(0)
+
+    @pl.when(number == 0)
+    def _():
+        total[...] = jnp.zeros_like(total)
+
+    for start in range(0, total.shape[0], LANES):
+        cut = slice(start, start + LANES)
+        gate_act = contract_last(tokens[cut, :], gate[...])
+        up_act = contract_last(tokens[cut, :], up[...])
+        hidden = (gate_act / (1.0 + jnp.exp(-gate_act)) * up_act).astype(BF16)
+        total[cut, :] += jnp.dot(hidden, down[...], preferred_element_type=F32)
+
+
+def experts(tokens, gate, up, down):
+    rows, width = tokens.shape
+    hidden = gate.shape[0]
+    block = hidden if hidden <= 512 else math.gcd(hidden, 512)
+    weights = pl.BlockSpec((block, width), lambda i: (i, 0))
+    return pl.pallas_call(
+        expert_kernel,
+        grid=(hidden // block,),
+        out_shape=jax.ShapeDtypeStruct((rows, width), F32),
+        in_specs=[WHOLE] + [weights] * 3,
+        out_specs=WHOLE,
         compiler_params=pltpu.CompilerParams(vmem_limit_bytes=40 << 20),
         cost_estimate=pl.CostEstimate(
-            flops=6 * groups * rows * hidden * width,
+            flops=6 * rows * hidden * width,
             bytes_accessed=6 * hidden * width,
             transcendentals=rows * hidden,
         ),
         name="experts",
-    )(half, *tokens, gate, up, down)
+    )(tokens, gate, up, down)
 
 
 def combine_kernel(targets, own, other, weight, *outs):
@@ -488,11 +559,10 @@
         [filter_taps, filter_bias[None], step_bias[None], skip_gain[None], jnp.zeros_like(tail_pad)[: 5 - taps],
          tail_pad, carried_tail.astype(F32)]
     )
-    rates = jnp.exp(log_rate) * (-LOG2E)
     ready = [jnp.concatenate([z_input, extra[:, width:]], axis=1), extra[:, :width]]
     router_rows = jnp.pad(router.T, ((0, 16 - EXPERTS), (0, 0)))
     gain = jnp.pad(norm_gain[None, :], ((0, 7), (0, 0)))
-    params, rates, router_rows, gain = lax.optimization_barrier((params, rates, router_rows, gain))
+    params, router_rows, gain = lax.optimization_barrier((params, router_rows, gain))
 
     active, proj = activate(places, x_pieces, params, taps, select_weight)
     own_proj, other_proj = pair_sum(proj, "exp")
@@ -502,24 +572,29 @@
         channels = z_input.shape[1]
         return jnp.concatenate([ready[0][:, :channels], piece, ready[0][:, channels:]], axis=1)
 
-    z_pieces = spread(bundle, "ctx", 0, x_pieces[min(1, len(x_pieces) - 1)])
-    value = scan(own_proj, other_proj, active, params, taps, rates, step_weight, carried_state)
+    z_pieces = spread(bundle, "ctx", 0, active)
+    value = scan(own_proj, other_proj, active, params, taps, log_rate, step_weight, carried_state)
     base, sent, all_routes = project(places, value, output_weight, z_pieces)
     if exp == 2:
         mixed = (base + rotate(sent, "exp", 1).astype(F32)).astype(BF16)
     else:
         mixed = (base - sent.astype(F32) + lax.psum(sent.astype(F32), "exp")).astype(BF16)
+    parts = ctx * exp
+    shared = parts <= 8 and mixed.shape[0] == LANES and lax.axis_size("doc") % 2 == 0
+    if shared:
+        half = lax.rem(lax.axis_index("doc"), 2).astype(jnp.int32)[None]
+        half, mixed = lax.optimization_barrier((half, mixed))
+        gate_half, up_half, half = fetch(half, [gate_weight, up_weight])
     mixed_pieces = spread(lambda k: mixed, "ctx", 1)
-
-    parts = ctx * exp
     me = ctx_at * exp + exp_at
     spots = jnp.stack([ctx_at // (ctx // EXPERTS), me]).astype(jnp.int32)
+    if shared:
+        spots, half = lax.optimization_barrier((spots, half))
     normed, weight, mine = norm(places, spots, gain, router_rows, all_routes, mixed_pieces, own)
     total = mine.astype(F32)
     axes = ("ctx", "exp")
-    if parts <= 8 and normed.shape[0] == LANES and lax.axis_size("doc") % 2 == 0:
-        half = lax.rem(lax.axis_index("doc"), 2).astype(jnp.int32)[None]
-        kept, given = experts(half, [normed, swap(normed)], gate_weight, up_weight, down_weight)
+    if shared:
+        kept, given = shared_experts(half, normed, swap(normed), gate_half, up_half, down_weight)
         targets = jnp.stack([lax.rem(me + s, parts) for s in range(parts)]).astype(jnp.int32)
         outs = combine(targets, kept, swap(given), weight, own)
         arrived = [outs[0]]
@@ -528,7 +603,7 @@
         for piece in arrived:
             total = total + piece.astype(F32)
     else:
-        (kept,) = experts(jnp.zeros((1,), jnp.int32), [normed], gate_weight, up_weight, down_weight)
+        kept = experts(normed, gate_weight, up_weight, down_weight)
         partial = (kept * weight[:, :1]).astype(BF16)
         moved = lax.all_to_all(partial, axes, split_axis=0, concat_axis=0, tiled=True)
         total = total + jnp.sum(moved.reshape(parts, own, width).astype(F32), axis=0)

time: 96.2 us -> 103 us (1.071)
  Pallas kernels: 33 us -> 44 us
  waiting for transfers between devices: 22.3 us -> 17.1 us
  starting transfers between devices: 31.5 us -> 33.5 us
    pallas_call x1 -> x2, Pallas kernels: 19.3 us -> 30.2 us  [the longest x1 20.2 us: shared_experts(): pl.pallas_call(functools.partial(shared_kernel, steps, block), out_shape=...]
    ppermute x12, waiting for transfers between devices: 15.3 us -> 9.79 us  [rotate(): lax.ppermute(value, axis, [(i, (i + steps) % count) for i in range(count)])]
  transfers between devices with their start and end apart: 21 -> 21, of which waited for: 11 -> 8; matrix products, arithmetic and copies ran while one was open for 7% -> 6% of each run, Pallas kernels for 9% -> 16%
where the time goes in v3:
time: 103 us; the launch traced here: 102 us
  Pallas kernels  44 us (43%)
  starting transfers between devices  33.5 us (33%)
  waiting for transfers between devices  17.1 us (17%)
  local copies, waits for them, and re-layouts  4.25 us (4%)
  other arithmetic  3.42 us (3%)
    ppermute x12, starting transfers between devices, rotate(): lax.ppermute(value, axis, [(i, (i + steps) % count) for i in range(count)])  21.2 us
    pallas_call x1, Pallas kernels, shared_experts(): pl.pallas_call(functools.partial(shared_kernel, steps, block), out_shape=...  20.2 us
    ppermute x7, starting transfers between devices, body(): lax.ppermute(outs[s], axes, [(i, (i + s) % parts) for i in range(parts)])  12 us
    pallas_call x1, Pallas kernels, fetch(): pl.pallas_call(functools.partial(fetch_kernel, parts), out_shape=tuple([V...  10 us
    ppermute x12, waiting for transfers between devices, rotate(): lax.ppermute(value, axis, [(i, (i + steps) % count) for i in range(count)])  9.79 us
    pallas_call x1, Pallas kernels, scan(): pl.pallas_call(functools.partial(scan_kernel, taps), out_shape=jax.ShapeD...  6.66 us
    ppermute x7, waiting for transfers between devices, body(): lax.ppermute(outs[s], axes, [(i, (i + s) % parts) for i in range(parts)])  3.75 us
    ppermute x2, waiting for transfers between devices, swap(): lax.ppermute(value, 'doc', [(i, i + 1 - 2 * (i % 2)) for i in range(count)])  3.58 us
  transfers between devices with their start and end apart: 21, of which 8 were waited for; matrix products, arithmetic and copies ran while one was open for 6% of the time, Pallas kernels for 16%

profile of v3, /device:TPU:0, one launch (start us, length us, event | category | flops | bytes accessed | tf_op | source)
XLA Modules:
  0.0 102.5 jit_solution(7461209000774107837)
XLA Ops:
  0.0 1.0 slice_bitcast_fusion
  1.0 5.1 %collective-permute-start.2 = (bf16[32,2048]{1,0:T(8,128)(2,1)S(1)}, bf16[32,2048]{1,0:T(8,128)(2,1)S(1)}, u32[]{:S(2)}, u32[]{:S(2)}) collective-permute-start(bf16[32,2048]{1,0:T(8,128)(2,1)S(1)} %get-tuple-element.68.refs_0_), channel_id=1, source_target_pairs={{0,24},{8,0},{16,8},{24,16},{1,25},{9,1},{17,9},{25,17},{2,26},{10... | collective-permute-start | bytes 393224 | tf_op jit(solution)/shard_map/ppermute | solution.py:27
  6.1 0.0 collective-permute-start.1
  6.1 1.0 collective-permute-start
  7.1 0.7 convert_element_type.49
  7.8 0.1 copy.20
  7.9 0.8 pad_maximum_fusion.8
  8.7 1.5 %collective-permute-start.4 = (bf16[16,2176]{1,0:T(8,128)(2,1)S(1)}, bf16[16,2176]{1,0:T(8,128)(2,1)S(1)}, u32[]{:S(2)}, u32[]{:S(2)}) collective-permute-start(bf16[16,2176]{1,0:T(8,128)(2,1)S(1)} %pad_maximum_fusion.8), channel_id=1, source_target_pairs={{0,4},{4,0},{1,5},{5,1},{2,6},{6,2},{3,7},{7,3},{8,12},{12,8},{9,1... | collective-permute-start | bytes 208904 | tf_op jit(solution)/shard_map/ppermute | solution.py:27
  10.3 0.7 pad.12.router
  11.0 0.7 pad.13.gain
  11.7 1.6 %concatenate.24.params = f32[16,2048]{1,0:T(8,128)S(1)} concatenate(f32[4,2048]{1,0:T(4,128)} %param.21, f32[1,2048]{1,0:T(1,128)} %bitcast.26, f32[1,2048]{1,0:T(1,128)} %bitcast.27, f32[1,2048]{1,0:T(1,128)} %bitcast.28, f32[1,2048]{1,0:T(1,128)S(1)} %slice.15, f32[5,2048]{1,0:T(8,128)S(1)} %broadcast_in_dim.22, bf16[3,2048]{1,0:T(4,128)(2,1)} %param.19), dimensions={0} | concatenate | bytes 249856 | tf_op jit(solution)/shard_map/concatenate | solution.py:558
  13.3 0.1 pad_add_fusion.places
  13.4 0.0 collective-permute-done.4
  13.4 1.0 maximum_select_fusion
  14.4 0.0 collective-permute-done.2.refs_3_
  14.4 2.9 %collective-permute-done.1.refs_2_ = bf16[32,2048]{1,0:T(8,128)(2,1)S(1)} collective-permute-done((bf16[32,2048]{1,0:T(8,128)(2,1)S(1)}, bf16[32,2048]{1,0:T(8,128)(2,1)S(1)}, u32[]{:S(2)}, u32[]{:S(2)}) %collective-permute-start.1) | collective-permute-done | bytes 131104 | tf_op jit(solution)/shard_map/ppermute | solution.py:27
  17.3 0.0 collective-permute-done.refs_1_
  17.3 2.1 %activate.1 = (bf16[128,2048]{1,0:T(8,128)(2,1)S(1)}, f32[160,128]{1,0:T(8,128)S(1)}) custom-call(s32[4]{0:T(128)S(1)} %pad_add_fusion.places, f32[16,2048]{1,0:T(8,128)S(1)} %concatenate.24.params, bf16[160,2048]{1,0:T(8,128)(2,1)} %select.38, bf16[32,2048]{1,0:T(8,128)(2,1)S(1)} %get-tuple-element.68.refs_0_, ...), custom_call_target="tpu_custom_call" | custom-call | flops 83886080 | bytes 1048576 | tf_op jit(solution)/shard_map/activate/pallas_call | solution.py:106
  19.4 1.6 %collective-permute-start.3 = (f32[160,128]{1,0:T(8,128)S(1)}, f32[160,128]{1,0:T(8,128)S(1)}, u32[]{:S(2)}, u32[]{:S(2)}) collective-permute-start(f32[160,128]{1,0:T(8,128)S(1)} %get-tuple-element.37.own), channel_id=1, source_target_pairs={{0,4},{4,0},{1,5},{5,1},{2,6},{6,2},{3,7},{7,3},{8,12},{12,8},{9,1... | collective-permute-start | bytes 245768 | tf_op jit(solution)/shard_map/ppermute | solution.py:27
  21.1 0.8 collective-permute-start.5
  21.8 2.0 %collective-permute-start.6 = (bf16[32,2688]{1,0:T(8,128)(2,1)S(1)}, bf16[32,2688]{1,0:T(8,128)(2,1)S(1)}, u32[]{:S(2)}, u32[]{:S(2)}) collective-permute-start(bf16[32,2688]{1,0:T(8,128)(2,1)S(1)} %get-tuple-element.40), channel_id=1, source_target_pairs={{0,16},{8,24},{16,0},{24,8},{1,17},{9,25},{17,1},{25,9},{2,18},{10... | collective-permute-start | bytes 516104 | tf_op jit(solution)/shard_map/ppermute | solution.py:27
  23.8 2.8 %collective-permute-start.7 = (bf16[32,2688]{1,0:T(8,128)(2,1)S(1)}, bf16[32,2688]{1,0:T(8,128)(2,1)S(1)}, u32[]{:S(2)}, u32[]{:S(2)}) collective-permute-start(bf16[32,2688]{1,0:T(8,128)(2,1)S(1)} %get-tuple-element.41), channel_id=1, source_target_pairs={{0,24},{8,0},{16,8},{24,16},{1,25},{9,1},{17,9},{25,17},{2,26},{10... | collective-permute-start | bytes 516104 | tf_op jit(solution)/shard_map/ppermute | solution.py:27
  26.7 0.0 collective-permute-done.3.other
  26.7 6.7 %scan.1.value_in = f32[128,2048]{1,0:T(8,128)S(1)} custom-call(f32[160,128]{1,0:T(8,128)S(1)} %get-tuple-element.37.own, f32[160,128]{1,0:T(8,128)S(1)} %collective-permute-done.3.other, bf16[128,2048]{1,0:T(8,128)(2,1)S(1)} %get-tuple-element.38.active, f32[16,2048]{1,0:T(8,128)S(1)} %concatenate.24.params, f32[16,2048]{1,0:T(8,128)} %log_rate_hbm.1, ...), custom_call_target="tpu_custom_call" | custom-call | flops 12582912000 | bytes 2097152 | tf_op jit(solution)/shard_map/scan/pallas_call | solution.py:228
  33.4 0.0 collective-permute-done.5.refs_1_
  33.4 2.4 %collective-permute-done.6.refs_2_ = bf16[32,2688]{1,0:T(8,128)(2,1)S(1)} collective-permute-done((bf16[32,2688]{1,0:T(8,128)(2,1)S(1)}, bf16[32,2688]{1,0:T(8,128)(2,1)S(1)}, u32[]{:S(2)}, u32[]{:S(2)}) %collective-permute-start.6) | collective-permute-done | bytes 172064 | tf_op jit(solution)/shard_map/ppermute | solution.py:27
  35.8 0.0 collective-permute-done.7.refs_3_
  35.8 2.6 %project.1 = (f32[128,512]{1,0:T(8,128)S(1)}, bf16[128,512]{1,0:T(8,128)(2,1)S(1)}, bf16[128,128]{1,0:T(8,128)(2,1)S(1)}) custom-call(s32[4]{0:T(128)S(1)} %pad_add_fusion.places, f32[128,2048]{1,0:T(8,128)S(1)} %scan.1.value_in, bf16[2048,512]{1,0:T(8,128)(2,1)} %weight_hbm.1, bf16[32,2688]{1,0:T(8,128)(2,1)S(1)} %get-tuple-element.72.refs_0_, ...), custom_call_target="tpu_custom_call" | custom-call | flops 268435456 | bytes 2097152 | tf_op jit(solution)/shard_map/project/pallas_call | solution.py:290
  38.4 0.6 collective-permute-start.8
  39.0 4.5 %collective-permute-done.8 = bf16[128,512]{1,0:T(8,128)(2,1)S(1)} collective-permute-done((bf16[128,512]{1,0:T(8,128)(2,1)S(1)}, bf16[128,512]{1,0:T(8,128)(2,1)S(1)}, u32[]{:S(2)}, u32[]{:S(2)}) %collective-permute-start.8) | collective-permute-done | bytes 131104 | tf_op jit(solution)/shard_map/ppermute | solution.py:27
  43.5 5.2 %collective-permute-start.11 = (bf16[128,512]{1,0:T(8,128)(2,1)S(1)}, bf16[128,512]{1,0:T(8,128)(2,1)S(1)}, u32[]{:S(2)}, u32[]{:S(2)}) collective-permute-start(bf16[128,512]{1,0:T(8,128)(2,1)S(1)} %add_convert_fusion.refs_0_), channel_id=1, source_target_pairs={{0,24},{8,0},{16,8},{24,16},{1,25},{9,1},{17,9},{25,17},{2,26},{10... | collective-permute-start | bytes 393224 | tf_op jit(solution)/shard_map/ppermute | solution.py:27
  48.7 0.0 collective-permute-start.10
  48.7 0.6 collective-permute-start.9
  49.4 0.1 pad_add_fusion.1.spots
  49.4 10.0 %fetch.1 = (bf16[3584,2048]{1,0:T(8,128)(2,1)S(1)}, bf16[3584,2048]{1,0:T(8,128)(2,1)S(1)}, s32[1]{0:T(128)}) custom-call(s32[1]{0:T(128)} %bitcast.6.half, bf16[7168,2048]{1,0:T(8,128)(2,1)} %refs_0_.1, bf16[7168,2048]{1,0:T(8,128)(2,1)} %refs_1_.1), custom_call_target="tpu_custom_call" | custom-call | bytes 58720256 | tf_op jit(solution)/shard_map/fetch/pallas_call | solution.py:395
  59.4 0.0 collective-permute-done.11.refs_3_
  59.5 0.0 collective-permute-done.10.refs_2_
  59.5 0.0 collective-permute-done.9.refs_1_
  59.5 1.6 %norm.1 = (bf16[128,2048]{1,0:T(8,128)(2,1)S(1)}, f32[128,128]{1,0:T(8,128)S(1)}, bf16[16,2048]{1,0:T(8,128)(2,1)S(1)}) custom-call(s32[4]{0:T(128)S(1)} %pad_add_fusion.places, s32[2]{0:T(128)S(1)} %pad_add_fusion.1.spots, f32[8,2048]{1,0:T(8,128)S(1)} %pad.13.gain, bf16[16,2048]{1,0:T(8,128)(2,1)S(1)} %pad.12.router, ...), custom_call_target="tpu_custom_call" | custom-call | tf_op jit(solution)/shard_map/norm/pallas_call | solution.py:354
  61.1 0.1 collective-permute-start.12
  61.2 1.9 %collective-permute-done.12.other = bf16[128,2048]{1,0:T(8,128)(2,1)S(1)} collective-permute-done((bf16[128,2048]{1,0:T(8,128)(2,1)S(1)}, bf16[128,2048]{1,0:T(8,128)(2,1)S(1)}, u32[]{:S(2)}, u32[]{:S(2)}) %collective-permute-start.12) | collective-permute-done | bytes 524320 | tf_op jit(solution)/shard_map/ppermute | solution.py:53
  63.1 20.2 %experts.1 = (f32[128,2048]{1,0:T(8,128)S(1)}, bf16[128,2048]{1,0:T(8,128)(2,1)S(1)}) custom-call(s32[1]{0:T(128)} %get-tuple-element.52.half, bf16[128,2048]{1,0:T(8,128)(2,1)S(1)} %get-tuple-element.53.own, bf16[128,2048]{1,0:T(8,128)(2,1)S(1)} %collective-permute-done.12.other, bf16[3584,2048]{1,0:T(8,128)(2,1)S(1)} %get-tuple-element.54.gate, ...), custom_call_target="tpu_custom_call" | custom-call | flops 11274289152 | bytes 44040192 | tf_op jit(solution)/shard_map/experts/pallas_call | solution.py:441
  83.3 0.2 collective-permute-start.13
  83.5 0.1 stack.67.targets
  83.6 1.7 %collective-permute-done.13.other = bf16[128,2048]{1,0:T(8,128)(2,1)S(1)} collective-permute-done((bf16[128,2048]{1,0:T(8,128)(2,1)S(1)}, bf16[128,2048]{1,0:T(8,128)(2,1)S(1)}, u32[]{:S(2)}, u32[]{:S(2)}) %collective-permute-start.13) | collective-permute-done | bytes 524320 | tf_op jit(solution)/shard_map/ppermute | solution.py:53
  85.3 0.7 combine.1
  86.0 0.6 collective-permute-start.14
  86.5 2.8 %collective-permute-start.15 = (bf16[16,2048]{1,0:T(8,128)(2,1)S(1)}, bf16[16,2048]{1,0:T(8,128)(2,1)S(1)}, u32[]{:S(2)}, u32[]{:S(2)}) collective-permute-start(bf16[16,2048]{1,0:T(8,128)(2,1)S(1)} %get-tuple-element.61), channel_id=1, source_target_pairs={{0,8},{4,12},{8,16},{12,20},{16,24},{20,28},{24,0},{28,4},{1,9},{5... | collective-permute-start | bytes 196616 | tf_op jit(solution)/shard_map/ppermute | solution.py:602
  89.4 1.9 %collective-permute-start.16 = (bf16[16,2048]{1,0:T(8,128)(2,1)S(1)}, bf16[16,2048]{1,0:T(8,128)(2,1)S(1)}, u32[]{:S(2)}, u32[]{:S(2)}) collective-permute-start(bf16[16,2048]{1,0:T(8,128)(2,1)S(1)} %get-tuple-element.62), channel_id=1, source_target_pairs={{0,12},{4,16},{8,20},{12,24},{16,28},{20,0},{24,4},{28,8},{1,13},{... | collective-permute-start | bytes 196616 | tf_op jit(solution)/shard_map/ppermute | solution.py:602
  91.3 2.9 %collective-permute-start.17 = (bf16[16,2048]{1,0:T(8,128)(2,1)S(1)}, bf16[16,2048]{1,0:T(8,128)(2,1)S(1)}, u32[]{:S(2)}, u32[]{:S(2)}) collective-permute-start(bf16[16,2048]{1,0:T(8,128)(2,1)S(1)} %get-tuple-element.63), channel_id=1, source_target_pairs={{0,16},{4,20},{8,24},{12,28},{16,0},{20,4},{24,8},{28,12},{1,17},{... | collective-permute-start | bytes 196616 | tf_op jit(solution)/shard_map/ppermute | solution.py:602
  94.2 0.0 collective-permute-start.18
  94.2 0.0 collective-permute-done.14
  94.2 2.4 %collective-permute-start.19 = (bf16[16,2048]{1,0:T(8,128)(2,1)S(1)}, bf16[16,2048]{1,0:T(8,128)(2,1)S(1)}, u32[]{:S(2)}, u32[]{:S(2)}) collective-permute-start(bf16[16,2048]{1,0:T(8,128)(2,1)S(1)} %get-tuple-element.65), channel_id=1, source_target_pairs={{0,24},{4,28},{8,0},{12,4},{16,8},{20,12},{24,16},{28,20},{1,25},{... | collective-permute-start | bytes 196616 | tf_op jit(solution)/shard_map/ppermute | solution.py:602
  96.5 0.0 collective-permute-done.15
  96.6 1.5 %collective-permute-start.20 = (bf16[16,2048]{1,0:T(8,128)(2,1)S(1)}, bf16[16,2048]{1,0:T(8,128)(2,1)S(1)}, u32[]{:S(2)}, u32[]{:S(2)}) collective-permute-start(bf16[16,2048]{1,0:T(8,128)(2,1)S(1)} %get-tuple-element.66), channel_id=1, source_target_pairs={{0,28},{4,0},{8,4},{12,8},{16,12},{20,16},{24,20},{28,24},{1,29},{... | collective-permute-start | bytes 196616 | tf_op jit(solution)/shard_map/ppermute | solution.py:602
  98.0 1.8 %collective-permute-done.16 = bf16[16,2048]{1,0:T(8,128)(2,1)S(1)} collective-permute-done((bf16[16,2048]{1,0:T(8,128)(2,1)S(1)}, bf16[16,2048]{1,0:T(8,128)(2,1)S(1)}, u32[]{:S(2)}, u32[]{:S(2)}) %collective-permute-start.16) | collective-permute-done | bytes 65568 | tf_op jit(solution)/shard_map/ppermute | solution.py:602
  99.8 0.0 collective-permute-done.17
  99.9 0.6 collective-permute-done.18
  100.4 1.3 %collective-permute-done.19 = bf16[16,2048]{1,0:T(8,128)(2,1)S(1)} collective-permute-done((bf16[16,2048]{1,0:T(8,128)(2,1)S(1)}, bf16[16,2048]{1,0:T(8,128)(2,1)S(1)}, u32[]{:S(2)}, u32[]{:S(2)}) %collective-permute-start.19) | collective-permute-done | bytes 65568 | tf_op jit(solution)/shard_map/ppermute | solution.py:602
  101.8 0.0 collective-permute-done.20
  101.8 0.7 add_convert_fusion.1
  (8 shorter events, 0.1 us)
Async XLA Ops:
  1.0 13.4 %collective-permute-start.2 = (bf16[32,2048]{1,0:T(8,128)(2,1)S(1)}, bf16[32,2048]{1,0:T(8,128)(2,1)S(1)}, u32[]{:S(2)}, u32[]{:S(2)}) collective-permute-start(bf16[32,2048]{1,0:T(8,128)(2,1)S(1)} %get-tuple-element.68.refs_0_), channel_id=1, source_target_pairs={{0,24},{8,0},{16,8},{24,16},{1,25},{9,1},{17,9},{25,17},{2,26},{10... | collective-permute-start | bytes 393224 | tf_op jit(solution)/shard_map/ppermute | solution.py:27
  6.1 11.2 %collective-permute-start.1 = (bf16[32,2048]{1,0:T(8,128)(2,1)S(1)}, bf16[32,2048]{1,0:T(8,128)(2,1)S(1)}, u32[]{:S(2)}, u32[]{:S(2)}) collective-permute-start(bf16[32,2048]{1,0:T(8,128)(2,1)S(1)} %get-tuple-element.68.refs_0_), channel_id=1, source_target_pairs={{0,16},{8,24},{16,0},{24,8},{1,17},{9,25},{17,1},{25,9},{2,18},{10... | collective-permute-start | bytes 393224 | tf_op jit(solution)/shard_map/ppermute | solution.py:27
  6.1 11.2 %collective-permute-start = (bf16[32,2048]{1,0:T(8,128)(2,1)S(1)}, bf16[32,2048]{1,0:T(8,128)(2,1)S(1)}, u32[]{:S(2)}, u32[]{:S(2)}) collective-permute-start(bf16[32,2048]{1,0:T(8,128)(2,1)S(1)} %get-tuple-element.68.refs_0_), channel_id=1, source_target_pairs={{0,8},{8,16},{16,24},{24,0},{1,9},{9,17},{17,25},{25,1},{2,10},{10... | collective-permute-start | bytes 393224 | tf_op jit(solution)/shard_map/ppermute | solution.py:27
  8.7 4.7 %collective-permute-start.4 = (bf16[16,2176]{1,0:T(8,128)(2,1)S(1)}, bf16[16,2176]{1,0:T(8,128)(2,1)S(1)}, u32[]{:S(2)}, u32[]{:S(2)}) collective-permute-start(bf16[16,2176]{1,0:T(8,128)(2,1)S(1)} %pad_maximum_fusion.8), channel_id=1, source_target_pairs={{0,4},{4,0},{1,5},{5,1},{2,6},{6,2},{3,7},{7,3},{8,12},{12,8},{9,1... | collective-permute-start | bytes 208904 | tf_op jit(solution)/shard_map/ppermute | solution.py:27
  19.4 7.2 %collective-permute-start.3 = (f32[160,128]{1,0:T(8,128)S(1)}, f32[160,128]{1,0:T(8,128)S(1)}, u32[]{:S(2)}, u32[]{:S(2)}) collective-permute-start(f32[160,128]{1,0:T(8,128)S(1)} %get-tuple-element.37.own), channel_id=1, source_target_pairs={{0,4},{4,0},{1,5},{5,1},{2,6},{6,2},{3,7},{7,3},{8,12},{12,8},{9,1... | collective-permute-start | bytes 245768 | tf_op jit(solution)/shard_map/ppermute | solution.py:27
  21.1 12.3 %collective-permute-start.5 = (bf16[32,2688]{1,0:T(8,128)(2,1)S(1)}, bf16[32,2688]{1,0:T(8,128)(2,1)S(1)}, u32[]{:S(2)}, u32[]{:S(2)}) collective-permute-start(bf16[32,2688]{1,0:T(8,128)(2,1)S(1)} %get-tuple-element.39), channel_id=1, source_target_pairs={{0,8},{8,16},{16,24},{24,0},{1,9},{9,17},{17,25},{25,1},{2,10},{10... | collective-permute-start | bytes 516104 | tf_op jit(solution)/shard_map/ppermute | solution.py:27
  21.8 14.0 %collective-permute-start.6 = (bf16[32,2688]{1,0:T(8,128)(2,1)S(1)}, bf16[32,2688]{1,0:T(8,128)(2,1)S(1)}, u32[]{:S(2)}, u32[]{:S(2)}) collective-permute-start(bf16[32,2688]{1,0:T(8,128)(2,1)S(1)} %get-tuple-element.40), channel_id=1, source_target_pairs={{0,16},{8,24},{16,0},{24,8},{1,17},{9,25},{17,1},{25,9},{2,18},{10... | collective-permute-start | bytes 516104 | tf_op jit(solution)/shard_map/ppermute | solution.py:27
  23.8 12.0 %collective-permute-start.7 = (bf16[32,2688]{1,0:T(8,128)(2,1)S(1)}, bf16[32,2688]{1,0:T(8,128)(2,1)S(1)}, u32[]{:S(2)}, u32[]{:S(2)}) collective-permute-start(bf16[32,2688]{1,0:T(8,128)(2,1)S(1)} %get-tuple-element.41), channel_id=1, source_target_pairs={{0,24},{8,0},{16,8},{24,16},{1,25},{9,1},{17,9},{25,17},{2,26},{10... | collective-permute-start | bytes 516104 | tf_op jit(solution)/shard_map/ppermute | solution.py:27
  38.4 5.0 %collective-permute-start.8 = (bf16[128,512]{1,0:T(8,128)(2,1)S(1)}, bf16[128,512]{1,0:T(8,128)(2,1)S(1)}, u32[]{:S(2)}, u32[]{:S(2)}) collective-permute-start(bf16[128,512]{1,0:T(8,128)(2,1)S(1)} %get-tuple-element.43), channel_id=1, source_target_pairs={{0,4},{4,0},{1,5},{5,1},{2,6},{6,2},{3,7},{7,3},{8,12},{12,8},{9,1... | collective-permute-start | bytes 393224 | tf_op jit(solution)/shard_map/ppermute | solution.py:27
  43.5 15.9 %collective-permute-start.11 = (bf16[128,512]{1,0:T(8,128)(2,1)S(1)}, bf16[128,512]{1,0:T(8,128)(2,1)S(1)}, u32[]{:S(2)}, u32[]{:S(2)}) collective-permute-start(bf16[128,512]{1,0:T(8,128)(2,1)S(1)} %add_convert_fusion.refs_0_), channel_id=1, source_target_pairs={{0,24},{8,0},{16,8},{24,16},{1,25},{9,1},{17,9},{25,17},{2,26},{10... | collective-permute-start | bytes 393224 | tf_op jit(solution)/shard_map/ppermute | solution.py:27
  48.7 10.7 %collective-permute-start.10 = (bf16[128,512]{1,0:T(8,128)(2,1)S(1)}, bf16[128,512]{1,0:T(8,128)(2,1)S(1)}, u32[]{:S(2)}, u32[]{:S(2)}) collective-permute-start(bf16[128,512]{1,0:T(8,128)(2,1)S(1)} %add_convert_fusion.refs_0_), channel_id=1, source_target_pairs={{0,16},{8,24},{16,0},{24,8},{1,17},{9,25},{17,1},{25,9},{2,18},{10... | collective-permute-start | bytes 393224 | tf_op jit(solution)/shard_map/ppermute | solution.py:27
  48.7 10.8 %collective-permute-start.9 = (bf16[128,512]{1,0:T(8,128)(2,1)S(1)}, bf16[128,512]{1,0:T(8,128)(2,1)S(1)}, u32[]{:S(2)}, u32[]{:S(2)}) collective-permute-start(bf16[128,512]{1,0:T(8,128)(2,1)S(1)} %add_convert_fusion.refs_0_), channel_id=1, source_target_pairs={{0,8},{8,16},{16,24},{24,0},{1,9},{9,17},{17,25},{25,1},{2,10},{10... | collective-permute-start | bytes 393224 | tf_op jit(solution)/shard_map/ppermute | solution.py:27
  61.1 2.0 %collective-permute-start.12 = (bf16[128,2048]{1,0:T(8,128)(2,1)S(1)}, bf16[128,2048]{1,0:T(8,128)(2,1)S(1)}, u32[]{:S(2)}, u32[]{:S(2)}) collective-permute-start(bf16[128,2048]{1,0:T(8,128)(2,1)S(1)} %get-tuple-element.53.own), channel_id=1, source_target_pairs={{0,1},{1,0},{2,3},{3,2},{4,5},{5,4},{6,7},{7,6},{8,9},{9,8},{10,11... | collective-permute-start | bytes 1572872 | tf_op jit(solution)/shard_map/ppermute | solution.py:53
  83.3 2.0 %collective-permute-start.13 = (bf16[128,2048]{1,0:T(8,128)(2,1)S(1)}, bf16[128,2048]{1,0:T(8,128)(2,1)S(1)}, u32[]{:S(2)}, u32[]{:S(2)}) collective-permute-start(bf16[128,2048]{1,0:T(8,128)(2,1)S(1)} %get-tuple-element.57), channel_id=1, source_target_pairs={{0,1},{1,0},{2,3},{3,2},{4,5},{5,4},{6,7},{7,6},{8,9},{9,8},{10,11... | collective-permute-start | bytes 1572872 | tf_op jit(solution)/shard_map/ppermute | solution.py:53
  86.0 8.2 %collective-permute-start.14 = (bf16[16,2048]{1,0:T(8,128)(2,1)S(1)}, bf16[16,2048]{1,0:T(8,128)(2,1)S(1)}, u32[]{:S(2)}, u32[]{:S(2)}) collective-permute-start(bf16[16,2048]{1,0:T(8,128)(2,1)S(1)} %get-tuple-element.60), channel_id=1, source_target_pairs={{0,4},{4,8},{8,12},{12,16},{16,20},{20,24},{24,28},{28,0},{1,5},{5... | collective-permute-start | bytes 196616 | tf_op jit(solution)/shard_map/ppermute | solution.py:602
  86.5 10.0 %collective-permute-start.15 = (bf16[16,2048]{1,0:T(8,128)(2,1)S(1)}, bf16[16,2048]{1,0:T(8,128)(2,1)S(1)}, u32[]{:S(2)}, u32[]{:S(2)}) collective-permute-start(bf16[16,2048]{1,0:T(8,128)(2,1)S(1)} %get-tuple-element.61), channel_id=1, source_target_pairs={{0,8},{4,12},{8,16},{12,20},{16,24},{20,28},{24,0},{28,4},{1,9},{5... | collective-permute-start | bytes 196616 | tf_op jit(solution)/shard_map/ppermute | solution.py:602
  89.4 10.4 %collective-permute-start.16 = (bf16[16,2048]{1,0:T(8,128)(2,1)S(1)}, bf16[16,2048]{1,0:T(8,128)(2,1)S(1)}, u32[]{:S(2)}, u32[]{:S(2)}) collective-permute-start(bf16[16,2048]{1,0:T(8,128)(2,1)S(1)} %get-tuple-element.62), channel_id=1, source_target_pairs={{0,12},{4,16},{8,20},{12,24},{16,28},{20,0},{24,4},{28,8},{1,13},{... | collective-permute-start | bytes 196616 | tf_op jit(solution)/shard_map/ppermute | solution.py:602
  91.3 8.6 %collective-permute-start.17 = (bf16[16,2048]{1,0:T(8,128)(2,1)S(1)}, bf16[16,2048]{1,0:T(8,128)(2,1)S(1)}, u32[]{:S(2)}, u32[]{:S(2)}) collective-permute-start(bf16[16,2048]{1,0:T(8,128)(2,1)S(1)} %get-tuple-element.63), channel_id=1, source_target_pairs={{0,16},{4,20},{8,24},{12,28},{16,0},{20,4},{24,8},{28,12},{1,17},{... | collective-permute-start | bytes 196616 | tf_op jit(solution)/shard_map/ppermute | solution.py:602
  94.2 6.3 %collective-permute-start.18 = (bf16[16,2048]{1,0:T(8,128)(2,1)S(1)}, bf16[16,2048]{1,0:T(8,128)(2,1)S(1)}, u32[]{:S(2)}, u32[]{:S(2)}) collective-permute-start(bf16[16,2048]{1,0:T(8,128)(2,1)S(1)} %get-tuple-element.64), channel_id=1, source_target_pairs={{0,20},{4,24},{8,28},{12,0},{16,4},{20,8},{24,12},{28,16},{1,21},{... | collective-permute-start | bytes 196616 | tf_op jit(solution)/shard_map/ppermute | solution.py:602
  94.2 7.6 %collective-permute-start.19 = (bf16[16,2048]{1,0:T(8,128)(2,1)S(1)}, bf16[16,2048]{1,0:T(8,128)(2,1)S(1)}, u32[]{:S(2)}, u32[]{:S(2)}) collective-permute-start(bf16[16,2048]{1,0:T(8,128)(2,1)S(1)} %get-tuple-element.65), channel_id=1, source_target_pairs={{0,24},{4,28},{8,0},{12,4},{16,8},{20,12},{24,16},{28,20},{1,25},{... | collective-permute-start | bytes 196616 | tf_op jit(solution)/shard_map/ppermute | solution.py:602
  96.6 5.2 %collective-permute-start.20 = (bf16[16,2048]{1,0:T(8,128)(2,1)S(1)}, bf16[16,2048]{1,0:T(8,128)(2,1)S(1)}, u32[]{:S(2)}, u32[]{:S(2)}) collective-permute-start(bf16[16,2048]{1,0:T(8,128)(2,1)S(1)} %get-tuple-element.66), channel_id=1, source_target_pairs={{0,28},{4,0},{8,4},{12,8},{16,12},{20,16},{24,20},{28,24},{1,29},{... | collective-permute-start | bytes 196616 | tf_op jit(solution)/shard_map/ppermute | solution.py:602

commit v4 on v3

--- a/solution.py
+++ b/solution.py
@@ -366,7 +366,7 @@
     )(places, spots, gain, router, routes, *pieces)
 
 
-def fetch_kernel(parts, half, *refs):
+def fetch_kernel(parts, half_rows, half, *refs):
     count = len(refs) // 2 - 1
     sources, targets, done, sems = refs[:count], refs[count : 2 * count], refs[-2], refs[-1]
     rows = targets[0].shape[0]
@@ -374,7 +374,7 @@
     copies = []
     for index in range(count):
         for k in range(parts):
-            start = pl.multiple_of(half[0] * rows + k * part, 16)
+            start = pl.multiple_of(half[0] * half_rows + k * part, 16)
             copies.append(
                 pltpu.make_async_copy(
                     sources[index].at[pl.ds(start, part), :],
@@ -390,10 +390,11 @@
 
 
 def fetch(half, weights):
-    rows, width = weights[0].shape[0] // 2, weights[0].shape[1]
+    half_rows, width = weights[0].shape[0] // 2, weights[0].shape[1]
+    rows = half_rows // 2
     parts = 4
     return pl.pallas_call(
-        functools.partial(fetch_kernel, parts),
+        functools.partial(fetch_kernel, parts, half_rows),
         out_shape=tuple([VMEM((rows, width), BF16)] * len(weights)) + (jax.ShapeDtypeStruct((1,), jnp.int32),),
         in_specs=[SCALARS] + [FAR] * len(weights),
         out_specs=tuple([WHOLE] * len(weights)) + (SCALARS,),
@@ -406,57 +407,64 @@
     )(half, *[far(w) for w in weights])
 
 
-def shared_kernel(steps, block, half, own, other, gate, up, down, kept, given, tokens, hidden):
-    number = pl.program_id(0)
+def shared_kernel(half, own, other, gate_first, up_first, gate, up, down, kept, given, tokens, hidden, late, last, sems):
     rows = own.shape[0]
-
-    @pl.when(number == 0)
-    def _():
-        tokens[0:rows, :] = own[...]
-        tokens[rows:, :] = other[...]
-
-    @pl.when(number < steps)
-    def _():
-        here = pl.ds(pl.multiple_of(number * block, block), block)
-        gate_act = contract_last(tokens[...], gate[here, :])
-        up_act = contract_last(tokens[...], up[here, :])
+    quarter, width = gate_first.shape
+    begin = half[0] * (2 * quarter)
+    copies = []
+    for index, (source, offset) in enumerate(((gate, quarter), (up, quarter), (down, 0), (down, quarter))):
+        here = pl.ds(pl.multiple_of(begin + offset, 16), quarter)
+        target = late.at[index] if index < 2 else last.at[index - 2]
+        copies.append(pltpu.make_async_copy(source.at[here, :], target, sems.at[index]))
+    for copy in copies:
+        copy.start()
+    tokens[0:rows, :] = own[...]
+    tokens[rows:, :] = other[...]
+
+    def activate_hidden(gate_rows, up_rows, place):
+        gate_act = contract_last(tokens[...], gate_rows[...])
+        up_act = contract_last(tokens[...], up_rows[...])
         value = gate_act / (1.0 + jnp.exp(-gate_act)) * up_act
-        hidden[:, here] = value.astype(BF16)
-
-    @pl.when(number >= steps)
-    def _():
-        width = down.shape[1]
-        here = pl.ds(pl.multiple_of((number - steps) * width, width), width)
-        product = jnp.dot(hidden[...], down[...], preferred_element_type=F32)
+        hidden[:, place * quarter : (place + 1) * quarter] = value.astype(BF16)
+
+    activate_hidden(gate_first, up_first, 0)
+    copies[0].wait()
+    copies[1].wait()
+    activate_hidden(late.at[0], late.at[1], 1)
+    copies[2].wait()
+    copies[3].wait()
+    step = 256
+    for start in range(0, width, step):
+        here = slice(start, start + step)
+        product = jnp.dot(hidden[:, :quarter], last[0, :, here], preferred_element_type=F32)
+        product += jnp.dot(hidden[:, quarter:], last[1, :, here], preferred_element_type=F32)
         kept[:, here] = product[0:rows, :]
         given[:, here] = product[rows:, :].astype(BF16)
 
 
-def shared_experts(half, own, other, gate, up, down):
+def shared_experts(half, own, other, gate_first, up_first, gate, up, down):
     rows, width = own.shape
-    depth = gate.shape[0]
-    block = math.gcd(depth, 512)
-    steps = depth // block
-    columns = 256
-    return pl.pallas_call(
-        functools.partial(shared_kernel, steps, block),
+    quarter = gate_first.shape[0]
+    return pl.pallas_call(
+        shared_kernel,
         out_shape=(jax.ShapeDtypeStruct((rows, width), F32), jax.ShapeDtypeStruct((rows, width), BF16)),
-        grid_spec=pltpu.PrefetchScalarGridSpec(
-            num_scalar_prefetch=1,
-            grid=(steps + width // columns,),
-            in_specs=[WHOLE] * 4
-            + [pl.BlockSpec((depth, columns), lambda i, half: (half[0], jnp.maximum(i - steps, 0)))],
-            out_specs=(WHOLE,) * 2,
-            scratch_shapes=[VMEM((2 * rows, width), BF16), VMEM((2 * rows, depth), BF16)],
-        ),
-        compiler_params=pltpu.CompilerParams(vmem_limit_bytes=16 << 20),
+        in_specs=[SCALARS] + [WHOLE] * 4 + [FAR] * 3,
+        out_specs=(WHOLE,) * 2,
+        scratch_shapes=[
+            VMEM((2 * rows, width), BF16),
+            VMEM((2 * rows, 2 * quarter), BF16),
+            VMEM((2, quarter, width), BF16),
+            VMEM((2, quarter, width), BF16),
+            pltpu.SemaphoreType.DMA((4,)),
+        ],
+        compiler_params=pltpu.CompilerParams(vmem_limit_bytes=36 << 20),
         cost_estimate=pl.CostEstimate(
-            flops=12 * rows * depth * width,
-            bytes_accessed=6 * depth * width,
-            transcendentals=2 * rows * depth,
+            flops=24 * rows * quarter * width,
+            bytes_accessed=8 * quarter * width,
+            transcendentals=4 * rows * quarter,
         ),
         name="experts",
-    )(half, own, other, gate, up, far(down))
+    )(half, own, other, gate_first, up_first, far(gate), far(up), far(down))
 
 
 def expert_kernel(tokens, gate, up, down, total):
@@ -584,7 +592,7 @@
     if shared:
         half = lax.rem(lax.axis_index("doc"), 2).astype(jnp.int32)[None]
         half, mixed = lax.optimization_barrier((half, mixed))
-        gate_half, up_half, half = fetch(half, [gate_weight, up_weight])
+        gate_first, up_first, half = fetch(half, [gate_weight, up_weight])
     mixed_pieces = spread(lambda k: mixed, "ctx", 1)
     me = ctx_at * exp + exp_at
     spots = jnp.stack([ctx_at // (ctx // EXPERTS), me]).astype(jnp.int32)
@@ -594,7 +602,7 @@
     total = mine.astype(F32)
     axes = ("ctx", "exp")
     if shared:
-        kept, given = shared_experts(half, normed, swap(normed), gate_half, up_half, down_weight)
+        kept, given = shared_experts(half, normed, swap(normed), gate_first, up_first, gate_weight, up_weight, down_weight)
         targets = jnp.stack([lax.rem(me + s, parts) for s in range(parts)]).astype(jnp.int32)
         outs = combine(targets, kept, swap(given), weight, own)
         arrived = [outs[0]]

time: 103 us -> 94.9 us (0.921)
  Pallas kernels: 44 us -> 34.5 us
  waiting for transfers between devices: 17.1 us -> 21.1 us
  starting transfers between devices: 33.5 us -> 30.8 us
    pallas_call x2, Pallas kernels: 30.2 us -> 20.7 us  [the longest x1 14.9 us: shared_experts(): pl.pallas_call(shared_kernel, out_shape=(jax.ShapeDtypeStruct((rows, widt...]
    ppermute x12, waiting for transfers between devices: 9.79 us -> 13.1 us  [rotate(): lax.ppermute(value, axis, [(i, (i + steps) % count) for i in range(count)])]
    ppermute x7, starting transfers between devices: 12 us -> 9.33 us  [body(): lax.ppermute(outs[s], axes, [(i, (i + s) % parts) for i in range(parts)])]
  transfers between devices with their start and end apart: 21 -> 21, of which waited for: 8 -> 9; matrix products, arithmetic and copies ran while one was open for 6% -> 6% of each run, Pallas kernels for 16% -> 13%
where the time goes in v4:
time: 94.9 us; the launch traced here: 94.2 us
  Pallas kernels  34.5 us (36%)
  starting transfers between devices  30.8 us (32%)
  waiting for transfers between devices  21.1 us (22%)
  local copies, waits for them, and re-layouts  4.25 us (4%)
  other arithmetic  3.42 us (4%)
    ppermute x12, starting transfers between devices, rotate(): lax.ppermute(value, axis, [(i, (i + steps) % count) for i in range(count)])  21.2 us
    pallas_call x1, Pallas kernels, shared_experts(): pl.pallas_call(shared_kernel, out_shape=(jax.ShapeDtypeStruct((rows, widt...  14.9 us
    ppermute x12, waiting for transfers between devices, rotate(): lax.ppermute(value, axis, [(i, (i + steps) % count) for i in range(count)])  13.1 us
    ppermute x7, starting transfers between devices, body(): lax.ppermute(outs[s], axes, [(i, (i + s) % parts) for i in range(parts)])  9.33 us
    pallas_call x1, Pallas kernels, scan(): pl.pallas_call(functools.partial(scan_kernel, taps), out_shape=jax.ShapeD...  6.67 us
    pallas_call x1, Pallas kernels, fetch(): pl.pallas_call(functools.partial(fetch_kernel, parts, half_rows), out_sha...  5.82 us
    ppermute x7, waiting for transfers between devices, body(): lax.ppermute(outs[s], axes, [(i, (i + s) % parts) for i in range(parts)])  4.41 us
    ppermute x2, waiting for transfers between devices, swap(): lax.ppermute(value, 'doc', [(i, i + 1 - 2 * (i % 2)) for i in range(count)])  3.58 us
  transfers between devices with their start and end apart: 21, of which 9 were waited for; matrix products, arithmetic and copies ran while one was open for 6% of the time, Pallas kernels for 13%

profile of v4, /device:TPU:0, one launch (start us, length us, event | category | flops | bytes accessed | tf_op | source)
XLA Modules:
  0.0 94.2 jit_solution(13957245306620966080)
XLA Ops:
  0.0 1.0 %slice_bitcast_fusion = (bf16[32,2048]{1,0:T(8,128)(2,1)S(1)}, bf16[32,2048]{1,0:T(8,128)(2,1)S(1)}) fusion(bf16[2,32,2048]{2,1,0:T(8,128)(2,1)} %param.18), kind=kLoop, calls=%fused_computation.11 | loop fusion | bytes 524288 | tf_op jit(solution)/shard_map/squeeze | solution.py:549
  1.0 5.1 %collective-permute-start.2 = (bf16[32,2048]{1,0:T(8,128)(2,1)S(1)}, bf16[32,2048]{1,0:T(8,128)(2,1)S(1)}, u32[]{:S(2)}, u32[]{:S(2)}) collective-permute-start(bf16[32,2048]{1,0:T(8,128)(2,1)S(1)} %get-tuple-element.68.refs_0_), channel_id=1, source_target_pairs={{0,24},{8,0},{16,8},{24,16},{1,25},{9,1},{17,9},{25,17},{2,26},{10... | collective-permute-start | bytes 393224 | tf_op jit(solution)/shard_map/ppermute | solution.py:27
  6.1 0.0 collective-permute-start.1
  6.1 1.0 %collective-permute-start = (bf16[32,2048]{1,0:T(8,128)(2,1)S(1)}, bf16[32,2048]{1,0:T(8,128)(2,1)S(1)}, u32[]{:S(2)}, u32[]{:S(2)}) collective-permute-start(bf16[32,2048]{1,0:T(8,128)(2,1)S(1)} %get-tuple-element.68.refs_0_), channel_id=1, source_target_pairs={{0,8},{8,16},{16,24},{24,0},{1,9},{9,17},{17,25},{25,1},{2,10},{10... | collective-permute-start | bytes 393224 | tf_op jit(solution)/shard_map/ppermute | solution.py:27
  7.1 0.7 convert_element_type.49
  7.8 0.1 copy.20
  7.9 0.8 pad_maximum_fusion.8
  8.7 1.5 %collective-permute-start.4 = (bf16[16,2176]{1,0:T(8,128)(2,1)S(1)}, bf16[16,2176]{1,0:T(8,128)(2,1)S(1)}, u32[]{:S(2)}, u32[]{:S(2)}) collective-permute-start(bf16[16,2176]{1,0:T(8,128)(2,1)S(1)} %pad_maximum_fusion.8), channel_id=1, source_target_pairs={{0,4},{4,0},{1,5},{5,1},{2,6},{6,2},{3,7},{7,3},{8,12},{12,8},{9,1... | collective-permute-start | bytes 208904 | tf_op jit(solution)/shard_map/ppermute | solution.py:27
  10.3 0.7 pad.12.router
  11.0 0.7 pad.13.gain
  11.7 1.6 %concatenate.24.params = f32[16,2048]{1,0:T(8,128)S(1)} concatenate(f32[4,2048]{1,0:T(4,128)} %param.21, f32[1,2048]{1,0:T(1,128)} %bitcast.26, f32[1,2048]{1,0:T(1,128)} %bitcast.27, f32[1,2048]{1,0:T(1,128)} %bitcast.28, f32[1,2048]{1,0:T(1,128)S(1)} %slice.15, f32[5,2048]{1,0:T(8,128)S(1)} %broadcast_in_dim.22, bf16[3,2048]{1,0:T(4,128)(2,1)} %param.19), dimensions={0} | concatenate | bytes 249856 | tf_op jit(solution)/shard_map/concatenate | solution.py:566
  13.3 0.1 pad_add_fusion.places
  13.4 0.0 collective-permute-done.4
  13.4 1.0 %maximum_select_fusion = bf16[32,2176]{1,0:T(8,128)(2,1)S(1)} fusion(bf16[16,2176]{1,0:T(8,128)(2,1)S(1)} %collective-permute-done.4, bf16[16,128]{1,0:T(8,128)(2,1)S(1)} %pad.14, bf16[16,2048]{1,0:T(8,128)(2,1)} %param.29, pred[]{:T(512)S(6)} %eq.3), kind=kLoop, calls=%fused_computation.9 | loop fusion | flops 905216 | bytes 278529 | tf_op jit(solution)/shard_map/jit(_where)/select_n | solution.py:558
  14.4 0.0 collective-permute-done.2.refs_3_
  14.4 2.9 %collective-permute-done.1.refs_2_ = bf16[32,2048]{1,0:T(8,128)(2,1)S(1)} collective-permute-done((bf16[32,2048]{1,0:T(8,128)(2,1)S(1)}, bf16[32,2048]{1,0:T(8,128)(2,1)S(1)}, u32[]{:S(2)}, u32[]{:S(2)}) %collective-permute-start.1) | collective-permute-done | bytes 131104 | tf_op jit(solution)/shard_map/ppermute | solution.py:27
  17.3 0.0 collective-permute-done.refs_1_
  17.3 2.1 %activate.1 = (bf16[128,2048]{1,0:T(8,128)(2,1)S(1)}, f32[160,128]{1,0:T(8,128)S(1)}) custom-call(s32[4]{0:T(128)S(1)} %pad_add_fusion.places, f32[16,2048]{1,0:T(8,128)S(1)} %concatenate.24.params, bf16[160,2048]{1,0:T(8,128)(2,1)} %select.38, bf16[32,2048]{1,0:T(8,128)(2,1)S(1)} %get-tuple-element.68.refs_0_, ...), custom_call_target="tpu_custom_call" | custom-call | flops 83886080 | bytes 1048576 | tf_op jit(solution)/shard_map/activate/pallas_call | solution.py:106
  19.4 1.6 %collective-permute-start.3 = (f32[160,128]{1,0:T(8,128)S(1)}, f32[160,128]{1,0:T(8,128)S(1)}, u32[]{:S(2)}, u32[]{:S(2)}) collective-permute-start(f32[160,128]{1,0:T(8,128)S(1)} %get-tuple-element.37.own), channel_id=1, source_target_pairs={{0,4},{4,0},{1,5},{5,1},{2,6},{6,2},{3,7},{7,3},{8,12},{12,8},{9,1... | collective-permute-start | bytes 245768 | tf_op jit(solution)/shard_map/ppermute | solution.py:27
  21.1 0.8 collective-permute-start.5
  21.8 2.0 %collective-permute-start.6 = (bf16[32,2688]{1,0:T(8,128)(2,1)S(1)}, bf16[32,2688]{1,0:T(8,128)(2,1)S(1)}, u32[]{:S(2)}, u32[]{:S(2)}) collective-permute-start(bf16[32,2688]{1,0:T(8,128)(2,1)S(1)} %get-tuple-element.40), channel_id=1, source_target_pairs={{0,16},{8,24},{16,0},{24,8},{1,17},{9,25},{17,1},{25,9},{2,18},{10... | collective-permute-start | bytes 516104 | tf_op jit(solution)/shard_map/ppermute | solution.py:27
  23.8 2.8 %collective-permute-start.7 = (bf16[32,2688]{1,0:T(8,128)(2,1)S(1)}, bf16[32,2688]{1,0:T(8,128)(2,1)S(1)}, u32[]{:S(2)}, u32[]{:S(2)}) collective-permute-start(bf16[32,2688]{1,0:T(8,128)(2,1)S(1)} %get-tuple-element.41), channel_id=1, source_target_pairs={{0,24},{8,0},{16,8},{24,16},{1,25},{9,1},{17,9},{25,17},{2,26},{10... | collective-permute-start | bytes 516104 | tf_op jit(solution)/shard_map/ppermute | solution.py:27
  26.7 0.0 collective-permute-done.3.other
  26.7 6.7 %scan.1.value_in = f32[128,2048]{1,0:T(8,128)S(1)} custom-call(f32[160,128]{1,0:T(8,128)S(1)} %get-tuple-element.37.own, f32[160,128]{1,0:T(8,128)S(1)} %collective-permute-done.3.other, bf16[128,2048]{1,0:T(8,128)(2,1)S(1)} %get-tuple-element.38.active, f32[16,2048]{1,0:T(8,128)S(1)} %concatenate.24.params, f32[16,2048]{1,0:T(8,128)} %log_rate_hbm.1, ...), custom_call_target="tpu_custom_call" | custom-call | flops 12582912000 | bytes 2097152 | tf_op jit(solution)/shard_map/scan/pallas_call | solution.py:228
  33.4 0.0 collective-permute-done.5.refs_1_
  33.4 2.4 %collective-permute-done.6.refs_2_ = bf16[32,2688]{1,0:T(8,128)(2,1)S(1)} collective-permute-done((bf16[32,2688]{1,0:T(8,128)(2,1)S(1)}, bf16[32,2688]{1,0:T(8,128)(2,1)S(1)}, u32[]{:S(2)}, u32[]{:S(2)}) %collective-permute-start.6) | collective-permute-done | bytes 172064 | tf_op jit(solution)/shard_map/ppermute | solution.py:27
  35.8 0.0 collective-permute-done.7.refs_3_
  35.8 2.6 %project.1 = (f32[128,512]{1,0:T(8,128)S(1)}, bf16[128,512]{1,0:T(8,128)(2,1)S(1)}, bf16[128,128]{1,0:T(8,128)(2,1)S(1)}) custom-call(s32[4]{0:T(128)S(1)} %pad_add_fusion.places, f32[128,2048]{1,0:T(8,128)S(1)} %scan.1.value_in, bf16[2048,512]{1,0:T(8,128)(2,1)} %weight_hbm.1, bf16[32,2688]{1,0:T(8,128)(2,1)S(1)} %get-tuple-element.72.refs_0_, ...), custom_call_target="tpu_custom_call" | custom-call | flops 268435456 | bytes 2097152 | tf_op jit(solution)/shard_map/project/pallas_call | solution.py:290
  38.5 0.6 collective-permute-start.8
  39.0 4.5 %collective-permute-done.8 = bf16[128,512]{1,0:T(8,128)(2,1)S(1)} collective-permute-done((bf16[128,512]{1,0:T(8,128)(2,1)S(1)}, bf16[128,512]{1,0:T(8,128)(2,1)S(1)}, u32[]{:S(2)}, u32[]{:S(2)}) %collective-permute-start.8) | collective-permute-done | bytes 131104 | tf_op jit(solution)/shard_map/ppermute | solution.py:27
  43.5 5.2 %collective-permute-start.11 = (bf16[128,512]{1,0:T(8,128)(2,1)S(1)}, bf16[128,512]{1,0:T(8,128)(2,1)S(1)}, u32[]{:S(2)}, u32[]{:S(2)}) collective-permute-start(bf16[128,512]{1,0:T(8,128)(2,1)S(1)} %add_convert_fusion.refs_0_), channel_id=1, source_target_pairs={{0,24},{8,0},{16,8},{24,16},{1,25},{9,1},{17,9},{25,17},{2,26},{10... | collective-permute-start | bytes 393224 | tf_op jit(solution)/shard_map/ppermute | solution.py:27
  48.7 0.0 collective-permute-start.10
  48.7 0.6 collective-permute-start.9
  49.3 0.1 pad_add_fusion.1.spots
  49.4 5.8 %fetch.1 = (bf16[1792,2048]{1,0:T(8,128)(2,1)S(1)}, bf16[1792,2048]{1,0:T(8,128)(2,1)S(1)}, s32[1]{0:T(128)}) custom-call(s32[1]{0:T(128)} %bitcast.6.half, bf16[7168,2048]{1,0:T(8,128)(2,1)} %gate.1, bf16[7168,2048]{1,0:T(8,128)(2,1)} %up.1), custom_call_target="tpu_custom_call" | custom-call | bytes 29360128 | tf_op jit(solution)/shard_map/fetch/pallas_call | solution.py:396
  55.3 0.0 collective-permute-done.11.refs_3_
  55.3 3.3 %collective-permute-done.10.refs_2_ = bf16[128,512]{1,0:T(8,128)(2,1)S(1)} collective-permute-done((bf16[128,512]{1,0:T(8,128)(2,1)S(1)}, bf16[128,512]{1,0:T(8,128)(2,1)S(1)}, u32[]{:S(2)}, u32[]{:S(2)}) %collective-permute-start.10) | collective-permute-done | bytes 131104 | tf_op jit(solution)/shard_map/ppermute | solution.py:27
  58.5 0.0 collective-permute-done.9.refs_1_
  58.5 1.6 %norm.1 = (bf16[128,2048]{1,0:T(8,128)(2,1)S(1)}, f32[128,128]{1,0:T(8,128)S(1)}, bf16[16,2048]{1,0:T(8,128)(2,1)S(1)}) custom-call(s32[4]{0:T(128)S(1)} %pad_add_fusion.places, s32[2]{0:T(128)S(1)} %pad_add_fusion.1.spots, f32[8,2048]{1,0:T(8,128)S(1)} %pad.13.gain, bf16[16,2048]{1,0:T(8,128)(2,1)S(1)} %pad.12.router, ...), custom_call_target="tpu_custom_call" | custom-call | tf_op jit(solution)/shard_map/norm/pallas_call | solution.py:354
  60.2 0.1 collective-permute-start.12
  60.2 1.9 %collective-permute-done.12.other = bf16[128,2048]{1,0:T(8,128)(2,1)S(1)} collective-permute-done((bf16[128,2048]{1,0:T(8,128)(2,1)S(1)}, bf16[128,2048]{1,0:T(8,128)(2,1)S(1)}, u32[]{:S(2)}, u32[]{:S(2)}) %collective-permute-start.12) | collective-permute-done | bytes 524320 | tf_op jit(solution)/shard_map/ppermute | solution.py:53
  62.1 14.9 %experts.1 = (f32[128,2048]{1,0:T(8,128)S(1)}, bf16[128,2048]{1,0:T(8,128)(2,1)S(1)}) custom-call(s32[1]{0:T(128)} %get-tuple-element.52.half, bf16[128,2048]{1,0:T(8,128)(2,1)S(1)} %get-tuple-element.53.own, bf16[128,2048]{1,0:T(8,128)(2,1)S(1)} %collective-permute-done.12.other, bf16[1792,2048]{1,0:T(8,128)(2,1)S(1)} %get-tuple-element.54.gate_first, ...), custom_call_target="tpu_custom_call" | custom-call | flops 11274289152 | bytes 29360128 | tf_op jit(solution)/shard_map/experts/pallas_call | solution.py:448
  77.0 0.2 collective-permute-start.13
  77.2 0.1 stack.67.targets
  77.3 1.7 %collective-permute-done.13.other = bf16[128,2048]{1,0:T(8,128)(2,1)S(1)} collective-permute-done((bf16[128,2048]{1,0:T(8,128)(2,1)S(1)}, bf16[128,2048]{1,0:T(8,128)(2,1)S(1)}, u32[]{:S(2)}, u32[]{:S(2)}) %collective-permute-start.13) | collective-permute-done | bytes 524320 | tf_op jit(solution)/shard_map/ppermute | solution.py:53
  79.0 0.7 combine.1
  79.7 0.6 collective-permute-start.14
  80.3 0.0 collective-permute-start.15
  80.3 2.4 %collective-permute-start.16 = (bf16[16,2048]{1,0:T(8,128)(2,1)S(1)}, bf16[16,2048]{1,0:T(8,128)(2,1)S(1)}, u32[]{:S(2)}, u32[]{:S(2)}) collective-permute-start(bf16[16,2048]{1,0:T(8,128)(2,1)S(1)} %get-tuple-element.62), channel_id=1, source_target_pairs={{0,12},{4,16},{8,20},{12,24},{16,28},{20,0},{24,4},{28,8},{1,13},{... | collective-permute-start | bytes 196616 | tf_op jit(solution)/shard_map/ppermute | solution.py:610
  82.7 2.4 %collective-permute-start.17 = (bf16[16,2048]{1,0:T(8,128)(2,1)S(1)}, bf16[16,2048]{1,0:T(8,128)(2,1)S(1)}, u32[]{:S(2)}, u32[]{:S(2)}) collective-permute-start(bf16[16,2048]{1,0:T(8,128)(2,1)S(1)} %get-tuple-element.63), channel_id=1, source_target_pairs={{0,16},{4,20},{8,24},{12,28},{16,0},{20,4},{24,8},{28,12},{1,17},{... | collective-permute-start | bytes 196616 | tf_op jit(solution)/shard_map/ppermute | solution.py:610
  85.1 0.6 collective-permute-start.18
  85.6 1.9 %collective-permute-done.14 = bf16[16,2048]{1,0:T(8,128)(2,1)S(1)} collective-permute-done((bf16[16,2048]{1,0:T(8,128)(2,1)S(1)}, bf16[16,2048]{1,0:T(8,128)(2,1)S(1)}, u32[]{:S(2)}, u32[]{:S(2)}) %collective-permute-start.14) | collective-permute-done | bytes 65568 | tf_op jit(solution)/shard_map/ppermute | solution.py:610
  87.5 1.0 %collective-permute-start.19 = (bf16[16,2048]{1,0:T(8,128)(2,1)S(1)}, bf16[16,2048]{1,0:T(8,128)(2,1)S(1)}, u32[]{:S(2)}, u32[]{:S(2)}) collective-permute-start(bf16[16,2048]{1,0:T(8,128)(2,1)S(1)} %get-tuple-element.65), channel_id=1, source_target_pairs={{0,24},{4,28},{8,0},{12,4},{16,8},{20,12},{24,16},{28,20},{1,25},{... | collective-permute-start | bytes 196616 | tf_op jit(solution)/shard_map/ppermute | solution.py:610
  88.5 0.0 collective-permute-done.15
  88.5 2.4 %collective-permute-start.20 = (bf16[16,2048]{1,0:T(8,128)(2,1)S(1)}, bf16[16,2048]{1,0:T(8,128)(2,1)S(1)}, u32[]{:S(2)}, u32[]{:S(2)}) collective-permute-start(bf16[16,2048]{1,0:T(8,128)(2,1)S(1)} %get-tuple-element.66), channel_id=1, source_target_pairs={{0,28},{4,0},{8,4},{12,8},{16,12},{20,16},{24,20},{28,24},{1,29},{... | collective-permute-start | bytes 196616 | tf_op jit(solution)/shard_map/ppermute | solution.py:610
  90.9 1.4 %collective-permute-done.16 = bf16[16,2048]{1,0:T(8,128)(2,1)S(1)} collective-permute-done((bf16[16,2048]{1,0:T(8,128)(2,1)S(1)}, bf16[16,2048]{1,0:T(8,128)(2,1)S(1)}, u32[]{:S(2)}, u32[]{:S(2)}) %collective-permute-start.16) | collective-permute-done | bytes 65568 | tf_op jit(solution)/shard_map/ppermute | solution.py:610
  92.3 0.0 collective-permute-done.17
  92.3 0.0 collective-permute-done.18
  92.3 1.1 %collective-permute-done.19 = bf16[16,2048]{1,0:T(8,128)(2,1)S(1)} collective-permute-done((bf16[16,2048]{1,0:T(8,128)(2,1)S(1)}, bf16[16,2048]{1,0:T(8,128)(2,1)S(1)}, u32[]{:S(2)}, u32[]{:S(2)}) %collective-permute-start.19) | collective-permute-done | bytes 65568 | tf_op jit(solution)/shard_map/ppermute | solution.py:610
  93.5 0.0 collective-permute-done.20
  93.5 0.7 add_convert_fusion.1
  (8 shorter events, 0.1 us)
Async XLA Ops:
  1.0 13.4 %collective-permute-start.2 = (bf16[32,2048]{1,0:T(8,128)(2,1)S(1)}, bf16[32,2048]{1,0:T(8,128)(2,1)S(1)}, u32[]{:S(2)}, u32[]{:S(2)}) collective-permute-start(bf16[32,2048]{1,0:T(8,128)(2,1)S(1)} %get-tuple-element.68.refs_0_), channel_id=1, source_target_pairs={{0,24},{8,0},{16,8},{24,16},{1,25},{9,1},{17,9},{25,17},{2,26},{10... | collective-permute-start | bytes 393224 | tf_op jit(solution)/shard_map/ppermute | solution.py:27
  6.1 11.2 %collective-permute-start.1 = (bf16[32,2048]{1,0:T(8,128)(2,1)S(1)}, bf16[32,2048]{1,0:T(8,128)(2,1)S(1)}, u32[]{:S(2)}, u32[]{:S(2)}) collective-permute-start(bf16[32,2048]{1,0:T(8,128)(2,1)S(1)} %get-tuple-element.68.refs_0_), channel_id=1, source_target_pairs={{0,16},{8,24},{16,0},{24,8},{1,17},{9,25},{17,1},{25,9},{2,18},{10... | collective-permute-start | bytes 393224 | tf_op jit(solution)/shard_map/ppermute | solution.py:27
  6.1 11.2 %collective-permute-start = (bf16[32,2048]{1,0:T(8,128)(2,1)S(1)}, bf16[32,2048]{1,0:T(8,128)(2,1)S(1)}, u32[]{:S(2)}, u32[]{:S(2)}) collective-permute-start(bf16[32,2048]{1,0:T(8,128)(2,1)S(1)} %get-tuple-element.68.refs_0_), channel_id=1, source_target_pairs={{0,8},{8,16},{16,24},{24,0},{1,9},{9,17},{17,25},{25,1},{2,10},{10... | collective-permute-start | bytes 393224 | tf_op jit(solution)/shard_map/ppermute | solution.py:27
  8.7 4.7 %collective-permute-start.4 = (bf16[16,2176]{1,0:T(8,128)(2,1)S(1)}, bf16[16,2176]{1,0:T(8,128)(2,1)S(1)}, u32[]{:S(2)}, u32[]{:S(2)}) collective-permute-start(bf16[16,2176]{1,0:T(8,128)(2,1)S(1)} %pad_maximum_fusion.8), channel_id=1, source_target_pairs={{0,4},{4,0},{1,5},{5,1},{2,6},{6,2},{3,7},{7,3},{8,12},{12,8},{9,1... | collective-permute-start | bytes 208904 | tf_op jit(solution)/shard_map/ppermute | solution.py:27
  19.4 7.2 %collective-permute-start.3 = (f32[160,128]{1,0:T(8,128)S(1)}, f32[160,128]{1,0:T(8,128)S(1)}, u32[]{:S(2)}, u32[]{:S(2)}) collective-permute-start(f32[160,128]{1,0:T(8,128)S(1)} %get-tuple-element.37.own), channel_id=1, source_target_pairs={{0,4},{4,0},{1,5},{5,1},{2,6},{6,2},{3,7},{7,3},{8,12},{12,8},{9,1... | collective-permute-start | bytes 245768 | tf_op jit(solution)/shard_map/ppermute | solution.py:27
  21.1 12.3 %collective-permute-start.5 = (bf16[32,2688]{1,0:T(8,128)(2,1)S(1)}, bf16[32,2688]{1,0:T(8,128)(2,1)S(1)}, u32[]{:S(2)}, u32[]{:S(2)}) collective-permute-start(bf16[32,2688]{1,0:T(8,128)(2,1)S(1)} %get-tuple-element.39), channel_id=1, source_target_pairs={{0,8},{8,16},{16,24},{24,0},{1,9},{9,17},{17,25},{25,1},{2,10},{10... | collective-permute-start | bytes 516104 | tf_op jit(solution)/shard_map/ppermute | solution.py:27
  21.8 14.0 %collective-permute-start.6 = (bf16[32,2688]{1,0:T(8,128)(2,1)S(1)}, bf16[32,2688]{1,0:T(8,128)(2,1)S(1)}, u32[]{:S(2)}, u32[]{:S(2)}) collective-permute-start(bf16[32,2688]{1,0:T(8,128)(2,1)S(1)} %get-tuple-element.40), channel_id=1, source_target_pairs={{0,16},{8,24},{16,0},{24,8},{1,17},{9,25},{17,1},{25,9},{2,18},{10... | collective-permute-start | bytes 516104 | tf_op jit(solution)/shard_map/ppermute | solution.py:27
  23.8 12.0 %collective-permute-start.7 = (bf16[32,2688]{1,0:T(8,128)(2,1)S(1)}, bf16[32,2688]{1,0:T(8,128)(2,1)S(1)}, u32[]{:S(2)}, u32[]{:S(2)}) collective-permute-start(bf16[32,2688]{1,0:T(8,128)(2,1)S(1)} %get-tuple-element.41), channel_id=1, source_target_pairs={{0,24},{8,0},{16,8},{24,16},{1,25},{9,1},{17,9},{25,17},{2,26},{10... | collective-permute-start | bytes 516104 | tf_op jit(solution)/shard_map/ppermute | solution.py:27
  38.5 5.0 %collective-permute-start.8 = (bf16[128,512]{1,0:T(8,128)(2,1)S(1)}, bf16[128,512]{1,0:T(8,128)(2,1)S(1)}, u32[]{:S(2)}, u32[]{:S(2)}) collective-permute-start(bf16[128,512]{1,0:T(8,128)(2,1)S(1)} %get-tuple-element.43), channel_id=1, source_target_pairs={{0,4},{4,0},{1,5},{5,1},{2,6},{6,2},{3,7},{7,3},{8,12},{12,8},{9,1... | collective-permute-start | bytes 393224 | tf_op jit(solution)/shard_map/ppermute | solution.py:27
  43.5 11.7 %collective-permute-start.11 = (bf16[128,512]{1,0:T(8,128)(2,1)S(1)}, bf16[128,512]{1,0:T(8,128)(2,1)S(1)}, u32[]{:S(2)}, u32[]{:S(2)}) collective-permute-start(bf16[128,512]{1,0:T(8,128)(2,1)S(1)} %add_convert_fusion.refs_0_), channel_id=1, source_target_pairs={{0,24},{8,0},{16,8},{24,16},{1,25},{9,1},{17,9},{25,17},{2,26},{10... | collective-permute-start | bytes 393224 | tf_op jit(solution)/shard_map/ppermute | solution.py:27
  48.7 9.8 %collective-permute-start.10 = (bf16[128,512]{1,0:T(8,128)(2,1)S(1)}, bf16[128,512]{1,0:T(8,128)(2,1)S(1)}, u32[]{:S(2)}, u32[]{:S(2)}) collective-permute-start(bf16[128,512]{1,0:T(8,128)(2,1)S(1)} %add_convert_fusion.refs_0_), channel_id=1, source_target_pairs={{0,16},{8,24},{16,0},{24,8},{1,17},{9,25},{17,1},{25,9},{2,18},{10... | collective-permute-start | bytes 393224 | tf_op jit(solution)/shard_map/ppermute | solution.py:27
  48.7 9.8 %collective-permute-start.9 = (bf16[128,512]{1,0:T(8,128)(2,1)S(1)}, bf16[128,512]{1,0:T(8,128)(2,1)S(1)}, u32[]{:S(2)}, u32[]{:S(2)}) collective-permute-start(bf16[128,512]{1,0:T(8,128)(2,1)S(1)} %add_convert_fusion.refs_0_), channel_id=1, source_target_pairs={{0,8},{8,16},{16,24},{24,0},{1,9},{9,17},{17,25},{25,1},{2,10},{10... | collective-permute-start | bytes 393224 | tf_op jit(solution)/shard_map/ppermute | solution.py:27
  60.2 2.0 %collective-permute-start.12 = (bf16[128,2048]{1,0:T(8,128)(2,1)S(1)}, bf16[128,2048]{1,0:T(8,128)(2,1)S(1)}, u32[]{:S(2)}, u32[]{:S(2)}) collective-permute-start(bf16[128,2048]{1,0:T(8,128)(2,1)S(1)} %get-tuple-element.53.own), channel_id=1, source_target_pairs={{0,1},{1,0},{2,3},{3,2},{4,5},{5,4},{6,7},{7,6},{8,9},{9,8},{10,11... | collective-permute-start | bytes 1572872 | tf_op jit(solution)/shard_map/ppermute | solution.py:53
  77.0 2.0 %collective-permute-start.13 = (bf16[128,2048]{1,0:T(8,128)(2,1)S(1)}, bf16[128,2048]{1,0:T(8,128)(2,1)S(1)}, u32[]{:S(2)}, u32[]{:S(2)}) collective-permute-start(bf16[128,2048]{1,0:T(8,128)(2,1)S(1)} %get-tuple-element.57), channel_id=1, source_target_pairs={{0,1},{1,0},{2,3},{3,2},{4,5},{5,4},{6,7},{7,6},{8,9},{9,8},{10,11... | collective-permute-start | bytes 1572872 | tf_op jit(solution)/shard_map/ppermute | solution.py:53
  79.7 7.8 %collective-permute-start.14 = (bf16[16,2048]{1,0:T(8,128)(2,1)S(1)}, bf16[16,2048]{1,0:T(8,128)(2,1)S(1)}, u32[]{:S(2)}, u32[]{:S(2)}) collective-permute-start(bf16[16,2048]{1,0:T(8,128)(2,1)S(1)} %get-tuple-element.60), channel_id=1, source_target_pairs={{0,4},{4,8},{8,12},{12,16},{16,20},{20,24},{24,28},{28,0},{1,5},{5... | collective-permute-start | bytes 196616 | tf_op jit(solution)/shard_map/ppermute | solution.py:610
  80.3 8.2 %collective-permute-start.15 = (bf16[16,2048]{1,0:T(8,128)(2,1)S(1)}, bf16[16,2048]{1,0:T(8,128)(2,1)S(1)}, u32[]{:S(2)}, u32[]{:S(2)}) collective-permute-start(bf16[16,2048]{1,0:T(8,128)(2,1)S(1)} %get-tuple-element.61), channel_id=1, source_target_pairs={{0,8},{4,12},{8,16},{12,20},{16,24},{20,28},{24,0},{28,4},{1,9},{5... | collective-permute-start | bytes 196616 | tf_op jit(solution)/shard_map/ppermute | solution.py:610
  80.3 12.1 %collective-permute-start.16 = (bf16[16,2048]{1,0:T(8,128)(2,1)S(1)}, bf16[16,2048]{1,0:T(8,128)(2,1)S(1)}, u32[]{:S(2)}, u32[]{:S(2)}) collective-permute-start(bf16[16,2048]{1,0:T(8,128)(2,1)S(1)} %get-tuple-element.62), channel_id=1, source_target_pairs={{0,12},{4,16},{8,20},{12,24},{16,28},{20,0},{24,4},{28,8},{1,13},{... | collective-permute-start | bytes 196616 | tf_op jit(solution)/shard_map/ppermute | solution.py:610
  82.7 9.6 %collective-permute-start.17 = (bf16[16,2048]{1,0:T(8,128)(2,1)S(1)}, bf16[16,2048]{1,0:T(8,128)(2,1)S(1)}, u32[]{:S(2)}, u32[]{:S(2)}) collective-permute-start(bf16[16,2048]{1,0:T(8,128)(2,1)S(1)} %get-tuple-element.63), channel_id=1, source_target_pairs={{0,16},{4,20},{8,24},{12,28},{16,0},{20,4},{24,8},{28,12},{1,17},{... | collective-permute-start | bytes 196616 | tf_op jit(solution)/shard_map/ppermute | solution.py:610
  85.1 7.3 %collective-permute-start.18 = (bf16[16,2048]{1,0:T(8,128)(2,1)S(1)}, bf16[16,2048]{1,0:T(8,128)(2,1)S(1)}, u32[]{:S(2)}, u32[]{:S(2)}) collective-permute-start(bf16[16,2048]{1,0:T(8,128)(2,1)S(1)} %get-tuple-element.64), channel_id=1, source_target_pairs={{0,20},{4,24},{8,28},{12,0},{16,4},{20,8},{24,12},{28,16},{1,21},{... | collective-permute-start | bytes 196616 | tf_op jit(solution)/shard_map/ppermute | solution.py:610
  87.5 6.0 %collective-permute-start.19 = (bf16[16,2048]{1,0:T(8,128)(2,1)S(1)}, bf16[16,2048]{1,0:T(8,128)(2,1)S(1)}, u32[]{:S(2)}, u32[]{:S(2)}) collective-permute-start(bf16[16,2048]{1,0:T(8,128)(2,1)S(1)} %get-tuple-element.65), channel_id=1, source_target_pairs={{0,24},{4,28},{8,0},{12,4},{16,8},{20,12},{24,16},{28,20},{1,25},{... | collective-permute-start | bytes 196616 | tf_op jit(solution)/shard_map/ppermute | solution.py:610
  88.5 5.0 %collective-permute-start.20 = (bf16[16,2048]{1,0:T(8,128)(2,1)S(1)}, bf16[16,2048]{1,0:T(8,128)(2,1)S(1)}, u32[]{:S(2)}, u32[]{:S(2)}) collective-permute-start(bf16[16,2048]{1,0:T(8,128)(2,1)S(1)} %get-tuple-element.66), channel_id=1, source_target_pairs={{0,28},{4,0},{8,4},{12,8},{16,12},{20,16},{24,20},{28,24},{1,29},{... | collective-permute-start | bytes 196616 | tf_op jit(solution)/shard_map/ppermute | solution.py:610

commit v5 on v4

--- a/solution.py
+++ b/solution.py
@@ -33,6 +33,10 @@
         return jnp.zeros((1,), jnp.int32)
     me = lax.axis_index(axis)
     return jnp.stack([lax.rem(me + count - s, count) for s in range(count)]).astype(jnp.int32)
+
+
+def layer(piece, index):
+    return piece.at[index] if len(piece.shape) == 3 else piece
 
 
 def spread(make, axis, join, after=None):
@@ -77,7 +81,7 @@
     padded[0:8, :] = params[8:16, :]
     for index in range(count):
         start = pl.multiple_of(8 + places[index] * rows, 8)
-        padded[pl.ds(start, rows), :] = pieces[index][...].astype(F32)
+        padded[pl.ds(start, rows), :] = layer(pieces[index], 0)[...].astype(F32)
     tokens = active.shape[0]
     step = 32
 
@@ -252,22 +256,24 @@
     )(own, other, active, params, far(log_rate), far(step_weight), far(state_in))
 
 
-def project_kernel(count, columns, places, value_in, weight_hbm, *refs):
-    pieces = refs[:count]
-    base_out, send_out, routes_out, gated, out_weight, sem = refs[count:]
+def project_kernel(count, places, value_in, weight_hbm, *refs):
+    pieces, extras = refs[:count], refs[count : 2 * count]
+    base_out, send_out, routes_out, gated, out_weight, sem = refs[2 * count :]
     copy = pltpu.make_async_copy(weight_hbm, out_weight, sem)
     copy.start()
-    tokens, channels = value_in.shape
+    tokens = value_in.shape[0]
+    columns = base_out.shape[1]
     rows = pieces[0].shape[0]
     tile = 16
     for index in range(count):
         begin = pl.multiple_of(places[index] * rows, tile)
-        routes_out[pl.ds(begin, rows), :] = pieces[index][:, channels + columns :]
+        routes_out[pl.ds(begin, rows), :] = extras[index][:, columns:]
+        source = layer(pieces[index], 1)
 
         def gate(number, carry):
             local = pl.ds(pl.multiple_of(number * tile, tile), tile)
             here = pl.ds(pl.multiple_of(begin + number * tile, tile), tile)
-            z = pieces[index][local, :channels].astype(F32)
+            z = source[local, :].astype(F32)
             gated[here, :] = (value_in[here, :] * (z / (1.0 + jnp.exp(-z)))).astype(BF16)
             return carry
 
@@ -280,21 +286,21 @@
         base_out[cut, :] = sent.astype(F32)
     for index in range(count):
         here = pl.ds(pl.multiple_of(places[index] * rows, tile), rows)
-        base_out[here, :] += pieces[index][:, channels : channels + columns].astype(F32)
-
-
-def project(places, value, out_weight, pieces):
+        base_out[here, :] += extras[index][:, :columns].astype(F32)
+
+
+def project(places, value, out_weight, pieces, extras):
     tokens, channels = value.shape
     columns = out_weight.shape[1]
     count = len(pieces)
     return pl.pallas_call(
-        functools.partial(project_kernel, count, columns),
+        functools.partial(project_kernel, count),
         out_shape=(
             jax.ShapeDtypeStruct((tokens, columns), F32),
             jax.ShapeDtypeStruct((tokens, columns), BF16),
             jax.ShapeDtypeStruct((tokens, LANES), BF16),
         ),
-        in_specs=[SCALARS, WHOLE, FAR] + [WHOLE] * count,
+        in_specs=[SCALARS, WHOLE, FAR] + [WHOLE] * (2 * count),
         out_specs=(WHOLE,) * 3,
         scratch_shapes=[
             VMEM((tokens, channels), BF16),
@@ -308,13 +314,29 @@
             transcendentals=tokens * channels,
         ),
         name="project",
-    )(places, value, far(out_weight), *pieces)
-
-
-def norm_kernel(count, places, spots, gain, router, routes, *refs):
-    pieces = refs[:count]
-    normed, weight, own_rows = refs[count : count + 3]
-    mixed = pieces[0] if count == 1 else refs[-1]
+    )(places, value, far(out_weight), *pieces, *extras)
+
+
+def norm_kernel(count, early, places, spots, gain, router, routes, *refs):
+    pieces, sources = refs[:count], refs[count : count + early]
+    normed, weight, own_rows = refs[count + early : count + early + 3]
+    firsts, rest = refs[count + early + 3 : count + 2 * early + 3], refs[count + 2 * early + 3 :]
+    mixed = pieces[0] if count == 1 else rest[0]
+    copies = []
+    for index in range(early):
+        first = firsts[index].shape[0]
+        begin = pl.multiple_of(spots[2] * (sources[index].shape[0] // 2), 16)
+        part = first // 2
+        for k in range(2):
+            copies.append(
+                pltpu.make_async_copy(
+                    sources[index].at[pl.ds(begin + k * part, part), :],
+                    firsts[index].at[pl.ds(k * part, part), :],
+                    rest[-1].at[2 * index + k],
+                )
+            )
+    for copy in copies:
+        copy.start()
     tokens = normed.shape[0]
     columns = pieces[0].shape[1]
     for index in range(count if count > 1 else 0):
@@ -345,106 +367,83 @@
         weight[cut, :] = jnp.broadcast_to(first_gate + second_gate, (LANES, LANES))
     rows = own_rows.shape[0]
     own_rows[...] = mixed[pl.ds(pl.multiple_of(spots[1] * rows, 16), rows), :]
-
-
-def norm(places, spots, gain, router, routes, pieces, own):
-    count = len(pieces)
+    for copy in copies:
+        copy.wait()
+
+
+def norm(places, spots, gain, router, routes, pieces, own, weights, first):
+    count, early = len(pieces), len(weights)
     tokens = pieces[0].shape[0]
     width = count * pieces[0].shape[1]
     return pl.pallas_call(
-        functools.partial(norm_kernel, count),
+        functools.partial(norm_kernel, count, early),
         out_shape=(
             jax.ShapeDtypeStruct((tokens, width), BF16),
             jax.ShapeDtypeStruct((tokens, LANES), F32),
             jax.ShapeDtypeStruct((own, width), BF16),
-        ),
-        in_specs=[SCALARS] * 2 + [WHOLE] * (3 + count),
-        out_specs=(WHOLE,) * 3,
-        scratch_shapes=[VMEM((tokens, width), BF16)] if count > 1 else [],
+        )
+        + tuple(VMEM((first, width), BF16) for _ in weights),
+        in_specs=[SCALARS] * 2 + [WHOLE] * (3 + count) + [FAR] * early,
+        out_specs=(WHOLE,) * (3 + early),
+        scratch_shapes=([VMEM((tokens, width), BF16)] if count > 1 else [])
+        + ([pltpu.SemaphoreType.DMA((2 * early,))] if early else []),
         compiler_params=pltpu.CompilerParams(vmem_limit_bytes=8 << 20),
         name="norm",
-    )(places, spots, gain, router, routes, *pieces)
-
-
-def fetch_kernel(parts, half_rows, half, *refs):
-    count = len(refs) // 2 - 1
-    sources, targets, done, sems = refs[:count], refs[count : 2 * count], refs[-2], refs[-1]
-    rows = targets[0].shape[0]
-    part = rows // parts
-    copies = []
-    for index in range(count):
-        for k in range(parts):
-            start = pl.multiple_of(half[0] * half_rows + k * part, 16)
-            copies.append(
-                pltpu.make_async_copy(
-                    sources[index].at[pl.ds(start, part), :],
-                    targets[index].at[pl.ds(k * part, part), :],
-                    sems.at[index * parts + k],
-                )
-            )
-    for copy in copies:
-        copy.start()
-    for copy in copies:
-        copy.wait()
-    done[0] = half[0]
-
-
-def fetch(half, weights):
-    half_rows, width = weights[0].shape[0] // 2, weights[0].shape[1]
-    rows = half_rows // 2
-    parts = 4
-    return pl.pallas_call(
-        functools.partial(fetch_kernel, parts, half_rows),
-        out_shape=tuple([VMEM((rows, width), BF16)] * len(weights)) + (jax.ShapeDtypeStruct((1,), jnp.int32),),
-        in_specs=[SCALARS] + [FAR] * len(weights),
-        out_specs=tuple([WHOLE] * len(weights)) + (SCALARS,),
-        scratch_shapes=[pltpu.SemaphoreType.DMA((parts * len(weights),))],
-        compiler_params=pltpu.CompilerParams(vmem_limit_bytes=1 << 20),
-        cost_estimate=pl.CostEstimate(
-            flops=0, bytes_accessed=4 * rows * width * len(weights), transcendentals=0
-        ),
-        name="fetch",
-    )(half, *[far(w) for w in weights])
+    )(places, spots, gain, router, routes, *pieces, *[far(w) for w in weights])
 
 
 def shared_kernel(half, own, other, gate_first, up_first, gate, up, down, kept, given, tokens, hidden, late, last, sems):
     rows = own.shape[0]
-    quarter, width = gate_first.shape
-    begin = half[0] * (2 * quarter)
+    first, width = gate_first.shape
+    block = late.shape[2]
+    depth = hidden.shape[1]
+    begin = half[0] * depth
     copies = []
-    for index, (source, offset) in enumerate(((gate, quarter), (up, quarter), (down, 0), (down, quarter))):
-        here = pl.ds(pl.multiple_of(begin + offset, 16), quarter)
-        target = late.at[index] if index < 2 else last.at[index - 2]
-        copies.append(pltpu.make_async_copy(source.at[here, :], target, sems.at[index]))
-    for copy in copies:
-        copy.start()
+
+    def bring(source, offset, count, target):
+        here = pl.ds(pl.multiple_of(begin + offset, 16), count)
+        copies.append(pltpu.make_async_copy(source.at[here, :], target, sems.at[len(copies)]))
+        copies[-1].start()
+
+    for place in range(2):
+        bring(gate, first + place * block, block, late.at[place, 0])
+        bring(up, first + place * block, block, late.at[place, 1])
+    part = depth // 2
+    for place in range(2):
+        bring(down, place * part, part, last.at[pl.ds(place * part, part), :])
     tokens[0:rows, :] = own[...]
     tokens[rows:, :] = other[...]
 
-    def activate_hidden(gate_rows, up_rows, place):
+    def activate_hidden(gate_rows, up_rows, start):
         gate_act = contract_last(tokens[...], gate_rows[...])
         up_act = contract_last(tokens[...], up_rows[...])
         value = gate_act / (1.0 + jnp.exp(-gate_act)) * up_act
-        hidden[:, place * quarter : (place + 1) * quarter] = value.astype(BF16)
+        hidden[:, start : start + gate_rows.shape[0]] = value.astype(BF16)
 
     activate_hidden(gate_first, up_first, 0)
-    copies[0].wait()
-    copies[1].wait()
-    activate_hidden(late.at[0], late.at[1], 1)
-    copies[2].wait()
-    copies[3].wait()
+    for place in range(2):
+        copies[2 * place].wait()
+        copies[2 * place + 1].wait()
+        activate_hidden(late.at[place, 0], late.at[place, 1], first + place * block)
+    copies[4].wait()
+    copies[5].wait()
     step = 256
     for start in range(0, width, step):
         here = slice(start, start + step)
-        product = jnp.dot(hidden[:, :quarter], last[0, :, here], preferred_element_type=F32)
-        product += jnp.dot(hidden[:, quarter:], last[1, :, here], preferred_element_type=F32)
+        product = jnp.dot(hidden[...], last[:, here], preferred_element_type=F32)
         kept[:, here] = product[0:rows, :]
         given[:, here] = product[rows:, :].astype(BF16)
 
 
+def first_rows(depth):
+    first = 768
+    return first if depth > first and (depth - first) % (2 * LANES) == 0 else 0
+
+
 def shared_experts(half, own, other, gate_first, up_first, gate, up, down):
     rows, width = own.shape
-    quarter = gate_first.shape[0]
+    first = gate_first.shape[0]
+    depth = gate.shape[0] // 2
     return pl.pallas_call(
         shared_kernel,
         out_shape=(jax.ShapeDtypeStruct((rows, width), F32), jax.ShapeDtypeStruct((rows, width), BF16)),
@@ -452,16 +451,16 @@
         out_specs=(WHOLE,) * 2,
         scratch_shapes=[
             VMEM((2 * rows, width), BF16),
-            VMEM((2 * rows, 2 * quarter), BF16),
-            VMEM((2, quarter, width), BF16),
-            VMEM((2, quarter, width), BF16),
-            pltpu.SemaphoreType.DMA((4,)),
+            VMEM((2 * rows, depth), BF16),
+            VMEM((2, 2, (depth - first) // 2, width), BF16),
+            VMEM((depth, width), BF16),
+            pltpu.SemaphoreType.DMA((6,)),
         ],
-        compiler_params=pltpu.CompilerParams(vmem_limit_bytes=36 << 20),
+        compiler_params=pltpu.CompilerParams(vmem_limit_bytes=43 << 20),
         cost_estimate=pl.CostEstimate(
-            flops=24 * rows * quarter * width,
-            bytes_accessed=8 * quarter * width,
-            transcendentals=4 * rows * quarter,
+            flops=12 * rows * depth * width,
+            bytes_accessed=6 * depth * width,
+            transcendentals=2 * rows * depth,
         ),
         name="experts",
     )(half, own, other, gate_first, up_first, far(gate), far(up), far(down))
@@ -551,7 +550,12 @@
     columns = output_weight.shape[1]
     taps = filter_taps.shape[0]
 
-    x_pieces = spread(lambda k: x_input, "ctx", 0)
+    if ctx <= FEW:
+        passed = [rotate(projected, "ctx", s) for s in range(1, ctx)]
+        x_pieces, z_pieces = [x_input] + passed, [z_input] + passed
+    else:
+        passed = lax.all_gather(projected, "ctx", axis=1, tiled=True)
+        x_pieces, z_pieces = [passed[0]], [passed[1]]
     extra = jnp.concatenate([residual, jnp.pad(routes.astype(BF16), ((0, 0), (0, LANES - 2)))], axis=1)
     if exp == 2:
         partner = rotate(extra, "exp", 1)
@@ -567,7 +571,6 @@
         [filter_taps, filter_bias[None], step_bias[None], skip_gain[None], jnp.zeros_like(tail_pad)[: 5 - taps],
          tail_pad, carried_tail.astype(F32)]
     )
-    ready = [jnp.concatenate([z_input, extra[:, width:]], axis=1), extra[:, :width]]
     router_rows = jnp.pad(router.T, ((0, 16 - EXPERTS), (0, 0)))
     gain = jnp.pad(norm_gain[None, :], ((0, 7), (0, 0)))
     params, router_rows, gain = lax.optimization_barrier((params, router_rows, gain))
@@ -576,33 +579,33 @@
     own_proj, other_proj = pair_sum(proj, "exp")
 
     def bundle(k):
-        piece = lax.dynamic_slice_in_dim(ready[1], k * columns, columns, axis=1)
-        channels = z_input.shape[1]
-        return jnp.concatenate([ready[0][:, :channels], piece, ready[0][:, channels:]], axis=1)
-
-    z_pieces = spread(bundle, "ctx", 0, active)
+        piece = lax.dynamic_slice_in_dim(extra, k * columns, columns, axis=1)
+        return jnp.concatenate([piece, extra[:, width:]], axis=1)
+
+    extras = spread(bundle, "ctx", 0, active)
     value = scan(own_proj, other_proj, active, params, taps, log_rate, step_weight, carried_state)
-    base, sent, all_routes = project(places, value, output_weight, z_pieces)
+    base, sent, all_routes = project(places, value, output_weight, z_pieces, extras)
     if exp == 2:
         mixed = (base + rotate(sent, "exp", 1).astype(F32)).astype(BF16)
     else:
         mixed = (base - sent.astype(F32) + lax.psum(sent.astype(F32), "exp")).astype(BF16)
     parts = ctx * exp
-    shared = parts <= 8 and mixed.shape[0] == LANES and lax.axis_size("doc") % 2 == 0
-    if shared:
-        half = lax.rem(lax.axis_index("doc"), 2).astype(jnp.int32)[None]
-        half, mixed = lax.optimization_barrier((half, mixed))
-        gate_first, up_first, half = fetch(half, [gate_weight, up_weight])
+    first = first_rows(gate_weight.shape[0] // 2)
+    shared = parts <= 8 and mixed.shape[0] == LANES and lax.axis_size("doc") % 2 == 0 and first > 0
+    half = lax.rem(lax.axis_index("doc"), 2)
     mixed_pieces = spread(lambda k: mixed, "ctx", 1)
     me = ctx_at * exp + exp_at
-    spots = jnp.stack([ctx_at // (ctx // EXPERTS), me]).astype(jnp.int32)
-    if shared:
-        spots, half = lax.optimization_barrier((spots, half))
-    normed, weight, mine = norm(places, spots, gain, router_rows, all_routes, mixed_pieces, own)
+    spots = jnp.stack([ctx_at // (ctx // EXPERTS), me, half]).astype(jnp.int32)
+    early = [gate_weight, up_weight] if shared else []
+    normed, weight, mine, *firsts = norm(
+        places, spots, gain, router_rows, all_routes, mixed_pieces, own, early, first
+    )
     total = mine.astype(F32)
     axes = ("ctx", "exp")
     if shared:
-        kept, given = shared_experts(half, normed, swap(normed), gate_first, up_first, gate_weight, up_weight, down_weight)
+        kept, given = shared_experts(
+            half.astype(jnp.int32)[None], normed, swap(normed), *firsts, gate_weight, up_weight, down_weight
+        )
         targets = jnp.stack([lax.rem(me + s, parts) for s in range(parts)]).astype(jnp.int32)
         outs = combine(targets, kept, swap(given), weight, own)
         arrived = [outs[0]]

time: 94.9 us -> 102 us (1.075)
  waiting for transfers between devices: 21.1 us -> 30.8 us
  Pallas kernels: 34.5 us -> 32.6 us
    ppermute x12, waiting for transfers between devices: 13.1 us -> 21.9 us  [rotate(): lax.ppermute(value, axis, [(i, (i + steps) % count) for i in range(count)])]
    pallas_call x3 -> x2, Pallas kernels: 10.1 us -> 6.04 us  [the longest x1 3.42 us: norm(): pl.pallas_call(functools.partial(norm_kernel, count, early), out_shape=(j...]
    pallas_call x1, Pallas kernels: 14.9 us -> 17 us  [shared_experts(): pl.pallas_call(shared_kernel, out_shape=(jax.ShapeDtypeStruct((rows, widt...]
  transfers between devices with their start and end apart: 21 -> 21, of which waited for: 9 -> 9; matrix products, arithmetic and copies ran while one was open for 6% -> 7% of each run, Pallas kernels for 13% -> 7%
where the time goes in v5:
time: 102 us
  Pallas kernels  32.6 us (32%)
  starting transfers between devices  30.8 us (30%)
  waiting for transfers between devices  30.8 us (30%)
  local copies, waits for them, and re-layouts  4.24 us (4%)
  other arithmetic  3.39 us (3%)
    ppermute x12, starting transfers between devices, rotate(): lax.ppermute(value, axis, [(i, (i + steps) % count) for i in range(count)])  22 us
    ppermute x12, waiting for transfers between devices, rotate(): lax.ppermute(value, axis, [(i, (i + steps) % count) for i in range(count)])  21.9 us
    pallas_call x1, Pallas kernels, shared_experts(): pl.pallas_call(shared_kernel, out_shape=(jax.ShapeDtypeStruct((rows, widt...  17 us
    ppermute x7, starting transfers between devices, body(): lax.ppermute(outs[s], axes, [(i, (i + s) % parts) for i in range(parts)])  8.53 us
    pallas_call x1, Pallas kernels, scan(): pl.pallas_call(functools.partial(scan_kernel, taps), out_shape=jax.ShapeD...  6.68 us
    ppermute x7, waiting for transfers between devices, body(): lax.ppermute(outs[s], axes, [(i, (i + s) % parts) for i in range(parts)])  5.31 us
    ppermute x2, waiting for transfers between devices, swap(): lax.ppermute(value, 'doc', [(i, i + 1 - 2 * (i % 2)) for i in range(count)])  3.58 us
    pallas_call x1, Pallas kernels, norm(): pl.pallas_call(functools.partial(norm_kernel, count, early), out_shape=(j...  3.42 us
  transfers between devices with their start and end apart: 21, of which 9 were waited for; matrix products, arithmetic and copies ran while one was open for 7% of the time, Pallas kernels for 7%

profile of v5, /device:TPU:0, one launch (start us, length us, event | category | flops | bytes accessed | tf_op | source)
XLA Modules:
  0.0 102.0 jit_solution(2381088691596747521)
XLA Ops:
  0.0 3.0 %collective-permute-start = (bf16[2,32,2048]{2,1,0:T(8,128)(2,1)}, bf16[2,32,2048]{2,1,0:T(8,128)(2,1)S(1)}, u32[]{:S(2)}, u32[]{:S(2)}) collective-permute-start(bf16[2,32,2048]{2,1,0:T(8,128)(2,1)} %param.18), channel_id=1, source_target_pairs={{0,8},{8,16},{16,24},{24,0},{1,9},{9,17},{17,25},{25,1},{2,10},{10... | collective-permute-start | bytes 786440 | tf_op jit(solution)/shard_map/ppermute | solution.py:27
  3.0 2.6 %collective-permute-start.1 = (bf16[2,32,2048]{2,1,0:T(8,128)(2,1)}, bf16[2,32,2048]{2,1,0:T(8,128)(2,1)S(1)}, u32[]{:S(2)}, u32[]{:S(2)}) collective-permute-start(bf16[2,32,2048]{2,1,0:T(8,128)(2,1)} %param.18), channel_id=1, source_target_pairs={{0,16},{8,24},{16,0},{24,8},{1,17},{9,25},{17,1},{25,9},{2,18},{10... | collective-permute-start | bytes 786440 | tf_op jit(solution)/shard_map/ppermute | solution.py:27
  5.6 1.3 %collective-permute-start.2 = (bf16[2,32,2048]{2,1,0:T(8,128)(2,1)}, bf16[2,32,2048]{2,1,0:T(8,128)(2,1)S(1)}, u32[]{:S(2)}, u32[]{:S(2)}) collective-permute-start(bf16[2,32,2048]{2,1,0:T(8,128)(2,1)} %param.18), channel_id=1, source_target_pairs={{0,24},{8,0},{16,8},{24,16},{1,25},{9,1},{17,9},{25,17},{2,26},{10... | collective-permute-start | bytes 786440 | tf_op jit(solution)/shard_map/ppermute | solution.py:27
  7.0 0.7 convert_element_type.49
  7.6 0.1 copy.20
  7.8 0.8 pad_maximum_fusion.4
  8.6 1.5 %collective-permute-start.4 = (bf16[16,2176]{1,0:T(8,128)(2,1)S(1)}, bf16[16,2176]{1,0:T(8,128)(2,1)S(1)}, u32[]{:S(2)}, u32[]{:S(2)}) collective-permute-start(bf16[16,2176]{1,0:T(8,128)(2,1)S(1)} %pad_maximum_fusion.4), channel_id=1, source_target_pairs={{0,4},{4,0},{1,5},{5,1},{2,6},{6,2},{3,7},{7,3},{8,12},{12,8},{9,1... | collective-permute-start | bytes 208904 | tf_op jit(solution)/shard_map/ppermute | solution.py:27
  10.1 1.0 slice_bitcast_fusion
  11.1 0.7 pad.12.router
  11.9 0.7 pad.13.gain
  12.6 1.6 %concatenate.24.params = f32[16,2048]{1,0:T(8,128)S(1)} concatenate(f32[4,2048]{1,0:T(4,128)} %param.21, f32[1,2048]{1,0:T(1,128)} %bitcast.26, f32[1,2048]{1,0:T(1,128)} %bitcast.27, f32[1,2048]{1,0:T(1,128)} %bitcast.28, f32[1,2048]{1,0:T(1,128)S(1)} %slice.15, f32[5,2048]{1,0:T(8,128)S(1)} %broadcast_in_dim.19, bf16[3,2048]{1,0:T(4,128)(2,1)} %param.19), dimensions={0} | concatenate | bytes 249856 | tf_op jit(solution)/shard_map/concatenate | solution.py:570
  14.2 0.1 pad_add_fusion.places
  14.3 0.0 collective-permute-done.4
  14.3 0.9 maximum_select_fusion
  15.3 0.0 collective-permute-done.refs_1_
  15.3 7.7 %collective-permute-done.1.refs_2_ = bf16[2,32,2048]{2,1,0:T(8,128)(2,1)S(1)} collective-permute-done((bf16[2,32,2048]{2,1,0:T(8,128)(2,1)}, bf16[2,32,2048]{2,1,0:T(8,128)(2,1)S(1)}, u32[]{:S(2)}, u32[]{:S(2)}) %collective-permute-start.1) | collective-permute-done | bytes 262176 | tf_op jit(solution)/shard_map/ppermute | solution.py:27
  22.9 0.0 collective-permute-done.2.refs_3_
  22.9 2.2 %activate.1 = (bf16[128,2048]{1,0:T(8,128)(2,1)S(1)}, f32[160,128]{1,0:T(8,128)S(1)}) custom-call(s32[4]{0:T(128)S(1)} %pad_add_fusion.places, f32[16,2048]{1,0:T(8,128)S(1)} %concatenate.24.params, bf16[160,2048]{1,0:T(8,128)(2,1)} %select.38, bf16[32,2048]{1,0:T(8,128)(2,1)S(1)} %get-tuple-element.58.refs_0_, ...), custom_call_target="tpu_custom_call" | custom-call | flops 83886080 | bytes 1048576 | tf_op jit(solution)/shard_map/activate/pallas_call | solution.py:110
  25.1 1.6 %collective-permute-start.3 = (f32[160,128]{1,0:T(8,128)S(1)}, f32[160,128]{1,0:T(8,128)S(1)}, u32[]{:S(2)}, u32[]{:S(2)}) collective-permute-start(f32[160,128]{1,0:T(8,128)S(1)} %get-tuple-element.34.own), channel_id=1, source_target_pairs={{0,4},{4,0},{1,5},{5,1},{2,6},{6,2},{3,7},{7,3},{8,12},{12,8},{9,1... | collective-permute-start | bytes 245768 | tf_op jit(solution)/shard_map/ppermute | solution.py:27
  26.7 6.1 %collective-permute-start.5 = (bf16[32,640]{1,0:T(8,128)(2,1)S(1)}, bf16[32,640]{1,0:T(8,128)(2,1)S(1)}, u32[]{:S(2)}, u32[]{:S(2)}) collective-permute-start(bf16[32,640]{1,0:T(8,128)(2,1)S(1)} %get-tuple-element.36), channel_id=1, source_target_pairs={{0,8},{8,16},{16,24},{24,0},{1,9},{9,17},{17,25},{25,1},{2,10},{10... | collective-permute-start | bytes 122888 | tf_op jit(solution)/shard_map/ppermute | solution.py:27
  32.8 1.6 %collective-permute-start.6 = (bf16[32,640]{1,0:T(8,128)(2,1)S(1)}, bf16[32,640]{1,0:T(8,128)(2,1)S(1)}, u32[]{:S(2)}, u32[]{:S(2)}) collective-permute-start(bf16[32,640]{1,0:T(8,128)(2,1)S(1)} %get-tuple-element.37), channel_id=1, source_target_pairs={{0,16},{8,24},{16,0},{24,8},{1,17},{9,25},{17,1},{25,9},{2,18},{10... | collective-permute-start | bytes 122888 | tf_op jit(solution)/shard_map/ppermute | solution.py:27
  34.4 0.8 collective-permute-start.7
  35.3 0.0 collective-permute-done.3.other
  35.3 6.7 %scan.1.value_in = f32[128,2048]{1,0:T(8,128)S(1)} custom-call(f32[160,128]{1,0:T(8,128)S(1)} %get-tuple-element.34.own, f32[160,128]{1,0:T(8,128)S(1)} %collective-permute-done.3.other, bf16[128,2048]{1,0:T(8,128)(2,1)S(1)} %get-tuple-element.35.active, f32[16,2048]{1,0:T(8,128)S(1)} %concatenate.24.params, f32[16,2048]{1,0:T(8,128)} %log_rate_hbm.1, ...), custom_call_target="tpu_custom_call" | custom-call | flops 12582912000 | bytes 2097152 | tf_op jit(solution)/shard_map/scan/pallas_call | solution.py:232
  42.0 0.0 collective-permute-done.5.refs_5_
  42.0 0.0 collective-permute-done.6.refs_6_
  42.0 0.0 collective-permute-done.7.refs_7_
  42.0 2.6 %project.1 = (f32[128,512]{1,0:T(8,128)S(1)}, bf16[128,512]{1,0:T(8,128)(2,1)S(1)}, bf16[128,128]{1,0:T(8,128)(2,1)S(1)}) custom-call(s32[4]{0:T(128)S(1)} %pad_add_fusion.places, f32[128,2048]{1,0:T(8,128)S(1)} %scan.1.value_in, bf16[2048,512]{1,0:T(8,128)(2,1)} %weight_hbm.1, bf16[32,2048]{1,0:T(8,128)(2,1)S(1)} %get-tuple-element.57.refs_0_, ...), custom_call_target="tpu_custom_call" | custom-call | flops 268435456 | bytes 2097152 | tf_op jit(solution)/shard_map/project/pallas_call | solution.py:296
  44.6 0.6 collective-permute-start.8
  45.2 4.5 %collective-permute-done.8 = bf16[128,512]{1,0:T(8,128)(2,1)S(1)} collective-permute-done((bf16[128,512]{1,0:T(8,128)(2,1)S(1)}, bf16[128,512]{1,0:T(8,128)(2,1)S(1)}, u32[]{:S(2)}, u32[]{:S(2)}) %collective-permute-start.8) | collective-permute-done | bytes 131104 | tf_op jit(solution)/shard_map/ppermute | solution.py:27
  49.7 2.0 %collective-permute-start.11 = (bf16[128,512]{1,0:T(8,128)(2,1)S(1)}, bf16[128,512]{1,0:T(8,128)(2,1)S(1)}, u32[]{:S(2)}, u32[]{:S(2)}) collective-permute-start(bf16[128,512]{1,0:T(8,128)(2,1)S(1)} %add_convert_fusion.refs_0_), channel_id=1, source_target_pairs={{0,24},{8,0},{16,8},{24,16},{1,25},{9,1},{17,9},{25,17},{2,26},{10... | collective-permute-start | bytes 393224 | tf_op jit(solution)/shard_map/ppermute | solution.py:27
  51.7 0.7 collective-permute-start.10
  52.4 0.1 collective-permute-start.9
  52.5 0.1 pad_add_fusion.1.spots
  52.5 4.1 %collective-permute-done.11.refs_3_ = bf16[128,512]{1,0:T(8,128)(2,1)S(1)} collective-permute-done((bf16[128,512]{1,0:T(8,128)(2,1)S(1)}, bf16[128,512]{1,0:T(8,128)(2,1)S(1)}, u32[]{:S(2)}, u32[]{:S(2)}) %collective-permute-start.11) | collective-permute-done | bytes 131104 | tf_op jit(solution)/shard_map/ppermute | solution.py:27
  56.7 5.6 %collective-permute-done.10.refs_2_ = bf16[128,512]{1,0:T(8,128)(2,1)S(1)} collective-permute-done((bf16[128,512]{1,0:T(8,128)(2,1)S(1)}, bf16[128,512]{1,0:T(8,128)(2,1)S(1)}, u32[]{:S(2)}, u32[]{:S(2)}) %collective-permute-start.10) | collective-permute-done | bytes 131104 | tf_op jit(solution)/shard_map/ppermute | solution.py:27
  62.3 0.0 collective-permute-done.9.refs_1_
  62.3 3.4 %norm.1 = (bf16[128,2048]{1,0:T(8,128)(2,1)S(1)}, f32[128,128]{1,0:T(8,128)S(1)}, bf16[16,2048]{1,0:T(8,128)(2,1)S(1)}, bf16[768,2048]{1,0:T(8,128)(2,1)S(1)}, bf16[768,2048]{1,0:T(8,128)(2,1)S(1)}) custom-call(s32[4]{0:T(128)S(1)} %pad_add_fusion.places, s32[3]{0:T(128)S(1)} %pad_add_fusion.1.spots, f32[8,2048]{1,0:T(8,128)S(1)} %pad.13.gain, ...), custom_call_target="tpu_custom_call" | custom-call | tf_op jit(solution)/shard_map/norm/pallas_call | solution.py:378
  65.7 0.1 collective-permute-start.12
  65.8 1.9 %collective-permute-done.12.other = bf16[128,2048]{1,0:T(8,128)(2,1)S(1)} collective-permute-done((bf16[128,2048]{1,0:T(8,128)(2,1)S(1)}, bf16[128,2048]{1,0:T(8,128)(2,1)S(1)}, u32[]{:S(2)}, u32[]{:S(2)}) %collective-permute-start.12) | collective-permute-done | bytes 524320 | tf_op jit(solution)/shard_map/ppermute | solution.py:57
  67.7 17.0 %experts.1 = (f32[128,2048]{1,0:T(8,128)S(1)}, bf16[128,2048]{1,0:T(8,128)(2,1)S(1)}) custom-call(s32[1]{0:T(128)} %bitcast.6.half, bf16[128,2048]{1,0:T(8,128)(2,1)S(1)} %get-tuple-element.43.own, bf16[128,2048]{1,0:T(8,128)(2,1)S(1)} %collective-permute-done.12.other, bf16[768,2048]{1,0:T(8,128)(2,1)S(1)} %get-tuple-element.44.gate_first, ...), custom_call_target="tpu_custom_call" | custom-call | flops 11274289152 | bytes 44040192 | tf_op jit(solution)/shard_map/experts/pallas_call | solution.py:447
  84.7 0.2 collective-permute-start.13
  84.9 0.1 stack.71.targets
  85.0 1.7 %collective-permute-done.13.other = bf16[128,2048]{1,0:T(8,128)(2,1)S(1)} collective-permute-done((bf16[128,2048]{1,0:T(8,128)(2,1)S(1)}, bf16[128,2048]{1,0:T(8,128)(2,1)S(1)}, u32[]{:S(2)}, u32[]{:S(2)}) %collective-permute-start.13) | collective-permute-done | bytes 524320 | tf_op jit(solution)/shard_map/ppermute | solution.py:57
  86.7 0.7 combine.1
  87.4 0.6 collective-permute-start.14
  88.0 0.0 collective-permute-start.15
  88.0 2.0 %collective-permute-start.16 = (bf16[16,2048]{1,0:T(8,128)(2,1)S(1)}, bf16[16,2048]{1,0:T(8,128)(2,1)S(1)}, u32[]{:S(2)}, u32[]{:S(2)}) collective-permute-start(bf16[16,2048]{1,0:T(8,128)(2,1)S(1)} %get-tuple-element.52), channel_id=1, source_target_pairs={{0,12},{4,16},{8,20},{12,24},{16,28},{20,0},{24,4},{28,8},{1,13},{... | collective-permute-start | bytes 196616 | tf_op jit(solution)/shard_map/ppermute | solution.py:613
  90.0 2.8 %collective-permute-start.17 = (bf16[16,2048]{1,0:T(8,128)(2,1)S(1)}, bf16[16,2048]{1,0:T(8,128)(2,1)S(1)}, u32[]{:S(2)}, u32[]{:S(2)}) collective-permute-start(bf16[16,2048]{1,0:T(8,128)(2,1)S(1)} %get-tuple-element.53), channel_id=1, source_target_pairs={{0,16},{4,20},{8,24},{12,28},{16,0},{20,4},{24,8},{28,12},{1,17},{... | collective-permute-start | bytes 196616 | tf_op jit(solution)/shard_map/ppermute | solution.py:613
  92.8 0.2 collective-permute-start.18
  92.9 2.3 %collective-permute-done.14 = bf16[16,2048]{1,0:T(8,128)(2,1)S(1)} collective-permute-done((bf16[16,2048]{1,0:T(8,128)(2,1)S(1)}, bf16[16,2048]{1,0:T(8,128)(2,1)S(1)}, u32[]{:S(2)}, u32[]{:S(2)}) %collective-permute-start.14) | collective-permute-done | bytes 65568 | tf_op jit(solution)/shard_map/ppermute | solution.py:613
  95.2 0.6 collective-permute-start.19
  95.8 0.0 collective-permute-done.15
  95.8 2.4 %collective-permute-start.20 = (bf16[16,2048]{1,0:T(8,128)(2,1)S(1)}, bf16[16,2048]{1,0:T(8,128)(2,1)S(1)}, u32[]{:S(2)}, u32[]{:S(2)}) collective-permute-start(bf16[16,2048]{1,0:T(8,128)(2,1)S(1)} %get-tuple-element.56), channel_id=1, source_target_pairs={{0,28},{4,0},{8,4},{12,8},{16,12},{20,16},{24,20},{28,24},{1,29},{... | collective-permute-start | bytes 196616 | tf_op jit(solution)/shard_map/ppermute | solution.py:613
  98.2 1.8 %collective-permute-done.16 = bf16[16,2048]{1,0:T(8,128)(2,1)S(1)} collective-permute-done((bf16[16,2048]{1,0:T(8,128)(2,1)S(1)}, bf16[16,2048]{1,0:T(8,128)(2,1)S(1)}, u32[]{:S(2)}, u32[]{:S(2)}) %collective-permute-start.16) | collective-permute-done | bytes 65568 | tf_op jit(solution)/shard_map/ppermute | solution.py:613
  100.0 0.0 collective-permute-done.17
  100.0 0.0 collective-permute-done.18
  100.0 1.2 %collective-permute-done.19 = bf16[16,2048]{1,0:T(8,128)(2,1)S(1)} collective-permute-done((bf16[16,2048]{1,0:T(8,128)(2,1)S(1)}, bf16[16,2048]{1,0:T(8,128)(2,1)S(1)}, u32[]{:S(2)}, u32[]{:S(2)}) %collective-permute-start.19) | collective-permute-done | bytes 65568 | tf_op jit(solution)/shard_map/ppermute | solution.py:613
  101.3 0.0 collective-permute-done.20
  101.3 0.7 add_convert_fusion.1
  (7 shorter events, 0.1 us)
Async XLA Ops:
  0.0 15.3 %collective-permute-start = (bf16[2,32,2048]{2,1,0:T(8,128)(2,1)}, bf16[2,32,2048]{2,1,0:T(8,128)(2,1)S(1)}, u32[]{:S(2)}, u32[]{:S(2)}) collective-permute-start(bf16[2,32,2048]{2,1,0:T(8,128)(2,1)} %param.18), channel_id=1, source_target_pairs={{0,8},{8,16},{16,24},{24,0},{1,9},{9,17},{17,25},{25,1},{2,10},{10... | collective-permute-start | bytes 786440 | tf_op jit(solution)/shard_map/ppermute | solution.py:27
  3.0 19.9 %collective-permute-start.1 = (bf16[2,32,2048]{2,1,0:T(8,128)(2,1)}, bf16[2,32,2048]{2,1,0:T(8,128)(2,1)S(1)}, u32[]{:S(2)}, u32[]{:S(2)}) collective-permute-start(bf16[2,32,2048]{2,1,0:T(8,128)(2,1)} %param.18), channel_id=1, source_target_pairs={{0,16},{8,24},{16,0},{24,8},{1,17},{9,25},{17,1},{25,9},{2,18},{10... | collective-permute-start | bytes 786440 | tf_op jit(solution)/shard_map/ppermute | solution.py:27
  5.6 17.3 %collective-permute-start.2 = (bf16[2,32,2048]{2,1,0:T(8,128)(2,1)}, bf16[2,32,2048]{2,1,0:T(8,128)(2,1)S(1)}, u32[]{:S(2)}, u32[]{:S(2)}) collective-permute-start(bf16[2,32,2048]{2,1,0:T(8,128)(2,1)} %param.18), channel_id=1, source_target_pairs={{0,24},{8,0},{16,8},{24,16},{1,25},{9,1},{17,9},{25,17},{2,26},{10... | collective-permute-start | bytes 786440 | tf_op jit(solution)/shard_map/ppermute | solution.py:27
  8.6 5.7 %collective-permute-start.4 = (bf16[16,2176]{1,0:T(8,128)(2,1)S(1)}, bf16[16,2176]{1,0:T(8,128)(2,1)S(1)}, u32[]{:S(2)}, u32[]{:S(2)}) collective-permute-start(bf16[16,2176]{1,0:T(8,128)(2,1)S(1)} %pad_maximum_fusion.4), channel_id=1, source_target_pairs={{0,4},{4,0},{1,5},{5,1},{2,6},{6,2},{3,7},{7,3},{8,12},{12,8},{9,1... | collective-permute-start | bytes 208904 | tf_op jit(solution)/shard_map/ppermute | solution.py:27
  25.1 10.2 %collective-permute-start.3 = (f32[160,128]{1,0:T(8,128)S(1)}, f32[160,128]{1,0:T(8,128)S(1)}, u32[]{:S(2)}, u32[]{:S(2)}) collective-permute-start(f32[160,128]{1,0:T(8,128)S(1)} %get-tuple-element.34.own), channel_id=1, source_target_pairs={{0,4},{4,0},{1,5},{5,1},{2,6},{6,2},{3,7},{7,3},{8,12},{12,8},{9,1... | collective-permute-start | bytes 245768 | tf_op jit(solution)/shard_map/ppermute | solution.py:27
  26.7 15.3 %collective-permute-start.5 = (bf16[32,640]{1,0:T(8,128)(2,1)S(1)}, bf16[32,640]{1,0:T(8,128)(2,1)S(1)}, u32[]{:S(2)}, u32[]{:S(2)}) collective-permute-start(bf16[32,640]{1,0:T(8,128)(2,1)S(1)} %get-tuple-element.36), channel_id=1, source_target_pairs={{0,8},{8,16},{16,24},{24,0},{1,9},{9,17},{17,25},{25,1},{2,10},{10... | collective-permute-start | bytes 122888 | tf_op jit(solution)/shard_map/ppermute | solution.py:27
  32.8 9.1 %collective-permute-start.6 = (bf16[32,640]{1,0:T(8,128)(2,1)S(1)}, bf16[32,640]{1,0:T(8,128)(2,1)S(1)}, u32[]{:S(2)}, u32[]{:S(2)}) collective-permute-start(bf16[32,640]{1,0:T(8,128)(2,1)S(1)} %get-tuple-element.37), channel_id=1, source_target_pairs={{0,16},{8,24},{16,0},{24,8},{1,17},{9,25},{17,1},{25,9},{2,18},{10... | collective-permute-start | bytes 122888 | tf_op jit(solution)/shard_map/ppermute | solution.py:27
  34.4 7.6 %collective-permute-start.7 = (bf16[32,640]{1,0:T(8,128)(2,1)S(1)}, bf16[32,640]{1,0:T(8,128)(2,1)S(1)}, u32[]{:S(2)}, u32[]{:S(2)}) collective-permute-start(bf16[32,640]{1,0:T(8,128)(2,1)S(1)} %get-tuple-element.38), channel_id=1, source_target_pairs={{0,24},{8,0},{16,8},{24,16},{1,25},{9,1},{17,9},{25,17},{2,26},{10... | collective-permute-start | bytes 122888 | tf_op jit(solution)/shard_map/ppermute | solution.py:27
  44.6 5.0 %collective-permute-start.8 = (bf16[128,512]{1,0:T(8,128)(2,1)S(1)}, bf16[128,512]{1,0:T(8,128)(2,1)S(1)}, u32[]{:S(2)}, u32[]{:S(2)}) collective-permute-start(bf16[128,512]{1,0:T(8,128)(2,1)S(1)} %get-tuple-element.41), channel_id=1, source_target_pairs={{0,4},{4,0},{1,5},{5,1},{2,6},{6,2},{3,7},{7,3},{8,12},{12,8},{9,1... | collective-permute-start | bytes 393224 | tf_op jit(solution)/shard_map/ppermute | solution.py:27
  49.7 7.0 %collective-permute-start.11 = (bf16[128,512]{1,0:T(8,128)(2,1)S(1)}, bf16[128,512]{1,0:T(8,128)(2,1)S(1)}, u32[]{:S(2)}, u32[]{:S(2)}) collective-permute-start(bf16[128,512]{1,0:T(8,128)(2,1)S(1)} %add_convert_fusion.refs_0_), channel_id=1, source_target_pairs={{0,24},{8,0},{16,8},{24,16},{1,25},{9,1},{17,9},{25,17},{2,26},{10... | collective-permute-start | bytes 393224 | tf_op jit(solution)/shard_map/ppermute | solution.py:27
  51.7 10.6 %collective-permute-start.10 = (bf16[128,512]{1,0:T(8,128)(2,1)S(1)}, bf16[128,512]{1,0:T(8,128)(2,1)S(1)}, u32[]{:S(2)}, u32[]{:S(2)}) collective-permute-start(bf16[128,512]{1,0:T(8,128)(2,1)S(1)} %add_convert_fusion.refs_0_), channel_id=1, source_target_pairs={{0,16},{8,24},{16,0},{24,8},{1,17},{9,25},{17,1},{25,9},{2,18},{10... | collective-permute-start | bytes 393224 | tf_op jit(solution)/shard_map/ppermute | solution.py:27
  52.4 9.9 %collective-permute-start.9 = (bf16[128,512]{1,0:T(8,128)(2,1)S(1)}, bf16[128,512]{1,0:T(8,128)(2,1)S(1)}, u32[]{:S(2)}, u32[]{:S(2)}) collective-permute-start(bf16[128,512]{1,0:T(8,128)(2,1)S(1)} %add_convert_fusion.refs_0_), channel_id=1, source_target_pairs={{0,8},{8,16},{16,24},{24,0},{1,9},{9,17},{17,25},{25,1},{2,10},{10... | collective-permute-start | bytes 393224 | tf_op jit(solution)/shard_map/ppermute | solution.py:27
  65.7 2.0 %collective-permute-start.12 = (bf16[128,2048]{1,0:T(8,128)(2,1)S(1)}, bf16[128,2048]{1,0:T(8,128)(2,1)S(1)}, u32[]{:S(2)}, u32[]{:S(2)}) collective-permute-start(bf16[128,2048]{1,0:T(8,128)(2,1)S(1)} %get-tuple-element.43.own), channel_id=1, source_target_pairs={{0,1},{1,0},{2,3},{3,2},{4,5},{5,4},{6,7},{7,6},{8,9},{9,8},{10,11... | collective-permute-start | bytes 1572872 | tf_op jit(solution)/shard_map/ppermute | solution.py:57
  84.7 2.0 %collective-permute-start.13 = (bf16[128,2048]{1,0:T(8,128)(2,1)S(1)}, bf16[128,2048]{1,0:T(8,128)(2,1)S(1)}, u32[]{:S(2)}, u32[]{:S(2)}) collective-permute-start(bf16[128,2048]{1,0:T(8,128)(2,1)S(1)} %get-tuple-element.47), channel_id=1, source_target_pairs={{0,1},{1,0},{2,3},{3,2},{4,5},{5,4},{6,7},{7,6},{8,9},{9,8},{10,11... | collective-permute-start | bytes 1572872 | tf_op jit(solution)/shard_map/ppermute | solution.py:57
  87.4 7.8 %collective-permute-start.14 = (bf16[16,2048]{1,0:T(8,128)(2,1)S(1)}, bf16[16,2048]{1,0:T(8,128)(2,1)S(1)}, u32[]{:S(2)}, u32[]{:S(2)}) collective-permute-start(bf16[16,2048]{1,0:T(8,128)(2,1)S(1)} %get-tuple-element.50), channel_id=1, source_target_pairs={{0,4},{4,8},{8,12},{12,16},{16,20},{20,24},{24,28},{28,0},{1,5},{5... | collective-permute-start | bytes 196616 | tf_op jit(solution)/shard_map/ppermute | solution.py:613
  88.0 7.8 %collective-permute-start.15 = (bf16[16,2048]{1,0:T(8,128)(2,1)S(1)}, bf16[16,2048]{1,0:T(8,128)(2,1)S(1)}, u32[]{:S(2)}, u32[]{:S(2)}) collective-permute-start(bf16[16,2048]{1,0:T(8,128)(2,1)S(1)} %get-tuple-element.51), channel_id=1, source_target_pairs={{0,8},{4,12},{8,16},{12,20},{16,24},{20,28},{24,0},{28,4},{1,9},{5... | collective-permute-start | bytes 196616 | tf_op jit(solution)/shard_map/ppermute | solution.py:613
  88.0 12.1 %collective-permute-start.16 = (bf16[16,2048]{1,0:T(8,128)(2,1)S(1)}, bf16[16,2048]{1,0:T(8,128)(2,1)S(1)}, u32[]{:S(2)}, u32[]{:S(2)}) collective-permute-start(bf16[16,2048]{1,0:T(8,128)(2,1)S(1)} %get-tuple-element.52), channel_id=1, source_target_pairs={{0,12},{4,16},{8,20},{12,24},{16,28},{20,0},{24,4},{28,8},{1,13},{... | collective-permute-start | bytes 196616 | tf_op jit(solution)/shard_map/ppermute | solution.py:613
  90.0 10.0 %collective-permute-start.17 = (bf16[16,2048]{1,0:T(8,128)(2,1)S(1)}, bf16[16,2048]{1,0:T(8,128)(2,1)S(1)}, u32[]{:S(2)}, u32[]{:S(2)}) collective-permute-start(bf16[16,2048]{1,0:T(8,128)(2,1)S(1)} %get-tuple-element.53), channel_id=1, source_target_pairs={{0,16},{4,20},{8,24},{12,28},{16,0},{20,4},{24,8},{28,12},{1,17},{... | collective-permute-start | bytes 196616 | tf_op jit(solution)/shard_map/ppermute | solution.py:613
  92.8 7.3 %collective-permute-start.18 = (bf16[16,2048]{1,0:T(8,128)(2,1)S(1)}, bf16[16,2048]{1,0:T(8,128)(2,1)S(1)}, u32[]{:S(2)}, u32[]{:S(2)}) collective-permute-start(bf16[16,2048]{1,0:T(8,128)(2,1)S(1)} %get-tuple-element.54), channel_id=1, source_target_pairs={{0,20},{4,24},{8,28},{12,0},{16,4},{20,8},{24,12},{28,16},{1,21},{... | collective-permute-start | bytes 196616 | tf_op jit(solution)/shard_map/ppermute | solution.py:613
  95.2 6.1 %collective-permute-start.19 = (bf16[16,2048]{1,0:T(8,128)(2,1)S(1)}, bf16[16,2048]{1,0:T(8,128)(2,1)S(1)}, u32[]{:S(2)}, u32[]{:S(2)}) collective-permute-start(bf16[16,2048]{1,0:T(8,128)(2,1)S(1)} %get-tuple-element.55), channel_id=1, source_target_pairs={{0,24},{4,28},{8,0},{12,4},{16,8},{20,12},{24,16},{28,20},{1,25},{... | collective-permute-start | bytes 196616 | tf_op jit(solution)/shard_map/ppermute | solution.py:613
  95.8 5.5 %collective-permute-start.20 = (bf16[16,2048]{1,0:T(8,128)(2,1)S(1)}, bf16[16,2048]{1,0:T(8,128)(2,1)S(1)}, u32[]{:S(2)}, u32[]{:S(2)}) collective-permute-start(bf16[16,2048]{1,0:T(8,128)(2,1)S(1)} %get-tuple-element.56), channel_id=1, source_target_pairs={{0,28},{4,0},{8,4},{12,8},{16,12},{20,16},{24,20},{28,24},{1,29},{... | collective-permute-start | bytes 196616 | tf_op jit(solution)/shard_map/ppermute | solution.py:613

commit v6 on v4

--- a/solution.py
+++ b/solution.py
@@ -27,22 +27,36 @@
     return lax.ppermute(value, axis, [(i, (i + steps) % count) for i in range(count)])
 
 
+def partner(place, step, count):
+    paired = count & (count - 1) == 0
+    return place ^ step if paired else (place + step) % count
+
+
+def source(place, step, count):
+    paired = count & (count - 1) == 0
+    return place ^ step if paired else (place - step) % count
+
+
+def exchange(value, axes, step, count):
+    return lax.ppermute(value, axes, [(i, partner(i, step, count)) for i in range(count)])
+
+
 def ring_places(axis):
     count = lax.axis_size(axis)
     if count > FEW:
         return jnp.zeros((1,), jnp.int32)
     me = lax.axis_index(axis)
-    return jnp.stack([lax.rem(me + count - s, count) for s in range(count)]).astype(jnp.int32)
+    return jnp.stack([source(me, s, count) for s in range(count)]).astype(jnp.int32)
 
 
 def spread(make, axis, join, after=None):
     count = lax.axis_size(axis)
     me = lax.axis_index(axis)
     if count <= FEW:
-        sent = [make(lax.rem(me + s, count)) for s in range(1, count)]
+        sent = [make(partner(me, s, count)) for s in range(1, count)]
         if after is not None:
             sent, _ = lax.optimization_barrier((sent, after))
-        return [make(me)] + [rotate(sent[s - 1], axis, s) for s in range(1, count)]
+        return [make(me)] + [exchange(sent[s - 1], axis, s, count) for s in range(1, count)]
     stacked = jnp.stack([make(jnp.int32(k)) for k in range(count)])
     moved = lax.all_to_all(stacked, axis, split_axis=0, concat_axis=0, tiled=True)
     return [jnp.concatenate([moved[k] for k in range(count)], axis=join)]
@@ -309,6 +323,21 @@
         ),
         name="project",
     )(places, value, far(out_weight), *pieces)
+
+
+def mix_kernel(base, summand, mixed):
+    mixed[...] = (base[...] + summand[...].astype(F32)).astype(BF16)
+
+
+def mix(base, summand):
+    return pl.pallas_call(
+        mix_kernel,
+        out_shape=jax.ShapeDtypeStruct(base.shape, BF16),
+        in_specs=[WHOLE] * 2,
+        out_specs=WHOLE,
+        compiler_params=pltpu.CompilerParams(vmem_limit_bytes=4 << 20),
+        name="mix",
+    )(base, summand)
 
 
 def norm_kernel(count, places, spots, gain, router, routes, *refs):
@@ -550,15 +579,19 @@
     own, width = residual.shape
     columns = output_weight.shape[1]
     taps = filter_taps.shape[0]
+    parts = ctx * exp
+    me = ctx_at * exp + exp_at
+    spots = jnp.stack([ctx_at // (ctx // EXPERTS), me]).astype(jnp.int32)
+    targets = jnp.stack([partner(me, s, parts) for s in range(parts)]).astype(jnp.int32)
 
     x_pieces = spread(lambda k: x_input, "ctx", 0)
     extra = jnp.concatenate([residual, jnp.pad(routes.astype(BF16), ((0, 0), (0, LANES - 2)))], axis=1)
     if exp == 2:
-        partner = rotate(extra, "exp", 1)
+        other = rotate(extra, "exp", 1)
         extra = jnp.where(
             exp_at == 0,
-            jnp.concatenate([extra, partner], axis=0),
-            jnp.concatenate([partner, extra], axis=0),
+            jnp.concatenate([extra, other], axis=0),
+            jnp.concatenate([other, extra], axis=0),
         )
     else:
         extra = lax.all_gather(extra, "exp", axis=0, tiled=True)
@@ -570,7 +603,9 @@
     ready = [jnp.concatenate([z_input, extra[:, width:]], axis=1), extra[:, :width]]
     router_rows = jnp.pad(router.T, ((0, 16 - EXPERTS), (0, 0)))
     gain = jnp.pad(norm_gain[None, :], ((0, 7), (0, 0)))
-    params, router_rows, gain = lax.optimization_barrier((params, router_rows, gain))
+    params, router_rows, gain, spots, targets = lax.optimization_barrier(
+        (params, router_rows, gain, spots, targets)
+    )
 
     active, proj = activate(places, x_pieces, params, taps, select_weight)
     own_proj, other_proj = pair_sum(proj, "exp")
@@ -583,31 +618,27 @@
     z_pieces = spread(bundle, "ctx", 0, active)
     value = scan(own_proj, other_proj, active, params, taps, log_rate, step_weight, carried_state)
     base, sent, all_routes = project(places, value, output_weight, z_pieces)
+    shared = parts <= 8 and base.shape[0] == LANES and lax.axis_size("doc") % 2 == 0
+    half = lax.rem(lax.axis_index("doc"), 2).astype(jnp.int32)[None]
     if exp == 2:
-        mixed = (base + rotate(sent, "exp", 1).astype(F32)).astype(BF16)
+        summand = rotate(sent, "exp", 1)
     else:
-        mixed = (base - sent.astype(F32) + lax.psum(sent.astype(F32), "exp")).astype(BF16)
-    parts = ctx * exp
-    shared = parts <= 8 and mixed.shape[0] == LANES and lax.axis_size("doc") % 2 == 0
+        summand = lax.psum(sent.astype(F32), "exp") - sent.astype(F32)
     if shared:
-        half = lax.rem(lax.axis_index("doc"), 2).astype(jnp.int32)[None]
-        half, mixed = lax.optimization_barrier((half, mixed))
+        half, base = lax.optimization_barrier((half, base))
         gate_first, up_first, half = fetch(half, [gate_weight, up_weight])
+        half, base = lax.optimization_barrier((half, base))
+    mixed = mix(base, summand)
     mixed_pieces = spread(lambda k: mixed, "ctx", 1)
-    me = ctx_at * exp + exp_at
-    spots = jnp.stack([ctx_at // (ctx // EXPERTS), me]).astype(jnp.int32)
-    if shared:
-        spots, half = lax.optimization_barrier((spots, half))
     normed, weight, mine = norm(places, spots, gain, router_rows, all_routes, mixed_pieces, own)
     total = mine.astype(F32)
     axes = ("ctx", "exp")
     if shared:
         kept, given = shared_experts(half, normed, swap(normed), gate_first, up_first, gate_weight, up_weight, down_weight)
-        targets = jnp.stack([lax.rem(me + s, parts) for s in range(parts)]).astype(jnp.int32)
         outs = combine(targets, kept, swap(given), weight, own)
         arrived = [outs[0]]
         for s in range(1, parts):
-            arrived.append(lax.ppermute(outs[s], axes, [(i, (i + s) % parts) for i in range(parts)]))
+            arrived.append(exchange(outs[s], axes, s, parts))
         for piece in arrived:
             total = total + piece.astype(F32)
     else:

time: 94.9 us -> 97.4 us (1.026)
  waiting for transfers between devices: 21.1 us -> 24.5 us
    ppermute x12 -> x3, starting transfers between devices: 21.2 us -> 3.82 us  [rotate(): lax.ppermute(value, axis, [(i, (i + steps) % count) for i in range(count)])]
    ppermute x7 -> x16, starting transfers between devices: 9.33 us -> 25.9 us  [exchange(): lax.ppermute(value, axes, [(i, partner(i, step, count)) for i in range(co...]
    ppermute x7 -> x16, waiting for transfers between devices: 4.41 us -> 20.8 us  [exchange(): lax.ppermute(value, axes, [(i, partner(i, step, count)) for i in range(co...]
    ppermute x12 -> x3, waiting for transfers between devices: 13.1 us -> 0.01 us  [rotate(): lax.ppermute(value, axis, [(i, (i + steps) % count) for i in range(count)])]
where the time goes in v6:
time: 97.4 us; the launch traced here: 96.9 us
  Pallas kernels  34.6 us (36%)
  starting transfers between devices  29.9 us (31%)
  waiting for transfers between devices  24.5 us (25%)
  local copies, waits for them, and re-layouts  4.24 us (4%)
  other arithmetic  3.39 us (3%)
    ppermute x16, starting transfers between devices, exchange(): lax.ppermute(value, axes, [(i, partner(i, step, count)) for i in range(co...  25.9 us
    ppermute x16, waiting for transfers between devices, exchange(): lax.ppermute(value, axes, [(i, partner(i, step, count)) for i in range(co...  20.8 us
    pallas_call x1, Pallas kernels, shared_experts(): pl.pallas_call(shared_kernel, out_shape=(jax.ShapeDtypeStruct((rows, widt...  14.9 us
    pallas_call x1, Pallas kernels, scan(): pl.pallas_call(functools.partial(scan_kernel, taps), out_shape=jax.ShapeD...  6.66 us
    pallas_call x1, Pallas kernels, fetch(): pl.pallas_call(functools.partial(fetch_kernel, parts, half_rows), out_sha...  5.82 us
    ppermute x3, starting transfers between devices, rotate(): lax.ppermute(value, axis, [(i, (i + steps) % count) for i in range(count)])  3.82 us
    ppermute x2, waiting for transfers between devices, swap(): lax.ppermute(value, 'doc', [(i, i + 1 - 2 * (i % 2)) for i in range(count)])  3.67 us
    pallas_call x1, Pallas kernels, project(): pl.pallas_call(functools.partial(project_kernel, count, columns), out_sha...  2.62 us
  transfers between devices with their start and end apart: 21, of which 9 were waited for; matrix products, arithmetic and copies ran while one was open for 6% of the time, Pallas kernels for 13%

profile of v6, /device:TPU:0, one launch (start us, length us, event | category | flops | bytes accessed | tf_op | source)
XLA Modules:
  0.0 96.9 jit_solution(8134191584244161130)
XLA Ops:
  0.0 1.0 %slice_bitcast_fusion = (bf16[32,2048]{1,0:T(8,128)(2,1)S(1)}, bf16[32,2048]{1,0:T(8,128)(2,1)S(1)}) fusion(bf16[2,32,2048]{2,1,0:T(8,128)(2,1)} %param.18), kind=kLoop, calls=%fused_computation.10 | loop fusion | bytes 524288 | tf_op jit(solution)/shard_map/squeeze | solution.py:578
  1.0 5.1 %collective-permute-start.2 = (bf16[32,2048]{1,0:T(8,128)(2,1)S(1)}, bf16[32,2048]{1,0:T(8,128)(2,1)S(1)}, u32[]{:S(2)}, u32[]{:S(2)}) collective-permute-start(bf16[32,2048]{1,0:T(8,128)(2,1)S(1)} %get-tuple-element.72.refs_0_), channel_id=1, source_target_pairs={{0,24},{8,16},{16,8},{24,0},{1,25},{9,17},{17,9},{25,1},{2,26},{10... | collective-permute-start | bytes 393224 | tf_op jit(solution)/shard_map/ppermute | solution.py:41
  6.1 0.0 collective-permute-start.1
  6.1 0.6 collective-permute-start
  6.7 0.7 convert_element_type.43
  7.4 0.1 copy.20
  7.5 0.8 pad_maximum_fusion.8
  8.4 1.7 %collective-permute-start.4 = (bf16[16,2176]{1,0:T(8,128)(2,1)S(1)}, bf16[16,2176]{1,0:T(8,128)(2,1)S(1)}, u32[]{:S(2)}, u32[]{:S(2)}) collective-permute-start(bf16[16,2176]{1,0:T(8,128)(2,1)S(1)} %pad_maximum_fusion.8), channel_id=1, source_target_pairs={{0,4},{4,0},{1,5},{5,1},{2,6},{6,2},{3,7},{7,3},{8,12},{12,8},{9,1... | collective-permute-start | bytes 208904 | tf_op jit(solution)/shard_map/ppermute | solution.py:27
  10.0 0.7 pad.12.router
  10.8 0.1 pad_add_fusion.1.spots
  10.9 0.7 pad.13.gain
  11.6 0.1 stack.61.targets
  11.7 1.6 %concatenate.24.params = f32[16,2048]{1,0:T(8,128)S(1)} concatenate(f32[4,2048]{1,0:T(4,128)} %param.21, f32[1,2048]{1,0:T(1,128)} %bitcast.24, f32[1,2048]{1,0:T(1,128)} %bitcast.25, f32[1,2048]{1,0:T(1,128)} %bitcast.26, f32[1,2048]{1,0:T(1,128)S(1)} %slice.15, f32[5,2048]{1,0:T(8,128)S(1)} %broadcast_in_dim.21, bf16[3,2048]{1,0:T(4,128)(2,1)} %param.19), dimensions={0} | concatenate | bytes 249856 | tf_op jit(solution)/shard_map/concatenate | solution.py:599
  13.3 0.1 pad_add_fusion.places
  13.4 0.0 collective-permute-done.4
  13.4 0.9 maximum_select_fusion
  14.4 0.0 collective-permute-done.2.refs_3_
  14.4 2.8 %collective-permute-done.1.refs_2_ = bf16[32,2048]{1,0:T(8,128)(2,1)S(1)} collective-permute-done((bf16[32,2048]{1,0:T(8,128)(2,1)S(1)}, bf16[32,2048]{1,0:T(8,128)(2,1)S(1)}, u32[]{:S(2)}, u32[]{:S(2)}) %collective-permute-start.1) | collective-permute-done | bytes 131104 | tf_op jit(solution)/shard_map/ppermute | solution.py:41
  17.2 0.0 collective-permute-done.refs_1_
  17.2 2.1 %activate.1 = (bf16[128,2048]{1,0:T(8,128)(2,1)S(1)}, f32[160,128]{1,0:T(8,128)S(1)}) custom-call(s32[4]{0:T(128)S(1)} %pad_add_fusion.places, f32[16,2048]{1,0:T(8,128)S(1)} %concatenate.24.params, bf16[160,2048]{1,0:T(8,128)(2,1)} %select.8, bf16[32,2048]{1,0:T(8,128)(2,1)S(1)} %get-tuple-element.72.refs_0_, ...), custom_call_target="tpu_custom_call" | custom-call | flops 83886080 | bytes 1048576 | tf_op jit(solution)/shard_map/activate/pallas_call | solution.py:120
  19.3 1.6 %collective-permute-start.3 = (f32[160,128]{1,0:T(8,128)S(1)}, f32[160,128]{1,0:T(8,128)S(1)}, u32[]{:S(2)}, u32[]{:S(2)}) collective-permute-start(f32[160,128]{1,0:T(8,128)S(1)} %get-tuple-element.42.own), channel_id=1, source_target_pairs={{0,4},{4,0},{1,5},{5,1},{2,6},{6,2},{3,7},{7,3},{8,12},{12,8},{9,1... | collective-permute-start | bytes 245768 | tf_op jit(solution)/shard_map/ppermute | solution.py:27
  21.0 0.1 collective-permute-start.5
  21.1 3.0 %collective-permute-start.6 = (bf16[32,2688]{1,0:T(8,128)(2,1)S(1)}, bf16[32,2688]{1,0:T(8,128)(2,1)S(1)}, u32[]{:S(2)}, u32[]{:S(2)}) collective-permute-start(bf16[32,2688]{1,0:T(8,128)(2,1)S(1)} %get-tuple-element.45), channel_id=1, source_target_pairs={{0,16},{8,24},{16,0},{24,8},{1,17},{9,25},{17,1},{25,9},{2,18},{10... | collective-permute-start | bytes 516104 | tf_op jit(solution)/shard_map/ppermute | solution.py:41
  24.1 1.3 %collective-permute-start.7 = (bf16[32,2688]{1,0:T(8,128)(2,1)S(1)}, bf16[32,2688]{1,0:T(8,128)(2,1)S(1)}, u32[]{:S(2)}, u32[]{:S(2)}) collective-permute-start(bf16[32,2688]{1,0:T(8,128)(2,1)S(1)} %get-tuple-element.46), channel_id=1, source_target_pairs={{0,24},{8,16},{16,8},{24,0},{1,25},{9,17},{17,9},{25,1},{2,26},{10... | collective-permute-start | bytes 516104 | tf_op jit(solution)/shard_map/ppermute | solution.py:41
  25.4 0.0 collective-permute-done.3.other
  25.4 6.7 %scan.1.value_in = f32[128,2048]{1,0:T(8,128)S(1)} custom-call(f32[160,128]{1,0:T(8,128)S(1)} %get-tuple-element.42.own, f32[160,128]{1,0:T(8,128)S(1)} %collective-permute-done.3.other, bf16[128,2048]{1,0:T(8,128)(2,1)S(1)} %get-tuple-element.43.active, f32[16,2048]{1,0:T(8,128)S(1)} %concatenate.24.params, f32[16,2048]{1,0:T(8,128)} %log_rate_hbm.1, ...), custom_call_target="tpu_custom_call" | custom-call | flops 12582912000 | bytes 2097152 | tf_op jit(solution)/shard_map/scan/pallas_call | solution.py:242
  32.1 0.0 collective-permute-done.5.refs_1_
  32.1 4.2 %collective-permute-done.6.refs_2_ = bf16[32,2688]{1,0:T(8,128)(2,1)S(1)} collective-permute-done((bf16[32,2688]{1,0:T(8,128)(2,1)S(1)}, bf16[32,2688]{1,0:T(8,128)(2,1)S(1)}, u32[]{:S(2)}, u32[]{:S(2)}) %collective-permute-start.6) | collective-permute-done | bytes 172064 | tf_op jit(solution)/shard_map/ppermute | solution.py:41
  36.3 0.0 collective-permute-done.7.refs_3_
  36.3 2.6 %project.1 = (f32[128,512]{1,0:T(8,128)S(1)}, bf16[128,512]{1,0:T(8,128)(2,1)S(1)}, bf16[128,128]{1,0:T(8,128)(2,1)S(1)}) custom-call(s32[4]{0:T(128)S(1)} %pad_add_fusion.places, f32[128,2048]{1,0:T(8,128)S(1)} %scan.1.value_in, bf16[2048,512]{1,0:T(8,128)(2,1)} %weight_hbm.1, bf16[32,2688]{1,0:T(8,128)(2,1)S(1)} %get-tuple-element.76.refs_0_, ...), custom_call_target="tpu_custom_call" | custom-call | flops 268435456 | bytes 2097152 | tf_op jit(solution)/shard_map/project/pallas_call | solution.py:304
  38.9 0.6 collective-permute-start.8
  39.5 5.8 %fetch.1 = (bf16[1792,2048]{1,0:T(8,128)(2,1)S(1)}, bf16[1792,2048]{1,0:T(8,128)(2,1)S(1)}, s32[1]{0:T(128)}) custom-call(s32[1]{0:T(128)} %bitcast.19.half, bf16[7168,2048]{1,0:T(8,128)(2,1)} %gate.1, bf16[7168,2048]{1,0:T(8,128)(2,1)} %up.1), custom_call_target="tpu_custom_call" | custom-call | bytes 29360128 | tf_op jit(solution)/shard_map/fetch/pallas_call | solution.py:425
  45.3 0.0 collective-permute-done.8.summand
  45.3 2.4 %collective-permute-start.11 = (bf16[128,512]{1,0:T(8,128)(2,1)S(1)}, bf16[128,512]{1,0:T(8,128)(2,1)S(1)}, u32[]{:S(2)}, u32[]{:S(2)}) collective-permute-start(bf16[128,512]{1,0:T(8,128)(2,1)S(1)} %mix.1.refs_0_), channel_id=1, source_target_pairs={{0,24},{8,16},{16,8},{24,0},{1,25},{9,17},{17,9},{25,1},{2,26},{10... | collective-permute-start | bytes 393224 | tf_op jit(solution)/shard_map/ppermute | solution.py:41
  47.7 1.7 %collective-permute-start.10 = (bf16[128,512]{1,0:T(8,128)(2,1)S(1)}, bf16[128,512]{1,0:T(8,128)(2,1)S(1)}, u32[]{:S(2)}, u32[]{:S(2)}) collective-permute-start(bf16[128,512]{1,0:T(8,128)(2,1)S(1)} %mix.1.refs_0_), channel_id=1, source_target_pairs={{0,16},{8,24},{16,0},{24,8},{1,17},{9,25},{17,1},{25,9},{2,18},{10... | collective-permute-start | bytes 393224 | tf_op jit(solution)/shard_map/ppermute | solution.py:41
  49.4 0.4 collective-permute-start.9
  49.8 3.8 %collective-permute-done.11.refs_3_ = bf16[128,512]{1,0:T(8,128)(2,1)S(1)} collective-permute-done((bf16[128,512]{1,0:T(8,128)(2,1)S(1)}, bf16[128,512]{1,0:T(8,128)(2,1)S(1)}, u32[]{:S(2)}, u32[]{:S(2)}) %collective-permute-start.11) | collective-permute-done | bytes 131104 | tf_op jit(solution)/shard_map/ppermute | solution.py:41
  53.6 4.5 %collective-permute-done.10.refs_2_ = bf16[128,512]{1,0:T(8,128)(2,1)S(1)} collective-permute-done((bf16[128,512]{1,0:T(8,128)(2,1)S(1)}, bf16[128,512]{1,0:T(8,128)(2,1)S(1)}, u32[]{:S(2)}, u32[]{:S(2)}) %collective-permute-start.10) | collective-permute-done | bytes 131104 | tf_op jit(solution)/shard_map/ppermute | solution.py:41
  58.0 0.0 collective-permute-done.9.refs_1_
  58.0 1.8 %norm.1 = (bf16[128,2048]{1,0:T(8,128)(2,1)S(1)}, f32[128,128]{1,0:T(8,128)S(1)}, bf16[16,2048]{1,0:T(8,128)(2,1)S(1)}) custom-call(s32[4]{0:T(128)S(1)} %pad_add_fusion.places, s32[2]{0:T(128)S(1)} %pad_add_fusion.1.spots, f32[8,2048]{1,0:T(8,128)S(1)} %pad.13.gain, bf16[16,2048]{1,0:T(8,128)(2,1)S(1)} %pad.12.router, ...), custom_call_target="tpu_custom_call" | custom-call | tf_op jit(solution)/shard_map/norm/pallas_call | solution.py:383
  59.8 0.1 collective-permute-start.12
  59.9 1.9 %collective-permute-done.12.other = bf16[128,2048]{1,0:T(8,128)(2,1)S(1)} collective-permute-done((bf16[128,2048]{1,0:T(8,128)(2,1)S(1)}, bf16[128,2048]{1,0:T(8,128)(2,1)S(1)}, u32[]{:S(2)}, u32[]{:S(2)}) %collective-permute-start.12) | collective-permute-done | bytes 524320 | tf_op jit(solution)/shard_map/ppermute | solution.py:67
  61.8 14.9 %experts.1 = (f32[128,2048]{1,0:T(8,128)S(1)}, bf16[128,2048]{1,0:T(8,128)(2,1)S(1)}) custom-call(s32[1]{0:T(128)} %get-tuple-element.56.half, bf16[128,2048]{1,0:T(8,128)(2,1)S(1)} %get-tuple-element.57.own, bf16[128,2048]{1,0:T(8,128)(2,1)S(1)} %collective-permute-done.12.other, bf16[1792,2048]{1,0:T(8,128)(2,1)S(1)} %get-tuple-element.58.gate_first, ...), custom_call_target="tpu_custom_call" | custom-call | flops 11274289152 | bytes 29360128 | tf_op jit(solution)/shard_map/experts/pallas_call | solution.py:477
  76.7 0.2 collective-permute-start.13
  76.9 1.8 %collective-permute-done.13.other = bf16[128,2048]{1,0:T(8,128)(2,1)S(1)} collective-permute-done((bf16[128,2048]{1,0:T(8,128)(2,1)S(1)}, bf16[128,2048]{1,0:T(8,128)(2,1)S(1)}, u32[]{:S(2)}, u32[]{:S(2)}) %collective-permute-start.13) | collective-permute-done | bytes 524320 | tf_op jit(solution)/shard_map/ppermute | solution.py:67
  78.7 0.7 combine.1
  79.4 1.6 %collective-permute-start.14 = (bf16[16,2048]{1,0:T(8,128)(2,1)S(1)}, bf16[16,2048]{1,0:T(8,128)(2,1)S(1)}, u32[]{:S(2)}, u32[]{:S(2)}) collective-permute-start(bf16[16,2048]{1,0:T(8,128)(2,1)S(1)} %get-tuple-element.64), channel_id=1, source_target_pairs={{0,4},{4,0},{8,12},{12,8},{16,20},{20,16},{24,28},{28,24},{1,5},{5... | collective-permute-start | bytes 196616 | tf_op jit(solution)/shard_map/ppermute | solution.py:41
  80.9 0.0 collective-permute-start.15
  81.0 2.0 %collective-permute-start.16 = (bf16[16,2048]{1,0:T(8,128)(2,1)S(1)}, bf16[16,2048]{1,0:T(8,128)(2,1)S(1)}, u32[]{:S(2)}, u32[]{:S(2)}) collective-permute-start(bf16[16,2048]{1,0:T(8,128)(2,1)S(1)} %get-tuple-element.66), channel_id=1, source_target_pairs={{0,12},{4,8},{8,4},{12,0},{16,28},{20,24},{24,20},{28,16},{1,13},{... | collective-permute-start | bytes 196616 | tf_op jit(solution)/shard_map/ppermute | solution.py:41
  82.9 0.9 collective-permute-start.17
  83.8 3.0 %collective-permute-start.18 = (bf16[16,2048]{1,0:T(8,128)(2,1)S(1)}, bf16[16,2048]{1,0:T(8,128)(2,1)S(1)}, u32[]{:S(2)}, u32[]{:S(2)}) collective-permute-start(bf16[16,2048]{1,0:T(8,128)(2,1)S(1)} %get-tuple-element.68), channel_id=1, source_target_pairs={{0,20},{4,16},{8,28},{12,24},{16,4},{20,0},{24,12},{28,8},{1,21},{... | collective-permute-start | bytes 196616 | tf_op jit(solution)/shard_map/ppermute | solution.py:41
  86.8 0.0 collective-permute-done.14
  86.8 2.3 %collective-permute-start.19 = (bf16[16,2048]{1,0:T(8,128)(2,1)S(1)}, bf16[16,2048]{1,0:T(8,128)(2,1)S(1)}, u32[]{:S(2)}, u32[]{:S(2)}) collective-permute-start(bf16[16,2048]{1,0:T(8,128)(2,1)S(1)} %get-tuple-element.69), channel_id=1, source_target_pairs={{0,24},{4,28},{8,16},{12,20},{16,8},{20,12},{24,0},{28,4},{1,25},{... | collective-permute-start | bytes 196616 | tf_op jit(solution)/shard_map/ppermute | solution.py:41
  89.1 0.0 collective-permute-done.15
  89.1 1.5 %collective-permute-start.20 = (bf16[16,2048]{1,0:T(8,128)(2,1)S(1)}, bf16[16,2048]{1,0:T(8,128)(2,1)S(1)}, u32[]{:S(2)}, u32[]{:S(2)}) collective-permute-start(bf16[16,2048]{1,0:T(8,128)(2,1)S(1)} %get-tuple-element.70), channel_id=1, source_target_pairs={{0,28},{4,24},{8,20},{12,16},{16,12},{20,8},{24,4},{28,0},{1,29},{... | collective-permute-start | bytes 196616 | tf_op jit(solution)/shard_map/ppermute | solution.py:41
  90.6 0.0 collective-permute-done.16
  90.6 0.9 collective-permute-done.17
  91.5 4.0 %collective-permute-done.18 = bf16[16,2048]{1,0:T(8,128)(2,1)S(1)} collective-permute-done((bf16[16,2048]{1,0:T(8,128)(2,1)S(1)}, bf16[16,2048]{1,0:T(8,128)(2,1)S(1)}, u32[]{:S(2)}, u32[]{:S(2)}) %collective-permute-start.18) | collective-permute-done | bytes 65568 | tf_op jit(solution)/shard_map/ppermute | solution.py:41
  95.4 0.0 collective-permute-done.19
  95.4 0.7 collective-permute-done.20
  96.2 0.7 add_convert_fusion
  (8 shorter events, 0.1 us)
Async XLA Ops:
  1.0 13.4 %collective-permute-start.2 = (bf16[32,2048]{1,0:T(8,128)(2,1)S(1)}, bf16[32,2048]{1,0:T(8,128)(2,1)S(1)}, u32[]{:S(2)}, u32[]{:S(2)}) collective-permute-start(bf16[32,2048]{1,0:T(8,128)(2,1)S(1)} %get-tuple-element.72.refs_0_), channel_id=1, source_target_pairs={{0,24},{8,16},{16,8},{24,0},{1,25},{9,17},{17,9},{25,1},{2,26},{10... | collective-permute-start | bytes 393224 | tf_op jit(solution)/shard_map/ppermute | solution.py:41
  6.1 11.1 %collective-permute-start.1 = (bf16[32,2048]{1,0:T(8,128)(2,1)S(1)}, bf16[32,2048]{1,0:T(8,128)(2,1)S(1)}, u32[]{:S(2)}, u32[]{:S(2)}) collective-permute-start(bf16[32,2048]{1,0:T(8,128)(2,1)S(1)} %get-tuple-element.72.refs_0_), channel_id=1, source_target_pairs={{0,16},{8,24},{16,0},{24,8},{1,17},{9,25},{17,1},{25,9},{2,18},{10... | collective-permute-start | bytes 393224 | tf_op jit(solution)/shard_map/ppermute | solution.py:41
  6.1 11.1 %collective-permute-start = (bf16[32,2048]{1,0:T(8,128)(2,1)S(1)}, bf16[32,2048]{1,0:T(8,128)(2,1)S(1)}, u32[]{:S(2)}, u32[]{:S(2)}) collective-permute-start(bf16[32,2048]{1,0:T(8,128)(2,1)S(1)} %get-tuple-element.72.refs_0_), channel_id=1, source_target_pairs={{0,8},{8,0},{16,24},{24,16},{1,9},{9,1},{17,25},{25,17},{2,10},{10... | collective-permute-start | bytes 393224 | tf_op jit(solution)/shard_map/ppermute | solution.py:41
  8.4 5.0 %collective-permute-start.4 = (bf16[16,2176]{1,0:T(8,128)(2,1)S(1)}, bf16[16,2176]{1,0:T(8,128)(2,1)S(1)}, u32[]{:S(2)}, u32[]{:S(2)}) collective-permute-start(bf16[16,2176]{1,0:T(8,128)(2,1)S(1)} %pad_maximum_fusion.8), channel_id=1, source_target_pairs={{0,4},{4,0},{1,5},{5,1},{2,6},{6,2},{3,7},{7,3},{8,12},{12,8},{9,1... | collective-permute-start | bytes 208904 | tf_op jit(solution)/shard_map/ppermute | solution.py:27
  19.3 6.1 %collective-permute-start.3 = (f32[160,128]{1,0:T(8,128)S(1)}, f32[160,128]{1,0:T(8,128)S(1)}, u32[]{:S(2)}, u32[]{:S(2)}) collective-permute-start(f32[160,128]{1,0:T(8,128)S(1)} %get-tuple-element.42.own), channel_id=1, source_target_pairs={{0,4},{4,0},{1,5},{5,1},{2,6},{6,2},{3,7},{7,3},{8,12},{12,8},{9,1... | collective-permute-start | bytes 245768 | tf_op jit(solution)/shard_map/ppermute | solution.py:27
  21.0 11.1 %collective-permute-start.5 = (bf16[32,2688]{1,0:T(8,128)(2,1)S(1)}, bf16[32,2688]{1,0:T(8,128)(2,1)S(1)}, u32[]{:S(2)}, u32[]{:S(2)}) collective-permute-start(bf16[32,2688]{1,0:T(8,128)(2,1)S(1)} %get-tuple-element.44), channel_id=1, source_target_pairs={{0,8},{8,0},{16,24},{24,16},{1,9},{9,1},{17,25},{25,17},{2,10},{10... | collective-permute-start | bytes 516104 | tf_op jit(solution)/shard_map/ppermute | solution.py:41
  21.1 15.2 %collective-permute-start.6 = (bf16[32,2688]{1,0:T(8,128)(2,1)S(1)}, bf16[32,2688]{1,0:T(8,128)(2,1)S(1)}, u32[]{:S(2)}, u32[]{:S(2)}) collective-permute-start(bf16[32,2688]{1,0:T(8,128)(2,1)S(1)} %get-tuple-element.45), channel_id=1, source_target_pairs={{0,16},{8,24},{16,0},{24,8},{1,17},{9,25},{17,1},{25,9},{2,18},{10... | collective-permute-start | bytes 516104 | tf_op jit(solution)/shard_map/ppermute | solution.py:41
  24.1 12.2 %collective-permute-start.7 = (bf16[32,2688]{1,0:T(8,128)(2,1)S(1)}, bf16[32,2688]{1,0:T(8,128)(2,1)S(1)}, u32[]{:S(2)}, u32[]{:S(2)}) collective-permute-start(bf16[32,2688]{1,0:T(8,128)(2,1)S(1)} %get-tuple-element.46), channel_id=1, source_target_pairs={{0,24},{8,16},{16,8},{24,0},{1,25},{9,17},{17,9},{25,1},{2,26},{10... | collective-permute-start | bytes 516104 | tf_op jit(solution)/shard_map/ppermute | solution.py:41
  38.9 6.4 %collective-permute-start.8 = (bf16[128,512]{1,0:T(8,128)(2,1)S(1)}, bf16[128,512]{1,0:T(8,128)(2,1)S(1)}, u32[]{:S(2)}, u32[]{:S(2)}) collective-permute-start(bf16[128,512]{1,0:T(8,128)(2,1)S(1)} %get-tuple-element.53), channel_id=1, source_target_pairs={{0,4},{4,0},{1,5},{5,1},{2,6},{6,2},{3,7},{7,3},{8,12},{12,8},{9,1... | collective-permute-start | bytes 393224 | tf_op jit(solution)/shard_map/ppermute | solution.py:27
  45.3 8.2 %collective-permute-start.11 = (bf16[128,512]{1,0:T(8,128)(2,1)S(1)}, bf16[128,512]{1,0:T(8,128)(2,1)S(1)}, u32[]{:S(2)}, u32[]{:S(2)}) collective-permute-start(bf16[128,512]{1,0:T(8,128)(2,1)S(1)} %mix.1.refs_0_), channel_id=1, source_target_pairs={{0,24},{8,16},{16,8},{24,0},{1,25},{9,17},{17,9},{25,1},{2,26},{10... | collective-permute-start | bytes 393224 | tf_op jit(solution)/shard_map/ppermute | solution.py:41
  47.7 10.3 %collective-permute-start.10 = (bf16[128,512]{1,0:T(8,128)(2,1)S(1)}, bf16[128,512]{1,0:T(8,128)(2,1)S(1)}, u32[]{:S(2)}, u32[]{:S(2)}) collective-permute-start(bf16[128,512]{1,0:T(8,128)(2,1)S(1)} %mix.1.refs_0_), channel_id=1, source_target_pairs={{0,16},{8,24},{16,0},{24,8},{1,17},{9,25},{17,1},{25,9},{2,18},{10... | collective-permute-start | bytes 393224 | tf_op jit(solution)/shard_map/ppermute | solution.py:41
  49.4 8.6 %collective-permute-start.9 = (bf16[128,512]{1,0:T(8,128)(2,1)S(1)}, bf16[128,512]{1,0:T(8,128)(2,1)S(1)}, u32[]{:S(2)}, u32[]{:S(2)}) collective-permute-start(bf16[128,512]{1,0:T(8,128)(2,1)S(1)} %mix.1.refs_0_), channel_id=1, source_target_pairs={{0,8},{8,0},{16,24},{24,16},{1,9},{9,1},{17,25},{25,17},{2,10},{10... | collective-permute-start | bytes 393224 | tf_op jit(solution)/shard_map/ppermute | solution.py:41
  59.8 2.0 %collective-permute-start.12 = (bf16[128,2048]{1,0:T(8,128)(2,1)S(1)}, bf16[128,2048]{1,0:T(8,128)(2,1)S(1)}, u32[]{:S(2)}, u32[]{:S(2)}) collective-permute-start(bf16[128,2048]{1,0:T(8,128)(2,1)S(1)} %get-tuple-element.57.own), channel_id=1, source_target_pairs={{0,1},{1,0},{2,3},{3,2},{4,5},{5,4},{6,7},{7,6},{8,9},{9,8},{10,11... | collective-permute-start | bytes 1572872 | tf_op jit(solution)/shard_map/ppermute | solution.py:67
  76.7 2.0 %collective-permute-start.13 = (bf16[128,2048]{1,0:T(8,128)(2,1)S(1)}, bf16[128,2048]{1,0:T(8,128)(2,1)S(1)}, u32[]{:S(2)}, u32[]{:S(2)}) collective-permute-start(bf16[128,2048]{1,0:T(8,128)(2,1)S(1)} %get-tuple-element.61), channel_id=1, source_target_pairs={{0,1},{1,0},{2,3},{3,2},{4,5},{5,4},{6,7},{7,6},{8,9},{9,8},{10,11... | collective-permute-start | bytes 1572872 | tf_op jit(solution)/shard_map/ppermute | solution.py:67
  79.4 7.4 %collective-permute-start.14 = (bf16[16,2048]{1,0:T(8,128)(2,1)S(1)}, bf16[16,2048]{1,0:T(8,128)(2,1)S(1)}, u32[]{:S(2)}, u32[]{:S(2)}) collective-permute-start(bf16[16,2048]{1,0:T(8,128)(2,1)S(1)} %get-tuple-element.64), channel_id=1, source_target_pairs={{0,4},{4,0},{8,12},{12,8},{16,20},{20,16},{24,28},{28,24},{1,5},{5... | collective-permute-start | bytes 196616 | tf_op jit(solution)/shard_map/ppermute | solution.py:41
  80.9 8.2 %collective-permute-start.15 = (bf16[16,2048]{1,0:T(8,128)(2,1)S(1)}, bf16[16,2048]{1,0:T(8,128)(2,1)S(1)}, u32[]{:S(2)}, u32[]{:S(2)}) collective-permute-start(bf16[16,2048]{1,0:T(8,128)(2,1)S(1)} %get-tuple-element.65), channel_id=1, source_target_pairs={{0,8},{4,12},{8,0},{12,4},{16,24},{20,28},{24,16},{28,20},{1,9},{5... | collective-permute-start | bytes 196616 | tf_op jit(solution)/shard_map/ppermute | solution.py:41
  81.0 9.6 %collective-permute-start.16 = (bf16[16,2048]{1,0:T(8,128)(2,1)S(1)}, bf16[16,2048]{1,0:T(8,128)(2,1)S(1)}, u32[]{:S(2)}, u32[]{:S(2)}) collective-permute-start(bf16[16,2048]{1,0:T(8,128)(2,1)S(1)} %get-tuple-element.66), channel_id=1, source_target_pairs={{0,12},{4,8},{8,4},{12,0},{16,28},{20,24},{24,20},{28,16},{1,13},{... | collective-permute-start | bytes 196616 | tf_op jit(solution)/shard_map/ppermute | solution.py:41
  82.9 8.5 %collective-permute-start.17 = (bf16[16,2048]{1,0:T(8,128)(2,1)S(1)}, bf16[16,2048]{1,0:T(8,128)(2,1)S(1)}, u32[]{:S(2)}, u32[]{:S(2)}) collective-permute-start(bf16[16,2048]{1,0:T(8,128)(2,1)S(1)} %get-tuple-element.67), channel_id=1, source_target_pairs={{0,16},{4,20},{8,24},{12,28},{16,0},{20,4},{24,8},{28,12},{1,17},{... | collective-permute-start | bytes 196616 | tf_op jit(solution)/shard_map/ppermute | solution.py:41
  83.8 11.6 %collective-permute-start.18 = (bf16[16,2048]{1,0:T(8,128)(2,1)S(1)}, bf16[16,2048]{1,0:T(8,128)(2,1)S(1)}, u32[]{:S(2)}, u32[]{:S(2)}) collective-permute-start(bf16[16,2048]{1,0:T(8,128)(2,1)S(1)} %get-tuple-element.68), channel_id=1, source_target_pairs={{0,20},{4,16},{8,28},{12,24},{16,4},{20,0},{24,12},{28,8},{1,21},{... | collective-permute-start | bytes 196616 | tf_op jit(solution)/shard_map/ppermute | solution.py:41
  86.8 8.6 %collective-permute-start.19 = (bf16[16,2048]{1,0:T(8,128)(2,1)S(1)}, bf16[16,2048]{1,0:T(8,128)(2,1)S(1)}, u32[]{:S(2)}, u32[]{:S(2)}) collective-permute-start(bf16[16,2048]{1,0:T(8,128)(2,1)S(1)} %get-tuple-element.69), channel_id=1, source_target_pairs={{0,24},{4,28},{8,16},{12,20},{16,8},{20,12},{24,0},{28,4},{1,25},{... | collective-permute-start | bytes 196616 | tf_op jit(solution)/shard_map/ppermute | solution.py:41
  89.1 7.1 %collective-permute-start.20 = (bf16[16,2048]{1,0:T(8,128)(2,1)S(1)}, bf16[16,2048]{1,0:T(8,128)(2,1)S(1)}, u32[]{:S(2)}, u32[]{:S(2)}) collective-permute-start(bf16[16,2048]{1,0:T(8,128)(2,1)S(1)} %get-tuple-element.70), channel_id=1, source_target_pairs={{0,28},{4,24},{8,20},{12,16},{16,12},{20,8},{24,4},{28,0},{1,29},{... | collective-permute-start | bytes 196616 | tf_op jit(solution)/shard_map/ppermute | solution.py:41

commit v7 on v6

--- a/solution.py
+++ b/solution.py
@@ -28,13 +28,11 @@
 
 
 def partner(place, step, count):
-    paired = count & (count - 1) == 0
-    return place ^ step if paired else (place + step) % count
+    return (place + step) % count
 
 
 def source(place, step, count):
-    paired = count & (count - 1) == 0
-    return place ^ step if paired else (place - step) % count
+    return (place - step) % count
 
 
 def exchange(value, axes, step, count):
@@ -266,9 +264,10 @@
     )(own, other, active, params, far(log_rate), far(step_weight), far(state_in))
 
 
-def project_kernel(count, columns, places, value_in, weight_hbm, *refs):
+def project_kernel(count, columns, splits, places, value_in, weight_hbm, *refs):
     pieces = refs[:count]
-    base_out, send_out, routes_out, gated, out_weight, sem = refs[count:]
+    send_out, routes_out, base_out, gated, out_weight, sem = refs[count:]
+    lanes = columns // splits
     copy = pltpu.make_async_copy(weight_hbm, out_weight, sem)
     copy.start()
     tokens, channels = value_in.shape
@@ -276,7 +275,7 @@
     tile = 16
     for index in range(count):
         begin = pl.multiple_of(places[index] * rows, tile)
-        routes_out[pl.ds(begin, rows), :] = pieces[index][:, channels + columns :]
+        routes_out[pl.ds(begin, rows), :] = pieces[index][:, channels + lanes :]
 
         def gate(number, carry):
             local = pl.ds(pl.multiple_of(number * tile, tile), tile)
@@ -289,28 +288,33 @@
     copy.wait()
     for number in range(tokens // LANES):
         cut = slice(number * LANES, (number + 1) * LANES)
-        sent = jnp.dot(gated[cut, :], out_weight[...], preferred_element_type=F32).astype(BF16)
-        send_out[cut, :] = sent
-        base_out[cut, :] = sent.astype(F32)
+        base_out[cut, :] = jnp.dot(gated[cut, :], out_weight[...], preferred_element_type=F32)
+    part = rows // splits
     for index in range(count):
-        here = pl.ds(pl.multiple_of(places[index] * rows, tile), rows)
-        base_out[here, :] += pieces[index][:, channels : channels + columns].astype(F32)
-
-
-def project(places, value, out_weight, pieces):
+        begin = places[index] * rows + (places[count] * part if splits > 1 else 0)
+        here = pl.ds(pl.multiple_of(begin, tile), part)
+        for k in range(splits):
+            piece = pieces[index][k * part : (k + 1) * part, channels : channels + lanes]
+            base_out[here, k * lanes : (k + 1) * lanes] += piece.astype(F32)
+    for number in range(tokens // LANES):
+        cut = slice(number * LANES, (number + 1) * LANES)
+        send_out[cut, :] = base_out[cut, :].astype(BF16)
+
+
+def project(places, value, out_weight, pieces, splits):
     tokens, channels = value.shape
     columns = out_weight.shape[1]
     count = len(pieces)
     return pl.pallas_call(
-        functools.partial(project_kernel, count, columns),
+        functools.partial(project_kernel, count, columns, splits),
         out_shape=(
-            jax.ShapeDtypeStruct((tokens, columns), F32),
             jax.ShapeDtypeStruct((tokens, columns), BF16),
             jax.ShapeDtypeStruct((tokens, LANES), BF16),
         ),
         in_specs=[SCALARS, WHOLE, FAR] + [WHOLE] * count,
-        out_specs=(WHOLE,) * 3,
+        out_specs=(WHOLE,) * 2,
         scratch_shapes=[
+            VMEM((tokens, columns), F32),
             VMEM((tokens, channels), BF16),
             VMEM(out_weight.shape, BF16),
             pltpu.SemaphoreType.DMA,
@@ -326,7 +330,7 @@
 
 
 def mix_kernel(base, summand, mixed):
-    mixed[...] = (base[...] + summand[...].astype(F32)).astype(BF16)
+    mixed[...] = (base[...].astype(F32) + summand[...].astype(F32)).astype(BF16)
 
 
 def mix(base, summand):
@@ -585,7 +589,7 @@
     targets = jnp.stack([partner(me, s, parts) for s in range(parts)]).astype(jnp.int32)
 
     x_pieces = spread(lambda k: x_input, "ctx", 0)
-    extra = jnp.concatenate([residual, jnp.pad(routes.astype(BF16), ((0, 0), (0, LANES - 2)))], axis=1)
+    extra = jnp.pad(routes.astype(BF16), ((0, 0), (0, LANES - 2)))
     if exp == 2:
         other = rotate(extra, "exp", 1)
         extra = jnp.where(
@@ -594,13 +598,12 @@
             jnp.concatenate([other, extra], axis=0),
         )
     else:
-        extra = lax.all_gather(extra, "exp", axis=0, tiled=True)
+        extra = lax.all_gather(jnp.concatenate([residual, extra], axis=1), "exp", axis=0, tiled=True)
     tail_pad = jnp.zeros((8 - carried_tail.shape[0], carried_tail.shape[1]), F32)
     params = jnp.concatenate(
         [filter_taps, filter_bias[None], step_bias[None], skip_gain[None], jnp.zeros_like(tail_pad)[: 5 - taps],
          tail_pad, carried_tail.astype(F32)]
     )
-    ready = [jnp.concatenate([z_input, extra[:, width:]], axis=1), extra[:, :width]]
     router_rows = jnp.pad(router.T, ((0, 16 - EXPERTS), (0, 0)))
     gain = jnp.pad(norm_gain[None, :], ((0, 7), (0, 0)))
     params, router_rows, gain, spots, targets = lax.optimization_barrier(
@@ -610,25 +613,30 @@
     active, proj = activate(places, x_pieces, params, taps, select_weight)
     own_proj, other_proj = pair_sum(proj, "exp")
 
+    splits = exp if exp == 2 else 1
+
     def bundle(k):
-        piece = lax.dynamic_slice_in_dim(ready[1], k * columns, columns, axis=1)
-        channels = z_input.shape[1]
-        return jnp.concatenate([ready[0][:, :channels], piece, ready[0][:, channels:]], axis=1)
+        rows = residual if splits > 1 else jnp.where(exp_at == 0, extra[:, :width], 0)
+        piece = lax.dynamic_slice_in_dim(rows, k * columns, columns, axis=1)
+        lanes = columns // splits
+        piece = jnp.concatenate([piece[:, i * lanes : (i + 1) * lanes] for i in range(splits)], axis=0)
+        return jnp.concatenate([z_input, piece, extra[:, -LANES:]], axis=1)
 
     z_pieces = spread(bundle, "ctx", 0, active)
     value = scan(own_proj, other_proj, active, params, taps, log_rate, step_weight, carried_state)
-    base, sent, all_routes = project(places, value, output_weight, z_pieces)
-    shared = parts <= 8 and base.shape[0] == LANES and lax.axis_size("doc") % 2 == 0
+    spread_places = jnp.concatenate([places, exp_at.astype(jnp.int32)[None]])
+    sent, all_routes = project(spread_places, value, output_weight, z_pieces, splits)
+    shared = exp == 2 and parts <= 8 and sent.shape[0] == LANES and lax.axis_size("doc") % 2 == 0
     half = lax.rem(lax.axis_index("doc"), 2).astype(jnp.int32)[None]
     if exp == 2:
         summand = rotate(sent, "exp", 1)
+        if shared:
+            half, sent = lax.optimization_barrier((half, sent))
+            gate_first, up_first, half = fetch(half, [gate_weight, up_weight])
+            half, sent = lax.optimization_barrier((half, sent))
+        mixed = mix(sent, summand)
     else:
-        summand = lax.psum(sent.astype(F32), "exp") - sent.astype(F32)
-    if shared:
-        half, base = lax.optimization_barrier((half, base))
-        gate_first, up_first, half = fetch(half, [gate_weight, up_weight])
-        half, base = lax.optimization_barrier((half, base))
-    mixed = mix(base, summand)
+        mixed = lax.psum(sent.astype(F32), "exp").astype(BF16)
     mixed_pieces = spread(lambda k: mixed, "ctx", 1)
     normed, weight, mine = norm(places, spots, gain, router_rows, all_routes, mixed_pieces, own)
     total = mine.astype(F32)

time: 97.4 us -> 96.3 us (0.989)
  waiting for transfers between devices: 24.5 us -> 22.5 us
  other arithmetic: 3.39 us -> 1.59 us
  starting transfers between devices: 29.9 us -> 31.5 us
    ppermute x16, waiting for transfers between devices: 20.8 us -> 18.8 us  [exchange(): lax.ppermute(value, axes, [(i, partner(i, step, count)) for i in range(co...]
    ppermute x16, starting transfers between devices: 25.9 us -> 27.6 us  [exchange(): lax.ppermute(value, axes, [(i, partner(i, step, count)) for i in range(co...]
  transfers between devices with their start and end apart: 21 -> 21, of which waited for: 9 -> 11; matrix products, arithmetic and copies ran while one was open for 6% -> 5% of each run, Pallas kernels for 13% -> 13%
where the time goes in v7:
time: 96.3 us; the launch traced here: 95.4 us
  Pallas kernels  34.5 us (36%)
  starting transfers between devices  31.5 us (33%)
  waiting for transfers between devices  22.5 us (23%)
  local copies, waits for them, and re-layouts  5.12 us (5%)
  other arithmetic  1.59 us (2%)
    ppermute x16, starting transfers between devices, exchange(): lax.ppermute(value, axes, [(i, partner(i, step, count)) for i in range(co...  27.6 us
    ppermute x16, waiting for transfers between devices, exchange(): lax.ppermute(value, axes, [(i, partner(i, step, count)) for i in range(co...  18.8 us
    pallas_call x1, Pallas kernels, shared_experts(): pl.pallas_call(shared_kernel, out_shape=(jax.ShapeDtypeStruct((rows, widt...  14.9 us
    pallas_call x1, Pallas kernels, scan(): pl.pallas_call(functools.partial(scan_kernel, taps), out_shape=jax.ShapeD...  6.66 us
    pallas_call x1, Pallas kernels, fetch(): pl.pallas_call(functools.partial(fetch_kernel, parts, half_rows), out_sha...  5.82 us
    ppermute x3, starting transfers between devices, rotate(): lax.ppermute(value, axis, [(i, (i + steps) % count) for i in range(count)])  3.68 us
    ppermute x2, waiting for transfers between devices, swap(): lax.ppermute(value, 'doc', [(i, i + 1 - 2 * (i % 2)) for i in range(count)])  3.67 us
    pallas_call x1, Pallas kernels, project(): pl.pallas_call(functools.partial(project_kernel, count, columns, splits),...  2.62 us
  transfers between devices with their start and end apart: 21, of which 11 were waited for; matrix products, arithmetic and copies ran while one was open for 5% of the time, Pallas kernels for 13%

profile of v7, /device:TPU:0, one launch (start us, length us, event | category | flops | bytes accessed | tf_op | source)
XLA Modules:
  0.0 95.4 jit_solution(5209136503899032686)
XLA Ops:
  0.0 1.0 %slice_bitcast_fusion = (bf16[32,2048]{1,0:T(8,128)(2,1)S(1)}, bf16[32,2048]{1,0:T(8,128)(2,1)S(1)}) fusion(bf16[2,32,2048]{2,1,0:T(8,128)(2,1)} %param.18), kind=kLoop, calls=%fused_computation.5 | loop fusion | bytes 524288 | tf_op jit(solution)/shard_map/squeeze | solution.py:582
  1.0 5.1 %collective-permute-start.2 = (bf16[32,2048]{1,0:T(8,128)(2,1)S(1)}, bf16[32,2048]{1,0:T(8,128)(2,1)S(1)}, u32[]{:S(2)}, u32[]{:S(2)}) collective-permute-start(bf16[32,2048]{1,0:T(8,128)(2,1)S(1)} %get-tuple-element.70.refs_0_), channel_id=1, source_target_pairs={{0,24},{8,0},{16,8},{24,16},{1,25},{9,1},{17,9},{25,17},{2,26},{10... | collective-permute-start | bytes 393224 | tf_op jit(solution)/shard_map/ppermute | solution.py:39
  6.1 0.0 collective-permute-start.1
  6.1 1.0 %collective-permute-start = (bf16[32,2048]{1,0:T(8,128)(2,1)S(1)}, bf16[32,2048]{1,0:T(8,128)(2,1)S(1)}, u32[]{:S(2)}, u32[]{:S(2)}) collective-permute-start(bf16[32,2048]{1,0:T(8,128)(2,1)S(1)} %get-tuple-element.70.refs_0_), channel_id=1, source_target_pairs={{0,8},{8,16},{16,24},{24,0},{1,9},{9,17},{17,25},{25,1},{2,10},{10... | collective-permute-start | bytes 393224 | tf_op jit(solution)/shard_map/ppermute | solution.py:39
  7.1 0.7 convert_element_type.43
  7.8 0.1 copy.20
  7.9 1.5 %collective-permute-start.4 = (bf16[16,128]{1,0:T(8,128)(2,1)S(1)}, bf16[16,128]{1,0:T(8,128)(2,1)S(1)}, u32[]{:S(2)}, u32[]{:S(2)}) collective-permute-start(bf16[16,128]{1,0:T(8,128)(2,1)S(1)} %pad.14), channel_id=1, source_target_pairs={{0,4},{4,0},{1,5},{5,1},{2,6},{6,2},{3,7},{7,3},{8,12},{12,8},{9,1... | collective-permute-start | bytes 12296 | tf_op jit(solution)/shard_map/ppermute | solution.py:27
  9.4 0.1 pad_add_fusion.1.spots
  9.5 0.8 constant_dynamic-slice_fusion
  10.3 0.1 pad_add_fusion.places
  10.4 0.1 concatenate.38.places
  10.5 0.7 pad.12.router
  11.3 0.7 pad.13.gain
  12.0 1.6 %concatenate.37.params = f32[16,2048]{1,0:T(8,128)S(1)} concatenate(f32[4,2048]{1,0:T(4,128)} %param.21, f32[1,2048]{1,0:T(1,128)} %bitcast.27, f32[1,2048]{1,0:T(1,128)} %bitcast.28, f32[1,2048]{1,0:T(1,128)} %bitcast.29, f32[1,2048]{1,0:T(1,128)S(1)} %slice.33, f32[5,2048]{1,0:T(8,128)S(1)} %broadcast_in_dim.24, bf16[3,2048]{1,0:T(4,128)(2,1)} %param.19), dimensions={0} | concatenate | bytes 249856 | tf_op jit(solution)/shard_map/concatenate | solution.py:603
  13.6 0.1 stack.67.targets
  13.7 0.0 collective-permute-done.4
  13.7 0.0 collective-permute-done.2.refs_3_
  13.7 3.6 %collective-permute-done.1.refs_2_ = bf16[32,2048]{1,0:T(8,128)(2,1)S(1)} collective-permute-done((bf16[32,2048]{1,0:T(8,128)(2,1)S(1)}, bf16[32,2048]{1,0:T(8,128)(2,1)S(1)}, u32[]{:S(2)}, u32[]{:S(2)}) %collective-permute-start.1) | collective-permute-done | bytes 131104 | tf_op jit(solution)/shard_map/ppermute | solution.py:39
  17.3 0.0 collective-permute-done.refs_1_
  17.3 2.1 %activate.1 = (bf16[128,2048]{1,0:T(8,128)(2,1)S(1)}, f32[160,128]{1,0:T(8,128)S(1)}) custom-call(s32[4]{0:T(128)S(1)} %pad_add_fusion.places, f32[16,2048]{1,0:T(8,128)S(1)} %concatenate.37.params, bf16[160,2048]{1,0:T(8,128)(2,1)} %select.38, bf16[32,2048]{1,0:T(8,128)(2,1)S(1)} %get-tuple-element.70.refs_0_, ...), custom_call_target="tpu_custom_call" | custom-call | flops 83886080 | bytes 1048576 | tf_op jit(solution)/shard_map/activate/pallas_call | solution.py:118
  19.4 1.6 %collective-permute-start.3 = (f32[160,128]{1,0:T(8,128)S(1)}, f32[160,128]{1,0:T(8,128)S(1)}, u32[]{:S(2)}, u32[]{:S(2)}) collective-permute-start(f32[160,128]{1,0:T(8,128)S(1)} %get-tuple-element.41.own), channel_id=1, source_target_pairs={{0,4},{4,0},{1,5},{5,1},{2,6},{6,2},{3,7},{7,3},{8,12},{12,8},{9,1... | collective-permute-start | bytes 245768 | tf_op jit(solution)/shard_map/ppermute | solution.py:27
  21.1 0.8 collective-permute-start.5
  21.8 2.0 %collective-permute-start.6 = (bf16[32,2432]{1,0:T(8,128)(2,1)S(1)}, bf16[32,2432]{1,0:T(8,128)(2,1)S(1)}, u32[]{:S(2)}, u32[]{:S(2)}) collective-permute-start(bf16[32,2432]{1,0:T(8,128)(2,1)S(1)} %get-tuple-element.44), channel_id=1, source_target_pairs={{0,16},{8,24},{16,0},{24,8},{1,17},{9,25},{17,1},{25,9},{2,18},{10... | collective-permute-start | bytes 466952 | tf_op jit(solution)/shard_map/ppermute | solution.py:39
  23.8 2.8 %collective-permute-start.7 = (bf16[32,2432]{1,0:T(8,128)(2,1)S(1)}, bf16[32,2432]{1,0:T(8,128)(2,1)S(1)}, u32[]{:S(2)}, u32[]{:S(2)}) collective-permute-start(bf16[32,2432]{1,0:T(8,128)(2,1)S(1)} %get-tuple-element.45), channel_id=1, source_target_pairs={{0,24},{8,0},{16,8},{24,16},{1,25},{9,1},{17,9},{25,17},{2,26},{10... | collective-permute-start | bytes 466952 | tf_op jit(solution)/shard_map/ppermute | solution.py:39
  26.7 0.0 collective-permute-done.3.other
  26.7 6.7 %scan.1.value_in = f32[128,2048]{1,0:T(8,128)S(1)} custom-call(f32[160,128]{1,0:T(8,128)S(1)} %get-tuple-element.41.own, f32[160,128]{1,0:T(8,128)S(1)} %collective-permute-done.3.other, bf16[128,2048]{1,0:T(8,128)(2,1)S(1)} %get-tuple-element.42.active, f32[16,2048]{1,0:T(8,128)S(1)} %concatenate.37.params, f32[16,2048]{1,0:T(8,128)} %log_rate_hbm.1, ...), custom_call_target="tpu_custom_call" | custom-call | flops 12582912000 | bytes 2097152 | tf_op jit(solution)/shard_map/scan/pallas_call | solution.py:240
  33.4 0.0 collective-permute-done.5.refs_1_
  33.4 1.4 %collective-permute-done.6.refs_2_ = bf16[32,2432]{1,0:T(8,128)(2,1)S(1)} collective-permute-done((bf16[32,2432]{1,0:T(8,128)(2,1)S(1)}, bf16[32,2432]{1,0:T(8,128)(2,1)S(1)}, u32[]{:S(2)}, u32[]{:S(2)}) %collective-permute-start.6) | collective-permute-done | bytes 155680 | tf_op jit(solution)/shard_map/ppermute | solution.py:39
  34.8 0.0 collective-permute-done.7.refs_3_
  34.8 2.6 %project.1 = (bf16[128,512]{1,0:T(8,128)(2,1)S(1)}, bf16[128,128]{1,0:T(8,128)(2,1)S(1)}) custom-call(s32[5]{0:T(128)S(1)} %concatenate.38.places, f32[128,2048]{1,0:T(8,128)S(1)} %scan.1.value_in, bf16[2048,512]{1,0:T(8,128)(2,1)} %weight_hbm.1, bf16[32,2432]{1,0:T(8,128)(2,1)S(1)} %get-tuple-element.74.refs_0_, ...), custom_call_target="tpu_custom_call" | custom-call | flops 268435456 | bytes 2097152 | tf_op jit(solution)/shard_map/project/pallas_call | solution.py:308
  37.4 0.6 collective-permute-start.8
  38.0 5.8 %fetch.1 = (bf16[1792,2048]{1,0:T(8,128)(2,1)S(1)}, bf16[1792,2048]{1,0:T(8,128)(2,1)S(1)}, s32[1]{0:T(128)}) custom-call(s32[1]{0:T(128)} %bitcast.22.half, bf16[7168,2048]{1,0:T(8,128)(2,1)} %gate.1, bf16[7168,2048]{1,0:T(8,128)(2,1)} %up.1), custom_call_target="tpu_custom_call" | custom-call | bytes 29360128 | tf_op jit(solution)/shard_map/fetch/pallas_call | solution.py:429
  43.8 0.0 collective-permute-done.8.summand
  43.9 4.8 %collective-permute-start.11 = (bf16[128,512]{1,0:T(8,128)(2,1)S(1)}, bf16[128,512]{1,0:T(8,128)(2,1)S(1)}, u32[]{:S(2)}, u32[]{:S(2)}) collective-permute-start(bf16[128,512]{1,0:T(8,128)(2,1)S(1)} %mix.1.refs_0_), channel_id=1, source_target_pairs={{0,24},{8,0},{16,8},{24,16},{1,25},{9,1},{17,9},{25,17},{2,26},{10... | collective-permute-start | bytes 393224 | tf_op jit(solution)/shard_map/ppermute | solution.py:39
  48.7 0.0 collective-permute-start.10
  48.7 0.6 collective-permute-start.9
  49.3 3.3 %collective-permute-done.11.refs_3_ = bf16[128,512]{1,0:T(8,128)(2,1)S(1)} collective-permute-done((bf16[128,512]{1,0:T(8,128)(2,1)S(1)}, bf16[128,512]{1,0:T(8,128)(2,1)S(1)}, u32[]{:S(2)}, u32[]{:S(2)}) %collective-permute-start.11) | collective-permute-done | bytes 131104 | tf_op jit(solution)/shard_map/ppermute | solution.py:39
  52.7 6.8 %collective-permute-done.10.refs_2_ = bf16[128,512]{1,0:T(8,128)(2,1)S(1)} collective-permute-done((bf16[128,512]{1,0:T(8,128)(2,1)S(1)}, bf16[128,512]{1,0:T(8,128)(2,1)S(1)}, u32[]{:S(2)}, u32[]{:S(2)}) %collective-permute-start.10) | collective-permute-done | bytes 131104 | tf_op jit(solution)/shard_map/ppermute | solution.py:39
  59.4 0.0 collective-permute-done.9.refs_1_
  59.4 1.6 %norm.1 = (bf16[128,2048]{1,0:T(8,128)(2,1)S(1)}, f32[128,128]{1,0:T(8,128)S(1)}, bf16[16,2048]{1,0:T(8,128)(2,1)S(1)}) custom-call(s32[4]{0:T(128)S(1)} %pad_add_fusion.places, s32[2]{0:T(128)S(1)} %pad_add_fusion.1.spots, f32[8,2048]{1,0:T(8,128)S(1)} %pad.13.gain, bf16[16,2048]{1,0:T(8,128)(2,1)S(1)} %pad.12.router, ...), custom_call_target="tpu_custom_call" | custom-call | tf_op jit(solution)/shard_map/norm/pallas_call | solution.py:387
  61.0 0.1 collective-permute-start.12
  61.1 1.9 %collective-permute-done.12.other = bf16[128,2048]{1,0:T(8,128)(2,1)S(1)} collective-permute-done((bf16[128,2048]{1,0:T(8,128)(2,1)S(1)}, bf16[128,2048]{1,0:T(8,128)(2,1)S(1)}, u32[]{:S(2)}, u32[]{:S(2)}) %collective-permute-start.12) | collective-permute-done | bytes 524320 | tf_op jit(solution)/shard_map/ppermute | solution.py:65
  63.0 14.9 %experts.1 = (f32[128,2048]{1,0:T(8,128)S(1)}, bf16[128,2048]{1,0:T(8,128)(2,1)S(1)}) custom-call(s32[1]{0:T(128)} %get-tuple-element.54.half, bf16[128,2048]{1,0:T(8,128)(2,1)S(1)} %get-tuple-element.55.own, bf16[128,2048]{1,0:T(8,128)(2,1)S(1)} %collective-permute-done.12.other, bf16[1792,2048]{1,0:T(8,128)(2,1)S(1)} %get-tuple-element.56.gate_first, ...), custom_call_target="tpu_custom_call" | custom-call | flops 11274289152 | bytes 29360128 | tf_op jit(solution)/shard_map/experts/pallas_call | solution.py:481
  77.9 0.2 collective-permute-start.13
  78.1 1.8 %collective-permute-done.13.other = bf16[128,2048]{1,0:T(8,128)(2,1)S(1)} collective-permute-done((bf16[128,2048]{1,0:T(8,128)(2,1)S(1)}, bf16[128,2048]{1,0:T(8,128)(2,1)S(1)}, u32[]{:S(2)}, u32[]{:S(2)}) %collective-permute-start.13) | collective-permute-done | bytes 524320 | tf_op jit(solution)/shard_map/ppermute | solution.py:65
  79.9 0.7 combine.1
  80.6 1.6 %collective-permute-start.14 = (bf16[16,2048]{1,0:T(8,128)(2,1)S(1)}, bf16[16,2048]{1,0:T(8,128)(2,1)S(1)}, u32[]{:S(2)}, u32[]{:S(2)}) collective-permute-start(bf16[16,2048]{1,0:T(8,128)(2,1)S(1)} %get-tuple-element.62), channel_id=1, source_target_pairs={{0,4},{4,8},{8,12},{12,16},{16,20},{20,24},{24,28},{28,0},{1,5},{5... | collective-permute-start | bytes 196616 | tf_op jit(solution)/shard_map/ppermute | solution.py:39
  82.2 0.0 collective-permute-start.15
  82.2 1.6 %collective-permute-start.16 = (bf16[16,2048]{1,0:T(8,128)(2,1)S(1)}, bf16[16,2048]{1,0:T(8,128)(2,1)S(1)}, u32[]{:S(2)}, u32[]{:S(2)}) collective-permute-start(bf16[16,2048]{1,0:T(8,128)(2,1)S(1)} %get-tuple-element.64), channel_id=1, source_target_pairs={{0,12},{4,16},{8,20},{12,24},{16,28},{20,0},{24,4},{28,8},{1,13},{... | collective-permute-start | bytes 196616 | tf_op jit(solution)/shard_map/ppermute | solution.py:39
  83.7 2.3 %collective-permute-start.17 = (bf16[16,2048]{1,0:T(8,128)(2,1)S(1)}, bf16[16,2048]{1,0:T(8,128)(2,1)S(1)}, u32[]{:S(2)}, u32[]{:S(2)}) collective-permute-start(bf16[16,2048]{1,0:T(8,128)(2,1)S(1)} %get-tuple-element.65), channel_id=1, source_target_pairs={{0,16},{4,20},{8,24},{12,28},{16,0},{20,4},{24,8},{28,12},{1,17},{... | collective-permute-start | bytes 196616 | tf_op jit(solution)/shard_map/ppermute | solution.py:39
  86.1 1.4 %collective-permute-start.18 = (bf16[16,2048]{1,0:T(8,128)(2,1)S(1)}, bf16[16,2048]{1,0:T(8,128)(2,1)S(1)}, u32[]{:S(2)}, u32[]{:S(2)}) collective-permute-start(bf16[16,2048]{1,0:T(8,128)(2,1)S(1)} %get-tuple-element.66), channel_id=1, source_target_pairs={{0,20},{4,24},{8,28},{12,0},{16,4},{20,8},{24,12},{28,16},{1,21},{... | collective-permute-start | bytes 196616 | tf_op jit(solution)/shard_map/ppermute | solution.py:39
  87.5 0.9 collective-permute-done.14
  88.4 2.0 %collective-permute-start.19 = (bf16[16,2048]{1,0:T(8,128)(2,1)S(1)}, bf16[16,2048]{1,0:T(8,128)(2,1)S(1)}, u32[]{:S(2)}, u32[]{:S(2)}) collective-permute-start(bf16[16,2048]{1,0:T(8,128)(2,1)S(1)} %get-tuple-element.67), channel_id=1, source_target_pairs={{0,24},{4,28},{8,0},{12,4},{16,8},{20,12},{24,16},{28,20},{1,25},{... | collective-permute-start | bytes 196616 | tf_op jit(solution)/shard_map/ppermute | solution.py:39
  90.4 0.0 collective-permute-done.15
  90.4 1.4 %collective-permute-start.20 = (bf16[16,2048]{1,0:T(8,128)(2,1)S(1)}, bf16[16,2048]{1,0:T(8,128)(2,1)S(1)}, u32[]{:S(2)}, u32[]{:S(2)}) collective-permute-start(bf16[16,2048]{1,0:T(8,128)(2,1)S(1)} %get-tuple-element.68), channel_id=1, source_target_pairs={{0,28},{4,0},{8,4},{12,8},{16,12},{20,16},{24,20},{28,24},{1,29},{... | collective-permute-start | bytes 196616 | tf_op jit(solution)/shard_map/ppermute | solution.py:39
  91.8 1.4 %collective-permute-done.16 = bf16[16,2048]{1,0:T(8,128)(2,1)S(1)} collective-permute-done((bf16[16,2048]{1,0:T(8,128)(2,1)S(1)}, bf16[16,2048]{1,0:T(8,128)(2,1)S(1)}, u32[]{:S(2)}, u32[]{:S(2)}) %collective-permute-start.16) | collective-permute-done | bytes 65568 | tf_op jit(solution)/shard_map/ppermute | solution.py:39
  93.2 0.7 collective-permute-done.17
  94.0 0.0 collective-permute-done.18
  94.0 0.7 collective-permute-done.19
  94.6 0.1 collective-permute-done.20
  94.7 0.7 add_convert_fusion
  (6 shorter events, 0.1 us)
Async XLA Ops:
  1.0 12.7 %collective-permute-start.2 = (bf16[32,2048]{1,0:T(8,128)(2,1)S(1)}, bf16[32,2048]{1,0:T(8,128)(2,1)S(1)}, u32[]{:S(2)}, u32[]{:S(2)}) collective-permute-start(bf16[32,2048]{1,0:T(8,128)(2,1)S(1)} %get-tuple-element.70.refs_0_), channel_id=1, source_target_pairs={{0,24},{8,0},{16,8},{24,16},{1,25},{9,1},{17,9},{25,17},{2,26},{10... | collective-permute-start | bytes 393224 | tf_op jit(solution)/shard_map/ppermute | solution.py:39
  6.1 11.2 %collective-permute-start.1 = (bf16[32,2048]{1,0:T(8,128)(2,1)S(1)}, bf16[32,2048]{1,0:T(8,128)(2,1)S(1)}, u32[]{:S(2)}, u32[]{:S(2)}) collective-permute-start(bf16[32,2048]{1,0:T(8,128)(2,1)S(1)} %get-tuple-element.70.refs_0_), channel_id=1, source_target_pairs={{0,16},{8,24},{16,0},{24,8},{1,17},{9,25},{17,1},{25,9},{2,18},{10... | collective-permute-start | bytes 393224 | tf_op jit(solution)/shard_map/ppermute | solution.py:39
  6.1 11.2 %collective-permute-start = (bf16[32,2048]{1,0:T(8,128)(2,1)S(1)}, bf16[32,2048]{1,0:T(8,128)(2,1)S(1)}, u32[]{:S(2)}, u32[]{:S(2)}) collective-permute-start(bf16[32,2048]{1,0:T(8,128)(2,1)S(1)} %get-tuple-element.70.refs_0_), channel_id=1, source_target_pairs={{0,8},{8,16},{16,24},{24,0},{1,9},{9,17},{17,25},{25,1},{2,10},{10... | collective-permute-start | bytes 393224 | tf_op jit(solution)/shard_map/ppermute | solution.py:39
  7.9 5.8 %collective-permute-start.4 = (bf16[16,128]{1,0:T(8,128)(2,1)S(1)}, bf16[16,128]{1,0:T(8,128)(2,1)S(1)}, u32[]{:S(2)}, u32[]{:S(2)}) collective-permute-start(bf16[16,128]{1,0:T(8,128)(2,1)S(1)} %pad.14), channel_id=1, source_target_pairs={{0,4},{4,0},{1,5},{5,1},{2,6},{6,2},{3,7},{7,3},{8,12},{12,8},{9,1... | collective-permute-start | bytes 12296 | tf_op jit(solution)/shard_map/ppermute | solution.py:27
  19.4 7.2 %collective-permute-start.3 = (f32[160,128]{1,0:T(8,128)S(1)}, f32[160,128]{1,0:T(8,128)S(1)}, u32[]{:S(2)}, u32[]{:S(2)}) collective-permute-start(f32[160,128]{1,0:T(8,128)S(1)} %get-tuple-element.41.own), channel_id=1, source_target_pairs={{0,4},{4,0},{1,5},{5,1},{2,6},{6,2},{3,7},{7,3},{8,12},{12,8},{9,1... | collective-permute-start | bytes 245768 | tf_op jit(solution)/shard_map/ppermute | solution.py:27
  21.1 12.3 %collective-permute-start.5 = (bf16[32,2432]{1,0:T(8,128)(2,1)S(1)}, bf16[32,2432]{1,0:T(8,128)(2,1)S(1)}, u32[]{:S(2)}, u32[]{:S(2)}) collective-permute-start(bf16[32,2432]{1,0:T(8,128)(2,1)S(1)} %get-tuple-element.43), channel_id=1, source_target_pairs={{0,8},{8,16},{16,24},{24,0},{1,9},{9,17},{17,25},{25,1},{2,10},{10... | collective-permute-start | bytes 466952 | tf_op jit(solution)/shard_map/ppermute | solution.py:39
  21.8 12.9 %collective-permute-start.6 = (bf16[32,2432]{1,0:T(8,128)(2,1)S(1)}, bf16[32,2432]{1,0:T(8,128)(2,1)S(1)}, u32[]{:S(2)}, u32[]{:S(2)}) collective-permute-start(bf16[32,2432]{1,0:T(8,128)(2,1)S(1)} %get-tuple-element.44), channel_id=1, source_target_pairs={{0,16},{8,24},{16,0},{24,8},{1,17},{9,25},{17,1},{25,9},{2,18},{10... | collective-permute-start | bytes 466952 | tf_op jit(solution)/shard_map/ppermute | solution.py:39
  23.8 10.9 %collective-permute-start.7 = (bf16[32,2432]{1,0:T(8,128)(2,1)S(1)}, bf16[32,2432]{1,0:T(8,128)(2,1)S(1)}, u32[]{:S(2)}, u32[]{:S(2)}) collective-permute-start(bf16[32,2432]{1,0:T(8,128)(2,1)S(1)} %get-tuple-element.45), channel_id=1, source_target_pairs={{0,24},{8,0},{16,8},{24,16},{1,25},{9,1},{17,9},{25,17},{2,26},{10... | collective-permute-start | bytes 466952 | tf_op jit(solution)/shard_map/ppermute | solution.py:39
  37.4 6.4 %collective-permute-start.8 = (bf16[128,512]{1,0:T(8,128)(2,1)S(1)}, bf16[128,512]{1,0:T(8,128)(2,1)S(1)}, u32[]{:S(2)}, u32[]{:S(2)}) collective-permute-start(bf16[128,512]{1,0:T(8,128)(2,1)S(1)} %get-tuple-element.51.base), channel_id=1, source_target_pairs={{0,4},{4,0},{1,5},{5,1},{2,6},{6,2},{3,7},{7,3},{8,12},{12,8},{9,1... | collective-permute-start | bytes 393224 | tf_op jit(solution)/shard_map/ppermute | solution.py:27
  43.9 8.8 %collective-permute-start.11 = (bf16[128,512]{1,0:T(8,128)(2,1)S(1)}, bf16[128,512]{1,0:T(8,128)(2,1)S(1)}, u32[]{:S(2)}, u32[]{:S(2)}) collective-permute-start(bf16[128,512]{1,0:T(8,128)(2,1)S(1)} %mix.1.refs_0_), channel_id=1, source_target_pairs={{0,24},{8,0},{16,8},{24,16},{1,25},{9,1},{17,9},{25,17},{2,26},{10... | collective-permute-start | bytes 393224 | tf_op jit(solution)/shard_map/ppermute | solution.py:39
  48.7 10.7 %collective-permute-start.10 = (bf16[128,512]{1,0:T(8,128)(2,1)S(1)}, bf16[128,512]{1,0:T(8,128)(2,1)S(1)}, u32[]{:S(2)}, u32[]{:S(2)}) collective-permute-start(bf16[128,512]{1,0:T(8,128)(2,1)S(1)} %mix.1.refs_0_), channel_id=1, source_target_pairs={{0,16},{8,24},{16,0},{24,8},{1,17},{9,25},{17,1},{25,9},{2,18},{10... | collective-permute-start | bytes 393224 | tf_op jit(solution)/shard_map/ppermute | solution.py:39
  48.7 10.7 %collective-permute-start.9 = (bf16[128,512]{1,0:T(8,128)(2,1)S(1)}, bf16[128,512]{1,0:T(8,128)(2,1)S(1)}, u32[]{:S(2)}, u32[]{:S(2)}) collective-permute-start(bf16[128,512]{1,0:T(8,128)(2,1)S(1)} %mix.1.refs_0_), channel_id=1, source_target_pairs={{0,8},{8,16},{16,24},{24,0},{1,9},{9,17},{17,25},{25,1},{2,10},{10... | collective-permute-start | bytes 393224 | tf_op jit(solution)/shard_map/ppermute | solution.py:39
  61.0 2.0 %collective-permute-start.12 = (bf16[128,2048]{1,0:T(8,128)(2,1)S(1)}, bf16[128,2048]{1,0:T(8,128)(2,1)S(1)}, u32[]{:S(2)}, u32[]{:S(2)}) collective-permute-start(bf16[128,2048]{1,0:T(8,128)(2,1)S(1)} %get-tuple-element.55.own), channel_id=1, source_target_pairs={{0,1},{1,0},{2,3},{3,2},{4,5},{5,4},{6,7},{7,6},{8,9},{9,8},{10,11... | collective-permute-start | bytes 1572872 | tf_op jit(solution)/shard_map/ppermute | solution.py:65
  77.9 2.0 %collective-permute-start.13 = (bf16[128,2048]{1,0:T(8,128)(2,1)S(1)}, bf16[128,2048]{1,0:T(8,128)(2,1)S(1)}, u32[]{:S(2)}, u32[]{:S(2)}) collective-permute-start(bf16[128,2048]{1,0:T(8,128)(2,1)S(1)} %get-tuple-element.59), channel_id=1, source_target_pairs={{0,1},{1,0},{2,3},{3,2},{4,5},{5,4},{6,7},{7,6},{8,9},{9,8},{10,11... | collective-permute-start | bytes 1572872 | tf_op jit(solution)/shard_map/ppermute | solution.py:65
  80.6 7.8 %collective-permute-start.14 = (bf16[16,2048]{1,0:T(8,128)(2,1)S(1)}, bf16[16,2048]{1,0:T(8,128)(2,1)S(1)}, u32[]{:S(2)}, u32[]{:S(2)}) collective-permute-start(bf16[16,2048]{1,0:T(8,128)(2,1)S(1)} %get-tuple-element.62), channel_id=1, source_target_pairs={{0,4},{4,8},{8,12},{12,16},{16,20},{20,24},{24,28},{28,0},{1,5},{5... | collective-permute-start | bytes 196616 | tf_op jit(solution)/shard_map/ppermute | solution.py:39
  82.2 8.3 %collective-permute-start.15 = (bf16[16,2048]{1,0:T(8,128)(2,1)S(1)}, bf16[16,2048]{1,0:T(8,128)(2,1)S(1)}, u32[]{:S(2)}, u32[]{:S(2)}) collective-permute-start(bf16[16,2048]{1,0:T(8,128)(2,1)S(1)} %get-tuple-element.63), channel_id=1, source_target_pairs={{0,8},{4,12},{8,16},{12,20},{16,24},{20,28},{24,0},{28,4},{1,9},{5... | collective-permute-start | bytes 196616 | tf_op jit(solution)/shard_map/ppermute | solution.py:39
  82.2 11.1 %collective-permute-start.16 = (bf16[16,2048]{1,0:T(8,128)(2,1)S(1)}, bf16[16,2048]{1,0:T(8,128)(2,1)S(1)}, u32[]{:S(2)}, u32[]{:S(2)}) collective-permute-start(bf16[16,2048]{1,0:T(8,128)(2,1)S(1)} %get-tuple-element.64), channel_id=1, source_target_pairs={{0,12},{4,16},{8,20},{12,24},{16,28},{20,0},{24,4},{28,8},{1,13},{... | collective-permute-start | bytes 196616 | tf_op jit(solution)/shard_map/ppermute | solution.py:39
  83.7 10.2 %collective-permute-start.17 = (bf16[16,2048]{1,0:T(8,128)(2,1)S(1)}, bf16[16,2048]{1,0:T(8,128)(2,1)S(1)}, u32[]{:S(2)}, u32[]{:S(2)}) collective-permute-start(bf16[16,2048]{1,0:T(8,128)(2,1)S(1)} %get-tuple-element.65), channel_id=1, source_target_pairs={{0,16},{4,20},{8,24},{12,28},{16,0},{20,4},{24,8},{28,12},{1,17},{... | collective-permute-start | bytes 196616 | tf_op jit(solution)/shard_map/ppermute | solution.py:39
  86.1 7.9 %collective-permute-start.18 = (bf16[16,2048]{1,0:T(8,128)(2,1)S(1)}, bf16[16,2048]{1,0:T(8,128)(2,1)S(1)}, u32[]{:S(2)}, u32[]{:S(2)}) collective-permute-start(bf16[16,2048]{1,0:T(8,128)(2,1)S(1)} %get-tuple-element.66), channel_id=1, source_target_pairs={{0,20},{4,24},{8,28},{12,0},{16,4},{20,8},{24,12},{28,16},{1,21},{... | collective-permute-start | bytes 196616 | tf_op jit(solution)/shard_map/ppermute | solution.py:39
  88.4 6.2 %collective-permute-start.19 = (bf16[16,2048]{1,0:T(8,128)(2,1)S(1)}, bf16[16,2048]{1,0:T(8,128)(2,1)S(1)}, u32[]{:S(2)}, u32[]{:S(2)}) collective-permute-start(bf16[16,2048]{1,0:T(8,128)(2,1)S(1)} %get-tuple-element.67), channel_id=1, source_target_pairs={{0,24},{4,28},{8,0},{12,4},{16,8},{20,12},{24,16},{28,20},{1,25},{... | collective-permute-start | bytes 196616 | tf_op jit(solution)/shard_map/ppermute | solution.py:39
  90.4 4.3 %collective-permute-start.20 = (bf16[16,2048]{1,0:T(8,128)(2,1)S(1)}, bf16[16,2048]{1,0:T(8,128)(2,1)S(1)}, u32[]{:S(2)}, u32[]{:S(2)}) collective-permute-start(bf16[16,2048]{1,0:T(8,128)(2,1)S(1)} %get-tuple-element.68), channel_id=1, source_target_pairs={{0,28},{4,0},{8,4},{12,8},{16,12},{20,16},{24,20},{28,24},{1,29},{... | collective-permute-start | bytes 196616 | tf_op jit(solution)/shard_map/ppermute | solution.py:39

commit v8 on v7

--- a/solution.py
+++ b/solution.py
@@ -28,15 +28,17 @@
 
 
 def partner(place, step, count):
-    return (place + step) % count
+    paired = count & (count - 1) == 0
+    return place ^ step if paired else (place + step) % count
 
 
 def source(place, step, count):
-    return (place - step) % count
-
-
-def exchange(value, axes, step, count):
-    return lax.ppermute(value, axes, [(i, partner(i, step, count)) for i in range(count)])
+    paired = count & (count - 1) == 0
+    return place ^ step if paired else (place - step) % count
+
+
+def exchange(value, axis, step, count):
+    return lax.ppermute(value, axis, [(i, partner(i, step, count)) for i in range(count)])
 
 
 def ring_places(axis):
@@ -586,7 +588,7 @@
     parts = ctx * exp
     me = ctx_at * exp + exp_at
     spots = jnp.stack([ctx_at // (ctx // EXPERTS), me]).astype(jnp.int32)
-    targets = jnp.stack([partner(me, s, parts) for s in range(parts)]).astype(jnp.int32)
+    targets = jnp.stack([(me + s) % parts for s in range(parts)]).astype(jnp.int32)
 
     x_pieces = spread(lambda k: x_input, "ctx", 0)
     extra = jnp.pad(routes.astype(BF16), ((0, 0), (0, LANES - 2)))
@@ -646,7 +648,7 @@
         outs = combine(targets, kept, swap(given), weight, own)
         arrived = [outs[0]]
         for s in range(1, parts):
-            arrived.append(exchange(outs[s], axes, s, parts))
+            arrived.append(lax.ppermute(outs[s], axes, [(i, (i + s) % parts) for i in range(parts)]))
         for piece in arrived:
             total = total + piece.astype(F32)
     else:

time: 96.3 us -> 94.1 us (0.977)
  starting transfers between devices: 31.5 us -> 28.5 us
    ppermute x16, starting transfers between devices: 27.6 us -> 24.4 us  [the longest x9 14.7 us: exchange(): lax.ppermute(value, axis, [(i, partner(i, step, count)) for i in range(co...]
  transfers between devices with their start and end apart: 21 -> 21, of which waited for: 11 -> 9; matrix products, arithmetic and copies ran while one was open for 5% -> 5% of each run, Pallas kernels for 13% -> 13%
where the time goes in v8:
time: 94.1 us; the launch traced here: 93.4 us
  Pallas kernels  34.7 us (37%)
  starting transfers between devices  28.5 us (30%)
  waiting for transfers between devices  23.3 us (25%)
  local copies, waits for them, and re-layouts  5.12 us (5%)
  other arithmetic  1.59 us (2%)
    pallas_call x1, Pallas kernels, shared_experts(): pl.pallas_call(shared_kernel, out_shape=(jax.ShapeDtypeStruct((rows, widt...  14.9 us
    ppermute x9, waiting for transfers between devices, exchange(): lax.ppermute(value, axis, [(i, partner(i, step, count)) for i in range(co...  14.8 us
    ppermute x9, starting transfers between devices, exchange(): lax.ppermute(value, axis, [(i, partner(i, step, count)) for i in range(co...  14.7 us
    ppermute x7, starting transfers between devices, body(): lax.ppermute(outs[s], axes, [(i, (i + s) % parts) for i in range(parts)])  9.79 us
    pallas_call x1, Pallas kernels, scan(): pl.pallas_call(functools.partial(scan_kernel, taps), out_shape=jax.ShapeD...  6.66 us
    pallas_call x1, Pallas kernels, fetch(): pl.pallas_call(functools.partial(fetch_kernel, parts, half_rows), out_sha...  5.82 us
    ppermute x7, waiting for transfers between devices, body(): lax.ppermute(outs[s], axes, [(i, (i + s) % parts) for i in range(parts)])  4.81 us
    ppermute x3, starting transfers between devices, rotate(): lax.ppermute(value, axis, [(i, (i + steps) % count) for i in range(count)])  3.82 us
  transfers between devices with their start and end apart: 21, of which 9 were waited for; matrix products, arithmetic and copies ran while one was open for 5% of the time, Pallas kernels for 13%

profile of v8, /device:TPU:0, one launch (start us, length us, event | category | flops | bytes accessed | tf_op | source)
XLA Modules:
  0.0 93.4 jit_solution(8262060371250935179)
XLA Ops:
  0.0 1.0 %slice_bitcast_fusion = (bf16[32,2048]{1,0:T(8,128)(2,1)S(1)}, bf16[32,2048]{1,0:T(8,128)(2,1)S(1)}) fusion(bf16[2,32,2048]{2,1,0:T(8,128)(2,1)} %param.18), kind=kLoop, calls=%fused_computation.5 | loop fusion | bytes 524288 | tf_op jit(solution)/shard_map/squeeze | solution.py:584
  1.0 5.1 %collective-permute-start.2 = (bf16[32,2048]{1,0:T(8,128)(2,1)S(1)}, bf16[32,2048]{1,0:T(8,128)(2,1)S(1)}, u32[]{:S(2)}, u32[]{:S(2)}) collective-permute-start(bf16[32,2048]{1,0:T(8,128)(2,1)S(1)} %get-tuple-element.70.refs_0_), channel_id=1, source_target_pairs={{0,24},{8,16},{16,8},{24,0},{1,25},{9,17},{17,9},{25,1},{2,26},{10... | collective-permute-start | bytes 393224 | tf_op jit(solution)/shard_map/ppermute | solution.py:41
  6.1 0.0 collective-permute-start.1
  6.1 0.6 collective-permute-start
  6.7 0.7 convert_element_type.43
  7.4 0.1 copy.20
  7.5 1.7 %collective-permute-start.4 = (bf16[16,128]{1,0:T(8,128)(2,1)S(1)}, bf16[16,128]{1,0:T(8,128)(2,1)S(1)}, u32[]{:S(2)}, u32[]{:S(2)}) collective-permute-start(bf16[16,128]{1,0:T(8,128)(2,1)S(1)} %pad.14), channel_id=1, source_target_pairs={{0,4},{4,0},{1,5},{5,1},{2,6},{6,2},{3,7},{7,3},{8,12},{12,8},{9,1... | collective-permute-start | bytes 12296 | tf_op jit(solution)/shard_map/ppermute | solution.py:27
  9.2 0.1 pad_add_fusion.1.spots
  9.3 0.8 constant_dynamic-slice_fusion
  10.1 0.1 pad_add_fusion.places
  10.2 0.1 concatenate.38.places
  10.3 0.7 pad.12.router
  11.1 0.7 pad.13.gain
  11.8 1.6 %concatenate.37.params = f32[16,2048]{1,0:T(8,128)S(1)} concatenate(f32[4,2048]{1,0:T(4,128)} %param.21, f32[1,2048]{1,0:T(1,128)} %bitcast.26, f32[1,2048]{1,0:T(1,128)} %bitcast.27, f32[1,2048]{1,0:T(1,128)} %bitcast.28, f32[1,2048]{1,0:T(1,128)S(1)} %slice.33, f32[5,2048]{1,0:T(8,128)S(1)} %broadcast_in_dim.24, bf16[3,2048]{1,0:T(4,128)(2,1)} %param.19), dimensions={0} | concatenate | bytes 249856 | tf_op jit(solution)/shard_map/concatenate | solution.py:605
  13.4 0.1 stack.64.targets
  13.5 0.0 collective-permute-done.4
  13.5 0.0 collective-permute-done.2.refs_3_
  13.5 3.7 %collective-permute-done.1.refs_2_ = bf16[32,2048]{1,0:T(8,128)(2,1)S(1)} collective-permute-done((bf16[32,2048]{1,0:T(8,128)(2,1)S(1)}, bf16[32,2048]{1,0:T(8,128)(2,1)S(1)}, u32[]{:S(2)}, u32[]{:S(2)}) %collective-permute-start.1) | collective-permute-done | bytes 131104 | tf_op jit(solution)/shard_map/ppermute | solution.py:41
  17.2 0.0 collective-permute-done.refs_1_
  17.2 2.1 %activate.1 = (bf16[128,2048]{1,0:T(8,128)(2,1)S(1)}, f32[160,128]{1,0:T(8,128)S(1)}) custom-call(s32[4]{0:T(128)S(1)} %pad_add_fusion.places, f32[16,2048]{1,0:T(8,128)S(1)} %concatenate.37.params, bf16[160,2048]{1,0:T(8,128)(2,1)} %select.24, bf16[32,2048]{1,0:T(8,128)(2,1)S(1)} %get-tuple-element.70.refs_0_, ...), custom_call_target="tpu_custom_call" | custom-call | flops 83886080 | bytes 1048576 | tf_op jit(solution)/shard_map/activate/pallas_call | solution.py:120
  19.3 1.6 %collective-permute-start.3 = (f32[160,128]{1,0:T(8,128)S(1)}, f32[160,128]{1,0:T(8,128)S(1)}, u32[]{:S(2)}, u32[]{:S(2)}) collective-permute-start(f32[160,128]{1,0:T(8,128)S(1)} %get-tuple-element.41.own), channel_id=1, source_target_pairs={{0,4},{4,0},{1,5},{5,1},{2,6},{6,2},{3,7},{7,3},{8,12},{12,8},{9,1... | collective-permute-start | bytes 245768 | tf_op jit(solution)/shard_map/ppermute | solution.py:27
  21.0 0.1 collective-permute-start.5
  21.0 3.0 %collective-permute-start.6 = (bf16[32,2432]{1,0:T(8,128)(2,1)S(1)}, bf16[32,2432]{1,0:T(8,128)(2,1)S(1)}, u32[]{:S(2)}, u32[]{:S(2)}) collective-permute-start(bf16[32,2432]{1,0:T(8,128)(2,1)S(1)} %get-tuple-element.44), channel_id=1, source_target_pairs={{0,16},{8,24},{16,0},{24,8},{1,17},{9,25},{17,1},{25,9},{2,18},{10... | collective-permute-start | bytes 466952 | tf_op jit(solution)/shard_map/ppermute | solution.py:41
  24.1 1.3 %collective-permute-start.7 = (bf16[32,2432]{1,0:T(8,128)(2,1)S(1)}, bf16[32,2432]{1,0:T(8,128)(2,1)S(1)}, u32[]{:S(2)}, u32[]{:S(2)}) collective-permute-start(bf16[32,2432]{1,0:T(8,128)(2,1)S(1)} %get-tuple-element.45), channel_id=1, source_target_pairs={{0,24},{8,16},{16,8},{24,0},{1,25},{9,17},{17,9},{25,1},{2,26},{10... | collective-permute-start | bytes 466952 | tf_op jit(solution)/shard_map/ppermute | solution.py:41
  25.4 0.0 collective-permute-done.3.other
  25.4 6.7 %scan.1.value_in = f32[128,2048]{1,0:T(8,128)S(1)} custom-call(f32[160,128]{1,0:T(8,128)S(1)} %get-tuple-element.41.own, f32[160,128]{1,0:T(8,128)S(1)} %collective-permute-done.3.other, bf16[128,2048]{1,0:T(8,128)(2,1)S(1)} %get-tuple-element.42.active, f32[16,2048]{1,0:T(8,128)S(1)} %concatenate.37.params, f32[16,2048]{1,0:T(8,128)} %log_rate_hbm.1, ...), custom_call_target="tpu_custom_call" | custom-call | flops 12582912000 | bytes 2097152 | tf_op jit(solution)/shard_map/scan/pallas_call | solution.py:242
  32.1 0.0 collective-permute-done.5.refs_1_
  32.1 2.9 %collective-permute-done.6.refs_2_ = bf16[32,2432]{1,0:T(8,128)(2,1)S(1)} collective-permute-done((bf16[32,2432]{1,0:T(8,128)(2,1)S(1)}, bf16[32,2432]{1,0:T(8,128)(2,1)S(1)}, u32[]{:S(2)}, u32[]{:S(2)}) %collective-permute-start.6) | collective-permute-done | bytes 155680 | tf_op jit(solution)/shard_map/ppermute | solution.py:41
  35.0 0.0 collective-permute-done.7.refs_3_
  35.0 2.6 %project.1 = (bf16[128,512]{1,0:T(8,128)(2,1)S(1)}, bf16[128,128]{1,0:T(8,128)(2,1)S(1)}) custom-call(s32[5]{0:T(128)S(1)} %concatenate.38.places, f32[128,2048]{1,0:T(8,128)S(1)} %scan.1.value_in, bf16[2048,512]{1,0:T(8,128)(2,1)} %weight_hbm.1, bf16[32,2432]{1,0:T(8,128)(2,1)S(1)} %get-tuple-element.74.refs_0_, ...), custom_call_target="tpu_custom_call" | custom-call | flops 268435456 | bytes 2097152 | tf_op jit(solution)/shard_map/project/pallas_call | solution.py:310
  37.7 0.6 collective-permute-start.8
  38.2 5.8 %fetch.1 = (bf16[1792,2048]{1,0:T(8,128)(2,1)S(1)}, bf16[1792,2048]{1,0:T(8,128)(2,1)S(1)}, s32[1]{0:T(128)}) custom-call(s32[1]{0:T(128)} %bitcast.21.half, bf16[7168,2048]{1,0:T(8,128)(2,1)} %gate.1, bf16[7168,2048]{1,0:T(8,128)(2,1)} %up.1), custom_call_target="tpu_custom_call" | custom-call | bytes 29360128 | tf_op jit(solution)/shard_map/fetch/pallas_call | solution.py:431
  44.1 0.0 collective-permute-done.8.summand
  44.1 2.5 %collective-permute-start.11 = (bf16[128,512]{1,0:T(8,128)(2,1)S(1)}, bf16[128,512]{1,0:T(8,128)(2,1)S(1)}, u32[]{:S(2)}, u32[]{:S(2)}) collective-permute-start(bf16[128,512]{1,0:T(8,128)(2,1)S(1)} %mix.1.refs_0_), channel_id=1, source_target_pairs={{0,24},{8,16},{16,8},{24,0},{1,25},{9,17},{17,9},{25,1},{2,26},{10... | collective-permute-start | bytes 393224 | tf_op jit(solution)/shard_map/ppermute | solution.py:41
  46.6 1.4 %collective-permute-start.10 = (bf16[128,512]{1,0:T(8,128)(2,1)S(1)}, bf16[128,512]{1,0:T(8,128)(2,1)S(1)}, u32[]{:S(2)}, u32[]{:S(2)}) collective-permute-start(bf16[128,512]{1,0:T(8,128)(2,1)S(1)} %mix.1.refs_0_), channel_id=1, source_target_pairs={{0,16},{8,24},{16,0},{24,8},{1,17},{9,25},{17,1},{25,9},{2,18},{10... | collective-permute-start | bytes 393224 | tf_op jit(solution)/shard_map/ppermute | solution.py:41
  48.0 0.5 collective-permute-start.9
  48.6 3.8 %collective-permute-done.11.refs_3_ = bf16[128,512]{1,0:T(8,128)(2,1)S(1)} collective-permute-done((bf16[128,512]{1,0:T(8,128)(2,1)S(1)}, bf16[128,512]{1,0:T(8,128)(2,1)S(1)}, u32[]{:S(2)}, u32[]{:S(2)}) %collective-permute-start.11) | collective-permute-done | bytes 131104 | tf_op jit(solution)/shard_map/ppermute | solution.py:41
  52.3 4.4 %collective-permute-done.10.refs_2_ = bf16[128,512]{1,0:T(8,128)(2,1)S(1)} collective-permute-done((bf16[128,512]{1,0:T(8,128)(2,1)S(1)}, bf16[128,512]{1,0:T(8,128)(2,1)S(1)}, u32[]{:S(2)}, u32[]{:S(2)}) %collective-permute-start.10) | collective-permute-done | bytes 131104 | tf_op jit(solution)/shard_map/ppermute | solution.py:41
  56.8 0.0 collective-permute-done.9.refs_1_
  56.8 1.8 %norm.1 = (bf16[128,2048]{1,0:T(8,128)(2,1)S(1)}, f32[128,128]{1,0:T(8,128)S(1)}, bf16[16,2048]{1,0:T(8,128)(2,1)S(1)}) custom-call(s32[4]{0:T(128)S(1)} %pad_add_fusion.places, s32[2]{0:T(128)S(1)} %pad_add_fusion.1.spots, f32[8,2048]{1,0:T(8,128)S(1)} %pad.13.gain, bf16[16,2048]{1,0:T(8,128)(2,1)S(1)} %pad.12.router, ...), custom_call_target="tpu_custom_call" | custom-call | tf_op jit(solution)/shard_map/norm/pallas_call | solution.py:389
  58.6 0.1 collective-permute-start.12
  58.7 1.9 %collective-permute-done.12.other = bf16[128,2048]{1,0:T(8,128)(2,1)S(1)} collective-permute-done((bf16[128,2048]{1,0:T(8,128)(2,1)S(1)}, bf16[128,2048]{1,0:T(8,128)(2,1)S(1)}, u32[]{:S(2)}, u32[]{:S(2)}) %collective-permute-start.12) | collective-permute-done | bytes 524320 | tf_op jit(solution)/shard_map/ppermute | solution.py:67
  60.6 14.9 %experts.1 = (f32[128,2048]{1,0:T(8,128)S(1)}, bf16[128,2048]{1,0:T(8,128)(2,1)S(1)}) custom-call(s32[1]{0:T(128)} %get-tuple-element.54.half, bf16[128,2048]{1,0:T(8,128)(2,1)S(1)} %get-tuple-element.55.own, bf16[128,2048]{1,0:T(8,128)(2,1)S(1)} %collective-permute-done.12.other, bf16[1792,2048]{1,0:T(8,128)(2,1)S(1)} %get-tuple-element.56.gate_first, ...), custom_call_target="tpu_custom_call" | custom-call | flops 11274289152 | bytes 29360128 | tf_op jit(solution)/shard_map/experts/pallas_call | solution.py:483
  75.4 0.2 collective-permute-start.13
  75.6 1.8 %collective-permute-done.13.other = bf16[128,2048]{1,0:T(8,128)(2,1)S(1)} collective-permute-done((bf16[128,2048]{1,0:T(8,128)(2,1)S(1)}, bf16[128,2048]{1,0:T(8,128)(2,1)S(1)}, u32[]{:S(2)}, u32[]{:S(2)}) %collective-permute-start.13) | collective-permute-done | bytes 524320 | tf_op jit(solution)/shard_map/ppermute | solution.py:67
  77.4 0.7 combine.1
  78.1 1.6 %collective-permute-start.14 = (bf16[16,2048]{1,0:T(8,128)(2,1)S(1)}, bf16[16,2048]{1,0:T(8,128)(2,1)S(1)}, u32[]{:S(2)}, u32[]{:S(2)}) collective-permute-start(bf16[16,2048]{1,0:T(8,128)(2,1)S(1)} %get-tuple-element.62), channel_id=1, source_target_pairs={{0,4},{4,8},{8,12},{12,16},{16,20},{20,24},{24,28},{28,0},{1,5},{5... | collective-permute-start | bytes 196616 | tf_op jit(solution)/shard_map/ppermute | solution.py:651
  79.7 0.0 collective-permute-start.15
  79.7 2.3 %collective-permute-start.16 = (bf16[16,2048]{1,0:T(8,128)(2,1)S(1)}, bf16[16,2048]{1,0:T(8,128)(2,1)S(1)}, u32[]{:S(2)}, u32[]{:S(2)}) collective-permute-start(bf16[16,2048]{1,0:T(8,128)(2,1)S(1)} %get-tuple-element.64), channel_id=1, source_target_pairs={{0,12},{4,16},{8,20},{12,24},{16,28},{20,0},{24,4},{28,8},{1,13},{... | collective-permute-start | bytes 196616 | tf_op jit(solution)/shard_map/ppermute | solution.py:651
  82.0 1.6 %collective-permute-start.17 = (bf16[16,2048]{1,0:T(8,128)(2,1)S(1)}, bf16[16,2048]{1,0:T(8,128)(2,1)S(1)}, u32[]{:S(2)}, u32[]{:S(2)}) collective-permute-start(bf16[16,2048]{1,0:T(8,128)(2,1)S(1)} %get-tuple-element.65), channel_id=1, source_target_pairs={{0,16},{4,20},{8,24},{12,28},{16,0},{20,4},{24,8},{28,12},{1,17},{... | collective-permute-start | bytes 196616 | tf_op jit(solution)/shard_map/ppermute | solution.py:651
  83.6 2.3 %collective-permute-start.18 = (bf16[16,2048]{1,0:T(8,128)(2,1)S(1)}, bf16[16,2048]{1,0:T(8,128)(2,1)S(1)}, u32[]{:S(2)}, u32[]{:S(2)}) collective-permute-start(bf16[16,2048]{1,0:T(8,128)(2,1)S(1)} %get-tuple-element.66), channel_id=1, source_target_pairs={{0,20},{4,24},{8,28},{12,0},{16,4},{20,8},{24,12},{28,16},{1,21},{... | collective-permute-start | bytes 196616 | tf_op jit(solution)/shard_map/ppermute | solution.py:651
  85.9 0.0 collective-permute-done.14
  85.9 1.4 %collective-permute-start.19 = (bf16[16,2048]{1,0:T(8,128)(2,1)S(1)}, bf16[16,2048]{1,0:T(8,128)(2,1)S(1)}, u32[]{:S(2)}, u32[]{:S(2)}) collective-permute-start(bf16[16,2048]{1,0:T(8,128)(2,1)S(1)} %get-tuple-element.67), channel_id=1, source_target_pairs={{0,24},{4,28},{8,0},{12,4},{16,8},{20,12},{24,16},{28,20},{1,25},{... | collective-permute-start | bytes 196616 | tf_op jit(solution)/shard_map/ppermute | solution.py:651
  87.4 0.0 collective-permute-done.15
  87.4 0.6 collective-permute-start.20
  87.9 2.8 %collective-permute-done.16 = bf16[16,2048]{1,0:T(8,128)(2,1)S(1)} collective-permute-done((bf16[16,2048]{1,0:T(8,128)(2,1)S(1)}, bf16[16,2048]{1,0:T(8,128)(2,1)S(1)}, u32[]{:S(2)}, u32[]{:S(2)}) %collective-permute-start.16) | collective-permute-done | bytes 65568 | tf_op jit(solution)/shard_map/ppermute | solution.py:651
  90.8 0.4 collective-permute-done.17
  91.2 0.0 collective-permute-done.18
  91.2 1.6 %collective-permute-done.19 = bf16[16,2048]{1,0:T(8,128)(2,1)S(1)} collective-permute-done((bf16[16,2048]{1,0:T(8,128)(2,1)S(1)}, bf16[16,2048]{1,0:T(8,128)(2,1)S(1)}, u32[]{:S(2)}, u32[]{:S(2)}) %collective-permute-start.19) | collective-permute-done | bytes 65568 | tf_op jit(solution)/shard_map/ppermute | solution.py:651
  92.7 0.0 collective-permute-done.20
  92.7 0.7 add_convert_fusion
  (6 shorter events, 0.1 us)
Async XLA Ops:
  1.0 12.5 %collective-permute-start.2 = (bf16[32,2048]{1,0:T(8,128)(2,1)S(1)}, bf16[32,2048]{1,0:T(8,128)(2,1)S(1)}, u32[]{:S(2)}, u32[]{:S(2)}) collective-permute-start(bf16[32,2048]{1,0:T(8,128)(2,1)S(1)} %get-tuple-element.70.refs_0_), channel_id=1, source_target_pairs={{0,24},{8,16},{16,8},{24,0},{1,25},{9,17},{17,9},{25,1},{2,26},{10... | collective-permute-start | bytes 393224 | tf_op jit(solution)/shard_map/ppermute | solution.py:41
  6.1 11.1 %collective-permute-start.1 = (bf16[32,2048]{1,0:T(8,128)(2,1)S(1)}, bf16[32,2048]{1,0:T(8,128)(2,1)S(1)}, u32[]{:S(2)}, u32[]{:S(2)}) collective-permute-start(bf16[32,2048]{1,0:T(8,128)(2,1)S(1)} %get-tuple-element.70.refs_0_), channel_id=1, source_target_pairs={{0,16},{8,24},{16,0},{24,8},{1,17},{9,25},{17,1},{25,9},{2,18},{10... | collective-permute-start | bytes 393224 | tf_op jit(solution)/shard_map/ppermute | solution.py:41
  6.1 11.1 %collective-permute-start = (bf16[32,2048]{1,0:T(8,128)(2,1)S(1)}, bf16[32,2048]{1,0:T(8,128)(2,1)S(1)}, u32[]{:S(2)}, u32[]{:S(2)}) collective-permute-start(bf16[32,2048]{1,0:T(8,128)(2,1)S(1)} %get-tuple-element.70.refs_0_), channel_id=1, source_target_pairs={{0,8},{8,0},{16,24},{24,16},{1,9},{9,1},{17,25},{25,17},{2,10},{10... | collective-permute-start | bytes 393224 | tf_op jit(solution)/shard_map/ppermute | solution.py:41
  7.5 5.9 %collective-permute-start.4 = (bf16[16,128]{1,0:T(8,128)(2,1)S(1)}, bf16[16,128]{1,0:T(8,128)(2,1)S(1)}, u32[]{:S(2)}, u32[]{:S(2)}) collective-permute-start(bf16[16,128]{1,0:T(8,128)(2,1)S(1)} %pad.14), channel_id=1, source_target_pairs={{0,4},{4,0},{1,5},{5,1},{2,6},{6,2},{3,7},{7,3},{8,12},{12,8},{9,1... | collective-permute-start | bytes 12296 | tf_op jit(solution)/shard_map/ppermute | solution.py:27
  19.3 6.1 %collective-permute-start.3 = (f32[160,128]{1,0:T(8,128)S(1)}, f32[160,128]{1,0:T(8,128)S(1)}, u32[]{:S(2)}, u32[]{:S(2)}) collective-permute-start(f32[160,128]{1,0:T(8,128)S(1)} %get-tuple-element.41.own), channel_id=1, source_target_pairs={{0,4},{4,0},{1,5},{5,1},{2,6},{6,2},{3,7},{7,3},{8,12},{12,8},{9,1... | collective-permute-start | bytes 245768 | tf_op jit(solution)/shard_map/ppermute | solution.py:27
  21.0 11.1 %collective-permute-start.5 = (bf16[32,2432]{1,0:T(8,128)(2,1)S(1)}, bf16[32,2432]{1,0:T(8,128)(2,1)S(1)}, u32[]{:S(2)}, u32[]{:S(2)}) collective-permute-start(bf16[32,2432]{1,0:T(8,128)(2,1)S(1)} %get-tuple-element.43), channel_id=1, source_target_pairs={{0,8},{8,0},{16,24},{24,16},{1,9},{9,1},{17,25},{25,17},{2,10},{10... | collective-permute-start | bytes 466952 | tf_op jit(solution)/shard_map/ppermute | solution.py:41
  21.0 14.0 %collective-permute-start.6 = (bf16[32,2432]{1,0:T(8,128)(2,1)S(1)}, bf16[32,2432]{1,0:T(8,128)(2,1)S(1)}, u32[]{:S(2)}, u32[]{:S(2)}) collective-permute-start(bf16[32,2432]{1,0:T(8,128)(2,1)S(1)} %get-tuple-element.44), channel_id=1, source_target_pairs={{0,16},{8,24},{16,0},{24,8},{1,17},{9,25},{17,1},{25,9},{2,18},{10... | collective-permute-start | bytes 466952 | tf_op jit(solution)/shard_map/ppermute | solution.py:41
  24.1 11.0 %collective-permute-start.7 = (bf16[32,2432]{1,0:T(8,128)(2,1)S(1)}, bf16[32,2432]{1,0:T(8,128)(2,1)S(1)}, u32[]{:S(2)}, u32[]{:S(2)}) collective-permute-start(bf16[32,2432]{1,0:T(8,128)(2,1)S(1)} %get-tuple-element.45), channel_id=1, source_target_pairs={{0,24},{8,16},{16,8},{24,0},{1,25},{9,17},{17,9},{25,1},{2,26},{10... | collective-permute-start | bytes 466952 | tf_op jit(solution)/shard_map/ppermute | solution.py:41
  37.7 6.4 %collective-permute-start.8 = (bf16[128,512]{1,0:T(8,128)(2,1)S(1)}, bf16[128,512]{1,0:T(8,128)(2,1)S(1)}, u32[]{:S(2)}, u32[]{:S(2)}) collective-permute-start(bf16[128,512]{1,0:T(8,128)(2,1)S(1)} %get-tuple-element.51.base), channel_id=1, source_target_pairs={{0,4},{4,0},{1,5},{5,1},{2,6},{6,2},{3,7},{7,3},{8,12},{12,8},{9,1... | collective-permute-start | bytes 393224 | tf_op jit(solution)/shard_map/ppermute | solution.py:27
  44.1 8.2 %collective-permute-start.11 = (bf16[128,512]{1,0:T(8,128)(2,1)S(1)}, bf16[128,512]{1,0:T(8,128)(2,1)S(1)}, u32[]{:S(2)}, u32[]{:S(2)}) collective-permute-start(bf16[128,512]{1,0:T(8,128)(2,1)S(1)} %mix.1.refs_0_), channel_id=1, source_target_pairs={{0,24},{8,16},{16,8},{24,0},{1,25},{9,17},{17,9},{25,1},{2,26},{10... | collective-permute-start | bytes 393224 | tf_op jit(solution)/shard_map/ppermute | solution.py:41
  46.6 10.1 %collective-permute-start.10 = (bf16[128,512]{1,0:T(8,128)(2,1)S(1)}, bf16[128,512]{1,0:T(8,128)(2,1)S(1)}, u32[]{:S(2)}, u32[]{:S(2)}) collective-permute-start(bf16[128,512]{1,0:T(8,128)(2,1)S(1)} %mix.1.refs_0_), channel_id=1, source_target_pairs={{0,16},{8,24},{16,0},{24,8},{1,17},{9,25},{17,1},{25,9},{2,18},{10... | collective-permute-start | bytes 393224 | tf_op jit(solution)/shard_map/ppermute | solution.py:41
  48.0 8.8 %collective-permute-start.9 = (bf16[128,512]{1,0:T(8,128)(2,1)S(1)}, bf16[128,512]{1,0:T(8,128)(2,1)S(1)}, u32[]{:S(2)}, u32[]{:S(2)}) collective-permute-start(bf16[128,512]{1,0:T(8,128)(2,1)S(1)} %mix.1.refs_0_), channel_id=1, source_target_pairs={{0,8},{8,0},{16,24},{24,16},{1,9},{9,1},{17,25},{25,17},{2,10},{10... | collective-permute-start | bytes 393224 | tf_op jit(solution)/shard_map/ppermute | solution.py:41
  58.6 2.0 %collective-permute-start.12 = (bf16[128,2048]{1,0:T(8,128)(2,1)S(1)}, bf16[128,2048]{1,0:T(8,128)(2,1)S(1)}, u32[]{:S(2)}, u32[]{:S(2)}) collective-permute-start(bf16[128,2048]{1,0:T(8,128)(2,1)S(1)} %get-tuple-element.55.own), channel_id=1, source_target_pairs={{0,1},{1,0},{2,3},{3,2},{4,5},{5,4},{6,7},{7,6},{8,9},{9,8},{10,11... | collective-permute-start | bytes 1572872 | tf_op jit(solution)/shard_map/ppermute | solution.py:67
  75.4 2.0 %collective-permute-start.13 = (bf16[128,2048]{1,0:T(8,128)(2,1)S(1)}, bf16[128,2048]{1,0:T(8,128)(2,1)S(1)}, u32[]{:S(2)}, u32[]{:S(2)}) collective-permute-start(bf16[128,2048]{1,0:T(8,128)(2,1)S(1)} %get-tuple-element.59), channel_id=1, source_target_pairs={{0,1},{1,0},{2,3},{3,2},{4,5},{5,4},{6,7},{7,6},{8,9},{9,8},{10,11... | collective-permute-start | bytes 1572872 | tf_op jit(solution)/shard_map/ppermute | solution.py:67
  78.1 7.8 %collective-permute-start.14 = (bf16[16,2048]{1,0:T(8,128)(2,1)S(1)}, bf16[16,2048]{1,0:T(8,128)(2,1)S(1)}, u32[]{:S(2)}, u32[]{:S(2)}) collective-permute-start(bf16[16,2048]{1,0:T(8,128)(2,1)S(1)} %get-tuple-element.62), channel_id=1, source_target_pairs={{0,4},{4,8},{8,12},{12,16},{16,20},{20,24},{24,28},{28,0},{1,5},{5... | collective-permute-start | bytes 196616 | tf_op jit(solution)/shard_map/ppermute | solution.py:651
  79.7 7.7 %collective-permute-start.15 = (bf16[16,2048]{1,0:T(8,128)(2,1)S(1)}, bf16[16,2048]{1,0:T(8,128)(2,1)S(1)}, u32[]{:S(2)}, u32[]{:S(2)}) collective-permute-start(bf16[16,2048]{1,0:T(8,128)(2,1)S(1)} %get-tuple-element.63), channel_id=1, source_target_pairs={{0,8},{4,12},{8,16},{12,20},{16,24},{20,28},{24,0},{28,4},{1,9},{5... | collective-permute-start | bytes 196616 | tf_op jit(solution)/shard_map/ppermute | solution.py:651
  79.7 11.1 %collective-permute-start.16 = (bf16[16,2048]{1,0:T(8,128)(2,1)S(1)}, bf16[16,2048]{1,0:T(8,128)(2,1)S(1)}, u32[]{:S(2)}, u32[]{:S(2)}) collective-permute-start(bf16[16,2048]{1,0:T(8,128)(2,1)S(1)} %get-tuple-element.64), channel_id=1, source_target_pairs={{0,12},{4,16},{8,20},{12,24},{16,28},{20,0},{24,4},{28,8},{1,13},{... | collective-permute-start | bytes 196616 | tf_op jit(solution)/shard_map/ppermute | solution.py:651
  82.0 9.1 %collective-permute-start.17 = (bf16[16,2048]{1,0:T(8,128)(2,1)S(1)}, bf16[16,2048]{1,0:T(8,128)(2,1)S(1)}, u32[]{:S(2)}, u32[]{:S(2)}) collective-permute-start(bf16[16,2048]{1,0:T(8,128)(2,1)S(1)} %get-tuple-element.65), channel_id=1, source_target_pairs={{0,16},{4,20},{8,24},{12,28},{16,0},{20,4},{24,8},{28,12},{1,17},{... | collective-permute-start | bytes 196616 | tf_op jit(solution)/shard_map/ppermute | solution.py:651
  83.6 7.6 %collective-permute-start.18 = (bf16[16,2048]{1,0:T(8,128)(2,1)S(1)}, bf16[16,2048]{1,0:T(8,128)(2,1)S(1)}, u32[]{:S(2)}, u32[]{:S(2)}) collective-permute-start(bf16[16,2048]{1,0:T(8,128)(2,1)S(1)} %get-tuple-element.66), channel_id=1, source_target_pairs={{0,20},{4,24},{8,28},{12,0},{16,4},{20,8},{24,12},{28,16},{1,21},{... | collective-permute-start | bytes 196616 | tf_op jit(solution)/shard_map/ppermute | solution.py:651
  85.9 6.8 %collective-permute-start.19 = (bf16[16,2048]{1,0:T(8,128)(2,1)S(1)}, bf16[16,2048]{1,0:T(8,128)(2,1)S(1)}, u32[]{:S(2)}, u32[]{:S(2)}) collective-permute-start(bf16[16,2048]{1,0:T(8,128)(2,1)S(1)} %get-tuple-element.67), channel_id=1, source_target_pairs={{0,24},{4,28},{8,0},{12,4},{16,8},{20,12},{24,16},{28,20},{1,25},{... | collective-permute-start | bytes 196616 | tf_op jit(solution)/shard_map/ppermute | solution.py:651
  87.4 5.4 %collective-permute-start.20 = (bf16[16,2048]{1,0:T(8,128)(2,1)S(1)}, bf16[16,2048]{1,0:T(8,128)(2,1)S(1)}, u32[]{:S(2)}, u32[]{:S(2)}) collective-permute-start(bf16[16,2048]{1,0:T(8,128)(2,1)S(1)} %get-tuple-element.68), channel_id=1, source_target_pairs={{0,28},{4,0},{8,4},{12,8},{16,12},{20,16},{24,20},{28,24},{1,29},{... | collective-permute-start | bytes 196616 | tf_op jit(solution)/shard_map/ppermute | solution.py:651

commit v9 on v8

--- a/solution.py
+++ b/solution.py
@@ -538,24 +538,100 @@
     )(tokens, gate, up, down)
 
 
-def combine_kernel(targets, own, other, weight, *outs):
+def one_hot(*conditions):
+    found = conditions[0]
+    for condition in conditions[1:]:
+        found = found & condition
+    return found.astype(F32).astype(BF16)
+
+
+def combine_kernel(targets, spots, own, other, weight, routes, *refs):
+    outs, packed = refs[:-1], refs[-1]
     rows = outs[0].shape[0]
+    tokens, width = own.shape
+    half, eighth = width // 2, width // 8
+    mine = spots[0].astype(F32)
+    across = jnp.transpose(routes[...].astype(F32))
+    named = (across[0:1, :] == mine) | (across[1:2, :] == mine)
+    q = lax.broadcasted_iota(jnp.int32, (tokens, tokens), 0)
+    t = lax.broadcasted_iota(jnp.int32, (tokens, tokens), 1)
+    same = (q // rows) == (t // rows)
+    counts = jnp.broadcast_to(named.astype(F32), (16, tokens)).astype(BF16)
+    place = jnp.dot(counts, one_hot(same, q <= t), preferred_element_type=F32)[0:1, :] - 1.0
+    named = jnp.broadcast_to(named.astype(F32), (tokens, tokens)) > 0.5
+    place = jnp.broadcast_to(place, (tokens, tokens)).astype(jnp.int32)
+    r = q % rows
+    value = ((own[...] + other[...].astype(F32)) * weight[:, 0:1]).astype(BF16)
+    low = one_hot(named, same, r < 8, place == r)
+    high = one_hot(named, same, r >= 8, place == r - 8)
+    packed[:, :half] = (
+        jnp.dot(low, value[:, :half], preferred_element_type=F32)
+        + jnp.dot(high, value[:, half:], preferred_element_type=F32)
+    ).astype(BF16)
+    late = jnp.zeros((tokens, eighth), F32)
+    for j in range(8):
+        pick = one_hot(named, same, r // 2 == j, place == 8 + r % 2)
+        late = late + jnp.dot(pick, value[:, j * eighth : (j + 1) * eighth], preferred_element_type=F32)
+    packed[:, half:] = late.astype(BF16)
     for index, out in enumerate(outs):
-        here = pl.ds(pl.multiple_of(targets[index] * rows, 16), rows)
-        out[...] = ((own[here, :] + other[here, :].astype(F32)) * weight[here, 0:1]).astype(BF16)
-
-
-def combine(targets, own, other, weight, rows):
-    width = own.shape[1]
-    sends = own.shape[0] // rows
+        out[...] = packed[pl.ds(pl.multiple_of(targets[index] * rows, 16), rows), :]
+
+
+def combine(targets, spots, own, other, weight, routes, rows):
+    tokens, width = own.shape
+    sends = tokens // rows
+    lanes = width // 2 + width // 8
     return pl.pallas_call(
         combine_kernel,
-        out_shape=tuple([jax.ShapeDtypeStruct((rows, width), BF16)] * sends),
-        in_specs=[SCALARS] + [WHOLE] * 3,
+        out_shape=tuple([jax.ShapeDtypeStruct((rows, lanes), BF16)] * sends),
+        in_specs=[SCALARS] * 2 + [WHOLE] * 4,
         out_specs=(WHOLE,) * sends,
-        compiler_params=pltpu.CompilerParams(vmem_limit_bytes=8 << 20),
+        scratch_shapes=[VMEM((tokens, lanes), BF16)],
+        compiler_params=pltpu.CompilerParams(vmem_limit_bytes=10 << 20),
         name="combine",
-    )(targets, own, other, weight)
+    )(targets, spots, own, other, weight, routes)
+
+
+def unpack_kernel(named_by, mixed, routes, *refs):
+    count = len(refs) - 2
+    pieces, out, packed = refs[:count], refs[count], refs[count + 1]
+    rows, width = mixed.shape
+    half, eighth = width // 2, width // 8
+    for index in range(count):
+        packed[index * rows : (index + 1) * rows, :] = pieces[index][...]
+    shape = (rows, count * rows)
+    lane = lax.broadcasted_iota(jnp.int32, shape, 1)
+    r = lane % rows
+    expert = jnp.zeros(shape, F32)
+    for index in range(count):
+        expert = jnp.where(lane // rows == index, named_by[index].astype(F32), expert)
+    named = (routes[:, 0:1].astype(F32) == expert) | (routes[:, 1:2].astype(F32) == expert)
+    above = lax.broadcasted_iota(jnp.int32, (rows, rows), 0) >= lax.broadcasted_iota(jnp.int32, (rows, rows), 1)
+    place = jnp.dot(one_hot(above), one_hot(named), preferred_element_type=F32) - 1.0
+    place = place.astype(jnp.int32)
+    low = one_hot(named, r < 8, place == r)
+    high = one_hot(named, r >= 8, place == r - 8)
+    for j in range(8):
+        pick = one_hot(named, r // 2 == j, place == 8 + r % 2)
+        here = slice(j * eighth, (j + 1) * eighth)
+        there = slice((j % 4) * eighth, (j % 4 + 1) * eighth)
+        total = mixed[:, here].astype(F32)
+        total += jnp.dot(low if j < 4 else high, packed[:, there], preferred_element_type=F32)
+        total += jnp.dot(pick, packed[:, half:], preferred_element_type=F32)
+        out[:, here] = total.astype(BF16)
+
+
+def unpack(named_by, mixed, routes, pieces):
+    rows, width = mixed.shape
+    return pl.pallas_call(
+        unpack_kernel,
+        out_shape=jax.ShapeDtypeStruct((rows, width), BF16),
+        in_specs=[SCALARS] + [WHOLE] * (2 + len(pieces)),
+        out_specs=WHOLE,
+        scratch_shapes=[VMEM((rows * len(pieces), pieces[0].shape[1]), BF16)],
+        compiler_params=pltpu.CompilerParams(vmem_limit_bytes=6 << 20),
+        name="unpack",
+    )(named_by, mixed, routes, *pieces)
 
 
 def body(
@@ -589,9 +665,11 @@
     me = ctx_at * exp + exp_at
     spots = jnp.stack([ctx_at // (ctx // EXPERTS), me]).astype(jnp.int32)
     targets = jnp.stack([(me + s) % parts for s in range(parts)]).astype(jnp.int32)
+    named_by = jnp.stack([(me - s) % parts for s in range(parts)]) // exp // (ctx // EXPERTS)
 
     x_pieces = spread(lambda k: x_input, "ctx", 0)
-    extra = jnp.pad(routes.astype(BF16), ((0, 0), (0, LANES - 2)))
+    own_routes = jnp.pad(routes.astype(BF16), ((0, 0), (0, LANES - 2)))
+    extra = own_routes
     if exp == 2:
         other = rotate(extra, "exp", 1)
         extra = jnp.where(
@@ -608,8 +686,8 @@
     )
     router_rows = jnp.pad(router.T, ((0, 16 - EXPERTS), (0, 0)))
     gain = jnp.pad(norm_gain[None, :], ((0, 7), (0, 0)))
-    params, router_rows, gain, spots, targets = lax.optimization_barrier(
-        (params, router_rows, gain, spots, targets)
+    params, router_rows, gain, spots, targets, named_by = lax.optimization_barrier(
+        (params, router_rows, gain, spots, targets, named_by.astype(jnp.int32))
     )
 
     active, proj = activate(places, x_pieces, params, taps, select_weight)
@@ -628,7 +706,7 @@
     value = scan(own_proj, other_proj, active, params, taps, log_rate, step_weight, carried_state)
     spread_places = jnp.concatenate([places, exp_at.astype(jnp.int32)[None]])
     sent, all_routes = project(spread_places, value, output_weight, z_pieces, splits)
-    shared = exp == 2 and parts <= 8 and sent.shape[0] == LANES and lax.axis_size("doc") % 2 == 0
+    shared = exp == 2 and parts <= 8 and own == 16 and sent.shape[0] == LANES and lax.axis_size("doc") % 2 == 0
     half = lax.rem(lax.axis_index("doc"), 2).astype(jnp.int32)[None]
     if exp == 2:
         summand = rotate(sent, "exp", 1)
@@ -645,12 +723,11 @@
     axes = ("ctx", "exp")
     if shared:
         kept, given = shared_experts(half, normed, swap(normed), gate_first, up_first, gate_weight, up_weight, down_weight)
-        outs = combine(targets, kept, swap(given), weight, own)
+        outs = combine(targets, spots, kept, swap(given), weight, all_routes, own)
         arrived = [outs[0]]
         for s in range(1, parts):
             arrived.append(lax.ppermute(outs[s], axes, [(i, (i + s) % parts) for i in range(parts)]))
-        for piece in arrived:
-            total = total + piece.astype(F32)
+        return unpack(named_by, mine, own_routes, arrived)
     else:
         kept = experts(normed, gate_weight, up_weight, down_weight)
         partial = (kept * weight[:, :1]).astype(BF16)

time: 94.1 us -> 93.9 us (level)
  Pallas kernels: 34.7 us -> 36.7 us
  waiting for transfers between devices: 23.3 us -> 21.9 us
    pallas_call x0 -> x1, Pallas kernels: none -> 1.6 us  [unpack(): pl.pallas_call(unpack_kernel, out_shape=jax.ShapeDtypeStruct((rows, width...]
    ppermute x7, waiting for transfers between devices: 4.81 us -> 3.44 us  [body(): lax.ppermute(outs[s], axes, [(i, (i + s) % parts) for i in range(parts)])]
  transfers between devices with their start and end apart: 21 -> 21, of which waited for: 9 -> 10; matrix products, arithmetic and copies ran while one was open for 5% -> 5% of each run, Pallas kernels for 13% -> 13%
where the time goes in v9:
time: 93.9 us; the launch traced here: 93.4 us
  Pallas kernels  36.7 us (39%)
  starting transfers between devices  28.5 us (30%)
  waiting for transfers between devices  21.9 us (23%)
  local copies, waits for them, and re-layouts  5.2 us (6%)
    pallas_call x1, Pallas kernels, shared_experts(): pl.pallas_call(shared_kernel, out_shape=(jax.ShapeDtypeStruct((rows, widt...  14.8 us
    ppermute x9, waiting for transfers between devices, exchange(): lax.ppermute(value, axis, [(i, partner(i, step, count)) for i in range(co...  14.7 us
    ppermute x9, starting transfers between devices, exchange(): lax.ppermute(value, axis, [(i, partner(i, step, count)) for i in range(co...  14.7 us
    ppermute x7, starting transfers between devices, body(): lax.ppermute(outs[s], axes, [(i, (i + s) % parts) for i in range(parts)])  9.8 us
    pallas_call x1, Pallas kernels, scan(): pl.pallas_call(functools.partial(scan_kernel, taps), out_shape=jax.ShapeD...  6.66 us
    pallas_call x1, Pallas kernels, fetch(): pl.pallas_call(functools.partial(fetch_kernel, parts, half_rows), out_sha...  5.82 us
    ppermute x3, starting transfers between devices, rotate(): lax.ppermute(value, axis, [(i, (i + steps) % count) for i in range(count)])  3.82 us
    ppermute x2, waiting for transfers between devices, swap(): lax.ppermute(value, 'doc', [(i, i + 1 - 2 * (i % 2)) for i in range(count)])  3.67 us
  transfers between devices with their start and end apart: 21, of which 10 were waited for; matrix products, arithmetic and copies ran while one was open for 5% of the time, Pallas kernels for 13%

profile of v9, /device:TPU:0, one launch (start us, length us, event | category | flops | bytes accessed | tf_op | source)
XLA Modules:
  0.0 93.4 jit_solution(4720775736544044108)
XLA Ops:
  0.0 1.0 %slice_bitcast_fusion = (bf16[32,2048]{1,0:T(8,128)(2,1)S(1)}, bf16[32,2048]{1,0:T(8,128)(2,1)S(1)}) fusion(bf16[2,32,2048]{2,1,0:T(8,128)(2,1)} %param.18), kind=kLoop, calls=%fused_computation.4 | loop fusion | bytes 524288 | tf_op jit(solution)/shard_map/squeeze | solution.py:660
  1.0 5.1 %collective-permute-start.2 = (bf16[32,2048]{1,0:T(8,128)(2,1)S(1)}, bf16[32,2048]{1,0:T(8,128)(2,1)S(1)}, u32[]{:S(2)}, u32[]{:S(2)}) collective-permute-start(bf16[32,2048]{1,0:T(8,128)(2,1)S(1)} %get-tuple-element.72.refs_0_), channel_id=1, source_target_pairs={{0,24},{8,16},{16,8},{24,0},{1,25},{9,17},{17,9},{25,1},{2,26},{10... | collective-permute-start | bytes 393224 | tf_op jit(solution)/shard_map/ppermute | solution.py:41
  6.1 0.0 collective-permute-start.1
  6.1 0.6 collective-permute-start
  6.7 0.7 convert_element_type.13
  7.4 0.1 copy.20
  7.5 1.7 %collective-permute-start.4 = (bf16[16,128]{1,0:T(8,128)(2,1)S(1)}, bf16[16,128]{1,0:T(8,128)(2,1)S(1)}, u32[]{:S(2)}, u32[]{:S(2)}) collective-permute-start(bf16[16,128]{1,0:T(8,128)(2,1)S(1)} %pad.14.routes), channel_id=1, source_target_pairs={{0,4},{4,0},{1,5},{5,1},{2,6},{6,2},{3,7},{7,3},{8,12},{12,8},{9,1... | collective-permute-start | bytes 12296 | tf_op jit(solution)/shard_map/ppermute | solution.py:27
  9.2 0.1 stack.93
  9.3 0.1 pad_add_fusion.spots
  9.4 0.8 constant_dynamic-slice_fusion
  10.2 0.1 pad_add_fusion.1.places
  10.3 0.1 concatenate.38.places
  10.4 0.7 pad.12.router
  11.2 0.7 pad.13.gain
  11.9 0.1 stack.85.targets
  12.0 1.6 %concatenate.37.params = f32[16,2048]{1,0:T(8,128)S(1)} concatenate(f32[4,2048]{1,0:T(4,128)} %param.21, f32[1,2048]{1,0:T(1,128)} %bitcast.33, f32[1,2048]{1,0:T(1,128)} %bitcast.34, f32[1,2048]{1,0:T(1,128)} %bitcast.35, f32[1,2048]{1,0:T(1,128)S(1)} %slice.33, f32[5,2048]{1,0:T(8,128)S(1)} %broadcast_in_dim.24, bf16[3,2048]{1,0:T(4,128)(2,1)} %param.19), dimensions={0} | concatenate | bytes 249856 | tf_op jit(solution)/shard_map/concatenate | solution.py:683
  13.6 0.0 collective-permute-done.4
  13.6 0.0 collective-permute-done.2.refs_3_
  13.6 3.6 %collective-permute-done.1.refs_2_ = bf16[32,2048]{1,0:T(8,128)(2,1)S(1)} collective-permute-done((bf16[32,2048]{1,0:T(8,128)(2,1)S(1)}, bf16[32,2048]{1,0:T(8,128)(2,1)S(1)}, u32[]{:S(2)}, u32[]{:S(2)}) %collective-permute-start.1) | collective-permute-done | bytes 131104 | tf_op jit(solution)/shard_map/ppermute | solution.py:41
  17.2 0.0 collective-permute-done.refs_1_
  17.2 2.1 %activate.1 = (bf16[128,2048]{1,0:T(8,128)(2,1)S(1)}, f32[160,128]{1,0:T(8,128)S(1)}) custom-call(s32[4]{0:T(128)S(1)} %pad_add_fusion.1.places, f32[16,2048]{1,0:T(8,128)S(1)} %concatenate.37.params, bf16[160,2048]{1,0:T(8,128)(2,1)} %select.44, bf16[32,2048]{1,0:T(8,128)(2,1)S(1)} %get-tuple-element.72.refs_0_, ...), custom_call_target="tpu_custom_call" | custom-call | flops 83886080 | bytes 1048576 | tf_op jit(solution)/shard_map/activate/pallas_call | solution.py:120
  19.3 1.6 %collective-permute-start.3 = (f32[160,128]{1,0:T(8,128)S(1)}, f32[160,128]{1,0:T(8,128)S(1)}, u32[]{:S(2)}, u32[]{:S(2)}) collective-permute-start(f32[160,128]{1,0:T(8,128)S(1)} %get-tuple-element.43.own), channel_id=1, source_target_pairs={{0,4},{4,0},{1,5},{5,1},{2,6},{6,2},{3,7},{7,3},{8,12},{12,8},{9,1... | collective-permute-start | bytes 245768 | tf_op jit(solution)/shard_map/ppermute | solution.py:27
  21.0 0.1 collective-permute-start.5
  21.0 3.0 %collective-permute-start.6 = (bf16[32,2432]{1,0:T(8,128)(2,1)S(1)}, bf16[32,2432]{1,0:T(8,128)(2,1)S(1)}, u32[]{:S(2)}, u32[]{:S(2)}) collective-permute-start(bf16[32,2432]{1,0:T(8,128)(2,1)S(1)} %get-tuple-element.46), channel_id=1, source_target_pairs={{0,16},{8,24},{16,0},{24,8},{1,17},{9,25},{17,1},{25,9},{2,18},{10... | collective-permute-start | bytes 466952 | tf_op jit(solution)/shard_map/ppermute | solution.py:41
  24.1 1.3 %collective-permute-start.7 = (bf16[32,2432]{1,0:T(8,128)(2,1)S(1)}, bf16[32,2432]{1,0:T(8,128)(2,1)S(1)}, u32[]{:S(2)}, u32[]{:S(2)}) collective-permute-start(bf16[32,2432]{1,0:T(8,128)(2,1)S(1)} %get-tuple-element.47), channel_id=1, source_target_pairs={{0,24},{8,16},{16,8},{24,0},{1,25},{9,17},{17,9},{25,1},{2,26},{10... | collective-permute-start | bytes 466952 | tf_op jit(solution)/shard_map/ppermute | solution.py:41
  25.4 0.0 collective-permute-done.3.other
  25.4 6.7 %scan.1.value_in = f32[128,2048]{1,0:T(8,128)S(1)} custom-call(f32[160,128]{1,0:T(8,128)S(1)} %get-tuple-element.43.own, f32[160,128]{1,0:T(8,128)S(1)} %collective-permute-done.3.other, bf16[128,2048]{1,0:T(8,128)(2,1)S(1)} %get-tuple-element.44.active, f32[16,2048]{1,0:T(8,128)S(1)} %concatenate.37.params, f32[16,2048]{1,0:T(8,128)} %log_rate_hbm.1, ...), custom_call_target="tpu_custom_call" | custom-call | flops 12582912000 | bytes 2097152 | tf_op jit(solution)/shard_map/scan/pallas_call | solution.py:242
  32.1 0.0 collective-permute-done.5.refs_1_
  32.1 2.9 %collective-permute-done.6.refs_2_ = bf16[32,2432]{1,0:T(8,128)(2,1)S(1)} collective-permute-done((bf16[32,2432]{1,0:T(8,128)(2,1)S(1)}, bf16[32,2432]{1,0:T(8,128)(2,1)S(1)}, u32[]{:S(2)}, u32[]{:S(2)}) %collective-permute-start.6) | collective-permute-done | bytes 155680 | tf_op jit(solution)/shard_map/ppermute | solution.py:41
  35.0 0.0 collective-permute-done.7.refs_3_
  35.0 2.6 %project.1 = (bf16[128,512]{1,0:T(8,128)(2,1)S(1)}, bf16[128,128]{1,0:T(8,128)(2,1)S(1)}) custom-call(s32[5]{0:T(128)S(1)} %concatenate.38.places, f32[128,2048]{1,0:T(8,128)S(1)} %scan.1.value_in, bf16[2048,512]{1,0:T(8,128)(2,1)} %weight_hbm.1, bf16[32,2432]{1,0:T(8,128)(2,1)S(1)} %get-tuple-element.76.refs_0_, ...), custom_call_target="tpu_custom_call" | custom-call | flops 268435456 | bytes 2097152 | tf_op jit(solution)/shard_map/project/pallas_call | solution.py:310
  37.7 0.6 collective-permute-start.8
  38.2 5.8 %fetch.1 = (bf16[1792,2048]{1,0:T(8,128)(2,1)S(1)}, bf16[1792,2048]{1,0:T(8,128)(2,1)S(1)}, s32[1]{0:T(128)}) custom-call(s32[1]{0:T(128)} %bitcast.28.half, bf16[7168,2048]{1,0:T(8,128)(2,1)} %gate.1, bf16[7168,2048]{1,0:T(8,128)(2,1)} %up.1), custom_call_target="tpu_custom_call" | custom-call | bytes 29360128 | tf_op jit(solution)/shard_map/fetch/pallas_call | solution.py:431
  44.1 0.0 collective-permute-done.8.summand
  44.1 2.5 %collective-permute-start.11 = (bf16[128,512]{1,0:T(8,128)(2,1)S(1)}, bf16[128,512]{1,0:T(8,128)(2,1)S(1)}, u32[]{:S(2)}, u32[]{:S(2)}) collective-permute-start(bf16[128,512]{1,0:T(8,128)(2,1)S(1)} %mix.1.refs_0_), channel_id=1, source_target_pairs={{0,24},{8,16},{16,8},{24,0},{1,25},{9,17},{17,9},{25,1},{2,26},{10... | collective-permute-start | bytes 393224 | tf_op jit(solution)/shard_map/ppermute | solution.py:41
  46.6 1.4 %collective-permute-start.10 = (bf16[128,512]{1,0:T(8,128)(2,1)S(1)}, bf16[128,512]{1,0:T(8,128)(2,1)S(1)}, u32[]{:S(2)}, u32[]{:S(2)}) collective-permute-start(bf16[128,512]{1,0:T(8,128)(2,1)S(1)} %mix.1.refs_0_), channel_id=1, source_target_pairs={{0,16},{8,24},{16,0},{24,8},{1,17},{9,25},{17,1},{25,9},{2,18},{10... | collective-permute-start | bytes 393224 | tf_op jit(solution)/shard_map/ppermute | solution.py:41
  48.0 0.5 collective-permute-start.9
  48.6 3.8 %collective-permute-done.11.refs_3_ = bf16[128,512]{1,0:T(8,128)(2,1)S(1)} collective-permute-done((bf16[128,512]{1,0:T(8,128)(2,1)S(1)}, bf16[128,512]{1,0:T(8,128)(2,1)S(1)}, u32[]{:S(2)}, u32[]{:S(2)}) %collective-permute-start.11) | collective-permute-done | bytes 131104 | tf_op jit(solution)/shard_map/ppermute | solution.py:41
  52.3 4.4 %collective-permute-done.10.refs_2_ = bf16[128,512]{1,0:T(8,128)(2,1)S(1)} collective-permute-done((bf16[128,512]{1,0:T(8,128)(2,1)S(1)}, bf16[128,512]{1,0:T(8,128)(2,1)S(1)}, u32[]{:S(2)}, u32[]{:S(2)}) %collective-permute-start.10) | collective-permute-done | bytes 131104 | tf_op jit(solution)/shard_map/ppermute | solution.py:41
  56.8 0.0 collective-permute-done.9.refs_1_
  56.8 1.8 %norm.1 = (bf16[128,2048]{1,0:T(8,128)(2,1)S(1)}, f32[128,128]{1,0:T(8,128)S(1)}, bf16[16,2048]{1,0:T(8,128)(2,1)S(1)}) custom-call(s32[4]{0:T(128)S(1)} %pad_add_fusion.1.places, s32[2]{0:T(128)S(1)} %pad_add_fusion.spots, f32[8,2048]{1,0:T(8,128)S(1)} %pad.13.gain, bf16[16,2048]{1,0:T(8,128)(2,1)S(1)} %pad.12.router, ...), custom_call_target="tpu_custom_call" | custom-call | tf_op jit(solution)/shard_map/norm/pallas_call | solution.py:389
  58.6 0.1 collective-permute-start.12
  58.7 1.9 %collective-permute-done.12.other = bf16[128,2048]{1,0:T(8,128)(2,1)S(1)} collective-permute-done((bf16[128,2048]{1,0:T(8,128)(2,1)S(1)}, bf16[128,2048]{1,0:T(8,128)(2,1)S(1)}, u32[]{:S(2)}, u32[]{:S(2)}) %collective-permute-start.12) | collective-permute-done | bytes 524320 | tf_op jit(solution)/shard_map/ppermute | solution.py:67
  60.6 14.8 %experts.1 = (f32[128,2048]{1,0:T(8,128)S(1)}, bf16[128,2048]{1,0:T(8,128)(2,1)S(1)}) custom-call(s32[1]{0:T(128)} %get-tuple-element.56.half, bf16[128,2048]{1,0:T(8,128)(2,1)S(1)} %get-tuple-element.57.own, bf16[128,2048]{1,0:T(8,128)(2,1)S(1)} %collective-permute-done.12.other, bf16[1792,2048]{1,0:T(8,128)(2,1)S(1)} %get-tuple-element.58.gate_first, ...), custom_call_target="tpu_custom_call" | custom-call | flops 11274289152 | bytes 29360128 | tf_op jit(solution)/shard_map/experts/pallas_call | solution.py:483
  75.4 0.2 collective-permute-start.13
  75.6 1.8 %collective-permute-done.13.other = bf16[128,2048]{1,0:T(8,128)(2,1)S(1)} collective-permute-done((bf16[128,2048]{1,0:T(8,128)(2,1)S(1)}, bf16[128,2048]{1,0:T(8,128)(2,1)S(1)}, u32[]{:S(2)}, u32[]{:S(2)}) %collective-permute-start.13) | collective-permute-done | bytes 524320 | tf_op jit(solution)/shard_map/ppermute | solution.py:67
  77.4 1.2 %combine.1 = (bf16[16,1280]{1,0:T(8,128)(2,1)S(1)}, bf16[16,1280]{1,0:T(8,128)(2,1)S(1)}, bf16[16,1280]{1,0:T(8,128)(2,1)S(1)}, bf16[16,1280]{1,0:T(8,128)(2,1)S...) custom-call(s32[8]{0:T(128)S(1)} %stack.85.targets, ...), custom_call_target="tpu_custom_call" | custom-call | tf_op jit(solution)/shard_map/combine/pallas_call | solution.py:584
  78.6 1.6 %collective-permute-start.14 = (bf16[16,1280]{1,0:T(8,128)(2,1)S(1)}, bf16[16,1280]{1,0:T(8,128)(2,1)S(1)}, u32[]{:S(2)}, u32[]{:S(2)}) collective-permute-start(bf16[16,1280]{1,0:T(8,128)(2,1)S(1)} %get-tuple-element.64), channel_id=1, source_target_pairs={{0,4},{4,8},{8,12},{12,16},{16,20},{20,24},{24,28},{28,0},{1,5},{5... | collective-permute-start | bytes 122888 | tf_op jit(solution)/shard_map/ppermute | solution.py:729
  80.2 0.0 collective-permute-start.15
  80.2 2.3 %collective-permute-start.16 = (bf16[16,1280]{1,0:T(8,128)(2,1)S(1)}, bf16[16,1280]{1,0:T(8,128)(2,1)S(1)}, u32[]{:S(2)}, u32[]{:S(2)}) collective-permute-start(bf16[16,1280]{1,0:T(8,128)(2,1)S(1)} %get-tuple-element.66), channel_id=1, source_target_pairs={{0,12},{4,16},{8,20},{12,24},{16,28},{20,0},{24,4},{28,8},{1,13},{... | collective-permute-start | bytes 122888 | tf_op jit(solution)/shard_map/ppermute | solution.py:729
  82.5 1.6 %collective-permute-start.17 = (bf16[16,1280]{1,0:T(8,128)(2,1)S(1)}, bf16[16,1280]{1,0:T(8,128)(2,1)S(1)}, u32[]{:S(2)}, u32[]{:S(2)}) collective-permute-start(bf16[16,1280]{1,0:T(8,128)(2,1)S(1)} %get-tuple-element.67), channel_id=1, source_target_pairs={{0,16},{4,20},{8,24},{12,28},{16,0},{20,4},{24,8},{28,12},{1,17},{... | collective-permute-start | bytes 122888 | tf_op jit(solution)/shard_map/ppermute | solution.py:729
  84.1 2.3 %collective-permute-start.18 = (bf16[16,1280]{1,0:T(8,128)(2,1)S(1)}, bf16[16,1280]{1,0:T(8,128)(2,1)S(1)}, u32[]{:S(2)}, u32[]{:S(2)}) collective-permute-start(bf16[16,1280]{1,0:T(8,128)(2,1)S(1)} %get-tuple-element.68), channel_id=1, source_target_pairs={{0,20},{4,24},{8,28},{12,0},{16,4},{20,8},{24,12},{28,16},{1,21},{... | collective-permute-start | bytes 122888 | tf_op jit(solution)/shard_map/ppermute | solution.py:729
  86.4 0.0 collective-permute-done.14.refs_1_
  86.4 1.4 %collective-permute-start.19 = (bf16[16,1280]{1,0:T(8,128)(2,1)S(1)}, bf16[16,1280]{1,0:T(8,128)(2,1)S(1)}, u32[]{:S(2)}, u32[]{:S(2)}) collective-permute-start(bf16[16,1280]{1,0:T(8,128)(2,1)S(1)} %get-tuple-element.69), channel_id=1, source_target_pairs={{0,24},{4,28},{8,0},{12,4},{16,8},{20,12},{24,16},{28,20},{1,25},{... | collective-permute-start | bytes 122888 | tf_op jit(solution)/shard_map/ppermute | solution.py:729
  87.8 0.0 collective-permute-done.15.refs_2_
  87.8 0.6 collective-permute-start.20
  88.4 0.0 collective-permute-done.16.refs_3_
  88.4 0.2 collective-permute-done.17.refs_4_
  88.6 0.9 %collective-permute-done.18.refs_5_ = bf16[16,1280]{1,0:T(8,128)(2,1)S(1)} collective-permute-done((bf16[16,1280]{1,0:T(8,128)(2,1)S(1)}, bf16[16,1280]{1,0:T(8,128)(2,1)S(1)}, u32[]{:S(2)}, u32[]{:S(2)}) %collective-permute-start.18) | collective-permute-done | bytes 40992 | tf_op jit(solution)/shard_map/ppermute | solution.py:729
  89.5 0.8 collective-permute-done.19.refs_6_
  90.4 1.4 %collective-permute-done.20.refs_7_ = bf16[16,1280]{1,0:T(8,128)(2,1)S(1)} collective-permute-done((bf16[16,1280]{1,0:T(8,128)(2,1)S(1)}, bf16[16,1280]{1,0:T(8,128)(2,1)S(1)}, u32[]{:S(2)}, u32[]{:S(2)}) %collective-permute-start.20) | collective-permute-done | bytes 40992 | tf_op jit(solution)/shard_map/ppermute | solution.py:729
  91.8 1.6 %unpack.1 = bf16[16,2048]{1,0:T(8,128)(2,1)} custom-call(s32[8]{0:T(128)S(1)} %and_select_fusion.named_by, bf16[16,2048]{1,0:T(8,128)(2,1)S(1)} %get-tuple-element.54.mixed, bf16[16,128]{1,0:T(8,128)(2,1)S(1)} %pad.14.routes, bf16[16,1280]{1,0:T(8,128)(2,1)S(1)} %get-tuple-element.63.refs_0_, bf16[16,1280]{1,0:T(8,128)(2,1)S(1)} %collective-permute-done.14.refs_1_, ...), custom_call_target="tpu_custom_call" | custom-call | tf_op jit(solution)/shard_map/unpack/pallas_call | solution.py:626
  (7 shorter events, 0.1 us)
Async XLA Ops:
  1.0 12.6 %collective-permute-start.2 = (bf16[32,2048]{1,0:T(8,128)(2,1)S(1)}, bf16[32,2048]{1,0:T(8,128)(2,1)S(1)}, u32[]{:S(2)}, u32[]{:S(2)}) collective-permute-start(bf16[32,2048]{1,0:T(8,128)(2,1)S(1)} %get-tuple-element.72.refs_0_), channel_id=1, source_target_pairs={{0,24},{8,16},{16,8},{24,0},{1,25},{9,17},{17,9},{25,1},{2,26},{10... | collective-permute-start | bytes 393224 | tf_op jit(solution)/shard_map/ppermute | solution.py:41
  6.1 11.1 %collective-permute-start.1 = (bf16[32,2048]{1,0:T(8,128)(2,1)S(1)}, bf16[32,2048]{1,0:T(8,128)(2,1)S(1)}, u32[]{:S(2)}, u32[]{:S(2)}) collective-permute-start(bf16[32,2048]{1,0:T(8,128)(2,1)S(1)} %get-tuple-element.72.refs_0_), channel_id=1, source_target_pairs={{0,16},{8,24},{16,0},{24,8},{1,17},{9,25},{17,1},{25,9},{2,18},{10... | collective-permute-start | bytes 393224 | tf_op jit(solution)/shard_map/ppermute | solution.py:41
  6.1 11.1 %collective-permute-start = (bf16[32,2048]{1,0:T(8,128)(2,1)S(1)}, bf16[32,2048]{1,0:T(8,128)(2,1)S(1)}, u32[]{:S(2)}, u32[]{:S(2)}) collective-permute-start(bf16[32,2048]{1,0:T(8,128)(2,1)S(1)} %get-tuple-element.72.refs_0_), channel_id=1, source_target_pairs={{0,8},{8,0},{16,24},{24,16},{1,9},{9,1},{17,25},{25,17},{2,10},{10... | collective-permute-start | bytes 393224 | tf_op jit(solution)/shard_map/ppermute | solution.py:41
  7.5 6.0 %collective-permute-start.4 = (bf16[16,128]{1,0:T(8,128)(2,1)S(1)}, bf16[16,128]{1,0:T(8,128)(2,1)S(1)}, u32[]{:S(2)}, u32[]{:S(2)}) collective-permute-start(bf16[16,128]{1,0:T(8,128)(2,1)S(1)} %pad.14.routes), channel_id=1, source_target_pairs={{0,4},{4,0},{1,5},{5,1},{2,6},{6,2},{3,7},{7,3},{8,12},{12,8},{9,1... | collective-permute-start | bytes 12296 | tf_op jit(solution)/shard_map/ppermute | solution.py:27
  19.3 6.1 %collective-permute-start.3 = (f32[160,128]{1,0:T(8,128)S(1)}, f32[160,128]{1,0:T(8,128)S(1)}, u32[]{:S(2)}, u32[]{:S(2)}) collective-permute-start(f32[160,128]{1,0:T(8,128)S(1)} %get-tuple-element.43.own), channel_id=1, source_target_pairs={{0,4},{4,0},{1,5},{5,1},{2,6},{6,2},{3,7},{7,3},{8,12},{12,8},{9,1... | collective-permute-start | bytes 245768 | tf_op jit(solution)/shard_map/ppermute | solution.py:27
  21.0 11.1 %collective-permute-start.5 = (bf16[32,2432]{1,0:T(8,128)(2,1)S(1)}, bf16[32,2432]{1,0:T(8,128)(2,1)S(1)}, u32[]{:S(2)}, u32[]{:S(2)}) collective-permute-start(bf16[32,2432]{1,0:T(8,128)(2,1)S(1)} %get-tuple-element.45), channel_id=1, source_target_pairs={{0,8},{8,0},{16,24},{24,16},{1,9},{9,1},{17,25},{25,17},{2,10},{10... | collective-permute-start | bytes 466952 | tf_op jit(solution)/shard_map/ppermute | solution.py:41
  21.0 14.0 %collective-permute-start.6 = (bf16[32,2432]{1,0:T(8,128)(2,1)S(1)}, bf16[32,2432]{1,0:T(8,128)(2,1)S(1)}, u32[]{:S(2)}, u32[]{:S(2)}) collective-permute-start(bf16[32,2432]{1,0:T(8,128)(2,1)S(1)} %get-tuple-element.46), channel_id=1, source_target_pairs={{0,16},{8,24},{16,0},{24,8},{1,17},{9,25},{17,1},{25,9},{2,18},{10... | collective-permute-start | bytes 466952 | tf_op jit(solution)/shard_map/ppermute | solution.py:41
  24.1 11.0 %collective-permute-start.7 = (bf16[32,2432]{1,0:T(8,128)(2,1)S(1)}, bf16[32,2432]{1,0:T(8,128)(2,1)S(1)}, u32[]{:S(2)}, u32[]{:S(2)}) collective-permute-start(bf16[32,2432]{1,0:T(8,128)(2,1)S(1)} %get-tuple-element.47), channel_id=1, source_target_pairs={{0,24},{8,16},{16,8},{24,0},{1,25},{9,17},{17,9},{25,1},{2,26},{10... | collective-permute-start | bytes 466952 | tf_op jit(solution)/shard_map/ppermute | solution.py:41
  37.7 6.4 %collective-permute-start.8 = (bf16[128,512]{1,0:T(8,128)(2,1)S(1)}, bf16[128,512]{1,0:T(8,128)(2,1)S(1)}, u32[]{:S(2)}, u32[]{:S(2)}) collective-permute-start(bf16[128,512]{1,0:T(8,128)(2,1)S(1)} %get-tuple-element.53.base), channel_id=1, source_target_pairs={{0,4},{4,0},{1,5},{5,1},{2,6},{6,2},{3,7},{7,3},{8,12},{12,8},{9,1... | collective-permute-start | bytes 393224 | tf_op jit(solution)/shard_map/ppermute | solution.py:27
  44.1 8.2 %collective-permute-start.11 = (bf16[128,512]{1,0:T(8,128)(2,1)S(1)}, bf16[128,512]{1,0:T(8,128)(2,1)S(1)}, u32[]{:S(2)}, u32[]{:S(2)}) collective-permute-start(bf16[128,512]{1,0:T(8,128)(2,1)S(1)} %mix.1.refs_0_), channel_id=1, source_target_pairs={{0,24},{8,16},{16,8},{24,0},{1,25},{9,17},{17,9},{25,1},{2,26},{10... | collective-permute-start | bytes 393224 | tf_op jit(solution)/shard_map/ppermute | solution.py:41
  46.6 10.1 %collective-permute-start.10 = (bf16[128,512]{1,0:T(8,128)(2,1)S(1)}, bf16[128,512]{1,0:T(8,128)(2,1)S(1)}, u32[]{:S(2)}, u32[]{:S(2)}) collective-permute-start(bf16[128,512]{1,0:T(8,128)(2,1)S(1)} %mix.1.refs_0_), channel_id=1, source_target_pairs={{0,16},{8,24},{16,0},{24,8},{1,17},{9,25},{17,1},{25,9},{2,18},{10... | collective-permute-start | bytes 393224 | tf_op jit(solution)/shard_map/ppermute | solution.py:41
  48.0 8.8 %collective-permute-start.9 = (bf16[128,512]{1,0:T(8,128)(2,1)S(1)}, bf16[128,512]{1,0:T(8,128)(2,1)S(1)}, u32[]{:S(2)}, u32[]{:S(2)}) collective-permute-start(bf16[128,512]{1,0:T(8,128)(2,1)S(1)} %mix.1.refs_0_), channel_id=1, source_target_pairs={{0,8},{8,0},{16,24},{24,16},{1,9},{9,1},{17,25},{25,17},{2,10},{10... | collective-permute-start | bytes 393224 | tf_op jit(solution)/shard_map/ppermute | solution.py:41
  58.6 2.0 %collective-permute-start.12 = (bf16[128,2048]{1,0:T(8,128)(2,1)S(1)}, bf16[128,2048]{1,0:T(8,128)(2,1)S(1)}, u32[]{:S(2)}, u32[]{:S(2)}) collective-permute-start(bf16[128,2048]{1,0:T(8,128)(2,1)S(1)} %get-tuple-element.57.own), channel_id=1, source_target_pairs={{0,1},{1,0},{2,3},{3,2},{4,5},{5,4},{6,7},{7,6},{8,9},{9,8},{10,11... | collective-permute-start | bytes 1572872 | tf_op jit(solution)/shard_map/ppermute | solution.py:67
  75.4 2.0 %collective-permute-start.13 = (bf16[128,2048]{1,0:T(8,128)(2,1)S(1)}, bf16[128,2048]{1,0:T(8,128)(2,1)S(1)}, u32[]{:S(2)}, u32[]{:S(2)}) collective-permute-start(bf16[128,2048]{1,0:T(8,128)(2,1)S(1)} %get-tuple-element.61), channel_id=1, source_target_pairs={{0,1},{1,0},{2,3},{3,2},{4,5},{5,4},{6,7},{7,6},{8,9},{9,8},{10,11... | collective-permute-start | bytes 1572872 | tf_op jit(solution)/shard_map/ppermute | solution.py:67
  78.6 7.8 %collective-permute-start.14 = (bf16[16,1280]{1,0:T(8,128)(2,1)S(1)}, bf16[16,1280]{1,0:T(8,128)(2,1)S(1)}, u32[]{:S(2)}, u32[]{:S(2)}) collective-permute-start(bf16[16,1280]{1,0:T(8,128)(2,1)S(1)} %get-tuple-element.64), channel_id=1, source_target_pairs={{0,4},{4,8},{8,12},{12,16},{16,20},{20,24},{24,28},{28,0},{1,5},{5... | collective-permute-start | bytes 122888 | tf_op jit(solution)/shard_map/ppermute | solution.py:729
  80.2 7.7 %collective-permute-start.15 = (bf16[16,1280]{1,0:T(8,128)(2,1)S(1)}, bf16[16,1280]{1,0:T(8,128)(2,1)S(1)}, u32[]{:S(2)}, u32[]{:S(2)}) collective-permute-start(bf16[16,1280]{1,0:T(8,128)(2,1)S(1)} %get-tuple-element.65), channel_id=1, source_target_pairs={{0,8},{4,12},{8,16},{12,20},{16,24},{20,28},{24,0},{28,4},{1,9},{5... | collective-permute-start | bytes 122888 | tf_op jit(solution)/shard_map/ppermute | solution.py:729
  80.2 8.2 %collective-permute-start.16 = (bf16[16,1280]{1,0:T(8,128)(2,1)S(1)}, bf16[16,1280]{1,0:T(8,128)(2,1)S(1)}, u32[]{:S(2)}, u32[]{:S(2)}) collective-permute-start(bf16[16,1280]{1,0:T(8,128)(2,1)S(1)} %get-tuple-element.66), channel_id=1, source_target_pairs={{0,12},{4,16},{8,20},{12,24},{16,28},{20,0},{24,4},{28,8},{1,13},{... | collective-permute-start | bytes 122888 | tf_op jit(solution)/shard_map/ppermute | solution.py:729
  82.5 6.1 %collective-permute-start.17 = (bf16[16,1280]{1,0:T(8,128)(2,1)S(1)}, bf16[16,1280]{1,0:T(8,128)(2,1)S(1)}, u32[]{:S(2)}, u32[]{:S(2)}) collective-permute-start(bf16[16,1280]{1,0:T(8,128)(2,1)S(1)} %get-tuple-element.67), channel_id=1, source_target_pairs={{0,16},{4,20},{8,24},{12,28},{16,0},{20,4},{24,8},{28,12},{1,17},{... | collective-permute-start | bytes 122888 | tf_op jit(solution)/shard_map/ppermute | solution.py:729
  84.1 5.5 %collective-permute-start.18 = (bf16[16,1280]{1,0:T(8,128)(2,1)S(1)}, bf16[16,1280]{1,0:T(8,128)(2,1)S(1)}, u32[]{:S(2)}, u32[]{:S(2)}) collective-permute-start(bf16[16,1280]{1,0:T(8,128)(2,1)S(1)} %get-tuple-element.68), channel_id=1, source_target_pairs={{0,20},{4,24},{8,28},{12,0},{16,4},{20,8},{24,12},{28,16},{1,21},{... | collective-permute-start | bytes 122888 | tf_op jit(solution)/shard_map/ppermute | solution.py:729
  86.4 4.0 %collective-permute-start.19 = (bf16[16,1280]{1,0:T(8,128)(2,1)S(1)}, bf16[16,1280]{1,0:T(8,128)(2,1)S(1)}, u32[]{:S(2)}, u32[]{:S(2)}) collective-permute-start(bf16[16,1280]{1,0:T(8,128)(2,1)S(1)} %get-tuple-element.69), channel_id=1, source_target_pairs={{0,24},{4,28},{8,0},{12,4},{16,8},{20,12},{24,16},{28,20},{1,25},{... | collective-permute-start | bytes 122888 | tf_op jit(solution)/shard_map/ppermute | solution.py:729
  87.8 4.0 %collective-permute-start.20 = (bf16[16,1280]{1,0:T(8,128)(2,1)S(1)}, bf16[16,1280]{1,0:T(8,128)(2,1)S(1)}, u32[]{:S(2)}, u32[]{:S(2)}) collective-permute-start(bf16[16,1280]{1,0:T(8,128)(2,1)S(1)} %get-tuple-element.70), channel_id=1, source_target_pairs={{0,28},{4,0},{8,4},{12,8},{16,12},{20,16},{24,20},{28,24},{1,29},{... | collective-permute-start | bytes 122888 | tf_op jit(solution)/shard_map/ppermute | solution.py:729

commit v10 on v9

--- a/solution.py
+++ b/solution.py
@@ -451,7 +451,7 @@
         here = pl.ds(pl.multiple_of(begin + offset, 16), quarter)
         target = late.at[index] if index < 2 else last.at[index - 2]
         copies.append(pltpu.make_async_copy(source.at[here, :], target, sems.at[index]))
-    for copy in copies:
+    for copy in copies[:2]:
         copy.start()
     tokens[0:rows, :] = own[...]
     tokens[rows:, :] = other[...]
@@ -463,6 +463,8 @@
         hidden[:, place * quarter : (place + 1) * quarter] = value.astype(BF16)
 
     activate_hidden(gate_first, up_first, 0)
+    for copy in copies[2:]:
+        copy.start()
     copies[0].wait()
     copies[1].wait()
     activate_hidden(late.at[0], late.at[1], 1)

time: 93.9 us -> 93.9 us (level)
  no operation moved by 1% of the time
where the time goes in v10:
time: 93.9 us; the launch traced here: 93.4 us
  Pallas kernels  36.7 us (39%)
  starting transfers between devices  28.5 us (30%)
  waiting for transfers between devices  21.9 us (23%)
  local copies, waits for them, and re-layouts  5.2 us (6%)
    pallas_call x1, Pallas kernels, shared_experts(): pl.pallas_call(shared_kernel, out_shape=(jax.ShapeDtypeStruct((rows, widt...  14.8 us
    ppermute x9, waiting for transfers between devices, exchange(): lax.ppermute(value, axis, [(i, partner(i, step, count)) for i in range(co...  14.7 us
    ppermute x9, starting transfers between devices, exchange(): lax.ppermute(value, axis, [(i, partner(i, step, count)) for i in range(co...  14.7 us
    ppermute x7, starting transfers between devices, body(): lax.ppermute(outs[s], axes, [(i, (i + s) % parts) for i in range(parts)])  9.8 us
    pallas_call x1, Pallas kernels, scan(): pl.pallas_call(functools.partial(scan_kernel, taps), out_shape=jax.ShapeD...  6.66 us
    pallas_call x1, Pallas kernels, fetch(): pl.pallas_call(functools.partial(fetch_kernel, parts, half_rows), out_sha...  5.82 us
    ppermute x3, starting transfers between devices, rotate(): lax.ppermute(value, axis, [(i, (i + steps) % count) for i in range(count)])  3.82 us
    ppermute x2, waiting for transfers between devices, swap(): lax.ppermute(value, 'doc', [(i, i + 1 - 2 * (i % 2)) for i in range(count)])  3.67 us
  transfers between devices with their start and end apart: 21, of which 10 were waited for; matrix products, arithmetic and copies ran while one was open for 5% of the time, Pallas kernels for 13%

profile of v10, /device:TPU:0, one launch (start us, length us, event | category | flops | bytes accessed | tf_op | source)
XLA Modules:
  0.0 93.4 jit_solution(4720775736544044108)
XLA Ops:
  0.0 1.0 %slice_bitcast_fusion = (bf16[32,2048]{1,0:T(8,128)(2,1)S(1)}, bf16[32,2048]{1,0:T(8,128)(2,1)S(1)}) fusion(bf16[2,32,2048]{2,1,0:T(8,128)(2,1)} %param.18), kind=kLoop, calls=%fused_computation.4 | loop fusion | bytes 524288 | tf_op jit(solution)/shard_map/squeeze | solution.py:662
  1.0 5.1 %collective-permute-start.2 = (bf16[32,2048]{1,0:T(8,128)(2,1)S(1)}, bf16[32,2048]{1,0:T(8,128)(2,1)S(1)}, u32[]{:S(2)}, u32[]{:S(2)}) collective-permute-start(bf16[32,2048]{1,0:T(8,128)(2,1)S(1)} %get-tuple-element.72.refs_0_), channel_id=1, source_target_pairs={{0,24},{8,16},{16,8},{24,0},{1,25},{9,17},{17,9},{25,1},{2,26},{10... | collective-permute-start | bytes 393224 | tf_op jit(solution)/shard_map/ppermute | solution.py:41
  6.1 0.0 collective-permute-start.1
  6.1 0.6 collective-permute-start
  6.7 0.7 convert_element_type.13
  7.4 0.1 copy.20
  7.5 1.7 %collective-permute-start.4 = (bf16[16,128]{1,0:T(8,128)(2,1)S(1)}, bf16[16,128]{1,0:T(8,128)(2,1)S(1)}, u32[]{:S(2)}, u32[]{:S(2)}) collective-permute-start(bf16[16,128]{1,0:T(8,128)(2,1)S(1)} %pad.14.routes), channel_id=1, source_target_pairs={{0,4},{4,0},{1,5},{5,1},{2,6},{6,2},{3,7},{7,3},{8,12},{12,8},{9,1... | collective-permute-start | bytes 12296 | tf_op jit(solution)/shard_map/ppermute | solution.py:27
  9.2 0.1 stack.93
  9.3 0.1 pad_add_fusion.spots
  9.4 0.8 constant_dynamic-slice_fusion
  10.2 0.1 pad_add_fusion.1.places
  10.3 0.1 concatenate.38.places
  10.4 0.7 pad.12.router
  11.2 0.7 pad.13.gain
  11.9 0.1 stack.85.targets
  12.0 1.6 %concatenate.37.params = f32[16,2048]{1,0:T(8,128)S(1)} concatenate(f32[4,2048]{1,0:T(4,128)} %param.21, f32[1,2048]{1,0:T(1,128)} %bitcast.33, f32[1,2048]{1,0:T(1,128)} %bitcast.34, f32[1,2048]{1,0:T(1,128)} %bitcast.35, f32[1,2048]{1,0:T(1,128)S(1)} %slice.33, f32[5,2048]{1,0:T(8,128)S(1)} %broadcast_in_dim.24, bf16[3,2048]{1,0:T(4,128)(2,1)} %param.19), dimensions={0} | concatenate | bytes 249856 | tf_op jit(solution)/shard_map/concatenate | solution.py:685
  13.6 0.0 collective-permute-done.4
  13.6 0.0 collective-permute-done.2.refs_3_
  13.6 3.6 %collective-permute-done.1.refs_2_ = bf16[32,2048]{1,0:T(8,128)(2,1)S(1)} collective-permute-done((bf16[32,2048]{1,0:T(8,128)(2,1)S(1)}, bf16[32,2048]{1,0:T(8,128)(2,1)S(1)}, u32[]{:S(2)}, u32[]{:S(2)}) %collective-permute-start.1) | collective-permute-done | bytes 131104 | tf_op jit(solution)/shard_map/ppermute | solution.py:41
  17.2 0.0 collective-permute-done.refs_1_
  17.2 2.1 %activate.1 = (bf16[128,2048]{1,0:T(8,128)(2,1)S(1)}, f32[160,128]{1,0:T(8,128)S(1)}) custom-call(s32[4]{0:T(128)S(1)} %pad_add_fusion.1.places, f32[16,2048]{1,0:T(8,128)S(1)} %concatenate.37.params, bf16[160,2048]{1,0:T(8,128)(2,1)} %select.44, bf16[32,2048]{1,0:T(8,128)(2,1)S(1)} %get-tuple-element.72.refs_0_, ...), custom_call_target="tpu_custom_call" | custom-call | flops 83886080 | bytes 1048576 | tf_op jit(solution)/shard_map/activate/pallas_call | solution.py:120
  19.3 1.6 %collective-permute-start.3 = (f32[160,128]{1,0:T(8,128)S(1)}, f32[160,128]{1,0:T(8,128)S(1)}, u32[]{:S(2)}, u32[]{:S(2)}) collective-permute-start(f32[160,128]{1,0:T(8,128)S(1)} %get-tuple-element.43.own), channel_id=1, source_target_pairs={{0,4},{4,0},{1,5},{5,1},{2,6},{6,2},{3,7},{7,3},{8,12},{12,8},{9,1... | collective-permute-start | bytes 245768 | tf_op jit(solution)/shard_map/ppermute | solution.py:27
  21.0 0.1 collective-permute-start.5
  21.0 3.0 %collective-permute-start.6 = (bf16[32,2432]{1,0:T(8,128)(2,1)S(1)}, bf16[32,2432]{1,0:T(8,128)(2,1)S(1)}, u32[]{:S(2)}, u32[]{:S(2)}) collective-permute-start(bf16[32,2432]{1,0:T(8,128)(2,1)S(1)} %get-tuple-element.46), channel_id=1, source_target_pairs={{0,16},{8,24},{16,0},{24,8},{1,17},{9,25},{17,1},{25,9},{2,18},{10... | collective-permute-start | bytes 466952 | tf_op jit(solution)/shard_map/ppermute | solution.py:41
  24.1 1.3 %collective-permute-start.7 = (bf16[32,2432]{1,0:T(8,128)(2,1)S(1)}, bf16[32,2432]{1,0:T(8,128)(2,1)S(1)}, u32[]{:S(2)}, u32[]{:S(2)}) collective-permute-start(bf16[32,2432]{1,0:T(8,128)(2,1)S(1)} %get-tuple-element.47), channel_id=1, source_target_pairs={{0,24},{8,16},{16,8},{24,0},{1,25},{9,17},{17,9},{25,1},{2,26},{10... | collective-permute-start | bytes 466952 | tf_op jit(solution)/shard_map/ppermute | solution.py:41
  25.4 0.0 collective-permute-done.3.other
  25.4 6.7 %scan.1.value_in = f32[128,2048]{1,0:T(8,128)S(1)} custom-call(f32[160,128]{1,0:T(8,128)S(1)} %get-tuple-element.43.own, f32[160,128]{1,0:T(8,128)S(1)} %collective-permute-done.3.other, bf16[128,2048]{1,0:T(8,128)(2,1)S(1)} %get-tuple-element.44.active, f32[16,2048]{1,0:T(8,128)S(1)} %concatenate.37.params, f32[16,2048]{1,0:T(8,128)} %log_rate_hbm.1, ...), custom_call_target="tpu_custom_call" | custom-call | flops 12582912000 | bytes 2097152 | tf_op jit(solution)/shard_map/scan/pallas_call | solution.py:242
  32.1 0.0 collective-permute-done.5.refs_1_
  32.1 2.9 %collective-permute-done.6.refs_2_ = bf16[32,2432]{1,0:T(8,128)(2,1)S(1)} collective-permute-done((bf16[32,2432]{1,0:T(8,128)(2,1)S(1)}, bf16[32,2432]{1,0:T(8,128)(2,1)S(1)}, u32[]{:S(2)}, u32[]{:S(2)}) %collective-permute-start.6) | collective-permute-done | bytes 155680 | tf_op jit(solution)/shard_map/ppermute | solution.py:41
  35.0 0.0 collective-permute-done.7.refs_3_
  35.0 2.6 %project.1 = (bf16[128,512]{1,0:T(8,128)(2,1)S(1)}, bf16[128,128]{1,0:T(8,128)(2,1)S(1)}) custom-call(s32[5]{0:T(128)S(1)} %concatenate.38.places, f32[128,2048]{1,0:T(8,128)S(1)} %scan.1.value_in, bf16[2048,512]{1,0:T(8,128)(2,1)} %weight_hbm.1, bf16[32,2432]{1,0:T(8,128)(2,1)S(1)} %get-tuple-element.76.refs_0_, ...), custom_call_target="tpu_custom_call" | custom-call | flops 268435456 | bytes 2097152 | tf_op jit(solution)/shard_map/project/pallas_call | solution.py:310
  37.7 0.6 collective-permute-start.8
  38.2 5.8 %fetch.1 = (bf16[1792,2048]{1,0:T(8,128)(2,1)S(1)}, bf16[1792,2048]{1,0:T(8,128)(2,1)S(1)}, s32[1]{0:T(128)}) custom-call(s32[1]{0:T(128)} %bitcast.28.half, bf16[7168,2048]{1,0:T(8,128)(2,1)} %gate.1, bf16[7168,2048]{1,0:T(8,128)(2,1)} %up.1), custom_call_target="tpu_custom_call" | custom-call | bytes 29360128 | tf_op jit(solution)/shard_map/fetch/pallas_call | solution.py:431
  44.1 0.0 collective-permute-done.8.summand
  44.1 2.5 %collective-permute-start.11 = (bf16[128,512]{1,0:T(8,128)(2,1)S(1)}, bf16[128,512]{1,0:T(8,128)(2,1)S(1)}, u32[]{:S(2)}, u32[]{:S(2)}) collective-permute-start(bf16[128,512]{1,0:T(8,128)(2,1)S(1)} %mix.1.refs_0_), channel_id=1, source_target_pairs={{0,24},{8,16},{16,8},{24,0},{1,25},{9,17},{17,9},{25,1},{2,26},{10... | collective-permute-start | bytes 393224 | tf_op jit(solution)/shard_map/ppermute | solution.py:41
  46.6 1.4 %collective-permute-start.10 = (bf16[128,512]{1,0:T(8,128)(2,1)S(1)}, bf16[128,512]{1,0:T(8,128)(2,1)S(1)}, u32[]{:S(2)}, u32[]{:S(2)}) collective-permute-start(bf16[128,512]{1,0:T(8,128)(2,1)S(1)} %mix.1.refs_0_), channel_id=1, source_target_pairs={{0,16},{8,24},{16,0},{24,8},{1,17},{9,25},{17,1},{25,9},{2,18},{10... | collective-permute-start | bytes 393224 | tf_op jit(solution)/shard_map/ppermute | solution.py:41
  48.0 0.5 collective-permute-start.9
  48.6 3.8 %collective-permute-done.11.refs_3_ = bf16[128,512]{1,0:T(8,128)(2,1)S(1)} collective-permute-done((bf16[128,512]{1,0:T(8,128)(2,1)S(1)}, bf16[128,512]{1,0:T(8,128)(2,1)S(1)}, u32[]{:S(2)}, u32[]{:S(2)}) %collective-permute-start.11) | collective-permute-done | bytes 131104 | tf_op jit(solution)/shard_map/ppermute | solution.py:41
  52.3 4.4 %collective-permute-done.10.refs_2_ = bf16[128,512]{1,0:T(8,128)(2,1)S(1)} collective-permute-done((bf16[128,512]{1,0:T(8,128)(2,1)S(1)}, bf16[128,512]{1,0:T(8,128)(2,1)S(1)}, u32[]{:S(2)}, u32[]{:S(2)}) %collective-permute-start.10) | collective-permute-done | bytes 131104 | tf_op jit(solution)/shard_map/ppermute | solution.py:41
  56.8 0.0 collective-permute-done.9.refs_1_
  56.8 1.8 %norm.1 = (bf16[128,2048]{1,0:T(8,128)(2,1)S(1)}, f32[128,128]{1,0:T(8,128)S(1)}, bf16[16,2048]{1,0:T(8,128)(2,1)S(1)}) custom-call(s32[4]{0:T(128)S(1)} %pad_add_fusion.1.places, s32[2]{0:T(128)S(1)} %pad_add_fusion.spots, f32[8,2048]{1,0:T(8,128)S(1)} %pad.13.gain, bf16[16,2048]{1,0:T(8,128)(2,1)S(1)} %pad.12.router, ...), custom_call_target="tpu_custom_call" | custom-call | tf_op jit(solution)/shard_map/norm/pallas_call | solution.py:389
  58.6 0.1 collective-permute-start.12
  58.7 1.9 %collective-permute-done.12.other = bf16[128,2048]{1,0:T(8,128)(2,1)S(1)} collective-permute-done((bf16[128,2048]{1,0:T(8,128)(2,1)S(1)}, bf16[128,2048]{1,0:T(8,128)(2,1)S(1)}, u32[]{:S(2)}, u32[]{:S(2)}) %collective-permute-start.12) | collective-permute-done | bytes 524320 | tf_op jit(solution)/shard_map/ppermute | solution.py:67
  60.6 14.8 %experts.1 = (f32[128,2048]{1,0:T(8,128)S(1)}, bf16[128,2048]{1,0:T(8,128)(2,1)S(1)}) custom-call(s32[1]{0:T(128)} %get-tuple-element.56.half, bf16[128,2048]{1,0:T(8,128)(2,1)S(1)} %get-tuple-element.57.own, bf16[128,2048]{1,0:T(8,128)(2,1)S(1)} %collective-permute-done.12.other, bf16[1792,2048]{1,0:T(8,128)(2,1)S(1)} %get-tuple-element.58.gate_first, ...), custom_call_target="tpu_custom_call" | custom-call | flops 11274289152 | bytes 29360128 | tf_op jit(solution)/shard_map/experts/pallas_call | solution.py:485
  75.4 0.2 collective-permute-start.13
  75.6 1.8 %collective-permute-done.13.other = bf16[128,2048]{1,0:T(8,128)(2,1)S(1)} collective-permute-done((bf16[128,2048]{1,0:T(8,128)(2,1)S(1)}, bf16[128,2048]{1,0:T(8,128)(2,1)S(1)}, u32[]{:S(2)}, u32[]{:S(2)}) %collective-permute-start.13) | collective-permute-done | bytes 524320 | tf_op jit(solution)/shard_map/ppermute | solution.py:67
  77.4 1.2 %combine.1 = (bf16[16,1280]{1,0:T(8,128)(2,1)S(1)}, bf16[16,1280]{1,0:T(8,128)(2,1)S(1)}, bf16[16,1280]{1,0:T(8,128)(2,1)S(1)}, bf16[16,1280]{1,0:T(8,128)(2,1)S...) custom-call(s32[8]{0:T(128)S(1)} %stack.85.targets, ...), custom_call_target="tpu_custom_call" | custom-call | tf_op jit(solution)/shard_map/combine/pallas_call | solution.py:586
  78.6 1.6 %collective-permute-start.14 = (bf16[16,1280]{1,0:T(8,128)(2,1)S(1)}, bf16[16,1280]{1,0:T(8,128)(2,1)S(1)}, u32[]{:S(2)}, u32[]{:S(2)}) collective-permute-start(bf16[16,1280]{1,0:T(8,128)(2,1)S(1)} %get-tuple-element.64), channel_id=1, source_target_pairs={{0,4},{4,8},{8,12},{12,16},{16,20},{20,24},{24,28},{28,0},{1,5},{5... | collective-permute-start | bytes 122888 | tf_op jit(solution)/shard_map/ppermute | solution.py:731
  80.2 0.0 collective-permute-start.15
  80.2 2.3 %collective-permute-start.16 = (bf16[16,1280]{1,0:T(8,128)(2,1)S(1)}, bf16[16,1280]{1,0:T(8,128)(2,1)S(1)}, u32[]{:S(2)}, u32[]{:S(2)}) collective-permute-start(bf16[16,1280]{1,0:T(8,128)(2,1)S(1)} %get-tuple-element.66), channel_id=1, source_target_pairs={{0,12},{4,16},{8,20},{12,24},{16,28},{20,0},{24,4},{28,8},{1,13},{... | collective-permute-start | bytes 122888 | tf_op jit(solution)/shard_map/ppermute | solution.py:731
  82.5 1.6 %collective-permute-start.17 = (bf16[16,1280]{1,0:T(8,128)(2,1)S(1)}, bf16[16,1280]{1,0:T(8,128)(2,1)S(1)}, u32[]{:S(2)}, u32[]{:S(2)}) collective-permute-start(bf16[16,1280]{1,0:T(8,128)(2,1)S(1)} %get-tuple-element.67), channel_id=1, source_target_pairs={{0,16},{4,20},{8,24},{12,28},{16,0},{20,4},{24,8},{28,12},{1,17},{... | collective-permute-start | bytes 122888 | tf_op jit(solution)/shard_map/ppermute | solution.py:731
  84.1 2.3 %collective-permute-start.18 = (bf16[16,1280]{1,0:T(8,128)(2,1)S(1)}, bf16[16,1280]{1,0:T(8,128)(2,1)S(1)}, u32[]{:S(2)}, u32[]{:S(2)}) collective-permute-start(bf16[16,1280]{1,0:T(8,128)(2,1)S(1)} %get-tuple-element.68), channel_id=1, source_target_pairs={{0,20},{4,24},{8,28},{12,0},{16,4},{20,8},{24,12},{28,16},{1,21},{... | collective-permute-start | bytes 122888 | tf_op jit(solution)/shard_map/ppermute | solution.py:731
  86.4 0.0 collective-permute-done.14.refs_1_
  86.4 1.4 %collective-permute-start.19 = (bf16[16,1280]{1,0:T(8,128)(2,1)S(1)}, bf16[16,1280]{1,0:T(8,128)(2,1)S(1)}, u32[]{:S(2)}, u32[]{:S(2)}) collective-permute-start(bf16[16,1280]{1,0:T(8,128)(2,1)S(1)} %get-tuple-element.69), channel_id=1, source_target_pairs={{0,24},{4,28},{8,0},{12,4},{16,8},{20,12},{24,16},{28,20},{1,25},{... | collective-permute-start | bytes 122888 | tf_op jit(solution)/shard_map/ppermute | solution.py:731
  87.8 0.0 collective-permute-done.15.refs_2_
  87.8 0.6 collective-permute-start.20
  88.4 0.0 collective-permute-done.16.refs_3_
  88.4 0.2 collective-permute-done.17.refs_4_
  88.6 0.9 %collective-permute-done.18.refs_5_ = bf16[16,1280]{1,0:T(8,128)(2,1)S(1)} collective-permute-done((bf16[16,1280]{1,0:T(8,128)(2,1)S(1)}, bf16[16,1280]{1,0:T(8,128)(2,1)S(1)}, u32[]{:S(2)}, u32[]{:S(2)}) %collective-permute-start.18) | collective-permute-done | bytes 40992 | tf_op jit(solution)/shard_map/ppermute | solution.py:731
  89.5 0.8 collective-permute-done.19.refs_6_
  90.4 1.4 %collective-permute-done.20.refs_7_ = bf16[16,1280]{1,0:T(8,128)(2,1)S(1)} collective-permute-done((bf16[16,1280]{1,0:T(8,128)(2,1)S(1)}, bf16[16,1280]{1,0:T(8,128)(2,1)S(1)}, u32[]{:S(2)}, u32[]{:S(2)}) %collective-permute-start.20) | collective-permute-done | bytes 40992 | tf_op jit(solution)/shard_map/ppermute | solution.py:731
  91.8 1.6 %unpack.1 = bf16[16,2048]{1,0:T(8,128)(2,1)} custom-call(s32[8]{0:T(128)S(1)} %and_select_fusion.named_by, bf16[16,2048]{1,0:T(8,128)(2,1)S(1)} %get-tuple-element.54.mixed, bf16[16,128]{1,0:T(8,128)(2,1)S(1)} %pad.14.routes, bf16[16,1280]{1,0:T(8,128)(2,1)S(1)} %get-tuple-element.63.refs_0_, bf16[16,1280]{1,0:T(8,128)(2,1)S(1)} %collective-permute-done.14.refs_1_, ...), custom_call_target="tpu_custom_call" | custom-call | tf_op jit(solution)/shard_map/unpack/pallas_call | solution.py:628
  (7 shorter events, 0.1 us)
Async XLA Ops:
  1.0 12.6 %collective-permute-start.2 = (bf16[32,2048]{1,0:T(8,128)(2,1)S(1)}, bf16[32,2048]{1,0:T(8,128)(2,1)S(1)}, u32[]{:S(2)}, u32[]{:S(2)}) collective-permute-start(bf16[32,2048]{1,0:T(8,128)(2,1)S(1)} %get-tuple-element.72.refs_0_), channel_id=1, source_target_pairs={{0,24},{8,16},{16,8},{24,0},{1,25},{9,17},{17,9},{25,1},{2,26},{10... | collective-permute-start | bytes 393224 | tf_op jit(solution)/shard_map/ppermute | solution.py:41
  6.1 11.1 %collective-permute-start.1 = (bf16[32,2048]{1,0:T(8,128)(2,1)S(1)}, bf16[32,2048]{1,0:T(8,128)(2,1)S(1)}, u32[]{:S(2)}, u32[]{:S(2)}) collective-permute-start(bf16[32,2048]{1,0:T(8,128)(2,1)S(1)} %get-tuple-element.72.refs_0_), channel_id=1, source_target_pairs={{0,16},{8,24},{16,0},{24,8},{1,17},{9,25},{17,1},{25,9},{2,18},{10... | collective-permute-start | bytes 393224 | tf_op jit(solution)/shard_map/ppermute | solution.py:41
  6.1 11.1 %collective-permute-start = (bf16[32,2048]{1,0:T(8,128)(2,1)S(1)}, bf16[32,2048]{1,0:T(8,128)(2,1)S(1)}, u32[]{:S(2)}, u32[]{:S(2)}) collective-permute-start(bf16[32,2048]{1,0:T(8,128)(2,1)S(1)} %get-tuple-element.72.refs_0_), channel_id=1, source_target_pairs={{0,8},{8,0},{16,24},{24,16},{1,9},{9,1},{17,25},{25,17},{2,10},{10... | collective-permute-start | bytes 393224 | tf_op jit(solution)/shard_map/ppermute | solution.py:41
  7.5 6.0 %collective-permute-start.4 = (bf16[16,128]{1,0:T(8,128)(2,1)S(1)}, bf16[16,128]{1,0:T(8,128)(2,1)S(1)}, u32[]{:S(2)}, u32[]{:S(2)}) collective-permute-start(bf16[16,128]{1,0:T(8,128)(2,1)S(1)} %pad.14.routes), channel_id=1, source_target_pairs={{0,4},{4,0},{1,5},{5,1},{2,6},{6,2},{3,7},{7,3},{8,12},{12,8},{9,1... | collective-permute-start | bytes 12296 | tf_op jit(solution)/shard_map/ppermute | solution.py:27
  19.3 6.1 %collective-permute-start.3 = (f32[160,128]{1,0:T(8,128)S(1)}, f32[160,128]{1,0:T(8,128)S(1)}, u32[]{:S(2)}, u32[]{:S(2)}) collective-permute-start(f32[160,128]{1,0:T(8,128)S(1)} %get-tuple-element.43.own), channel_id=1, source_target_pairs={{0,4},{4,0},{1,5},{5,1},{2,6},{6,2},{3,7},{7,3},{8,12},{12,8},{9,1... | collective-permute-start | bytes 245768 | tf_op jit(solution)/shard_map/ppermute | solution.py:27
  21.0 11.1 %collective-permute-start.5 = (bf16[32,2432]{1,0:T(8,128)(2,1)S(1)}, bf16[32,2432]{1,0:T(8,128)(2,1)S(1)}, u32[]{:S(2)}, u32[]{:S(2)}) collective-permute-start(bf16[32,2432]{1,0:T(8,128)(2,1)S(1)} %get-tuple-element.45), channel_id=1, source_target_pairs={{0,8},{8,0},{16,24},{24,16},{1,9},{9,1},{17,25},{25,17},{2,10},{10... | collective-permute-start | bytes 466952 | tf_op jit(solution)/shard_map/ppermute | solution.py:41
  21.0 14.0 %collective-permute-start.6 = (bf16[32,2432]{1,0:T(8,128)(2,1)S(1)}, bf16[32,2432]{1,0:T(8,128)(2,1)S(1)}, u32[]{:S(2)}, u32[]{:S(2)}) collective-permute-start(bf16[32,2432]{1,0:T(8,128)(2,1)S(1)} %get-tuple-element.46), channel_id=1, source_target_pairs={{0,16},{8,24},{16,0},{24,8},{1,17},{9,25},{17,1},{25,9},{2,18},{10... | collective-permute-start | bytes 466952 | tf_op jit(solution)/shard_map/ppermute | solution.py:41
  24.1 11.0 %collective-permute-start.7 = (bf16[32,2432]{1,0:T(8,128)(2,1)S(1)}, bf16[32,2432]{1,0:T(8,128)(2,1)S(1)}, u32[]{:S(2)}, u32[]{:S(2)}) collective-permute-start(bf16[32,2432]{1,0:T(8,128)(2,1)S(1)} %get-tuple-element.47), channel_id=1, source_target_pairs={{0,24},{8,16},{16,8},{24,0},{1,25},{9,17},{17,9},{25,1},{2,26},{10... | collective-permute-start | bytes 466952 | tf_op jit(solution)/shard_map/ppermute | solution.py:41
  37.7 6.4 %collective-permute-start.8 = (bf16[128,512]{1,0:T(8,128)(2,1)S(1)}, bf16[128,512]{1,0:T(8,128)(2,1)S(1)}, u32[]{:S(2)}, u32[]{:S(2)}) collective-permute-start(bf16[128,512]{1,0:T(8,128)(2,1)S(1)} %get-tuple-element.53.base), channel_id=1, source_target_pairs={{0,4},{4,0},{1,5},{5,1},{2,6},{6,2},{3,7},{7,3},{8,12},{12,8},{9,1... | collective-permute-start | bytes 393224 | tf_op jit(solution)/shard_map/ppermute | solution.py:27
  44.1 8.2 %collective-permute-start.11 = (bf16[128,512]{1,0:T(8,128)(2,1)S(1)}, bf16[128,512]{1,0:T(8,128)(2,1)S(1)}, u32[]{:S(2)}, u32[]{:S(2)}) collective-permute-start(bf16[128,512]{1,0:T(8,128)(2,1)S(1)} %mix.1.refs_0_), channel_id=1, source_target_pairs={{0,24},{8,16},{16,8},{24,0},{1,25},{9,17},{17,9},{25,1},{2,26},{10... | collective-permute-start | bytes 393224 | tf_op jit(solution)/shard_map/ppermute | solution.py:41
  46.6 10.1 %collective-permute-start.10 = (bf16[128,512]{1,0:T(8,128)(2,1)S(1)}, bf16[128,512]{1,0:T(8,128)(2,1)S(1)}, u32[]{:S(2)}, u32[]{:S(2)}) collective-permute-start(bf16[128,512]{1,0:T(8,128)(2,1)S(1)} %mix.1.refs_0_), channel_id=1, source_target_pairs={{0,16},{8,24},{16,0},{24,8},{1,17},{9,25},{17,1},{25,9},{2,18},{10... | collective-permute-start | bytes 393224 | tf_op jit(solution)/shard_map/ppermute | solution.py:41
  48.0 8.8 %collective-permute-start.9 = (bf16[128,512]{1,0:T(8,128)(2,1)S(1)}, bf16[128,512]{1,0:T(8,128)(2,1)S(1)}, u32[]{:S(2)}, u32[]{:S(2)}) collective-permute-start(bf16[128,512]{1,0:T(8,128)(2,1)S(1)} %mix.1.refs_0_), channel_id=1, source_target_pairs={{0,8},{8,0},{16,24},{24,16},{1,9},{9,1},{17,25},{25,17},{2,10},{10... | collective-permute-start | bytes 393224 | tf_op jit(solution)/shard_map/ppermute | solution.py:41
  58.6 2.0 %collective-permute-start.12 = (bf16[128,2048]{1,0:T(8,128)(2,1)S(1)}, bf16[128,2048]{1,0:T(8,128)(2,1)S(1)}, u32[]{:S(2)}, u32[]{:S(2)}) collective-permute-start(bf16[128,2048]{1,0:T(8,128)(2,1)S(1)} %get-tuple-element.57.own), channel_id=1, source_target_pairs={{0,1},{1,0},{2,3},{3,2},{4,5},{5,4},{6,7},{7,6},{8,9},{9,8},{10,11... | collective-permute-start | bytes 1572872 | tf_op jit(solution)/shard_map/ppermute | solution.py:67
  75.4 2.0 %collective-permute-start.13 = (bf16[128,2048]{1,0:T(8,128)(2,1)S(1)}, bf16[128,2048]{1,0:T(8,128)(2,1)S(1)}, u32[]{:S(2)}, u32[]{:S(2)}) collective-permute-start(bf16[128,2048]{1,0:T(8,128)(2,1)S(1)} %get-tuple-element.61), channel_id=1, source_target_pairs={{0,1},{1,0},{2,3},{3,2},{4,5},{5,4},{6,7},{7,6},{8,9},{9,8},{10,11... | collective-permute-start | bytes 1572872 | tf_op jit(solution)/shard_map/ppermute | solution.py:67
  78.6 7.8 %collective-permute-start.14 = (bf16[16,1280]{1,0:T(8,128)(2,1)S(1)}, bf16[16,1280]{1,0:T(8,128)(2,1)S(1)}, u32[]{:S(2)}, u32[]{:S(2)}) collective-permute-start(bf16[16,1280]{1,0:T(8,128)(2,1)S(1)} %get-tuple-element.64), channel_id=1, source_target_pairs={{0,4},{4,8},{8,12},{12,16},{16,20},{20,24},{24,28},{28,0},{1,5},{5... | collective-permute-start | bytes 122888 | tf_op jit(solution)/shard_map/ppermute | solution.py:731
  80.2 7.7 %collective-permute-start.15 = (bf16[16,1280]{1,0:T(8,128)(2,1)S(1)}, bf16[16,1280]{1,0:T(8,128)(2,1)S(1)}, u32[]{:S(2)}, u32[]{:S(2)}) collective-permute-start(bf16[16,1280]{1,0:T(8,128)(2,1)S(1)} %get-tuple-element.65), channel_id=1, source_target_pairs={{0,8},{4,12},{8,16},{12,20},{16,24},{20,28},{24,0},{28,4},{1,9},{5... | collective-permute-start | bytes 122888 | tf_op jit(solution)/shard_map/ppermute | solution.py:731
  80.2 8.2 %collective-permute-start.16 = (bf16[16,1280]{1,0:T(8,128)(2,1)S(1)}, bf16[16,1280]{1,0:T(8,128)(2,1)S(1)}, u32[]{:S(2)}, u32[]{:S(2)}) collective-permute-start(bf16[16,1280]{1,0:T(8,128)(2,1)S(1)} %get-tuple-element.66), channel_id=1, source_target_pairs={{0,12},{4,16},{8,20},{12,24},{16,28},{20,0},{24,4},{28,8},{1,13},{... | collective-permute-start | bytes 122888 | tf_op jit(solution)/shard_map/ppermute | solution.py:731
  82.5 6.1 %collective-permute-start.17 = (bf16[16,1280]{1,0:T(8,128)(2,1)S(1)}, bf16[16,1280]{1,0:T(8,128)(2,1)S(1)}, u32[]{:S(2)}, u32[]{:S(2)}) collective-permute-start(bf16[16,1280]{1,0:T(8,128)(2,1)S(1)} %get-tuple-element.67), channel_id=1, source_target_pairs={{0,16},{4,20},{8,24},{12,28},{16,0},{20,4},{24,8},{28,12},{1,17},{... | collective-permute-start | bytes 122888 | tf_op jit(solution)/shard_map/ppermute | solution.py:731
  84.1 5.5 %collective-permute-start.18 = (bf16[16,1280]{1,0:T(8,128)(2,1)S(1)}, bf16[16,1280]{1,0:T(8,128)(2,1)S(1)}, u32[]{:S(2)}, u32[]{:S(2)}) collective-permute-start(bf16[16,1280]{1,0:T(8,128)(2,1)S(1)} %get-tuple-element.68), channel_id=1, source_target_pairs={{0,20},{4,24},{8,28},{12,0},{16,4},{20,8},{24,12},{28,16},{1,21},{... | collective-permute-start | bytes 122888 | tf_op jit(solution)/shard_map/ppermute | solution.py:731
  86.4 4.0 %collective-permute-start.19 = (bf16[16,1280]{1,0:T(8,128)(2,1)S(1)}, bf16[16,1280]{1,0:T(8,128)(2,1)S(1)}, u32[]{:S(2)}, u32[]{:S(2)}) collective-permute-start(bf16[16,1280]{1,0:T(8,128)(2,1)S(1)} %get-tuple-element.69), channel_id=1, source_target_pairs={{0,24},{4,28},{8,0},{12,4},{16,8},{20,12},{24,16},{28,20},{1,25},{... | collective-permute-start | bytes 122888 | tf_op jit(solution)/shard_map/ppermute | solution.py:731
  87.8 4.0 %collective-permute-start.20 = (bf16[16,1280]{1,0:T(8,128)(2,1)S(1)}, bf16[16,1280]{1,0:T(8,128)(2,1)S(1)}, u32[]{:S(2)}, u32[]{:S(2)}) collective-permute-start(bf16[16,1280]{1,0:T(8,128)(2,1)S(1)} %get-tuple-element.70), channel_id=1, source_target_pairs={{0,28},{4,0},{8,4},{12,8},{16,12},{20,16},{24,20},{28,24},{1,29},{... | collective-permute-start | bytes 122888 | tf_op jit(solution)/shard_map/ppermute | solution.py:731

commit v11 on v10

--- a/solution.py
+++ b/solution.py
@@ -447,10 +447,15 @@
     quarter, width = gate_first.shape
     begin = half[0] * (2 * quarter)
     copies = []
-    for index, (source, offset) in enumerate(((gate, quarter), (up, quarter), (down, 0), (down, quarter))):
-        here = pl.ds(pl.multiple_of(begin + offset, 16), quarter)
-        target = late.at[index] if index < 2 else last.at[index - 2]
-        copies.append(pltpu.make_async_copy(source.at[here, :], target, sems.at[index]))
+    for index, source in enumerate((gate, up)):
+        here = pl.ds(pl.multiple_of(begin + quarter, 16), quarter)
+        copies.append(pltpu.make_async_copy(source.at[here, :], late.at[index], sems.at[index]))
+    parts = sems.shape[0] - 2
+    lanes = width // parts
+    for k in range(parts):
+        here = pl.ds(pl.multiple_of(begin, 16), 2 * quarter)
+        cut = pl.ds(k * lanes, lanes)
+        copies.append(pltpu.make_async_copy(down.at[here, cut], last.at[:, cut], sems.at[2 + k]))
     for copy in copies[:2]:
         copy.start()
     tokens[0:rows, :] = own[...]
@@ -468,15 +473,14 @@
     copies[0].wait()
     copies[1].wait()
     activate_hidden(late.at[0], late.at[1], 1)
-    copies[2].wait()
-    copies[3].wait()
     step = 256
-    for start in range(0, width, step):
-        here = slice(start, start + step)
-        product = jnp.dot(hidden[:, :quarter], last[0, :, here], preferred_element_type=F32)
-        product += jnp.dot(hidden[:, quarter:], last[1, :, here], preferred_element_type=F32)
-        kept[:, here] = product[0:rows, :]
-        given[:, here] = product[rows:, :].astype(BF16)
+    for k in range(parts):
+        copies[2 + k].wait()
+        for start in range(k * lanes, (k + 1) * lanes, step):
+            here = slice(start, start + step)
+            product = jnp.dot(hidden[...], last[:, here], preferred_element_type=F32)
+            kept[:, here] = product[0:rows, :]
+            given[:, here] = product[rows:, :].astype(BF16)
 
 
 def shared_experts(half, own, other, gate_first, up_first, gate, up, down):
@@ -491,8 +495,8 @@
             VMEM((2 * rows, width), BF16),
             VMEM((2 * rows, 2 * quarter), BF16),
             VMEM((2, quarter, width), BF16),
-            VMEM((2, quarter, width), BF16),
-            pltpu.SemaphoreType.DMA((4,)),
+            VMEM((2 * quarter, width), BF16),
+            pltpu.SemaphoreType.DMA((6,)),
         ],
         compiler_params=pltpu.CompilerParams(vmem_limit_bytes=36 << 20),
         cost_estimate=pl.CostEstimate(

time: 93.9 us -> 94.1 us (level)
  no operation moved by 1% of the time
where the time goes in v11:
time: 94.1 us; the launch traced here: 93.6 us
  Pallas kernels  36.9 us (39%)
  starting transfers between devices  28.6 us (30%)
  waiting for transfers between devices  21.8 us (23%)
  local copies, waits for them, and re-layouts  5.2 us (6%)
    pallas_call x1, Pallas kernels, shared_experts(): pl.pallas_call(shared_kernel, out_shape=(jax.ShapeDtypeStruct((rows, widt...  15 us
    ppermute x9, waiting for transfers between devices, exchange(): lax.ppermute(value, axis, [(i, partner(i, step, count)) for i in range(co...  14.7 us
    ppermute x9, starting transfers between devices, exchange(): lax.ppermute(value, axis, [(i, partner(i, step, count)) for i in range(co...  14.7 us
    ppermute x7, starting transfers between devices, body(): lax.ppermute(outs[s], axes, [(i, (i + s) % parts) for i in range(parts)])  9.79 us
    pallas_call x1, Pallas kernels, scan(): pl.pallas_call(functools.partial(scan_kernel, taps), out_shape=jax.ShapeD...  6.66 us
    pallas_call x1, Pallas kernels, fetch(): pl.pallas_call(functools.partial(fetch_kernel, parts, half_rows), out_sha...  5.82 us
    ppermute x3, starting transfers between devices, rotate(): lax.ppermute(value, axis, [(i, (i + steps) % count) for i in range(count)])  3.82 us
    ppermute x2, waiting for transfers between devices, swap(): lax.ppermute(value, 'doc', [(i, i + 1 - 2 * (i % 2)) for i in range(count)])  3.64 us
  transfers between devices with their start and end apart: 21, of which 10 were waited for; matrix products, arithmetic and copies ran while one was open for 5% of the time, Pallas kernels for 13%

profile of v11, /device:TPU:0, one launch (start us, length us, event | category | flops | bytes accessed | tf_op | source)
XLA Modules:
  0.0 93.6 jit_solution(8899097746932225879)
XLA Ops:
  0.0 1.0 %slice_bitcast_fusion = (bf16[32,2048]{1,0:T(8,128)(2,1)S(1)}, bf16[32,2048]{1,0:T(8,128)(2,1)S(1)}) fusion(bf16[2,32,2048]{2,1,0:T(8,128)(2,1)} %param.18), kind=kLoop, calls=%fused_computation.4 | loop fusion | bytes 524288 | tf_op jit(solution)/shard_map/squeeze | solution.py:666
  1.0 5.1 %collective-permute-start.2 = (bf16[32,2048]{1,0:T(8,128)(2,1)S(1)}, bf16[32,2048]{1,0:T(8,128)(2,1)S(1)}, u32[]{:S(2)}, u32[]{:S(2)}) collective-permute-start(bf16[32,2048]{1,0:T(8,128)(2,1)S(1)} %get-tuple-element.72.refs_0_), channel_id=1, source_target_pairs={{0,24},{8,16},{16,8},{24,0},{1,25},{9,17},{17,9},{25,1},{2,26},{10... | collective-permute-start | bytes 393224 | tf_op jit(solution)/shard_map/ppermute | solution.py:41
  6.1 0.0 collective-permute-start.1
  6.1 0.6 collective-permute-start
  6.7 0.7 convert_element_type.13
  7.4 0.1 copy.20
  7.5 1.7 %collective-permute-start.4 = (bf16[16,128]{1,0:T(8,128)(2,1)S(1)}, bf16[16,128]{1,0:T(8,128)(2,1)S(1)}, u32[]{:S(2)}, u32[]{:S(2)}) collective-permute-start(bf16[16,128]{1,0:T(8,128)(2,1)S(1)} %pad.14.routes), channel_id=1, source_target_pairs={{0,4},{4,0},{1,5},{5,1},{2,6},{6,2},{3,7},{7,3},{8,12},{12,8},{9,1... | collective-permute-start | bytes 12296 | tf_op jit(solution)/shard_map/ppermute | solution.py:27
  9.2 0.1 stack.93
  9.3 0.1 pad_add_fusion.spots
  9.4 0.8 constant_dynamic-slice_fusion
  10.2 0.1 pad_add_fusion.1.places
  10.3 0.1 concatenate.38.places
  10.4 0.7 pad.12.router
  11.2 0.7 pad.13.gain
  11.9 0.1 stack.85.targets
  12.0 1.6 %concatenate.37.params = f32[16,2048]{1,0:T(8,128)S(1)} concatenate(f32[4,2048]{1,0:T(4,128)} %param.21, f32[1,2048]{1,0:T(1,128)} %bitcast.33, f32[1,2048]{1,0:T(1,128)} %bitcast.34, f32[1,2048]{1,0:T(1,128)} %bitcast.35, f32[1,2048]{1,0:T(1,128)S(1)} %slice.33, f32[5,2048]{1,0:T(8,128)S(1)} %broadcast_in_dim.24, bf16[3,2048]{1,0:T(4,128)(2,1)} %param.19), dimensions={0} | concatenate | bytes 249856 | tf_op jit(solution)/shard_map/concatenate | solution.py:689
  13.6 0.0 collective-permute-done.4
  13.6 0.0 collective-permute-done.2.refs_3_
  13.6 3.6 %collective-permute-done.1.refs_2_ = bf16[32,2048]{1,0:T(8,128)(2,1)S(1)} collective-permute-done((bf16[32,2048]{1,0:T(8,128)(2,1)S(1)}, bf16[32,2048]{1,0:T(8,128)(2,1)S(1)}, u32[]{:S(2)}, u32[]{:S(2)}) %collective-permute-start.1) | collective-permute-done | bytes 131104 | tf_op jit(solution)/shard_map/ppermute | solution.py:41
  17.2 0.0 collective-permute-done.refs_1_
  17.2 2.1 %activate.1 = (bf16[128,2048]{1,0:T(8,128)(2,1)S(1)}, f32[160,128]{1,0:T(8,128)S(1)}) custom-call(s32[4]{0:T(128)S(1)} %pad_add_fusion.1.places, f32[16,2048]{1,0:T(8,128)S(1)} %concatenate.37.params, bf16[160,2048]{1,0:T(8,128)(2,1)} %select.44, bf16[32,2048]{1,0:T(8,128)(2,1)S(1)} %get-tuple-element.72.refs_0_, ...), custom_call_target="tpu_custom_call" | custom-call | flops 83886080 | bytes 1048576 | tf_op jit(solution)/shard_map/activate/pallas_call | solution.py:120
  19.3 1.6 %collective-permute-start.3 = (f32[160,128]{1,0:T(8,128)S(1)}, f32[160,128]{1,0:T(8,128)S(1)}, u32[]{:S(2)}, u32[]{:S(2)}) collective-permute-start(f32[160,128]{1,0:T(8,128)S(1)} %get-tuple-element.43.own), channel_id=1, source_target_pairs={{0,4},{4,0},{1,5},{5,1},{2,6},{6,2},{3,7},{7,3},{8,12},{12,8},{9,1... | collective-permute-start | bytes 245768 | tf_op jit(solution)/shard_map/ppermute | solution.py:27
  21.0 0.1 collective-permute-start.5
  21.0 3.0 %collective-permute-start.6 = (bf16[32,2432]{1,0:T(8,128)(2,1)S(1)}, bf16[32,2432]{1,0:T(8,128)(2,1)S(1)}, u32[]{:S(2)}, u32[]{:S(2)}) collective-permute-start(bf16[32,2432]{1,0:T(8,128)(2,1)S(1)} %get-tuple-element.46), channel_id=1, source_target_pairs={{0,16},{8,24},{16,0},{24,8},{1,17},{9,25},{17,1},{25,9},{2,18},{10... | collective-permute-start | bytes 466952 | tf_op jit(solution)/shard_map/ppermute | solution.py:41
  24.1 1.3 %collective-permute-start.7 = (bf16[32,2432]{1,0:T(8,128)(2,1)S(1)}, bf16[32,2432]{1,0:T(8,128)(2,1)S(1)}, u32[]{:S(2)}, u32[]{:S(2)}) collective-permute-start(bf16[32,2432]{1,0:T(8,128)(2,1)S(1)} %get-tuple-element.47), channel_id=1, source_target_pairs={{0,24},{8,16},{16,8},{24,0},{1,25},{9,17},{17,9},{25,1},{2,26},{10... | collective-permute-start | bytes 466952 | tf_op jit(solution)/shard_map/ppermute | solution.py:41
  25.4 0.0 collective-permute-done.3.other
  25.4 6.7 %scan.1.value_in = f32[128,2048]{1,0:T(8,128)S(1)} custom-call(f32[160,128]{1,0:T(8,128)S(1)} %get-tuple-element.43.own, f32[160,128]{1,0:T(8,128)S(1)} %collective-permute-done.3.other, bf16[128,2048]{1,0:T(8,128)(2,1)S(1)} %get-tuple-element.44.active, f32[16,2048]{1,0:T(8,128)S(1)} %concatenate.37.params, f32[16,2048]{1,0:T(8,128)} %log_rate_hbm.1, ...), custom_call_target="tpu_custom_call" | custom-call | flops 12582912000 | bytes 2097152 | tf_op jit(solution)/shard_map/scan/pallas_call | solution.py:242
  32.1 0.0 collective-permute-done.5.refs_1_
  32.1 2.9 %collective-permute-done.6.refs_2_ = bf16[32,2432]{1,0:T(8,128)(2,1)S(1)} collective-permute-done((bf16[32,2432]{1,0:T(8,128)(2,1)S(1)}, bf16[32,2432]{1,0:T(8,128)(2,1)S(1)}, u32[]{:S(2)}, u32[]{:S(2)}) %collective-permute-start.6) | collective-permute-done | bytes 155680 | tf_op jit(solution)/shard_map/ppermute | solution.py:41
  35.0 0.0 collective-permute-done.7.refs_3_
  35.0 2.6 %project.1 = (bf16[128,512]{1,0:T(8,128)(2,1)S(1)}, bf16[128,128]{1,0:T(8,128)(2,1)S(1)}) custom-call(s32[5]{0:T(128)S(1)} %concatenate.38.places, f32[128,2048]{1,0:T(8,128)S(1)} %scan.1.value_in, bf16[2048,512]{1,0:T(8,128)(2,1)} %weight_hbm.1, bf16[32,2432]{1,0:T(8,128)(2,1)S(1)} %get-tuple-element.76.refs_0_, ...), custom_call_target="tpu_custom_call" | custom-call | flops 268435456 | bytes 2097152 | tf_op jit(solution)/shard_map/project/pallas_call | solution.py:310
  37.7 0.6 collective-permute-start.8
  38.2 5.8 %fetch.1 = (bf16[1792,2048]{1,0:T(8,128)(2,1)S(1)}, bf16[1792,2048]{1,0:T(8,128)(2,1)S(1)}, s32[1]{0:T(128)}) custom-call(s32[1]{0:T(128)} %bitcast.28.half, bf16[7168,2048]{1,0:T(8,128)(2,1)} %gate.1, bf16[7168,2048]{1,0:T(8,128)(2,1)} %up.1), custom_call_target="tpu_custom_call" | custom-call | bytes 29360128 | tf_op jit(solution)/shard_map/fetch/pallas_call | solution.py:431
  44.1 0.0 collective-permute-done.8.summand
  44.1 2.5 %collective-permute-start.11 = (bf16[128,512]{1,0:T(8,128)(2,1)S(1)}, bf16[128,512]{1,0:T(8,128)(2,1)S(1)}, u32[]{:S(2)}, u32[]{:S(2)}) collective-permute-start(bf16[128,512]{1,0:T(8,128)(2,1)S(1)} %mix.1.refs_0_), channel_id=1, source_target_pairs={{0,24},{8,16},{16,8},{24,0},{1,25},{9,17},{17,9},{25,1},{2,26},{10... | collective-permute-start | bytes 393224 | tf_op jit(solution)/shard_map/ppermute | solution.py:41
  46.6 1.4 %collective-permute-start.10 = (bf16[128,512]{1,0:T(8,128)(2,1)S(1)}, bf16[128,512]{1,0:T(8,128)(2,1)S(1)}, u32[]{:S(2)}, u32[]{:S(2)}) collective-permute-start(bf16[128,512]{1,0:T(8,128)(2,1)S(1)} %mix.1.refs_0_), channel_id=1, source_target_pairs={{0,16},{8,24},{16,0},{24,8},{1,17},{9,25},{17,1},{25,9},{2,18},{10... | collective-permute-start | bytes 393224 | tf_op jit(solution)/shard_map/ppermute | solution.py:41
  48.0 0.5 collective-permute-start.9
  48.6 3.8 %collective-permute-done.11.refs_3_ = bf16[128,512]{1,0:T(8,128)(2,1)S(1)} collective-permute-done((bf16[128,512]{1,0:T(8,128)(2,1)S(1)}, bf16[128,512]{1,0:T(8,128)(2,1)S(1)}, u32[]{:S(2)}, u32[]{:S(2)}) %collective-permute-start.11) | collective-permute-done | bytes 131104 | tf_op jit(solution)/shard_map/ppermute | solution.py:41
  52.3 4.4 %collective-permute-done.10.refs_2_ = bf16[128,512]{1,0:T(8,128)(2,1)S(1)} collective-permute-done((bf16[128,512]{1,0:T(8,128)(2,1)S(1)}, bf16[128,512]{1,0:T(8,128)(2,1)S(1)}, u32[]{:S(2)}, u32[]{:S(2)}) %collective-permute-start.10) | collective-permute-done | bytes 131104 | tf_op jit(solution)/shard_map/ppermute | solution.py:41
  56.8 0.0 collective-permute-done.9.refs_1_
  56.8 1.8 %norm.1 = (bf16[128,2048]{1,0:T(8,128)(2,1)S(1)}, f32[128,128]{1,0:T(8,128)S(1)}, bf16[16,2048]{1,0:T(8,128)(2,1)S(1)}) custom-call(s32[4]{0:T(128)S(1)} %pad_add_fusion.1.places, s32[2]{0:T(128)S(1)} %pad_add_fusion.spots, f32[8,2048]{1,0:T(8,128)S(1)} %pad.13.gain, bf16[16,2048]{1,0:T(8,128)(2,1)S(1)} %pad.12.router, ...), custom_call_target="tpu_custom_call" | custom-call | tf_op jit(solution)/shard_map/norm/pallas_call | solution.py:389
  58.6 0.1 collective-permute-start.12
  58.7 1.9 %collective-permute-done.12.other = bf16[128,2048]{1,0:T(8,128)(2,1)S(1)} collective-permute-done((bf16[128,2048]{1,0:T(8,128)(2,1)S(1)}, bf16[128,2048]{1,0:T(8,128)(2,1)S(1)}, u32[]{:S(2)}, u32[]{:S(2)}) %collective-permute-start.12) | collective-permute-done | bytes 524320 | tf_op jit(solution)/shard_map/ppermute | solution.py:67
  60.6 15.0 %experts.1 = (f32[128,2048]{1,0:T(8,128)S(1)}, bf16[128,2048]{1,0:T(8,128)(2,1)S(1)}) custom-call(s32[1]{0:T(128)} %get-tuple-element.56.half, bf16[128,2048]{1,0:T(8,128)(2,1)S(1)} %get-tuple-element.57.own, bf16[128,2048]{1,0:T(8,128)(2,1)S(1)} %collective-permute-done.12.other, bf16[1792,2048]{1,0:T(8,128)(2,1)S(1)} %get-tuple-element.58.gate_first, ...), custom_call_target="tpu_custom_call" | custom-call | flops 11274289152 | bytes 29360128 | tf_op jit(solution)/shard_map/experts/pallas_call | solution.py:489
  75.6 0.2 collective-permute-start.13
  75.8 1.7 %collective-permute-done.13.other = bf16[128,2048]{1,0:T(8,128)(2,1)S(1)} collective-permute-done((bf16[128,2048]{1,0:T(8,128)(2,1)S(1)}, bf16[128,2048]{1,0:T(8,128)(2,1)S(1)}, u32[]{:S(2)}, u32[]{:S(2)}) %collective-permute-start.13) | collective-permute-done | bytes 524320 | tf_op jit(solution)/shard_map/ppermute | solution.py:67
  77.5 1.2 %combine.1 = (bf16[16,1280]{1,0:T(8,128)(2,1)S(1)}, bf16[16,1280]{1,0:T(8,128)(2,1)S(1)}, bf16[16,1280]{1,0:T(8,128)(2,1)S(1)}, bf16[16,1280]{1,0:T(8,128)(2,1)S...) custom-call(s32[8]{0:T(128)S(1)} %stack.85.targets, ...), custom_call_target="tpu_custom_call" | custom-call | tf_op jit(solution)/shard_map/combine/pallas_call | solution.py:590
  78.7 1.6 %collective-permute-start.14 = (bf16[16,1280]{1,0:T(8,128)(2,1)S(1)}, bf16[16,1280]{1,0:T(8,128)(2,1)S(1)}, u32[]{:S(2)}, u32[]{:S(2)}) collective-permute-start(bf16[16,1280]{1,0:T(8,128)(2,1)S(1)} %get-tuple-element.64), channel_id=1, source_target_pairs={{0,4},{4,8},{8,12},{12,16},{16,20},{20,24},{24,28},{28,0},{1,5},{5... | collective-permute-start | bytes 122888 | tf_op jit(solution)/shard_map/ppermute | solution.py:735
  80.3 0.0 collective-permute-start.15
  80.3 2.3 %collective-permute-start.16 = (bf16[16,1280]{1,0:T(8,128)(2,1)S(1)}, bf16[16,1280]{1,0:T(8,128)(2,1)S(1)}, u32[]{:S(2)}, u32[]{:S(2)}) collective-permute-start(bf16[16,1280]{1,0:T(8,128)(2,1)S(1)} %get-tuple-element.66), channel_id=1, source_target_pairs={{0,12},{4,16},{8,20},{12,24},{16,28},{20,0},{24,4},{28,8},{1,13},{... | collective-permute-start | bytes 122888 | tf_op jit(solution)/shard_map/ppermute | solution.py:735
  82.7 1.6 %collective-permute-start.17 = (bf16[16,1280]{1,0:T(8,128)(2,1)S(1)}, bf16[16,1280]{1,0:T(8,128)(2,1)S(1)}, u32[]{:S(2)}, u32[]{:S(2)}) collective-permute-start(bf16[16,1280]{1,0:T(8,128)(2,1)S(1)} %get-tuple-element.67), channel_id=1, source_target_pairs={{0,16},{4,20},{8,24},{12,28},{16,0},{20,4},{24,8},{28,12},{1,17},{... | collective-permute-start | bytes 122888 | tf_op jit(solution)/shard_map/ppermute | solution.py:735
  84.2 2.3 %collective-permute-start.18 = (bf16[16,1280]{1,0:T(8,128)(2,1)S(1)}, bf16[16,1280]{1,0:T(8,128)(2,1)S(1)}, u32[]{:S(2)}, u32[]{:S(2)}) collective-permute-start(bf16[16,1280]{1,0:T(8,128)(2,1)S(1)} %get-tuple-element.68), channel_id=1, source_target_pairs={{0,20},{4,24},{8,28},{12,0},{16,4},{20,8},{24,12},{28,16},{1,21},{... | collective-permute-start | bytes 122888 | tf_op jit(solution)/shard_map/ppermute | solution.py:735
  86.5 0.0 collective-permute-done.14.refs_1_
  86.5 1.4 %collective-permute-start.19 = (bf16[16,1280]{1,0:T(8,128)(2,1)S(1)}, bf16[16,1280]{1,0:T(8,128)(2,1)S(1)}, u32[]{:S(2)}, u32[]{:S(2)}) collective-permute-start(bf16[16,1280]{1,0:T(8,128)(2,1)S(1)} %get-tuple-element.69), channel_id=1, source_target_pairs={{0,24},{4,28},{8,0},{12,4},{16,8},{20,12},{24,16},{28,20},{1,25},{... | collective-permute-start | bytes 122888 | tf_op jit(solution)/shard_map/ppermute | solution.py:735
  88.0 0.0 collective-permute-done.15.refs_2_
  88.0 0.6 collective-permute-start.20
  88.5 0.0 collective-permute-done.16.refs_3_
  88.5 0.3 collective-permute-done.17.refs_4_
  88.8 0.9 collective-permute-done.18.refs_5_
  89.7 0.8 collective-permute-done.19.refs_6_
  90.5 1.4 %collective-permute-done.20.refs_7_ = bf16[16,1280]{1,0:T(8,128)(2,1)S(1)} collective-permute-done((bf16[16,1280]{1,0:T(8,128)(2,1)S(1)}, bf16[16,1280]{1,0:T(8,128)(2,1)S(1)}, u32[]{:S(2)}, u32[]{:S(2)}) %collective-permute-start.20) | collective-permute-done | bytes 40992 | tf_op jit(solution)/shard_map/ppermute | solution.py:735
  92.0 1.6 %unpack.1 = bf16[16,2048]{1,0:T(8,128)(2,1)} custom-call(s32[8]{0:T(128)S(1)} %and_select_fusion.named_by, bf16[16,2048]{1,0:T(8,128)(2,1)S(1)} %get-tuple-element.54.mixed, bf16[16,128]{1,0:T(8,128)(2,1)S(1)} %pad.14.routes, bf16[16,1280]{1,0:T(8,128)(2,1)S(1)} %get-tuple-element.63.refs_0_, bf16[16,1280]{1,0:T(8,128)(2,1)S(1)} %collective-permute-done.14.refs_1_, ...), custom_call_target="tpu_custom_call" | custom-call | tf_op jit(solution)/shard_map/unpack/pallas_call | solution.py:632
  (7 shorter events, 0.1 us)
Async XLA Ops:
  1.0 12.6 %collective-permute-start.2 = (bf16[32,2048]{1,0:T(8,128)(2,1)S(1)}, bf16[32,2048]{1,0:T(8,128)(2,1)S(1)}, u32[]{:S(2)}, u32[]{:S(2)}) collective-permute-start(bf16[32,2048]{1,0:T(8,128)(2,1)S(1)} %get-tuple-element.72.refs_0_), channel_id=1, source_target_pairs={{0,24},{8,16},{16,8},{24,0},{1,25},{9,17},{17,9},{25,1},{2,26},{10... | collective-permute-start | bytes 393224 | tf_op jit(solution)/shard_map/ppermute | solution.py:41
  6.1 11.1 %collective-permute-start.1 = (bf16[32,2048]{1,0:T(8,128)(2,1)S(1)}, bf16[32,2048]{1,0:T(8,128)(2,1)S(1)}, u32[]{:S(2)}, u32[]{:S(2)}) collective-permute-start(bf16[32,2048]{1,0:T(8,128)(2,1)S(1)} %get-tuple-element.72.refs_0_), channel_id=1, source_target_pairs={{0,16},{8,24},{16,0},{24,8},{1,17},{9,25},{17,1},{25,9},{2,18},{10... | collective-permute-start | bytes 393224 | tf_op jit(solution)/shard_map/ppermute | solution.py:41
  6.1 11.1 %collective-permute-start = (bf16[32,2048]{1,0:T(8,128)(2,1)S(1)}, bf16[32,2048]{1,0:T(8,128)(2,1)S(1)}, u32[]{:S(2)}, u32[]{:S(2)}) collective-permute-start(bf16[32,2048]{1,0:T(8,128)(2,1)S(1)} %get-tuple-element.72.refs_0_), channel_id=1, source_target_pairs={{0,8},{8,0},{16,24},{24,16},{1,9},{9,1},{17,25},{25,17},{2,10},{10... | collective-permute-start | bytes 393224 | tf_op jit(solution)/shard_map/ppermute | solution.py:41
  7.5 6.0 %collective-permute-start.4 = (bf16[16,128]{1,0:T(8,128)(2,1)S(1)}, bf16[16,128]{1,0:T(8,128)(2,1)S(1)}, u32[]{:S(2)}, u32[]{:S(2)}) collective-permute-start(bf16[16,128]{1,0:T(8,128)(2,1)S(1)} %pad.14.routes), channel_id=1, source_target_pairs={{0,4},{4,0},{1,5},{5,1},{2,6},{6,2},{3,7},{7,3},{8,12},{12,8},{9,1... | collective-permute-start | bytes 12296 | tf_op jit(solution)/shard_map/ppermute | solution.py:27
  19.3 6.1 %collective-permute-start.3 = (f32[160,128]{1,0:T(8,128)S(1)}, f32[160,128]{1,0:T(8,128)S(1)}, u32[]{:S(2)}, u32[]{:S(2)}) collective-permute-start(f32[160,128]{1,0:T(8,128)S(1)} %get-tuple-element.43.own), channel_id=1, source_target_pairs={{0,4},{4,0},{1,5},{5,1},{2,6},{6,2},{3,7},{7,3},{8,12},{12,8},{9,1... | collective-permute-start | bytes 245768 | tf_op jit(solution)/shard_map/ppermute | solution.py:27
  21.0 11.1 %collective-permute-start.5 = (bf16[32,2432]{1,0:T(8,128)(2,1)S(1)}, bf16[32,2432]{1,0:T(8,128)(2,1)S(1)}, u32[]{:S(2)}, u32[]{:S(2)}) collective-permute-start(bf16[32,2432]{1,0:T(8,128)(2,1)S(1)} %get-tuple-element.45), channel_id=1, source_target_pairs={{0,8},{8,0},{16,24},{24,16},{1,9},{9,1},{17,25},{25,17},{2,10},{10... | collective-permute-start | bytes 466952 | tf_op jit(solution)/shard_map/ppermute | solution.py:41
  21.0 14.0 %collective-permute-start.6 = (bf16[32,2432]{1,0:T(8,128)(2,1)S(1)}, bf16[32,2432]{1,0:T(8,128)(2,1)S(1)}, u32[]{:S(2)}, u32[]{:S(2)}) collective-permute-start(bf16[32,2432]{1,0:T(8,128)(2,1)S(1)} %get-tuple-element.46), channel_id=1, source_target_pairs={{0,16},{8,24},{16,0},{24,8},{1,17},{9,25},{17,1},{25,9},{2,18},{10... | collective-permute-start | bytes 466952 | tf_op jit(solution)/shard_map/ppermute | solution.py:41
  24.1 11.0 %collective-permute-start.7 = (bf16[32,2432]{1,0:T(8,128)(2,1)S(1)}, bf16[32,2432]{1,0:T(8,128)(2,1)S(1)}, u32[]{:S(2)}, u32[]{:S(2)}) collective-permute-start(bf16[32,2432]{1,0:T(8,128)(2,1)S(1)} %get-tuple-element.47), channel_id=1, source_target_pairs={{0,24},{8,16},{16,8},{24,0},{1,25},{9,17},{17,9},{25,1},{2,26},{10... | collective-permute-start | bytes 466952 | tf_op jit(solution)/shard_map/ppermute | solution.py:41
  37.7 6.4 %collective-permute-start.8 = (bf16[128,512]{1,0:T(8,128)(2,1)S(1)}, bf16[128,512]{1,0:T(8,128)(2,1)S(1)}, u32[]{:S(2)}, u32[]{:S(2)}) collective-permute-start(bf16[128,512]{1,0:T(8,128)(2,1)S(1)} %get-tuple-element.53.base), channel_id=1, source_target_pairs={{0,4},{4,0},{1,5},{5,1},{2,6},{6,2},{3,7},{7,3},{8,12},{12,8},{9,1... | collective-permute-start | bytes 393224 | tf_op jit(solution)/shard_map/ppermute | solution.py:27
  44.1 8.2 %collective-permute-start.11 = (bf16[128,512]{1,0:T(8,128)(2,1)S(1)}, bf16[128,512]{1,0:T(8,128)(2,1)S(1)}, u32[]{:S(2)}, u32[]{:S(2)}) collective-permute-start(bf16[128,512]{1,0:T(8,128)(2,1)S(1)} %mix.1.refs_0_), channel_id=1, source_target_pairs={{0,24},{8,16},{16,8},{24,0},{1,25},{9,17},{17,9},{25,1},{2,26},{10... | collective-permute-start | bytes 393224 | tf_op jit(solution)/shard_map/ppermute | solution.py:41
  46.6 10.1 %collective-permute-start.10 = (bf16[128,512]{1,0:T(8,128)(2,1)S(1)}, bf16[128,512]{1,0:T(8,128)(2,1)S(1)}, u32[]{:S(2)}, u32[]{:S(2)}) collective-permute-start(bf16[128,512]{1,0:T(8,128)(2,1)S(1)} %mix.1.refs_0_), channel_id=1, source_target_pairs={{0,16},{8,24},{16,0},{24,8},{1,17},{9,25},{17,1},{25,9},{2,18},{10... | collective-permute-start | bytes 393224 | tf_op jit(solution)/shard_map/ppermute | solution.py:41
  48.0 8.8 %collective-permute-start.9 = (bf16[128,512]{1,0:T(8,128)(2,1)S(1)}, bf16[128,512]{1,0:T(8,128)(2,1)S(1)}, u32[]{:S(2)}, u32[]{:S(2)}) collective-permute-start(bf16[128,512]{1,0:T(8,128)(2,1)S(1)} %mix.1.refs_0_), channel_id=1, source_target_pairs={{0,8},{8,0},{16,24},{24,16},{1,9},{9,1},{17,25},{25,17},{2,10},{10... | collective-permute-start | bytes 393224 | tf_op jit(solution)/shard_map/ppermute | solution.py:41
  58.6 2.0 %collective-permute-start.12 = (bf16[128,2048]{1,0:T(8,128)(2,1)S(1)}, bf16[128,2048]{1,0:T(8,128)(2,1)S(1)}, u32[]{:S(2)}, u32[]{:S(2)}) collective-permute-start(bf16[128,2048]{1,0:T(8,128)(2,1)S(1)} %get-tuple-element.57.own), channel_id=1, source_target_pairs={{0,1},{1,0},{2,3},{3,2},{4,5},{5,4},{6,7},{7,6},{8,9},{9,8},{10,11... | collective-permute-start | bytes 1572872 | tf_op jit(solution)/shard_map/ppermute | solution.py:67
  75.6 2.0 %collective-permute-start.13 = (bf16[128,2048]{1,0:T(8,128)(2,1)S(1)}, bf16[128,2048]{1,0:T(8,128)(2,1)S(1)}, u32[]{:S(2)}, u32[]{:S(2)}) collective-permute-start(bf16[128,2048]{1,0:T(8,128)(2,1)S(1)} %get-tuple-element.61), channel_id=1, source_target_pairs={{0,1},{1,0},{2,3},{3,2},{4,5},{5,4},{6,7},{7,6},{8,9},{9,8},{10,11... | collective-permute-start | bytes 1572872 | tf_op jit(solution)/shard_map/ppermute | solution.py:67
  78.7 7.8 %collective-permute-start.14 = (bf16[16,1280]{1,0:T(8,128)(2,1)S(1)}, bf16[16,1280]{1,0:T(8,128)(2,1)S(1)}, u32[]{:S(2)}, u32[]{:S(2)}) collective-permute-start(bf16[16,1280]{1,0:T(8,128)(2,1)S(1)} %get-tuple-element.64), channel_id=1, source_target_pairs={{0,4},{4,8},{8,12},{12,16},{16,20},{20,24},{24,28},{28,0},{1,5},{5... | collective-permute-start | bytes 122888 | tf_op jit(solution)/shard_map/ppermute | solution.py:735
  80.3 7.7 %collective-permute-start.15 = (bf16[16,1280]{1,0:T(8,128)(2,1)S(1)}, bf16[16,1280]{1,0:T(8,128)(2,1)S(1)}, u32[]{:S(2)}, u32[]{:S(2)}) collective-permute-start(bf16[16,1280]{1,0:T(8,128)(2,1)S(1)} %get-tuple-element.65), channel_id=1, source_target_pairs={{0,8},{4,12},{8,16},{12,20},{16,24},{20,28},{24,0},{28,4},{1,9},{5... | collective-permute-start | bytes 122888 | tf_op jit(solution)/shard_map/ppermute | solution.py:735
  80.3 8.2 %collective-permute-start.16 = (bf16[16,1280]{1,0:T(8,128)(2,1)S(1)}, bf16[16,1280]{1,0:T(8,128)(2,1)S(1)}, u32[]{:S(2)}, u32[]{:S(2)}) collective-permute-start(bf16[16,1280]{1,0:T(8,128)(2,1)S(1)} %get-tuple-element.66), channel_id=1, source_target_pairs={{0,12},{4,16},{8,20},{12,24},{16,28},{20,0},{24,4},{28,8},{1,13},{... | collective-permute-start | bytes 122888 | tf_op jit(solution)/shard_map/ppermute | solution.py:735
  82.7 6.1 %collective-permute-start.17 = (bf16[16,1280]{1,0:T(8,128)(2,1)S(1)}, bf16[16,1280]{1,0:T(8,128)(2,1)S(1)}, u32[]{:S(2)}, u32[]{:S(2)}) collective-permute-start(bf16[16,1280]{1,0:T(8,128)(2,1)S(1)} %get-tuple-element.67), channel_id=1, source_target_pairs={{0,16},{4,20},{8,24},{12,28},{16,0},{20,4},{24,8},{28,12},{1,17},{... | collective-permute-start | bytes 122888 | tf_op jit(solution)/shard_map/ppermute | solution.py:735
  84.2 5.5 %collective-permute-start.18 = (bf16[16,1280]{1,0:T(8,128)(2,1)S(1)}, bf16[16,1280]{1,0:T(8,128)(2,1)S(1)}, u32[]{:S(2)}, u32[]{:S(2)}) collective-permute-start(bf16[16,1280]{1,0:T(8,128)(2,1)S(1)} %get-tuple-element.68), channel_id=1, source_target_pairs={{0,20},{4,24},{8,28},{12,0},{16,4},{20,8},{24,12},{28,16},{1,21},{... | collective-permute-start | bytes 122888 | tf_op jit(solution)/shard_map/ppermute | solution.py:735
  86.5 4.0 %collective-permute-start.19 = (bf16[16,1280]{1,0:T(8,128)(2,1)S(1)}, bf16[16,1280]{1,0:T(8,128)(2,1)S(1)}, u32[]{:S(2)}, u32[]{:S(2)}) collective-permute-start(bf16[16,1280]{1,0:T(8,128)(2,1)S(1)} %get-tuple-element.69), channel_id=1, source_target_pairs={{0,24},{4,28},{8,0},{12,4},{16,8},{20,12},{24,16},{28,20},{1,25},{... | collective-permute-start | bytes 122888 | tf_op jit(solution)/shard_map/ppermute | solution.py:735
  88.0 4.0 %collective-permute-start.20 = (bf16[16,1280]{1,0:T(8,128)(2,1)S(1)}, bf16[16,1280]{1,0:T(8,128)(2,1)S(1)}, u32[]{:S(2)}, u32[]{:S(2)}) collective-permute-start(bf16[16,1280]{1,0:T(8,128)(2,1)S(1)} %get-tuple-element.70), channel_id=1, source_target_pairs={{0,28},{4,0},{8,4},{12,8},{16,12},{20,16},{24,20},{28,24},{1,29},{... | collective-permute-start | bytes 122888 | tf_op jit(solution)/shard_map/ppermute | solution.py:735

commit v12 on v10

--- a/solution.py
+++ b/solution.py
@@ -238,7 +238,7 @@
 def scan(own, other, active, params, taps, log_rate, step_weight, state_in):
     tokens, channels = active.shape
     state_size = log_rate.shape[0]
-    folded = (state_size * channels // LANES, LANES)
+    folded = (state_size * channels // LANES + 8, LANES)
     return pl.pallas_call(
         functools.partial(scan_kernel, taps),
         out_shape=jax.ShapeDtypeStruct((tokens, channels), F32),
@@ -246,8 +246,8 @@
         out_specs=WHOLE,
         scratch_shapes=[
             VMEM(own.shape, F32),
-            VMEM((tokens * channels // LANES, LANES), F32),
-            VMEM((tokens * channels // LANES, LANES), F32),
+            VMEM((tokens * channels // LANES + 8, LANES), F32),
+            VMEM((tokens * channels // LANES + 8, LANES), F32),
             VMEM(folded, F32),
             VMEM(folded, F32),
             SMEM((2 * state_size, tokens), F32),

time: 93.9 us -> 93.9 us (level)
  no operation moved by 1% of the time
where the time goes in v12:
time: 93.9 us; the launch traced here: 93.4 us
  Pallas kernels  36.7 us (39%)
  starting transfers between devices  28.5 us (30%)
  waiting for transfers between devices  21.9 us (23%)
  local copies, waits for them, and re-layouts  5.2 us (6%)
    pallas_call x1, Pallas kernels, shared_experts(): pl.pallas_call(shared_kernel, out_shape=(jax.ShapeDtypeStruct((rows, widt...  14.8 us
    ppermute x9, waiting for transfers between devices, exchange(): lax.ppermute(value, axis, [(i, partner(i, step, count)) for i in range(co...  14.7 us
    ppermute x9, starting transfers between devices, exchange(): lax.ppermute(value, axis, [(i, partner(i, step, count)) for i in range(co...  14.7 us
    ppermute x7, starting transfers between devices, body(): lax.ppermute(outs[s], axes, [(i, (i + s) % parts) for i in range(parts)])  9.8 us
    pallas_call x1, Pallas kernels, scan(): pl.pallas_call(functools.partial(scan_kernel, taps), out_shape=jax.ShapeD...  6.66 us
    pallas_call x1, Pallas kernels, fetch(): pl.pallas_call(functools.partial(fetch_kernel, parts, half_rows), out_sha...  5.82 us
    ppermute x3, starting transfers between devices, rotate(): lax.ppermute(value, axis, [(i, (i + steps) % count) for i in range(count)])  3.82 us
    ppermute x2, waiting for transfers between devices, swap(): lax.ppermute(value, 'doc', [(i, i + 1 - 2 * (i % 2)) for i in range(count)])  3.67 us
  transfers between devices with their start and end apart: 21, of which 10 were waited for; matrix products, arithmetic and copies ran while one was open for 5% of the time, Pallas kernels for 13%

profile of v12, /device:TPU:0, one launch (start us, length us, event | category | flops | bytes accessed | tf_op | source)
XLA Modules:
  0.0 93.4 jit_solution(3812288647351783147)
XLA Ops:
  0.0 1.0 %slice_bitcast_fusion = (bf16[32,2048]{1,0:T(8,128)(2,1)S(1)}, bf16[32,2048]{1,0:T(8,128)(2,1)S(1)}) fusion(bf16[2,32,2048]{2,1,0:T(8,128)(2,1)} %param.18), kind=kLoop, calls=%fused_computation.4 | loop fusion | bytes 524288 | tf_op jit(solution)/shard_map/squeeze | solution.py:662
  1.0 5.1 %collective-permute-start.2 = (bf16[32,2048]{1,0:T(8,128)(2,1)S(1)}, bf16[32,2048]{1,0:T(8,128)(2,1)S(1)}, u32[]{:S(2)}, u32[]{:S(2)}) collective-permute-start(bf16[32,2048]{1,0:T(8,128)(2,1)S(1)} %get-tuple-element.72.refs_0_), channel_id=1, source_target_pairs={{0,24},{8,16},{16,8},{24,0},{1,25},{9,17},{17,9},{25,1},{2,26},{10... | collective-permute-start | bytes 393224 | tf_op jit(solution)/shard_map/ppermute | solution.py:41
  6.1 0.0 collective-permute-start.1
  6.1 0.6 collective-permute-start
  6.7 0.7 convert_element_type.13
  7.4 0.1 copy.20
  7.5 1.7 %collective-permute-start.4 = (bf16[16,128]{1,0:T(8,128)(2,1)S(1)}, bf16[16,128]{1,0:T(8,128)(2,1)S(1)}, u32[]{:S(2)}, u32[]{:S(2)}) collective-permute-start(bf16[16,128]{1,0:T(8,128)(2,1)S(1)} %pad.14.routes), channel_id=1, source_target_pairs={{0,4},{4,0},{1,5},{5,1},{2,6},{6,2},{3,7},{7,3},{8,12},{12,8},{9,1... | collective-permute-start | bytes 12296 | tf_op jit(solution)/shard_map/ppermute | solution.py:27
  9.2 0.1 stack.93
  9.3 0.1 pad_add_fusion.spots
  9.4 0.8 constant_dynamic-slice_fusion
  10.2 0.1 pad_add_fusion.1.places
  10.3 0.1 concatenate.38.places
  10.4 0.7 pad.12.router
  11.2 0.7 pad.13.gain
  11.9 0.1 stack.85.targets
  12.0 1.6 %concatenate.37.params = f32[16,2048]{1,0:T(8,128)S(1)} concatenate(f32[4,2048]{1,0:T(4,128)} %param.21, f32[1,2048]{1,0:T(1,128)} %bitcast.33, f32[1,2048]{1,0:T(1,128)} %bitcast.34, f32[1,2048]{1,0:T(1,128)} %bitcast.35, f32[1,2048]{1,0:T(1,128)S(1)} %slice.33, f32[5,2048]{1,0:T(8,128)S(1)} %broadcast_in_dim.24, bf16[3,2048]{1,0:T(4,128)(2,1)} %param.19), dimensions={0} | concatenate | bytes 249856 | tf_op jit(solution)/shard_map/concatenate | solution.py:685
  13.6 0.0 collective-permute-done.4
  13.6 0.0 collective-permute-done.2.refs_3_
  13.6 3.6 %collective-permute-done.1.refs_2_ = bf16[32,2048]{1,0:T(8,128)(2,1)S(1)} collective-permute-done((bf16[32,2048]{1,0:T(8,128)(2,1)S(1)}, bf16[32,2048]{1,0:T(8,128)(2,1)S(1)}, u32[]{:S(2)}, u32[]{:S(2)}) %collective-permute-start.1) | collective-permute-done | bytes 131104 | tf_op jit(solution)/shard_map/ppermute | solution.py:41
  17.2 0.0 collective-permute-done.refs_1_
  17.2 2.1 %activate.1 = (bf16[128,2048]{1,0:T(8,128)(2,1)S(1)}, f32[160,128]{1,0:T(8,128)S(1)}) custom-call(s32[4]{0:T(128)S(1)} %pad_add_fusion.1.places, f32[16,2048]{1,0:T(8,128)S(1)} %concatenate.37.params, bf16[160,2048]{1,0:T(8,128)(2,1)} %select.44, bf16[32,2048]{1,0:T(8,128)(2,1)S(1)} %get-tuple-element.72.refs_0_, ...), custom_call_target="tpu_custom_call" | custom-call | flops 83886080 | bytes 1048576 | tf_op jit(solution)/shard_map/activate/pallas_call | solution.py:120
  19.3 1.6 %collective-permute-start.3 = (f32[160,128]{1,0:T(8,128)S(1)}, f32[160,128]{1,0:T(8,128)S(1)}, u32[]{:S(2)}, u32[]{:S(2)}) collective-permute-start(f32[160,128]{1,0:T(8,128)S(1)} %get-tuple-element.43.own), channel_id=1, source_target_pairs={{0,4},{4,0},{1,5},{5,1},{2,6},{6,2},{3,7},{7,3},{8,12},{12,8},{9,1... | collective-permute-start | bytes 245768 | tf_op jit(solution)/shard_map/ppermute | solution.py:27
  21.0 0.1 collective-permute-start.5
  21.0 3.0 %collective-permute-start.6 = (bf16[32,2432]{1,0:T(8,128)(2,1)S(1)}, bf16[32,2432]{1,0:T(8,128)(2,1)S(1)}, u32[]{:S(2)}, u32[]{:S(2)}) collective-permute-start(bf16[32,2432]{1,0:T(8,128)(2,1)S(1)} %get-tuple-element.46), channel_id=1, source_target_pairs={{0,16},{8,24},{16,0},{24,8},{1,17},{9,25},{17,1},{25,9},{2,18},{10... | collective-permute-start | bytes 466952 | tf_op jit(solution)/shard_map/ppermute | solution.py:41
  24.1 1.3 %collective-permute-start.7 = (bf16[32,2432]{1,0:T(8,128)(2,1)S(1)}, bf16[32,2432]{1,0:T(8,128)(2,1)S(1)}, u32[]{:S(2)}, u32[]{:S(2)}) collective-permute-start(bf16[32,2432]{1,0:T(8,128)(2,1)S(1)} %get-tuple-element.47), channel_id=1, source_target_pairs={{0,24},{8,16},{16,8},{24,0},{1,25},{9,17},{17,9},{25,1},{2,26},{10... | collective-permute-start | bytes 466952 | tf_op jit(solution)/shard_map/ppermute | solution.py:41
  25.4 0.0 collective-permute-done.3.other
  25.4 6.7 %scan.1.value_in = f32[128,2048]{1,0:T(8,128)S(1)} custom-call(f32[160,128]{1,0:T(8,128)S(1)} %get-tuple-element.43.own, f32[160,128]{1,0:T(8,128)S(1)} %collective-permute-done.3.other, bf16[128,2048]{1,0:T(8,128)(2,1)S(1)} %get-tuple-element.44.active, f32[16,2048]{1,0:T(8,128)S(1)} %concatenate.37.params, f32[16,2048]{1,0:T(8,128)} %log_rate_hbm.1, ...), custom_call_target="tpu_custom_call" | custom-call | flops 12582912000 | bytes 2097152 | tf_op jit(solution)/shard_map/scan/pallas_call | solution.py:242
  32.1 0.0 collective-permute-done.5.refs_1_
  32.1 2.9 %collective-permute-done.6.refs_2_ = bf16[32,2432]{1,0:T(8,128)(2,1)S(1)} collective-permute-done((bf16[32,2432]{1,0:T(8,128)(2,1)S(1)}, bf16[32,2432]{1,0:T(8,128)(2,1)S(1)}, u32[]{:S(2)}, u32[]{:S(2)}) %collective-permute-start.6) | collective-permute-done | bytes 155680 | tf_op jit(solution)/shard_map/ppermute | solution.py:41
  35.0 0.0 collective-permute-done.7.refs_3_
  35.0 2.6 %project.1 = (bf16[128,512]{1,0:T(8,128)(2,1)S(1)}, bf16[128,128]{1,0:T(8,128)(2,1)S(1)}) custom-call(s32[5]{0:T(128)S(1)} %concatenate.38.places, f32[128,2048]{1,0:T(8,128)S(1)} %scan.1.value_in, bf16[2048,512]{1,0:T(8,128)(2,1)} %weight_hbm.1, bf16[32,2432]{1,0:T(8,128)(2,1)S(1)} %get-tuple-element.76.refs_0_, ...), custom_call_target="tpu_custom_call" | custom-call | flops 268435456 | bytes 2097152 | tf_op jit(solution)/shard_map/project/pallas_call | solution.py:310
  37.7 0.6 collective-permute-start.8
  38.2 5.8 %fetch.1 = (bf16[1792,2048]{1,0:T(8,128)(2,1)S(1)}, bf16[1792,2048]{1,0:T(8,128)(2,1)S(1)}, s32[1]{0:T(128)}) custom-call(s32[1]{0:T(128)} %bitcast.28.half, bf16[7168,2048]{1,0:T(8,128)(2,1)} %gate.1, bf16[7168,2048]{1,0:T(8,128)(2,1)} %up.1), custom_call_target="tpu_custom_call" | custom-call | bytes 29360128 | tf_op jit(solution)/shard_map/fetch/pallas_call | solution.py:431
  44.1 0.0 collective-permute-done.8.summand
  44.1 2.5 %collective-permute-start.11 = (bf16[128,512]{1,0:T(8,128)(2,1)S(1)}, bf16[128,512]{1,0:T(8,128)(2,1)S(1)}, u32[]{:S(2)}, u32[]{:S(2)}) collective-permute-start(bf16[128,512]{1,0:T(8,128)(2,1)S(1)} %mix.1.refs_0_), channel_id=1, source_target_pairs={{0,24},{8,16},{16,8},{24,0},{1,25},{9,17},{17,9},{25,1},{2,26},{10... | collective-permute-start | bytes 393224 | tf_op jit(solution)/shard_map/ppermute | solution.py:41
  46.6 1.4 %collective-permute-start.10 = (bf16[128,512]{1,0:T(8,128)(2,1)S(1)}, bf16[128,512]{1,0:T(8,128)(2,1)S(1)}, u32[]{:S(2)}, u32[]{:S(2)}) collective-permute-start(bf16[128,512]{1,0:T(8,128)(2,1)S(1)} %mix.1.refs_0_), channel_id=1, source_target_pairs={{0,16},{8,24},{16,0},{24,8},{1,17},{9,25},{17,1},{25,9},{2,18},{10... | collective-permute-start | bytes 393224 | tf_op jit(solution)/shard_map/ppermute | solution.py:41
  48.0 0.5 collective-permute-start.9
  48.6 3.8 %collective-permute-done.11.refs_3_ = bf16[128,512]{1,0:T(8,128)(2,1)S(1)} collective-permute-done((bf16[128,512]{1,0:T(8,128)(2,1)S(1)}, bf16[128,512]{1,0:T(8,128)(2,1)S(1)}, u32[]{:S(2)}, u32[]{:S(2)}) %collective-permute-start.11) | collective-permute-done | bytes 131104 | tf_op jit(solution)/shard_map/ppermute | solution.py:41
  52.3 4.4 %collective-permute-done.10.refs_2_ = bf16[128,512]{1,0:T(8,128)(2,1)S(1)} collective-permute-done((bf16[128,512]{1,0:T(8,128)(2,1)S(1)}, bf16[128,512]{1,0:T(8,128)(2,1)S(1)}, u32[]{:S(2)}, u32[]{:S(2)}) %collective-permute-start.10) | collective-permute-done | bytes 131104 | tf_op jit(solution)/shard_map/ppermute | solution.py:41
  56.8 0.0 collective-permute-done.9.refs_1_
  56.8 1.8 %norm.1 = (bf16[128,2048]{1,0:T(8,128)(2,1)S(1)}, f32[128,128]{1,0:T(8,128)S(1)}, bf16[16,2048]{1,0:T(8,128)(2,1)S(1)}) custom-call(s32[4]{0:T(128)S(1)} %pad_add_fusion.1.places, s32[2]{0:T(128)S(1)} %pad_add_fusion.spots, f32[8,2048]{1,0:T(8,128)S(1)} %pad.13.gain, bf16[16,2048]{1,0:T(8,128)(2,1)S(1)} %pad.12.router, ...), custom_call_target="tpu_custom_call" | custom-call | tf_op jit(solution)/shard_map/norm/pallas_call | solution.py:389
  58.6 0.1 collective-permute-start.12
  58.7 1.9 %collective-permute-done.12.other = bf16[128,2048]{1,0:T(8,128)(2,1)S(1)} collective-permute-done((bf16[128,2048]{1,0:T(8,128)(2,1)S(1)}, bf16[128,2048]{1,0:T(8,128)(2,1)S(1)}, u32[]{:S(2)}, u32[]{:S(2)}) %collective-permute-start.12) | collective-permute-done | bytes 524320 | tf_op jit(solution)/shard_map/ppermute | solution.py:67
  60.6 14.8 %experts.1 = (f32[128,2048]{1,0:T(8,128)S(1)}, bf16[128,2048]{1,0:T(8,128)(2,1)S(1)}) custom-call(s32[1]{0:T(128)} %get-tuple-element.56.half, bf16[128,2048]{1,0:T(8,128)(2,1)S(1)} %get-tuple-element.57.own, bf16[128,2048]{1,0:T(8,128)(2,1)S(1)} %collective-permute-done.12.other, bf16[1792,2048]{1,0:T(8,128)(2,1)S(1)} %get-tuple-element.58.gate_first, ...), custom_call_target="tpu_custom_call" | custom-call | flops 11274289152 | bytes 29360128 | tf_op jit(solution)/shard_map/experts/pallas_call | solution.py:485
  75.4 0.2 collective-permute-start.13
  75.6 1.8 %collective-permute-done.13.other = bf16[128,2048]{1,0:T(8,128)(2,1)S(1)} collective-permute-done((bf16[128,2048]{1,0:T(8,128)(2,1)S(1)}, bf16[128,2048]{1,0:T(8,128)(2,1)S(1)}, u32[]{:S(2)}, u32[]{:S(2)}) %collective-permute-start.13) | collective-permute-done | bytes 524320 | tf_op jit(solution)/shard_map/ppermute | solution.py:67
  77.4 1.2 %combine.1 = (bf16[16,1280]{1,0:T(8,128)(2,1)S(1)}, bf16[16,1280]{1,0:T(8,128)(2,1)S(1)}, bf16[16,1280]{1,0:T(8,128)(2,1)S(1)}, bf16[16,1280]{1,0:T(8,128)(2,1)S...) custom-call(s32[8]{0:T(128)S(1)} %stack.85.targets, ...), custom_call_target="tpu_custom_call" | custom-call | tf_op jit(solution)/shard_map/combine/pallas_call | solution.py:586
  78.6 1.6 %collective-permute-start.14 = (bf16[16,1280]{1,0:T(8,128)(2,1)S(1)}, bf16[16,1280]{1,0:T(8,128)(2,1)S(1)}, u32[]{:S(2)}, u32[]{:S(2)}) collective-permute-start(bf16[16,1280]{1,0:T(8,128)(2,1)S(1)} %get-tuple-element.64), channel_id=1, source_target_pairs={{0,4},{4,8},{8,12},{12,16},{16,20},{20,24},{24,28},{28,0},{1,5},{5... | collective-permute-start | bytes 122888 | tf_op jit(solution)/shard_map/ppermute | solution.py:731
  80.2 0.0 collective-permute-start.15
  80.2 2.3 %collective-permute-start.16 = (bf16[16,1280]{1,0:T(8,128)(2,1)S(1)}, bf16[16,1280]{1,0:T(8,128)(2,1)S(1)}, u32[]{:S(2)}, u32[]{:S(2)}) collective-permute-start(bf16[16,1280]{1,0:T(8,128)(2,1)S(1)} %get-tuple-element.66), channel_id=1, source_target_pairs={{0,12},{4,16},{8,20},{12,24},{16,28},{20,0},{24,4},{28,8},{1,13},{... | collective-permute-start | bytes 122888 | tf_op jit(solution)/shard_map/ppermute | solution.py:731
  82.5 1.6 %collective-permute-start.17 = (bf16[16,1280]{1,0:T(8,128)(2,1)S(1)}, bf16[16,1280]{1,0:T(8,128)(2,1)S(1)}, u32[]{:S(2)}, u32[]{:S(2)}) collective-permute-start(bf16[16,1280]{1,0:T(8,128)(2,1)S(1)} %get-tuple-element.67), channel_id=1, source_target_pairs={{0,16},{4,20},{8,24},{12,28},{16,0},{20,4},{24,8},{28,12},{1,17},{... | collective-permute-start | bytes 122888 | tf_op jit(solution)/shard_map/ppermute | solution.py:731
  84.1 2.3 %collective-permute-start.18 = (bf16[16,1280]{1,0:T(8,128)(2,1)S(1)}, bf16[16,1280]{1,0:T(8,128)(2,1)S(1)}, u32[]{:S(2)}, u32[]{:S(2)}) collective-permute-start(bf16[16,1280]{1,0:T(8,128)(2,1)S(1)} %get-tuple-element.68), channel_id=1, source_target_pairs={{0,20},{4,24},{8,28},{12,0},{16,4},{20,8},{24,12},{28,16},{1,21},{... | collective-permute-start | bytes 122888 | tf_op jit(solution)/shard_map/ppermute | solution.py:731
  86.4 0.0 collective-permute-done.14.refs_1_
  86.4 1.4 %collective-permute-start.19 = (bf16[16,1280]{1,0:T(8,128)(2,1)S(1)}, bf16[16,1280]{1,0:T(8,128)(2,1)S(1)}, u32[]{:S(2)}, u32[]{:S(2)}) collective-permute-start(bf16[16,1280]{1,0:T(8,128)(2,1)S(1)} %get-tuple-element.69), channel_id=1, source_target_pairs={{0,24},{4,28},{8,0},{12,4},{16,8},{20,12},{24,16},{28,20},{1,25},{... | collective-permute-start | bytes 122888 | tf_op jit(solution)/shard_map/ppermute | solution.py:731
  87.8 0.0 collective-permute-done.15.refs_2_
  87.8 0.6 collective-permute-start.20
  88.4 0.0 collective-permute-done.16.refs_3_
  88.4 0.2 collective-permute-done.17.refs_4_
  88.6 0.9 %collective-permute-done.18.refs_5_ = bf16[16,1280]{1,0:T(8,128)(2,1)S(1)} collective-permute-done((bf16[16,1280]{1,0:T(8,128)(2,1)S(1)}, bf16[16,1280]{1,0:T(8,128)(2,1)S(1)}, u32[]{:S(2)}, u32[]{:S(2)}) %collective-permute-start.18) | collective-permute-done | bytes 40992 | tf_op jit(solution)/shard_map/ppermute | solution.py:731
  89.5 0.8 collective-permute-done.19.refs_6_
  90.4 1.4 %collective-permute-done.20.refs_7_ = bf16[16,1280]{1,0:T(8,128)(2,1)S(1)} collective-permute-done((bf16[16,1280]{1,0:T(8,128)(2,1)S(1)}, bf16[16,1280]{1,0:T(8,128)(2,1)S(1)}, u32[]{:S(2)}, u32[]{:S(2)}) %collective-permute-start.20) | collective-permute-done | bytes 40992 | tf_op jit(solution)/shard_map/ppermute | solution.py:731
  91.8 1.6 %unpack.1 = bf16[16,2048]{1,0:T(8,128)(2,1)} custom-call(s32[8]{0:T(128)S(1)} %and_select_fusion.named_by, bf16[16,2048]{1,0:T(8,128)(2,1)S(1)} %get-tuple-element.54.mixed, bf16[16,128]{1,0:T(8,128)(2,1)S(1)} %pad.14.routes, bf16[16,1280]{1,0:T(8,128)(2,1)S(1)} %get-tuple-element.63.refs_0_, bf16[16,1280]{1,0:T(8,128)(2,1)S(1)} %collective-permute-done.14.refs_1_, ...), custom_call_target="tpu_custom_call" | custom-call | tf_op jit(solution)/shard_map/unpack/pallas_call | solution.py:628
  (7 shorter events, 0.1 us)
Async XLA Ops:
  1.0 12.6 %collective-permute-start.2 = (bf16[32,2048]{1,0:T(8,128)(2,1)S(1)}, bf16[32,2048]{1,0:T(8,128)(2,1)S(1)}, u32[]{:S(2)}, u32[]{:S(2)}) collective-permute-start(bf16[32,2048]{1,0:T(8,128)(2,1)S(1)} %get-tuple-element.72.refs_0_), channel_id=1, source_target_pairs={{0,24},{8,16},{16,8},{24,0},{1,25},{9,17},{17,9},{25,1},{2,26},{10... | collective-permute-start | bytes 393224 | tf_op jit(solution)/shard_map/ppermute | solution.py:41
  6.1 11.1 %collective-permute-start.1 = (bf16[32,2048]{1,0:T(8,128)(2,1)S(1)}, bf16[32,2048]{1,0:T(8,128)(2,1)S(1)}, u32[]{:S(2)}, u32[]{:S(2)}) collective-permute-start(bf16[32,2048]{1,0:T(8,128)(2,1)S(1)} %get-tuple-element.72.refs_0_), channel_id=1, source_target_pairs={{0,16},{8,24},{16,0},{24,8},{1,17},{9,25},{17,1},{25,9},{2,18},{10... | collective-permute-start | bytes 393224 | tf_op jit(solution)/shard_map/ppermute | solution.py:41
  6.1 11.1 %collective-permute-start = (bf16[32,2048]{1,0:T(8,128)(2,1)S(1)}, bf16[32,2048]{1,0:T(8,128)(2,1)S(1)}, u32[]{:S(2)}, u32[]{:S(2)}) collective-permute-start(bf16[32,2048]{1,0:T(8,128)(2,1)S(1)} %get-tuple-element.72.refs_0_), channel_id=1, source_target_pairs={{0,8},{8,0},{16,24},{24,16},{1,9},{9,1},{17,25},{25,17},{2,10},{10... | collective-permute-start | bytes 393224 | tf_op jit(solution)/shard_map/ppermute | solution.py:41
  7.5 6.0 %collective-permute-start.4 = (bf16[16,128]{1,0:T(8,128)(2,1)S(1)}, bf16[16,128]{1,0:T(8,128)(2,1)S(1)}, u32[]{:S(2)}, u32[]{:S(2)}) collective-permute-start(bf16[16,128]{1,0:T(8,128)(2,1)S(1)} %pad.14.routes), channel_id=1, source_target_pairs={{0,4},{4,0},{1,5},{5,1},{2,6},{6,2},{3,7},{7,3},{8,12},{12,8},{9,1... | collective-permute-start | bytes 12296 | tf_op jit(solution)/shard_map/ppermute | solution.py:27
  19.3 6.1 %collective-permute-start.3 = (f32[160,128]{1,0:T(8,128)S(1)}, f32[160,128]{1,0:T(8,128)S(1)}, u32[]{:S(2)}, u32[]{:S(2)}) collective-permute-start(f32[160,128]{1,0:T(8,128)S(1)} %get-tuple-element.43.own), channel_id=1, source_target_pairs={{0,4},{4,0},{1,5},{5,1},{2,6},{6,2},{3,7},{7,3},{8,12},{12,8},{9,1... | collective-permute-start | bytes 245768 | tf_op jit(solution)/shard_map/ppermute | solution.py:27
  21.0 11.1 %collective-permute-start.5 = (bf16[32,2432]{1,0:T(8,128)(2,1)S(1)}, bf16[32,2432]{1,0:T(8,128)(2,1)S(1)}, u32[]{:S(2)}, u32[]{:S(2)}) collective-permute-start(bf16[32,2432]{1,0:T(8,128)(2,1)S(1)} %get-tuple-element.45), channel_id=1, source_target_pairs={{0,8},{8,0},{16,24},{24,16},{1,9},{9,1},{17,25},{25,17},{2,10},{10... | collective-permute-start | bytes 466952 | tf_op jit(solution)/shard_map/ppermute | solution.py:41
  21.0 14.0 %collective-permute-start.6 = (bf16[32,2432]{1,0:T(8,128)(2,1)S(1)}, bf16[32,2432]{1,0:T(8,128)(2,1)S(1)}, u32[]{:S(2)}, u32[]{:S(2)}) collective-permute-start(bf16[32,2432]{1,0:T(8,128)(2,1)S(1)} %get-tuple-element.46), channel_id=1, source_target_pairs={{0,16},{8,24},{16,0},{24,8},{1,17},{9,25},{17,1},{25,9},{2,18},{10... | collective-permute-start | bytes 466952 | tf_op jit(solution)/shard_map/ppermute | solution.py:41
  24.1 11.0 %collective-permute-start.7 = (bf16[32,2432]{1,0:T(8,128)(2,1)S(1)}, bf16[32,2432]{1,0:T(8,128)(2,1)S(1)}, u32[]{:S(2)}, u32[]{:S(2)}) collective-permute-start(bf16[32,2432]{1,0:T(8,128)(2,1)S(1)} %get-tuple-element.47), channel_id=1, source_target_pairs={{0,24},{8,16},{16,8},{24,0},{1,25},{9,17},{17,9},{25,1},{2,26},{10... | collective-permute-start | bytes 466952 | tf_op jit(solution)/shard_map/ppermute | solution.py:41
  37.7 6.4 %collective-permute-start.8 = (bf16[128,512]{1,0:T(8,128)(2,1)S(1)}, bf16[128,512]{1,0:T(8,128)(2,1)S(1)}, u32[]{:S(2)}, u32[]{:S(2)}) collective-permute-start(bf16[128,512]{1,0:T(8,128)(2,1)S(1)} %get-tuple-element.53.base), channel_id=1, source_target_pairs={{0,4},{4,0},{1,5},{5,1},{2,6},{6,2},{3,7},{7,3},{8,12},{12,8},{9,1... | collective-permute-start | bytes 393224 | tf_op jit(solution)/shard_map/ppermute | solution.py:27
  44.1 8.2 %collective-permute-start.11 = (bf16[128,512]{1,0:T(8,128)(2,1)S(1)}, bf16[128,512]{1,0:T(8,128)(2,1)S(1)}, u32[]{:S(2)}, u32[]{:S(2)}) collective-permute-start(bf16[128,512]{1,0:T(8,128)(2,1)S(1)} %mix.1.refs_0_), channel_id=1, source_target_pairs={{0,24},{8,16},{16,8},{24,0},{1,25},{9,17},{17,9},{25,1},{2,26},{10... | collective-permute-start | bytes 393224 | tf_op jit(solution)/shard_map/ppermute | solution.py:41
  46.6 10.1 %collective-permute-start.10 = (bf16[128,512]{1,0:T(8,128)(2,1)S(1)}, bf16[128,512]{1,0:T(8,128)(2,1)S(1)}, u32[]{:S(2)}, u32[]{:S(2)}) collective-permute-start(bf16[128,512]{1,0:T(8,128)(2,1)S(1)} %mix.1.refs_0_), channel_id=1, source_target_pairs={{0,16},{8,24},{16,0},{24,8},{1,17},{9,25},{17,1},{25,9},{2,18},{10... | collective-permute-start | bytes 393224 | tf_op jit(solution)/shard_map/ppermute | solution.py:41
  48.0 8.8 %collective-permute-start.9 = (bf16[128,512]{1,0:T(8,128)(2,1)S(1)}, bf16[128,512]{1,0:T(8,128)(2,1)S(1)}, u32[]{:S(2)}, u32[]{:S(2)}) collective-permute-start(bf16[128,512]{1,0:T(8,128)(2,1)S(1)} %mix.1.refs_0_), channel_id=1, source_target_pairs={{0,8},{8,0},{16,24},{24,16},{1,9},{9,1},{17,25},{25,17},{2,10},{10... | collective-permute-start | bytes 393224 | tf_op jit(solution)/shard_map/ppermute | solution.py:41
  58.6 2.0 %collective-permute-start.12 = (bf16[128,2048]{1,0:T(8,128)(2,1)S(1)}, bf16[128,2048]{1,0:T(8,128)(2,1)S(1)}, u32[]{:S(2)}, u32[]{:S(2)}) collective-permute-start(bf16[128,2048]{1,0:T(8,128)(2,1)S(1)} %get-tuple-element.57.own), channel_id=1, source_target_pairs={{0,1},{1,0},{2,3},{3,2},{4,5},{5,4},{6,7},{7,6},{8,9},{9,8},{10,11... | collective-permute-start | bytes 1572872 | tf_op jit(solution)/shard_map/ppermute | solution.py:67
  75.4 2.0 %collective-permute-start.13 = (bf16[128,2048]{1,0:T(8,128)(2,1)S(1)}, bf16[128,2048]{1,0:T(8,128)(2,1)S(1)}, u32[]{:S(2)}, u32[]{:S(2)}) collective-permute-start(bf16[128,2048]{1,0:T(8,128)(2,1)S(1)} %get-tuple-element.61), channel_id=1, source_target_pairs={{0,1},{1,0},{2,3},{3,2},{4,5},{5,4},{6,7},{7,6},{8,9},{9,8},{10,11... | collective-permute-start | bytes 1572872 | tf_op jit(solution)/shard_map/ppermute | solution.py:67
  78.6 7.8 %collective-permute-start.14 = (bf16[16,1280]{1,0:T(8,128)(2,1)S(1)}, bf16[16,1280]{1,0:T(8,128)(2,1)S(1)}, u32[]{:S(2)}, u32[]{:S(2)}) collective-permute-start(bf16[16,1280]{1,0:T(8,128)(2,1)S(1)} %get-tuple-element.64), channel_id=1, source_target_pairs={{0,4},{4,8},{8,12},{12,16},{16,20},{20,24},{24,28},{28,0},{1,5},{5... | collective-permute-start | bytes 122888 | tf_op jit(solution)/shard_map/ppermute | solution.py:731
  80.2 7.7 %collective-permute-start.15 = (bf16[16,1280]{1,0:T(8,128)(2,1)S(1)}, bf16[16,1280]{1,0:T(8,128)(2,1)S(1)}, u32[]{:S(2)}, u32[]{:S(2)}) collective-permute-start(bf16[16,1280]{1,0:T(8,128)(2,1)S(1)} %get-tuple-element.65), channel_id=1, source_target_pairs={{0,8},{4,12},{8,16},{12,20},{16,24},{20,28},{24,0},{28,4},{1,9},{5... | collective-permute-start | bytes 122888 | tf_op jit(solution)/shard_map/ppermute | solution.py:731
  80.2 8.2 %collective-permute-start.16 = (bf16[16,1280]{1,0:T(8,128)(2,1)S(1)}, bf16[16,1280]{1,0:T(8,128)(2,1)S(1)}, u32[]{:S(2)}, u32[]{:S(2)}) collective-permute-start(bf16[16,1280]{1,0:T(8,128)(2,1)S(1)} %get-tuple-element.66), channel_id=1, source_target_pairs={{0,12},{4,16},{8,20},{12,24},{16,28},{20,0},{24,4},{28,8},{1,13},{... | collective-permute-start | bytes 122888 | tf_op jit(solution)/shard_map/ppermute | solution.py:731
  82.5 6.1 %collective-permute-start.17 = (bf16[16,1280]{1,0:T(8,128)(2,1)S(1)}, bf16[16,1280]{1,0:T(8,128)(2,1)S(1)}, u32[]{:S(2)}, u32[]{:S(2)}) collective-permute-start(bf16[16,1280]{1,0:T(8,128)(2,1)S(1)} %get-tuple-element.67), channel_id=1, source_target_pairs={{0,16},{4,20},{8,24},{12,28},{16,0},{20,4},{24,8},{28,12},{1,17},{... | collective-permute-start | bytes 122888 | tf_op jit(solution)/shard_map/ppermute | solution.py:731
  84.1 5.5 %collective-permute-start.18 = (bf16[16,1280]{1,0:T(8,128)(2,1)S(1)}, bf16[16,1280]{1,0:T(8,128)(2,1)S(1)}, u32[]{:S(2)}, u32[]{:S(2)}) collective-permute-start(bf16[16,1280]{1,0:T(8,128)(2,1)S(1)} %get-tuple-element.68), channel_id=1, source_target_pairs={{0,20},{4,24},{8,28},{12,0},{16,4},{20,8},{24,12},{28,16},{1,21},{... | collective-permute-start | bytes 122888 | tf_op jit(solution)/shard_map/ppermute | solution.py:731
  86.4 4.0 %collective-permute-start.19 = (bf16[16,1280]{1,0:T(8,128)(2,1)S(1)}, bf16[16,1280]{1,0:T(8,128)(2,1)S(1)}, u32[]{:S(2)}, u32[]{:S(2)}) collective-permute-start(bf16[16,1280]{1,0:T(8,128)(2,1)S(1)} %get-tuple-element.69), channel_id=1, source_target_pairs={{0,24},{4,28},{8,0},{12,4},{16,8},{20,12},{24,16},{28,20},{1,25},{... | collective-permute-start | bytes 122888 | tf_op jit(solution)/shard_map/ppermute | solution.py:731
  87.8 4.0 %collective-permute-start.20 = (bf16[16,1280]{1,0:T(8,128)(2,1)S(1)}, bf16[16,1280]{1,0:T(8,128)(2,1)S(1)}, u32[]{:S(2)}, u32[]{:S(2)}) collective-permute-start(bf16[16,1280]{1,0:T(8,128)(2,1)S(1)} %get-tuple-element.70), channel_id=1, source_target_pairs={{0,28},{4,0},{8,4},{12,8},{16,12},{20,16},{24,20},{28,24},{1,29},{... | collective-permute-start | bytes 122888 | tf_op jit(solution)/shard_map/ppermute | solution.py:731
